TPU v7x, 32 devices: a whole 2x2x4 slice. The times are simulated.
32 devices in a mesh: ctx: 8 (over y, x, core), tp: 4 (over z).
Axes of the slice: x: 2, y: 2, z: 4, core: 2. Of those that a mesh axis runs over, the one named last changes fastest.
Arguments:
- tokens: bfloat16 [12288, 2048], P(('ctx', 'tp')), may hold values from -6 to 6
- teacher: bfloat16 [12288, 2048], P(('ctx', 'tp')), may hold values from -6 to 6
- seq_lens: int32 [3], replicated, may hold values from 1024 to 4096, as said below
- block_order: int32 [3, 16], replicated, may hold values from 0 to 15, each once within a row
- in_gain: float32 [2048], replicated, may hold values from 0.5 to 1.5
- w_query: bfloat16 [2048, 2048], P('ctx', 'tp'), may hold values from -0.125 to 0.125
- key_weight_matrix: bfloat16 [2048, 1024], P('ctx', 'tp'), may hold values from -0.125 to 0.125
- value_weight_matrix: bfloat16 [2048, 1024], P('ctx', 'tp'), may hold values from -0.125 to 0.125
- q_gain: float32 [128], replicated, may hold values from 0.5 to 1.5
- k_gain: float32 [128], replicated, may hold values from 0.5 to 1.5
- w_out: bfloat16 [2048, 2048], P('tp', 'ctx'), may hold values from -1 to 1
- post_gain: float32 [2048], replicated, may hold values from 0.5 to 1.5
- w_gate: bfloat16 [2048, 6144], P('ctx', 'tp'), may hold values from -0.125 to 0.125
- w_up: bfloat16 [2048, 6144], P('ctx', 'tp'), may hold values from -0.125 to 0.125
- w_down: bfloat16 [6144, 2048], P('tp', 'ctx'), may hold values from -0.078125 to 0.078125
Outputs:
- output: bfloat16 [12288, 2048], P(('ctx', 'tp'))
- loss: float32 [], replicated
- d_tokens: bfloat16 [12288, 2048], P(('ctx', 'tp'))
- grad_in_gain: float32 [2048], replicated
- grad_w_query: float32 [2048, 2048], P('ctx', 'tp')
- grad_w_key: float32 [2048, 1024], P('ctx', 'tp')
- grad_w_value: float32 [2048, 1024], P('ctx', 'tp')
- grad_q_gain: float32 [128], replicated
- grad_k_gain: float32 [128], replicated
- grad_w_out: float32 [2048, 2048], P('tp', 'ctx')
- grad_post_gain: float32 [2048], replicated
- grad_w_gate: float32 [2048, 6144], P('ctx', 'tp')
- grad_w_up: float32 [2048, 6144], P('ctx', 'tp')
- grad_w_down: float32 [6144, 2048], P('tp', 'ctx')
Inputs may be any that keep to these rules, and one draw needn't show every extreme that they name: `seq_lens`: one sequence, drawn from the seed, has all 4096 slots valid. `block_order`: each row names every block of its sequence once.
All inputs are finite; a program needn't handle non-finite values.
Results may differ from a plain program's by a relative error of at most 0.024.
Values may be sent and summed in bfloat16 or wider, within the bound.
A program may use at most 256 MiB of HBM per device.

v0:
```python
import jax
import jax.numpy as jnp
from jax import lax
from jax.sharding import PartitionSpec as P

MODEL_WIDTH = 2048
HEAD_SIZE = 128
SEQS = 3
BLK = 256


EPS = 1e-06
THETA = 1000000.0
FLOOR = -1e30


def from_behind(x, axis, by):
    count = lax.axis_size(axis)
    return lax.ppermute(x, axis, [(i, (i + by) % count) for i in range(count)])


def rms_scale(value):
    return lax.rsqrt(jnp.mean(value * value, axis=-1, keepdims=True) + EPS)


def rms_back(value, scale, grad_normed):
    return scale * grad_normed - value * scale**3 * jnp.mean(
        grad_normed * value, axis=-1, keepdims=True
    )


def rotate(value, cosine, sine):
    half = value.shape[-1] // 2
    first = value[..., :half]
    second = value[..., half:]
    return jnp.concatenate(
        [first * cosine - second * sine, second * cosine + first * sine], axis=-1
    )


def rotate_back(grad, cosine, sine):
    half = grad.shape[-1] // 2
    first = grad[..., :half]
    second = grad[..., half:]
    return jnp.concatenate(
        [first * cosine + second * sine, second * cosine - first * sine], axis=-1
    )


def matmul(left, right):
    return jnp.dot(left, right, preferred_element_type=jnp.float32)


def matmul_tn(left, right):
    return lax.dot_general(
        left, right, (((0,), (0,)), ((), ())), preferred_element_type=jnp.float32
    )


def matmul_nt(left, right):
    return lax.dot_general(
        left, right, (((1,), (1,)), ((), ())), preferred_element_type=jnp.float32
    )


def row_slice(value, start, count):
    return lax.dynamic_slice_in_dim(value, start, count, 0)


def local(
    tokens,
    teacher,
    seq_lens,
    block_order,
    in_gain,
    w_query,
    key_weight_matrix,
    value_weight_matrix,
    q_gain,
    k_gain,
    w_out,
    post_gain,
    w_gate,
    w_up,
    w_down,
):
    ctx_count = lax.axis_size("ctx")
    ctx_index = lax.axis_index("ctx")
    tp_index = lax.axis_index("tp")
    tok_rows = tokens.shape[0]
    ctx_rows = tok_rows * lax.axis_size("tp")
    block_span = 2 * BLK
    q_heads = w_query.shape[1] // HEAD_SIZE
    kv_heads = key_weight_matrix.shape[1] // HEAD_SIZE
    group_width = q_heads // kv_heads
    scale_qk = HEAD_SIZE ** (-0.5)
    weights = (
        lax.all_gather(w_query, "ctx", axis=0, tiled=True),
        lax.all_gather(key_weight_matrix, "ctx", axis=0, tiled=True),
        lax.all_gather(value_weight_matrix, "ctx", axis=0, tiled=True),
        lax.all_gather(w_out, "ctx", axis=1, tiled=True),
        lax.all_gather(w_gate, "ctx", axis=0, tiled=True),
        lax.all_gather(w_up, "ctx", axis=0, tiled=True),
        lax.all_gather(w_down, "ctx", axis=1, tiled=True),
    )
    wq_full, wk_full, wv_full, wo_full, wg_full, wu_full, wd_full = weights
    offsets = jnp.arange(BLK, dtype=jnp.int32)

    def block_positions(owner):
        columns = lax.dynamic_slice_in_dim(block_order, 2 * owner, 2, 1)
        return (columns[:, :, None] * BLK + offsets).reshape(SEQS, block_span)

    query_pos = block_positions(ctx_index)
    flat_pos = query_pos.reshape(-1)
    inverse = THETA ** (-jnp.arange(0, HEAD_SIZE, 2, dtype=jnp.float32) / HEAD_SIZE)
    angle = flat_pos.astype(jnp.float32)[:, None] * inverse[None, :]
    cosine = jnp.cos(angle)[:, None, :]
    sine = jnp.sin(angle)[:, None, :]
    stream = tokens.astype(jnp.float32)
    scale_in = rms_scale(stream)
    unit_in = stream * scale_in
    normed_rows = (unit_in * in_gain).astype(jnp.bfloat16)
    normed_all = lax.all_gather(normed_rows, "tp", axis=0, tiled=True)
    query_lin = matmul(normed_all, wq_full).reshape(ctx_rows, q_heads, HEAD_SIZE)
    key_linear = matmul(normed_all, wk_full).reshape(ctx_rows, kv_heads, HEAD_SIZE)
    value_low = (
        matmul(normed_all, wv_full)
        .astype(jnp.bfloat16)
        .reshape(SEQS, block_span, kv_heads, HEAD_SIZE)
    )
    query_scale = rms_scale(query_lin)
    query_unit = query_lin * query_scale
    query_low = (
        rotate(query_unit * q_gain, cosine, sine)
        .astype(jnp.bfloat16)
        .reshape(SEQS, block_span, kv_heads, group_width, HEAD_SIZE)
    )
    key_scale = rms_scale(key_linear)
    key_unit = key_linear * key_scale
    key_low = (
        rotate(key_unit * k_gain, cosine, sine)
        .astype(jnp.bfloat16)
        .reshape(SEQS, block_span, kv_heads, HEAD_SIZE)
    )

    def scores_of(keys, key_pos):
        raw = (
            jnp.einsum("sqkgd,slkd->skgql", query_low, keys, preferred_element_type=jnp.float32)
            * scale_qk
        )
        allowed = (key_pos[:, None, :] <= query_pos[:, :, None]) & (
            key_pos[:, None, :] < seq_lens[:, None, None]
        )
        allowed = allowed[:, None, None, :, :]
        return (jnp.where(allowed, raw, FLOOR), allowed)

    def absorb(state, keys, value_rows, owner):
        running_top, running_total, running_acc = state
        scores, allowed = scores_of(keys, block_positions(owner))
        new_top = jnp.maximum(running_top, jnp.max(scores, axis=-1))
        weights_now = jnp.where(allowed, jnp.exp(scores - new_top[..., None]), 0.0)
        shrink = jnp.exp(running_top - new_top)
        running_total = running_total * shrink + jnp.sum(weights_now, axis=-1)
        running_acc = running_acc * shrink[..., None] + jnp.einsum(
            "skgql,slkd->skgqd",
            weights_now.astype(jnp.bfloat16),
            value_rows,
            preferred_element_type=jnp.float32,
        )
        return (new_top, running_total, running_acc)

    stat_shape = (SEQS, kv_heads, group_width, block_span)
    initial = (
        jnp.full(stat_shape, FLOOR, jnp.float32),
        jnp.zeros(stat_shape, jnp.float32),
        jnp.zeros(stat_shape + (HEAD_SIZE,), jnp.float32),
    )
    first_state = absorb(initial, key_low, value_low, ctx_index)

    def cycle_turn(carry, turn):
        keys, value_rows, state = carry
        keys, value_rows = from_behind((keys, value_rows), "ctx", 1)
        owner = (ctx_index - turn) % ctx_count
        state = absorb(state, keys, value_rows, owner)
        return ((keys, value_rows, state), (keys, value_rows))

    (unused_keys, unused_values, final_state), (kept_keys, kept_values) = lax.scan(
        cycle_turn, (key_low, value_low, first_state), jnp.arange(1, ctx_count, dtype=jnp.int32)
    )
    all_keys = jnp.concatenate([key_low[None], kept_keys], axis=0)
    all_values = jnp.concatenate([value_low[None], kept_values], axis=0)
    top_final, total_final, acc_final = final_state
    log_total = top_final + jnp.log(total_final)
    attn_exact = acc_final / total_final[..., None]
    mixed_low = (
        jnp.transpose(attn_exact, (0, 3, 1, 2, 4))
        .reshape(ctx_rows, q_heads * HEAD_SIZE)
        .astype(jnp.bfloat16)
    )
    middle = stream + lax.psum_scatter(
        matmul(row_slice(mixed_low, jnp.int32(0), lax.axis_size("tp") * tok_rows), wo_full).astype(
            jnp.bfloat16
        ),
        "tp",
        scatter_dimension=0,
        tiled=True,
    ).astype(jnp.float32)
    scale_post = rms_scale(middle)
    unit_post = middle * scale_post
    post_rows = (unit_post * post_gain).astype(jnp.bfloat16)
    post_all = lax.all_gather(post_rows, "tp", axis=0, tiled=True)
    gate = matmul(post_all, wg_full)
    up_val = matmul(post_all, wu_full)
    sigma = jax.nn.sigmoid(gate)
    active = gate * sigma
    hidden_low = (active * up_val).astype(jnp.bfloat16)
    result = middle + lax.psum_scatter(
        matmul(row_slice(hidden_low, jnp.int32(0), lax.axis_size("tp") * tok_rows), wd_full).astype(
            jnp.bfloat16
        ),
        "tp",
        scatter_dimension=0,
        tiled=True,
    ).astype(jnp.float32)
    output = result.astype(jnp.bfloat16)
    valid_all = (query_pos < seq_lens[:, None]).reshape(-1).astype(jnp.float32)
    valid_rows = row_slice(valid_all, tp_index * tok_rows, tok_rows)
    diff = (result - teacher.astype(jnp.float32)) * valid_rows[:, None]
    error_local = jnp.sum(diff * diff)
    diff_low = diff.astype(jnp.bfloat16)
    diff_all = lax.all_gather(diff_low, "tp", axis=0, tiled=True)
    weights_two = (
        lax.all_gather(w_query, "ctx", axis=0, tiled=True),
        lax.all_gather(key_weight_matrix, "ctx", axis=0, tiled=True),
        lax.all_gather(value_weight_matrix, "ctx", axis=0, tiled=True),
        lax.all_gather(w_out, "ctx", axis=1, tiled=True),
        lax.all_gather(w_gate, "ctx", axis=0, tiled=True),
        lax.all_gather(w_up, "ctx", axis=0, tiled=True),
        lax.all_gather(w_down, "ctx", axis=1, tiled=True),
    )
    bq_full, bk_full, bv_full, bo_full, bg_full, bu_full, bd_full = weights_two
    grad_wd = matmul_tn(hidden_low, diff_all)
    d_hidden = matmul_nt(diff_all, bd_full)
    d_gate = (d_hidden * up_val * sigma * (1.0 + gate * (1.0 - sigma))).astype(jnp.bfloat16)
    d_up = (d_hidden * active).astype(jnp.bfloat16)
    grad_wg = matmul_tn(post_all, d_gate)
    grad_wu = matmul_tn(post_all, d_up)
    start = jnp.int32(0)
    d_post = lax.psum_scatter(
        (
            matmul_nt(row_slice(d_gate, start, lax.axis_size("tp") * tok_rows), bg_full)
            + matmul_nt(row_slice(d_up, start, lax.axis_size("tp") * tok_rows), bu_full)
        ).astype(jnp.bfloat16),
        "tp",
        scatter_dimension=0,
        tiled=True,
    ).astype(jnp.float32)
    grad_post_local = jnp.sum(d_post * unit_post, axis=0)
    d_middle = diff + rms_back(middle, scale_post, d_post * post_gain)
    d_mid_low = d_middle.astype(jnp.bfloat16)
    d_mid_all = lax.all_gather(d_mid_low, "tp", axis=0, tiled=True)
    grad_wo = matmul_tn(mixed_low, d_mid_all)
    d_mixed = matmul_nt(d_mid_all, bo_full).astype(jnp.bfloat16)
    d_mixed_grid = jnp.transpose(
        d_mixed.reshape(SEQS, block_span, kv_heads, group_width, HEAD_SIZE), (0, 2, 3, 1, 4)
    )
    delta = jnp.sum(d_mixed_grid.astype(jnp.float32) * attn_exact, axis=-1)

    def revisit(carry, turn):
        grad_queries, grad_keys, grad_values = carry
        owner = (ctx_index - turn) % ctx_count
        keys = all_keys[turn]
        value_rows = all_values[turn]
        scores, allowed = scores_of(keys, block_positions(owner))
        probs = jnp.where(allowed, jnp.exp(scores - log_total[..., None]), 0.0)
        probs_low = probs.astype(jnp.bfloat16)
        d_probs = jnp.einsum(
            "skgqd,slkd->skgql", d_mixed_grid, value_rows, preferred_element_type=jnp.float32
        )
        d_scores = (probs * (d_probs - delta[..., None])).astype(jnp.bfloat16)
        grad_queries = grad_queries + jnp.einsum(
            "skgql,slkd->skgqd", d_scores, keys, preferred_element_type=jnp.float32
        )
        grad_keys = grad_keys + jnp.einsum(
            "skgql,sqkgd->slkd", d_scores, query_low, preferred_element_type=jnp.float32
        )
        grad_values = grad_values + jnp.einsum(
            "skgql,skgqd->slkd", probs_low, d_mixed_grid, preferred_element_type=jnp.float32
        )
        grad_keys, grad_values = (
            from_behind(grad_keys.astype(jnp.bfloat16), "ctx", 1).astype(grad_keys.dtype),
            from_behind(grad_values.astype(jnp.bfloat16), "ctx", 1).astype(grad_values.dtype),
        )
        return ((grad_queries, grad_keys, grad_values), None)

    kv_shape = (SEQS, block_span, kv_heads, HEAD_SIZE)
    start_carry = (
        jnp.zeros(stat_shape + (HEAD_SIZE,), jnp.float32),
        jnp.zeros(kv_shape, jnp.float32),
        jnp.zeros(kv_shape, jnp.float32),
    )
    (grad_queries, grad_keys, grad_values), unused_out = lax.scan(
        revisit, start_carry, jnp.arange(ctx_count, dtype=jnp.int32)
    )
    grad_queries = (
        jnp.transpose(grad_queries, (0, 3, 1, 2, 4)).reshape(ctx_rows, q_heads, HEAD_SIZE)
        * scale_qk
    )
    grad_keys = grad_keys.reshape(ctx_rows, kv_heads, HEAD_SIZE) * scale_qk
    d_values = grad_values.reshape(ctx_rows, kv_heads * HEAD_SIZE).astype(jnp.bfloat16)
    query_back = rotate_back(grad_queries, cosine, sine)
    grad_q_local = jnp.sum(query_back * query_unit, axis=(0, 1))
    d_query_lin = (
        rms_back(query_lin, query_scale, query_back * q_gain)
        .reshape(ctx_rows, q_heads * HEAD_SIZE)
        .astype(jnp.bfloat16)
    )
    key_back = rotate_back(grad_keys, cosine, sine)
    grad_k_local = jnp.sum(key_back * key_unit, axis=(0, 1))
    d_key_lin = (
        rms_back(key_linear, key_scale, key_back * k_gain)
        .reshape(ctx_rows, kv_heads * HEAD_SIZE)
        .astype(jnp.bfloat16)
    )
    grad_wq = matmul_tn(normed_all, d_query_lin)
    grad_wk = matmul_tn(normed_all, d_key_lin)
    grad_wv = matmul_tn(normed_all, d_values)
    start = jnp.int32(0)
    part_query = matmul_nt(row_slice(d_query_lin, start, lax.axis_size("tp") * tok_rows), bq_full)
    part_key = matmul_nt(row_slice(d_key_lin, start, lax.axis_size("tp") * tok_rows), bk_full)
    part_value = matmul_nt(row_slice(d_values, start, lax.axis_size("tp") * tok_rows), bv_full)
    d_normed = lax.psum_scatter(
        (part_query + part_key + part_value).astype(jnp.bfloat16),
        "tp",
        scatter_dimension=0,
        tiled=True,
    ).astype(jnp.float32)
    grad_in_local = jnp.sum(d_normed * unit_in, axis=0)
    d_tokens = (d_middle + rms_back(stream, scale_in, d_normed * in_gain)).astype(jnp.bfloat16)
    summed = (
        lax.psum_scatter(
            grad_wq.astype(jnp.bfloat16), "ctx", scatter_dimension=0, tiled=True
        ).astype(jnp.float32),
        lax.psum_scatter(
            grad_wk.astype(jnp.bfloat16), "ctx", scatter_dimension=0, tiled=True
        ).astype(jnp.float32),
        lax.psum_scatter(
            grad_wv.astype(jnp.bfloat16), "ctx", scatter_dimension=0, tiled=True
        ).astype(jnp.float32),
        lax.psum_scatter(
            grad_wo.astype(jnp.bfloat16), "ctx", scatter_dimension=1, tiled=True
        ).astype(jnp.float32),
        lax.psum_scatter(
            grad_wg.astype(jnp.bfloat16), "ctx", scatter_dimension=0, tiled=True
        ).astype(jnp.float32),
        lax.psum_scatter(
            grad_wu.astype(jnp.bfloat16), "ctx", scatter_dimension=0, tiled=True
        ).astype(jnp.float32),
        lax.psum_scatter(
            grad_wd.astype(jnp.bfloat16), "ctx", scatter_dimension=1, tiled=True
        ).astype(jnp.float32),
    )
    totals = lax.psum(
        (grad_in_local, grad_q_local, grad_k_local, grad_post_local, error_local), ("ctx", "tp")
    )
    count_valid = jnp.sum(seq_lens).astype(jnp.float32)
    loss = 0.5 * totals[4] / (count_valid * MODEL_WIDTH)
    return (
        output,
        loss,
        d_tokens,
        totals[0],
        summed[0],
        summed[1],
        summed[2],
        totals[1],
        totals[2],
        summed[3],
        totals[3],
        summed[4],
        summed[5],
        summed[6],
    )


def solution(mesh):
    in_specs = (
        P(("ctx", "tp"), None),
        P(("ctx", "tp"), None),
        P(),
        P(),
        P(),
        P("ctx", "tp"),
        P("ctx", "tp"),
        P("ctx", "tp"),
        P(),
        P(),
        P("tp", "ctx"),
        P(),
        P("ctx", "tp"),
        P("ctx", "tp"),
        P("tp", "ctx"),
    )
    out_specs = (
        P(("ctx", "tp"), None),
        P(),
        P(("ctx", "tp"), None),
        P(),
        P("ctx", "tp"),
        P("ctx", "tp"),
        P("ctx", "tp"),
        P(),
        P(),
        P("tp", "ctx"),
        P(),
        P("ctx", "tp"),
        P("ctx", "tp"),
        P("tp", "ctx"),
    )
    return jax.shard_map(local, mesh=mesh, in_specs=in_specs, out_specs=out_specs, check_vma=False)
```

profile of v0, /device:TPU:0, one launch (start us, length us, event | category | flops | bytes accessed | tf_op | source)
XLA Modules:
  0.0 2102.2 jit_solution(16190274161709028853)
XLA Ops:
  21.5 14.6 all-gather.14.cloned.1.call-done
  36.1 117.5 %all-gather.12.cloned.1.call-done = bf16[1536,2048]{1,0:T(8,128)(2,1)} async-done(((bf16[384,2048]{1,0:T(8,128)(2,1)}), bf16[1536,2048]{1,0:T(8,128)(2,1)}) %all-gather.12.cloned.1.call-update) | async-done | bytes 6291472 | tf_op jit(solution)/shard_map/all_gather | solution.py:123
  160.9 20.9 all-gather.18.cloned.1.call-done
  181.7 8.6 multiply_reduce_fusion.4
  217.0 8.9 fusion.75
  225.9 214.1 %while.42 = (s32[]{:T(128)}, bf16[3,512,2,128]{3,1,2,0:T(8,128)(2,1)}, bf16[3,512,2,128]{3,1,2,0:T(8,128)(2,1)}, f32[3,2,2,512]{3,2,1,0:T(2,128)S(1)}, f32[3,2,2...) while((s32[]{:T(128)}, ...), condition=%wide.region_8.9_spmd.clone, body=%wide.region_5.8_spmd.clone.sunk | while | flops 1654669824 | bytes 88546920 | solution.py:187
  229.8 14.3 collective-permute-done
  263.6 10.2 collective-permute-done
  293.4 10.2 collective-permute-done
  323.2 10.2 collective-permute-done
  352.9 10.2 collective-permute-done
  382.7 10.2 collective-permute-done
  412.5 10.2 collective-permute-done
  446.9 8.1 convolution_convert_fusion.4
  455.9 109.4 %reduce-scatter.12.cloned.1.call-done = bf16[384,2048]{1,0:T(8,128)(2,1)} async-done(((bf16[1536,2048]{1,0:T(8,128)(2,1)}), bf16[384,2048]{1,0:T(8,128)(2,1)}) %reduce-scatter.12.cloned.1.call-update) | async-done | bytes 1572880 | tf_op jit(solution)/shard_map/reduce_scatter | solution.py:200
  570.7 42.6 %all-gather.24.cloned.1.call-done = bf16[2048,1536]{1,0:T(8,128)(2,1)} async-done(((bf16[256,1536]{1,0:T(8,128)(2,1)}), bf16[2048,1536]{1,0:T(8,128)(2,1)}) %all-gather.24.cloned.1.call-update) | async-done | bytes 6291472 | tf_op jit(solution)/shard_map/all_gather | solution.py:102
  613.3 117.5 %all-gather.22.cloned.1.call-done = bf16[1536,2048]{1,0:T(8,128)(2,1)} async-done(((bf16[384,2048]{1,0:T(8,128)(2,1)}), bf16[1536,2048]{1,0:T(8,128)(2,1)}) %all-gather.22.cloned.1.call-update) | async-done | bytes 6291472 | tf_op jit(solution)/shard_map/all_gather | solution.py:211
  730.8 15.9 fusion.99
  746.7 29.8 %all-gather.26.cloned.1.call-done = bf16[2048,1536]{1,0:T(8,128)(2,1)} async-done(((bf16[256,1536]{1,0:T(8,128)(2,1)}), bf16[2048,1536]{1,0:T(8,128)(2,1)}) %all-gather.26.cloned.1.call-update) | async-done | bytes 6291472 | tf_op jit(solution)/shard_map/all_gather | solution.py:103
  776.5 19.2 multiply_convert_fusion.2
  795.7 29.2 %all-gather.28.cloned.1.call-done = bf16[1536,2048]{1,0:T(8,128)(2,1)} async-done(((bf16[1536,256]{1,0:T(8,128)(2,1)}), bf16[1536,2048]{1,0:T(8,128)(2,1)}) %all-gather.28.cloned.1.call-update) | async-done | bytes 6291472 | tf_op jit(solution)/shard_map/all_gather | solution.py:104
  824.9 15.2 convolution_convert_fusion.3
  841.6 109.4 %reduce-scatter.14.cloned.1.call-done = bf16[384,2048]{1,0:T(8,128)(2,1)} async-done(((bf16[1536,2048]{1,0:T(8,128)(2,1)}), bf16[384,2048]{1,0:T(8,128)(2,1)}) %reduce-scatter.14.cloned.1.call-update) | async-done | bytes 1572880 | tf_op jit(solution)/shard_map/reduce_scatter | solution.py:217
  955.4 116.0 %all-gather.30.cloned.1.call-done = bf16[1536,2048]{1,0:T(8,128)(2,1)} async-done(((bf16[384,2048]{1,0:T(8,128)(2,1)}), bf16[1536,2048]{1,0:T(8,128)(2,1)}) %all-gather.30.cloned.1.call-update) | async-done | bytes 6291472 | tf_op jit(solution)/shard_map/all_gather | solution.py:231
  1071.4 23.9 %multiply_convert_fusion = (bf16[1536,1536]{1,0:T(8,128)(2,1)}, bf16[1536,1536]{1,0:T(8,128)(2,1)}) fusion(f32[1536,1536]{1,0:T(8,128)} %fusion.99, f32[1536,1536]{1,0:T(8,128)} %get-tuple-element.657, bf16[1536,2048]{1,0:T(8,128)(2,1)} %all-gather.30.cloned.1.call-done, bf16[1536,2048]{1,0:T(8,128)(2,1)} %all-gather.28.cloned.1.call-done), kind=kOutput, calls=%fused_computation.68 | convolution fusion | flops 9694347264 | bytes 40894464 | tf_op jit(solution)/shard_map/dot_general | solution.py:61
  1095.3 16.3 fusion.100
  1111.6 15.9 add_convert_fusion.1
  1127.6 109.1 %reduce-scatter.16.cloned.1.call-done = bf16[384,2048]{1,0:T(8,128)(2,1)} async-done(((bf16[1536,2048]{1,0:T(8,128)(2,1)}), bf16[384,2048]{1,0:T(8,128)(2,1)}) %reduce-scatter.16.cloned.1.call-update) | async-done | bytes 1572880 | tf_op jit(solution)/shard_map/reduce_scatter | solution.py:249
  1246.1 15.2 convolution_convert_fusion
  1261.4 15.7 convolution_convert_fusion.2
  1283.2 9.7 pad_maximum_fusion
  1292.9 15.2 convolution_convert_fusion.1
  1308.4 53.7 %all-gather.32.cloned.1.call-done = bf16[1536,2048]{1,0:T(8,128)(2,1)} async-done(((bf16[384,2048]{1,0:T(8,128)(2,1)}), bf16[1536,2048]{1,0:T(8,128)(2,1)}) %all-gather.32.cloned.1.call-update) | async-done | bytes 6291472 | tf_op jit(solution)/shard_map/all_gather | solution.py:261
  1376.4 377.2 %while.43 = (s32[]{:T(128)}, f32[3,2,2,512,128]{4,3,2,1,0:T(8,128)}, f32[3,512,2,128]{3,1,2,0:T(8,128)}, f32[3,512,2,128]{3,1,2,0:T(8,128)}, s32[8]{0:T(128)S(1)...) while((s32[]{:T(128)}, ...), condition=%wide.region_19.20_spmd.clone, body=%wide.region_18.19_spmd.clone.sunk | while | flops 4070576640 | bytes 124403392 | solution.py:302
  1418.1 10.7 collective-permute-done.3
  1458.0 8.5 select_add_fusion.2
  1468.9 19.3 collective-permute-done.3
  1516.7 9.1 select_add_fusion.2
  1559.3 8.1 select_add_fusion.2
  1569.8 12.1 collective-permute-done.3
  1610.3 7.6 select_add_fusion.2
  1776.0 8.4 convolution_convert_fusion.5
  1799.5 7.9 convolution_convert_fusion.6
  1820.6 12.0 add_convert_fusion
  1844.7 43.0 %reduce-scatter.26.cloned.1.call-done = bf16[512,256]{1,0:T(8,128)(2,1)} async-done(((bf16[512,2048]{1,0:T(8,128)(2,1)}), bf16[512,256]{1,0:T(8,128)(2,1)}) %reduce-scatter.26.cloned.1.call-update) | async-done | bytes 262160 | tf_op jit(solution)/shard_map/reduce_scatter | solution.py:350
  1889.5 42.8 %reduce-scatter.20.cloned.1.call-done = bf16[256,512]{1,0:T(8,128)(2,1)} async-done(((bf16[2048,512]{1,0:T(8,128)(2,1)}), bf16[256,512]{1,0:T(8,128)(2,1)}) %reduce-scatter.20.cloned.1.call-update) | async-done | bytes 262160 | tf_op jit(solution)/shard_map/reduce_scatter | solution.py:341
  1934.1 111.4 %reduce-scatter.18.cloned.1.call-done = bf16[384,2048]{1,0:T(8,128)(2,1)} async-done(((bf16[1536,2048]{1,0:T(8,128)(2,1)}), bf16[384,2048]{1,0:T(8,128)(2,1)}) %reduce-scatter.18.cloned.1.call-update) | async-done | bytes 1572880 | tf_op jit(solution)/shard_map/reduce_scatter | solution.py:332
  2048.2 41.3 %all-reduce = (f32[]{:T(128)}, f32[2048]{0:T(1024)}, f32[128]{0:T(128)}, f32[128]{0:T(128)}, f32[2048]{0:T(1024)}) all-reduce(f32[]{:T(128)} %get-tuple-element.541, f32[2048]{0:T(1024)S(1)} %get-tuple-element.542, f32[128]{0:T(128)S(1)} %bitcast_reduce_fusion, ...), channel_id=1, replica_groups=mesh['ctx'=8,'tp'=4] {'ctx','tp'}, use_global_device_ids=true, to_apply=%region_13.14 | all-reduce | flops 4353 | bytes 34824 | tf_op jit(solution)/shard_map/psum | solution.py:363
  (696 shorter events, 581.7 us)
Async XLA Ops:
  7.2 29.0 %all-gather.14.cloned.1.call-start = ((), (), s32[]{:S(2)}) async-start(), calls=%async_computation.12 | async-start | bytes 1179648 | tf_op jit(solution)/shard_map/all_gather | solution.py:99
  7.9 145.7 %all-gather.12.cloned.1.call-start = ((), (), s32[]{:S(2)}) async-start(), calls=%async_computation.11 | async-start | bytes 7864320 | tf_op jit(solution)/shard_map/all_gather | solution.py:123
  13.4 168.3 %all-gather.18.cloned.1.call-start = ((), (), s32[]{:S(2)}) async-start(), calls=%async_computation.14 | async-start | bytes 2359296 | tf_op jit(solution)/shard_map/all_gather | solution.py:98
  14.1 194.8 %all-gather.16.cloned.1.call-start = ((), (), s32[]{:S(2)}) async-start(), calls=%async_computation.13 | async-start | bytes 1179648 | tf_op jit(solution)/shard_map/all_gather | solution.py:100
  14.7 432.2 %all-gather.20.cloned.1.call-start = ((), (), s32[]{:S(2)}) async-start(), calls=%async_computation.15 | async-start | bytes 2359296 | tf_op jit(solution)/shard_map/all_gather | solution.py:101
  15.3 550.0 %reduce-scatter.12.cloned.1.call-start = ((), (), s32[]{:S(2)}) async-start(), calls=%async_computation.16 | async-start | bytes 7864320 | tf_op jit(solution)/shard_map/reduce_scatter | solution.py:200
  225.9 18.1 collective-permute-start
  226.2 26.3 %collective-permute-start.1 = (bf16[3,512,2,128]{3,1,2,0:T(8,128)(2,1)}, bf16[3,512,2,128]{3,1,2,0:T(8,128)(2,1)S(1)}, u32[]{:S(2)}, u32[]{:S(2)}) collective-permute-start(bf16[3,512,2,128]{3,1,2,0:T(8,128)(2,1)} %get-tuple-element.874), channel_id=1, source_target_pairs={{0,4},{4,8},{8,12},{12,16},{16,20},{20,24},{24,28},{28,0},{1,5},{5... | collective-permute-start | bytes 2359304 | tf_op jit(solution)/shard_map/while/body/eval_jaxpr/ppermute | solution.py:19
  261.3 12.5 collective-permute-start
  261.3 20.9 collective-permute-start.1
  291.1 12.5 collective-permute-start
  291.1 20.9 collective-permute-start.1
  320.9 20.9 collective-permute-start.1
  350.7 20.9 collective-permute-start.1
  380.4 20.9 collective-permute-start.1
  410.2 20.9 collective-permute-start.1
  455.1 158.2 %all-gather.24.cloned.1.call-start = ((), (), s32[]{:S(2)}) async-start(), calls=%async_computation.18 | async-start | bytes 7077888 | tf_op jit(solution)/shard_map/all_gather | solution.py:102
  455.8 275.0 %all-gather.22.cloned.1.call-start = ((), (), s32[]{:S(2)}) async-start(), calls=%async_computation.17 | async-start | bytes 7864320 | tf_op jit(solution)/shard_map/all_gather | solution.py:211
  569.3 207.1 %all-gather.26.cloned.1.call-start = ((), (), s32[]{:S(2)}) async-start(), calls=%async_computation.19 | async-start | bytes 7077888 | tf_op jit(solution)/shard_map/all_gather | solution.py:103
  570.1 254.8 %all-gather.28.cloned.1.call-start = ((), (), s32[]{:S(2)}) async-start(), calls=%async_computation.20 | async-start | bytes 7077888 | tf_op jit(solution)/shard_map/all_gather | solution.py:104
  570.7 380.3 %reduce-scatter.14.cloned.1.call-start = ((), (), s32[]{:S(2)}) async-start(), calls=%async_computation.21 | async-start | bytes 7864320 | tf_op jit(solution)/shard_map/reduce_scatter | solution.py:217
  840.1 231.3 %all-gather.30.cloned.1.call-start = ((), (), s32[]{:S(2)}) async-start(), calls=%async_computation.22 | async-start | bytes 7864320 | tf_op jit(solution)/shard_map/all_gather | solution.py:231
  955.4 281.3 %reduce-scatter.16.cloned.1.call-start = ((), (), s32[]{:S(2)}) async-start(), calls=%async_computation.23 | async-start | bytes 7864320 | tf_op jit(solution)/shard_map/reduce_scatter | solution.py:249
  1127.5 234.5 %all-gather.32.cloned.1.call-start = ((), (), s32[]{:S(2)}) async-start(), calls=%async_computation.24 | async-start | bytes 7864320 | tf_op jit(solution)/shard_map/all_gather | solution.py:261
  1246.0 587.9 %reduce-scatter.32.cloned.1.call-start = ((), (), s32[]{:S(2)}) async-start(), calls=%async_computation.32 | async-start | bytes 7077888 | tf_op jit(solution)/shard_map/reduce_scatter | solution.py:359
  1261.3 575.0 %reduce-scatter.28.cloned.1.call-start = ((), (), s32[]{:S(2)}) async-start(), calls=%async_computation.30 | async-start | bytes 7077888 | tf_op jit(solution)/shard_map/reduce_scatter | solution.py:353
  1277.2 561.8 %reduce-scatter.30.cloned.1.call-start = ((), (), s32[]{:S(2)}) async-start(), calls=%async_computation.31 | async-start | bytes 7077888 | tf_op jit(solution)/shard_map/reduce_scatter | solution.py:356
  1308.2 533.3 %reduce-scatter.22.cloned.1.call-start = ((), (), s32[]{:S(2)}) async-start(), calls=%async_computation.27 | async-start | bytes 1179648 | tf_op jit(solution)/shard_map/reduce_scatter | solution.py:344
  1395.4 20.3 collective-permute-start.2
  1402.0 26.8 %collective-permute-start.3 = (bf16[3,512,2,128]{3,1,2,0:T(8,128)(2,1)}, bf16[3,512,2,128]{3,1,2,0:T(8,128)(2,1)S(1)}, u32[]{:S(2)}, u32[]{:S(2)}) collective-permute-start(bf16[3,512,2,128]{3,1,2,0:T(8,128)(2,1)} %fusion.187), channel_id=1, source_target_pairs={{0,4},{4,8},{8,12},{12,16},{16,20},{20,24},{24,28},{28,0},{1,5},{5... | collective-permute-start | bytes 2359304 | tf_op jit(solution)/shard_map/while/body/eval_jaxpr/ppermute | solution.py:19
  1451.1 15.4 collective-permute-start.2
  1458.0 30.2 %collective-permute-start.3 = (bf16[3,512,2,128]{3,1,2,0:T(8,128)(2,1)}, bf16[3,512,2,128]{3,1,2,0:T(8,128)(2,1)S(1)}, u32[]{:S(2)}, u32[]{:S(2)}) collective-permute-start(bf16[3,512,2,128]{3,1,2,0:T(8,128)(2,1)} %fusion.187), channel_id=1, source_target_pairs={{0,4},{4,8},{8,12},{12,16},{16,20},{20,24},{24,28},{28,0},{1,5},{5... | collective-permute-start | bytes 2359304 | tf_op jit(solution)/shard_map/while/body/eval_jaxpr/ppermute | solution.py:19
  1509.9 15.8 collective-permute-start.2
  1516.7 14.2 collective-permute-start.3
  1552.5 14.9 collective-permute-start.2
  1559.3 22.6 %collective-permute-start.3 = (bf16[3,512,2,128]{3,1,2,0:T(8,128)(2,1)}, bf16[3,512,2,128]{3,1,2,0:T(8,128)(2,1)S(1)}, u32[]{:S(2)}, u32[]{:S(2)}) collective-permute-start(bf16[3,512,2,128]{3,1,2,0:T(8,128)(2,1)} %fusion.187), channel_id=1, source_target_pairs={{0,4},{4,8},{8,12},{12,16},{16,20},{20,24},{24,28},{28,0},{1,5},{5... | collective-permute-start | bytes 2359304 | tf_op jit(solution)/shard_map/while/body/eval_jaxpr/ppermute | solution.py:19
  1603.5 14.4 collective-permute-start.2
  1610.3 14.2 collective-permute-start.3
  1646.1 14.4 collective-permute-start.2
  1652.9 14.2 collective-permute-start.3
  1688.7 14.4 collective-permute-start.2
  1695.4 14.2 collective-permute-start.3
  1731.3 14.4 collective-permute-start.2
  1738.0 14.2 collective-permute-start.3
  1768.2 74.9 %reduce-scatter.24.cloned.1.call-start = ((), (), s32[]{:S(2)}) async-start(), calls=%async_computation.28 | async-start | bytes 1179648 | tf_op jit(solution)/shard_map/reduce_scatter | solution.py:347
  1775.9 111.8 %reduce-scatter.26.cloned.1.call-start = ((), (), s32[]{:S(2)}) async-start(), calls=%async_computation.29 | async-start | bytes 2359296 | tf_op jit(solution)/shard_map/reduce_scatter | solution.py:350
  1784.4 147.9 %reduce-scatter.20.cloned.1.call-start = ((), (), s32[]{:S(2)}) async-start(), calls=%async_computation.26 | async-start | bytes 2359296 | tf_op jit(solution)/shard_map/reduce_scatter | solution.py:341
  1807.4 238.1 %reduce-scatter.18.cloned.1.call-start = ((), (), s32[]{:S(2)}) async-start(), calls=%async_computation.25 | async-start | bytes 7864320 | tf_op jit(solution)/shard_map/reduce_scatter | solution.py:332
  (114 other events, 2117.9 us)
Sparse Core Ops, SparseCore 0:
  9.9 26.1 all-gather.13
  38.3 115.3 all-gather.11
  155.6 26.1 all-gather.17
  183.4 23.4 all-gather.15
  208.7 30.9 all-gather.19
  455.2 110.0 reduce-scatter.11
  567.2 46.0 all-gather.23
  615.4 115.3 all-gather.21
  732.7 43.7 all-gather.25
  778.2 46.6 all-gather.27
  840.2 110.7 reduce-scatter.13
  955.5 115.8 all-gather.29
  1127.7 108.9 reduce-scatter.15
  1246.2 115.8 all-gather.31
  1365.3 68.4 reduce-scatter.31
  1437.4 69.5 reduce-scatter.27
  1510.2 67.7 reduce-scatter.29
  1768.3 35.0 reduce-scatter.21
  1806.9 36.0 reduce-scatter.23
  1846.4 41.2 reduce-scatter.25
  1891.0 41.2 reduce-scatter.19
  1934.7 110.7 reduce-scatter.17
where the time goes:
time: 2110 us; the launch traced here: 2100 us
  waiting for transfers between devices  1220 us (58%)
  matrix products  529 us (25%)
  other arithmetic  160 us (8%)
  local copies, waits for them, and re-layouts  103 us (5%)
  blocking collectives  41.3 us (2%)
  loops' own time  27.1 us (1%)
    ppermute x30, waiting for transfers between devices, from_behind(): return lax.ppermute(x, axis, [(i, (i + by) % count) for i in range(count)])  148 us
    all_gather x1, waiting for transfers between devices, local(): normed_all = lax.all_gather(normed_rows, 'tp', axis=0, tiled=True)  118 us
    all_gather x1, waiting for transfers between devices, local(): post_all = lax.all_gather(post_rows, 'tp', axis=0, tiled=True)  118 us
    all_gather x1, waiting for transfers between devices, local(): diff_all = lax.all_gather(diff_low, 'tp', axis=0, tiled=True)  116 us
    reduce_scatter x1, waiting for transfers between devices, local(): lax.psum_scatter((part_query + part_key + part_value).astype(jnp.bfloat16...  111 us
    reduce_scatter x1, waiting for transfers between devices, local(): lax.psum_scatter(matmul(row_slice(mixed_low, jnp.int32(0), lax.axis_size(...  109 us
    reduce_scatter x1, waiting for transfers between devices, local(): lax.psum_scatter(matmul(row_slice(hidden_low, jnp.int32(0), lax.axis_size...  109 us
    reduce_scatter x1, waiting for transfers between devices, local(): lax.psum_scatter((matmul_nt(row_slice(d_gate, start, lax.axis_size('tp')...  109 us
  transfers between devices with their start and end apart: 52, of which 38 were waited for; matrix products, arithmetic and copies ran while one was open for 31% of the time, Pallas kernels for 0%

commit v1 on v0

--- a/solution.py
+++ b/solution.py
@@ -1,6 +1,10 @@
+import functools
+
 import jax
 import jax.numpy as jnp
 from jax import lax
+from jax.experimental import pallas as pl
+from jax.experimental.pallas import tpu as pltpu
 from jax.sharding import PartitionSpec as P
 
 MODEL_WIDTH = 2048
@@ -383,6 +387,973 @@
     )
 
 
+F32 = jnp.float32
+BF16 = jnp.bfloat16
+MESH = pl.DeviceIdType.MESH
+VMEM_LIMIT = 62 << 20
+LOG2E = 1.4426950408889634
+UNIT = 128
+KEYS = 512
+CORE_GROUPS = [[0, 2, 4, 6], [1, 3, 5, 7]]
+SIBLING = [(i, i ^ 1) for i in range(8)]
+
+
+def spec_vmem():
+    return pl.BlockSpec(memory_space=pltpu.VMEM)
+
+
+def spec_any():
+    return pl.BlockSpec(memory_space=pl.ANY)
+
+
+def spec_smem():
+    return pl.BlockSpec(memory_space=pltpu.SMEM)
+
+
+def plane_neighbours():
+    me = lax.axis_index("ctx")
+    core = lax.rem(me, 2)
+    x = lax.rem(me // 2, 2)
+    y = me // 4
+    sib = me + 1 - 2 * core
+    nx = me + 2 - 4 * x
+    ny = me + 4 - 8 * y
+    dg = nx + 4 - 8 * y
+    return me, sib, nx, ny, dg
+
+
+def greet(devices):
+    barrier = pltpu.get_barrier_semaphore()
+    for device in devices:
+        pl.semaphore_signal(barrier, inc=1, device_id={"ctx": device}, device_id_type=MESH)
+    pl.semaphore_wait(barrier, len(devices))
+
+
+def pick(step, options):
+    value = options[0]
+    for i in range(1, len(options)):
+        value = jnp.where(step == i, options[i], value)
+    return value
+
+
+SUBS = 4
+
+
+class Gather:
+    def __init__(self, x_ref, xs, local_sem, send_sems, recv_sems):
+        self.x_ref, self.xs = x_ref, xs
+        self.local_sem, self.send_sems, self.recv_sems = local_sem, send_sems, recv_sems
+        self.me, self.sib, self.nx, self.ny, self.dg = plane_neighbours()
+        self.shift = self.sib - self.me
+        self.piece = x_ref.shape[0] // SUBS
+
+    def part(self, block, s):
+        return self.xs.at[block, pl.ds(s * self.piece, self.piece)]
+
+    def remote(self, src, kind, block, s, device):
+        return pltpu.make_async_remote_copy(
+            src_ref=src,
+            dst_ref=self.part(block, s),
+            send_sem=self.send_sems.at[kind, s],
+            recv_sem=self.recv_sems.at[block, s],
+            device_id={"ctx": device},
+            device_id_type=MESH,
+        )
+
+    def own(self, s):
+        return self.x_ref.at[pl.ds(s * self.piece, self.piece)]
+
+    def start(self):
+        greet((self.sib, self.nx, self.ny))
+        for s in range(SUBS):
+            t = (s + SUBS // 2) % SUBS
+            self.remote(self.own(s), 0, self.me, s, self.nx).start()
+            self.remote(self.own(t), 1, self.me, t, self.ny).start()
+        for s in range(SUBS):
+            self.remote(self.own(s), 2, self.me, s, self.sib).start()
+        keep = pltpu.make_async_copy(self.x_ref, self.xs.at[self.me], self.local_sem)
+        keep.start()
+        keep.wait()
+
+    def arrived(self, block, s):
+        self.remote(self.part(block, s), 0, block, s, self.sib).wait_recv()
+
+    def relay(self, kind, block, s, device):
+        self.remote(self.part(block, s), kind, block, s, device).start()
+
+    def before(self, step):
+        half = SUBS // 2
+
+        @pl.when(step == 1)
+        def _():
+            for s in range(SUBS):
+                self.arrived(self.sib, s)
+
+        @pl.when(step == 2)
+        def _():
+            for s in range(SUBS):
+                self.arrived(self.nx, s)
+                if s < half:
+                    self.relay(3, self.nx, s, self.ny)
+                self.relay(4, self.nx, s, self.sib)
+                t = (s + half) % SUBS
+                self.arrived(self.ny, t)
+                if t >= half:
+                    self.relay(3, self.ny, t, self.nx)
+                self.relay(5, self.ny, t, self.sib)
+
+        @pl.when(step == 3)
+        def _():
+            for s in range(SUBS):
+                self.arrived(self.nx + self.shift, s)
+
+        @pl.when(step == 4)
+        def _():
+            for s in (0, half):
+                self.arrived(self.dg, s)
+                self.relay(6, self.dg, s, self.sib)
+
+        @pl.when(step == 5)
+        def _():
+            for s in range(SUBS):
+                self.arrived(self.ny + self.shift, s)
+
+        @pl.when(step == 6)
+        def _():
+            for s in range(SUBS):
+                if s % half:
+                    self.arrived(self.dg, s)
+                    self.relay(6, self.dg, s, self.sib)
+
+        @pl.when(step == 7)
+        def _():
+            for s in range(SUBS):
+                self.arrived(self.dg + self.shift, s)
+
+    def block(self, step):
+        near = (self.me, self.nx, self.ny, self.dg)
+        return pick(step, [b + o for b in near for o in (0, self.shift)])
+
+    def finish(self):
+        for s in range(SUBS):
+            for kind in range(7):
+                self.remote(self.part(self.me, s), kind, self.me, s, self.sib).wait_send()
+
+
+def gather_scratch(rows, width):
+    return [
+        pltpu.VMEM((8, rows, width), BF16),
+        pltpu.SemaphoreType.DMA,
+        pltpu.SemaphoreType.DMA((7, SUBS)),
+        pltpu.SemaphoreType.DMA((8, SUBS)),
+    ]
+
+
+def nn(left, right):
+    return lax.dot_general(left, right, (((1,), (0,)), ((), ())), preferred_element_type=F32)
+
+
+def nt(left, right):
+    return lax.dot_general(left, right, (((1,), (1,)), ((), ())), preferred_element_type=F32)
+
+
+def tn(left, right):
+    return lax.dot_general(left, right, (((0,), (0,)), ((), ())), preferred_element_type=F32)
+
+
+def qkv_kernel(x_ref, w_ref, all_ref, qkv_ref, xs, local_sem, send_sems, recv_sems, keep_sems):
+    ring = Gather(x_ref, xs, local_sem, send_sems, recv_sems)
+    rows = x_ref.shape[0]
+    ring.start()
+
+    def keep(block):
+        return pltpu.make_async_copy(xs.at[block], all_ref.at[block], keep_sems.at[block])
+
+    def turn(step, carry):
+        ring.before(step)
+        block = ring.block(step)
+        keep(block).start()
+        qkv_ref[pl.ds(block * rows, rows), :] = nn(xs[block], w_ref[...])
+        return carry
+
+    lax.fori_loop(0, 8, turn, 0)
+    ring.finish()
+    for block in range(8):
+        keep(block).wait()
+
+
+def gather_qkv(normed, w_qkv):
+    rows, width = normed.shape
+    return pl.pallas_call(
+        qkv_kernel,
+        out_shape=(
+            jax.ShapeDtypeStruct((8, rows, width), BF16),
+            jax.ShapeDtypeStruct((8 * rows, w_qkv.shape[1]), F32),
+        ),
+        in_specs=[spec_vmem(), spec_vmem()],
+        out_specs=(spec_any(), spec_vmem()),
+        scratch_shapes=gather_scratch(rows, width) + [pltpu.SemaphoreType.DMA((8,))],
+        compiler_params=pltpu.CompilerParams(
+            collective_id=1, has_side_effects=True, vmem_limit_bytes=VMEM_LIMIT
+        ),
+        name="gather_qkv",
+    )(normed, w_qkv)
+
+
+def up_kernel(
+    x_ref, w_ref, all_ref, a_ref, b_ref, h_ref, xs, local_sem, send_sems, recv_sems, keep_sems, stage, stage_sems
+):
+    ring = Gather(x_ref, xs, local_sem, send_sems, recv_sems)
+    rows = x_ref.shape[0]
+    halves, _, wide = w_ref.shape
+    cols = wide // 2
+    outs = (a_ref, b_ref, h_ref)
+    ring.start()
+
+    def keep(block):
+        return pltpu.make_async_copy(xs.at[block], all_ref.at[block], keep_sems.at[block])
+
+    def put(slot, n, block):
+        return pltpu.make_async_copy(
+            stage.at[slot, n], outs[n].at[pl.ds(block * rows, rows)], stage_sems.at[slot, n]
+        )
+
+    def turn(step, carry):
+        ring.before(step)
+        block = ring.block(step)
+        keep(block).start()
+        slot = lax.rem(step, 2)
+
+        @pl.when(step >= 2)
+        def _():
+            for n in range(3):
+                put(slot, n, block).wait()
+
+        for z in range(halves):
+            both = nn(xs[block], w_ref[z])
+            gate, up = both[:, :cols], both[:, cols:]
+            sigma = jax.nn.sigmoid(gate)
+            active = gate * sigma
+            here = slice(z * cols, (z + 1) * cols)
+            stage[slot, 0, :, here] = (up * sigma * (1.0 + gate * (1.0 - sigma))).astype(BF16)
+            stage[slot, 1, :, here] = active.astype(BF16)
+            stage[slot, 2, :, here] = (active * up).astype(BF16)
+        for n in range(3):
+            put(slot, n, block).start()
+        return carry
+
+    lax.fori_loop(0, 8, turn, 0)
+    ring.finish()
+    for block in range(8):
+        keep(block).wait()
+    for slot in range(2):
+        for n in range(3):
+            put(slot, n, 0).wait()
+
+
+def gather_up(post, w_gu):
+    rows, width = post.shape
+    halves, _, wide = w_gu.shape
+    ff = halves * wide // 2
+    flat = jax.ShapeDtypeStruct((8 * rows, ff), BF16)
+    return pl.pallas_call(
+        up_kernel,
+        out_shape=(jax.ShapeDtypeStruct((8, rows, width), BF16), flat, flat, flat),
+        in_specs=[spec_vmem(), spec_vmem()],
+        out_specs=(spec_any(),) * 4,
+        scratch_shapes=gather_scratch(rows, width)
+        + [
+            pltpu.SemaphoreType.DMA((8,)),
+            pltpu.VMEM((2, 3, rows, ff), BF16),
+            pltpu.SemaphoreType.DMA((2, 3)),
+        ],
+        compiler_params=pltpu.CompilerParams(
+            collective_id=2, has_side_effects=True, vmem_limit_bytes=VMEM_LIMIT
+        ),
+        name="gather_up",
+    )(post, w_gu)
+
+
+def down_back_kernel(
+    x_ref, w_ref, a_ref, b_ref, h_ref, d_ref, gw_ref, xs, local_sem, send_sems, recv_sems, stage, stage_sems
+):
+    ring = Gather(x_ref, xs, local_sem, send_sems, recv_sems)
+    rows = x_ref.shape[0]
+    ff = w_ref.shape[0]
+    cols = ff // 2
+    width = x_ref.shape[1]
+    ring.start()
+    gw_ref[...] = jnp.zeros_like(gw_ref)
+
+    def put(slot, block):
+        return pltpu.make_async_copy(
+            stage.at[slot], d_ref.at[pl.ds(block * rows, rows)], stage_sems.at[slot]
+        )
+
+    def turn(step, carry):
+        ring.before(step)
+        block = ring.block(step)
+        slot = lax.rem(step, 2)
+
+        @pl.when(step >= 2)
+        def _():
+            put(slot, block).wait()
+
+        here = pl.ds(block * rows, rows)
+        for z in range(2):
+            part = slice(z * cols, (z + 1) * cols)
+            grad = nt(xs[block], w_ref[part, :])
+            stage[slot, :, 2 * z * cols : (2 * z + 1) * cols] = (
+                grad * a_ref[here, part].astype(F32)
+            ).astype(BF16)
+            stage[slot, :, (2 * z + 1) * cols : (2 * z + 2) * cols] = (
+                grad * b_ref[here, part].astype(F32)
+            ).astype(BF16)
+        put(slot, block).start()
+
+        @pl.when(slot == 1)
+        def _():
+            pair = block // 2
+            hidden = h_ref[pl.ds(pair * 2 * rows, 2 * rows), :]
+            for n in range(0, width, 512):
+                seen = xs[pl.ds(pair * 2, 2), :, n : n + 512].reshape(2 * rows, 512)
+                gw_ref[:, n : n + 512] += tn(hidden, seen)
+
+        return carry
+
+    lax.fori_loop(0, 8, turn, 0)
+    ring.finish()
+    for slot in range(2):
+        put(slot, 0).wait()
+
+
+def gather_down_back(diff, w_down, a, b, hidden):
+    rows, width = diff.shape
+    ff = w_down.shape[0]
+    return pl.pallas_call(
+        down_back_kernel,
+        out_shape=(
+            jax.ShapeDtypeStruct((8 * rows, 2 * ff), BF16),
+            jax.ShapeDtypeStruct((ff, width), F32),
+        ),
+        in_specs=[spec_vmem()] * 5,
+        out_specs=(spec_any(), spec_vmem()),
+        scratch_shapes=gather_scratch(rows, width)
+        + [pltpu.VMEM((2, rows, 2 * ff), BF16), pltpu.SemaphoreType.DMA((2,))],
+        compiler_params=pltpu.CompilerParams(
+            collective_id=3, has_side_effects=True, vmem_limit_bytes=VMEM_LIMIT
+        ),
+        name="gather_down_back",
+    )(diff, w_down, a, b, hidden)
+
+
+def out_back_kernel(x_ref, w_ref, m_ref, d_ref, gw_ref, xs, local_sem, send_sems, recv_sems):
+    ring = Gather(x_ref, xs, local_sem, send_sems, recv_sems)
+    rows, width = x_ref.shape
+    ring.start()
+    gw_ref[...] = jnp.zeros_like(gw_ref)
+
+    def turn(step, carry):
+        ring.before(step)
+        block = ring.block(step)
+        d_ref[pl.ds(block * rows, rows), :] = nt(xs[block], w_ref[...]).astype(BF16)
+
+        @pl.when(lax.rem(step, 2) == 1)
+        def _():
+            pair = block // 2
+            mixed = m_ref[pl.ds(pair * 2 * rows, 2 * rows), :]
+            for n in range(0, width, 512):
+                seen = xs[pl.ds(pair * 2, 2), :, n : n + 512].reshape(2 * rows, 512)
+                gw_ref[:, n : n + 512] += tn(mixed, seen)
+
+        return carry
+
+    lax.fori_loop(0, 8, turn, 0)
+    ring.finish()
+
+
+def gather_out_back(d_mid, w_out, mixed):
+    rows, width = d_mid.shape
+    heads = w_out.shape[0]
+    return pl.pallas_call(
+        out_back_kernel,
+        out_shape=(
+            jax.ShapeDtypeStruct((8 * rows, heads), BF16),
+            jax.ShapeDtypeStruct((heads, width), F32),
+        ),
+        in_specs=[spec_vmem()] * 3,
+        out_specs=(spec_vmem(), spec_vmem()),
+        scratch_shapes=gather_scratch(rows, width),
+        compiler_params=pltpu.CompilerParams(
+            collective_id=4, has_side_effects=True, vmem_limit_bytes=VMEM_LIMIT
+        ),
+        name="gather_out_back",
+    )(d_mid, w_out, mixed)
+
+
+def scatter_kernel(
+    product, a_ref, w_ref, o_ref, to_sib, from_sib, own, diag_out, diag_in, x_out, y_out, x_in, y_in, sends, recvs
+):
+    me, sib, nx, ny, dg = plane_neighbours()
+    shift = sib - me
+    rows, width = o_ref.shape
+    half = rows // 2
+    first, second = pl.ds(0, half), pl.ds(half, half)
+    greet((sib, nx, ny))
+
+    def remote(src, dst, n, device):
+        return pltpu.make_async_remote_copy(
+            src_ref=src,
+            dst_ref=dst,
+            send_sem=sends.at[n],
+            recv_sem=recvs.at[n],
+            device_id={"ctx": device},
+            device_id_type=MESH,
+        )
+
+    def sibling(n):
+        return remote(to_sib.at[n], from_sib.at[n], n, sib)
+
+    diag_x = remote(diag_out.at[first], diag_in.at[first], 4, nx)
+    diag_y = remote(diag_out.at[second], diag_in.at[second], 5, ny)
+    x_first = remote(x_out.at[first], x_in.at[first], 6, nx)
+    x_second = remote(x_out.at[second], x_in.at[second], 7, nx)
+    y_first = remote(y_out.at[first], y_in.at[first], 8, ny)
+    y_second = remote(y_out.at[second], y_in.at[second], 9, ny)
+    order = [b + o for b in (dg, nx, ny, me) for o in (shift, 0)]
+
+    def chip_sum(n, at):
+        return own[n, at].astype(F32) + from_sib[n, at].astype(F32)
+
+    def turn(step, carry):
+        block = pick(step, order)
+        n = step // 2
+
+        @pl.when(lax.rem(step, 2) == 0)
+        def _():
+            product(a_ref, w_ref, block, rows, to_sib, n)
+            sibling(n).start()
+
+        @pl.when(lax.rem(step, 2) == 1)
+        def _():
+            product(a_ref, w_ref, block, rows, own, n)
+            sibling(n).wait_recv()
+
+        @pl.when(step == 1)
+        def _():
+            diag_out[first] = chip_sum(0, first).astype(BF16)
+            diag_x.start()
+            diag_out[second] = chip_sum(0, second).astype(BF16)
+            diag_y.start()
+
+        @pl.when(step == 3)
+        def _():
+            x_out[first] = chip_sum(1, first).astype(BF16)
+            x_first.start()
+
+        @pl.when(step == 5)
+        def _():
+            y_out[second] = chip_sum(2, second).astype(BF16)
+            y_second.start()
+            diag_x.wait_recv()
+            y_out[first] = (chip_sum(2, first) + diag_in[first].astype(F32)).astype(BF16)
+            y_first.start()
+            diag_y.wait_recv()
+            x_out[second] = (chip_sum(1, second) + diag_in[second].astype(F32)).astype(BF16)
+            x_second.start()
+
+        return carry
+
+    lax.fori_loop(0, 8, turn, 0)
+    x_first.wait_recv()
+    y_second.wait_recv()
+    x_second.wait_recv()
+    y_first.wait_recv()
+    for at in (first, second):
+        o_ref[at] = chip_sum(3, at) + x_in[at].astype(F32) + y_in[at].astype(F32)
+    for n in range(4):
+        sibling(n).wait_send()
+    for copy in (diag_x, diag_y, x_first, x_second, y_first, y_second):
+        copy.wait_send()
+
+
+def product_nn(a_ref, w_ref, block, rows, out, n):
+    left = a_ref[pl.ds(block * rows, rows), :]
+    for c in range(0, w_ref.shape[1], 512):
+        out[n, :, c : c + 512] = nn(left, w_ref[:, c : c + 512]).astype(BF16)
+
+
+def product_nt(a_ref, w_ref, block, rows, out, n):
+    left = a_ref[pl.ds(block * rows, rows), :]
+    for c in range(0, w_ref.shape[0], 512):
+        out[n, :, c : c + 512] = nt(left, w_ref[c : c + 512, :]).astype(BF16)
+
+
+def product_nt_halves(a_ref, w_ref, block, rows, out, n):
+    wide = w_ref.shape[2]
+    here = pl.ds(block * rows, rows)
+    for c in range(0, w_ref.shape[1], 512):
+        total = nt(a_ref[here, :wide], w_ref[0, c : c + 512, :])
+        total += nt(a_ref[here, wide:], w_ref[1, c : c + 512, :])
+        out[n, :, c : c + 512] = total.astype(BF16)
+
+
+def scatter_sum(product, a, w, width, collective_id, name):
+    rows = a.shape[0] // 8
+    four = pltpu.VMEM((4, rows, width), BF16)
+    one = pltpu.VMEM((rows, width), BF16)
+    return pl.pallas_call(
+        functools.partial(scatter_kernel, product),
+        out_shape=jax.ShapeDtypeStruct((rows, width), F32),
+        in_specs=[spec_vmem(), spec_vmem()],
+        out_specs=spec_vmem(),
+        scratch_shapes=[four, four, four]
+        + [one] * 6
+        + [pltpu.SemaphoreType.DMA((10,)), pltpu.SemaphoreType.DMA((10,))],
+        compiler_params=pltpu.CompilerParams(
+            collective_id=collective_id, has_side_effects=True, vmem_limit_bytes=VMEM_LIMIT
+        ),
+        name=name,
+    )(a, w)
+
+
+class Places:
+    def __init__(self, order_ref, lens_ref):
+        self.order, self.lens = order_ref, lens_ref
+        self.plane = lax.axis_index("tp")
+        self.seq0 = (3 * self.plane) // 4
+        self.seq1 = (3 * self.plane + 2) // 4
+
+    def position(self, seq, quarter, c):
+        return 2 * self.order[seq, 2 * c + quarter // 2] + lax.rem(quarter, 2)
+
+    def unit(self, u):
+        c = u // 3
+        g = 3 * self.plane + lax.rem(u, 3)
+        seq = g // 4
+        return seq, seq - self.seq0, self.position(seq, lax.rem(g, 4), c)
+
+    def each(self, visit):
+        for slot, seq in ((0, self.seq0), (1, self.seq1)):
+
+            @pl.when((slot == 0) | (self.seq1 != self.seq0))
+            def _():
+                def one(i, carry):
+                    quarter, c = i // 8, lax.rem(i, 8)
+                    g = 4 * seq + quarter
+                    away = g // 3 - self.plane
+                    row = pl.multiple_of((c * 3 + lax.rem(g, 3)) * UNIT, UNIT)
+                    visit(slot, self.position(seq, quarter, c), away, row)
+                    return carry
+
+                lax.fori_loop(0, 32, one, 0)
+
+    def fetch(self, sources, keys, values, key_sem, value_sem):
+        def visit(slot, position, away, row):
+            at = pl.ds(pl.multiple_of(position * UNIT, UNIT), UNIT)
+            for n, source in enumerate(sources):
+
+                @pl.when(away == n - 1)
+                def _():
+                    pltpu.make_async_copy(
+                        source.at[pl.ds(row, UNIT), pl.ds(0, HEAD_SIZE)], keys.at[slot, at], key_sem.at[slot]
+                    ).start()
+                    pltpu.make_async_copy(
+                        source.at[pl.ds(row, UNIT), pl.ds(HEAD_SIZE, HEAD_SIZE)],
+                        values.at[slot, at, pl.ds(0, HEAD_SIZE)],
+                        value_sem.at[slot],
+                    ).start()
+
+        self.each(visit)
+        for slot in range(2):
+
+            @pl.when((slot == 0) | (self.seq1 != self.seq0))
+            def _():
+                pltpu.make_async_copy(keys.at[slot], keys.at[slot], key_sem.at[slot]).wait()
+                pltpu.make_async_copy(keys.at[slot], keys.at[slot], value_sem.at[slot]).wait()
+
+
+def attend_kernel(
+    order_ref, lens_ref, q_ref, lo_ref, own_ref, hi_ref, o_ref, lse_ref, keys, values, acc, key_sem, value_sem
+):
+    places = Places(order_ref, lens_ref)
+    values[:, :, HEAD_SIZE:] = jnp.ones((2, values.shape[1], HEAD_SIZE), BF16)
+    places.fetch((lo_ref, own_ref, hi_ref), keys, values, key_sem, value_sem)
+
+    def one_unit(u, carry):
+        seq, slot, position = places.unit(u)
+        length = lens_ref[seq]
+        rows = pl.ds(pl.multiple_of(u * UNIT, UNIT), UNIT)
+        both = q_ref[rows, :]
+        queries = jnp.concatenate([both[:, :HEAD_SIZE], both[:, HEAD_SIZE:]], axis=0)
+        clear = jnp.minimum(position * UNIT, length) // KEYS
+        acc[...] = jnp.zeros_like(acc)
+
+        def part(block, masked):
+            at = pl.ds(pl.multiple_of(block * KEYS, KEYS), KEYS)
+            weights = jnp.exp2(nt(queries, keys[slot, at, :]))
+            if masked:
+                key_pos = block * KEYS + lax.broadcasted_iota(jnp.int32, weights.shape, 1)
+                query_pos = position * UNIT + lax.rem(
+                    lax.broadcasted_iota(jnp.int32, weights.shape, 0), UNIT
+                )
+                weights = jnp.where((key_pos <= query_pos) & (key_pos < length), weights, 0.0)
+            acc[...] += nn(weights.astype(BF16), values[slot, at, :])
+
+        def full(block, carry):
+            part(block, False)
+            return carry
+
+        lax.fori_loop(0, clear, full, 0)
+        part(clear, True)
+        total = acc[:, HEAD_SIZE:]
+        mixed = (acc[:, :HEAD_SIZE] / total).astype(BF16)
+        o_ref[rows, :] = jnp.concatenate([mixed[:UNIT], mixed[UNIT:]], axis=1)
+        lse_ref[u] = jnp.transpose(jnp.log2(total))[:8, :]
+        return carry
+
+    lax.fori_loop(0, q_ref.shape[0] // UNIT, one_unit, 0)
+
+
+def attend(order, lens, q, lo, own, hi, seq_len):
+    rows = q.shape[0]
+    return pl.pallas_call(
+        attend_kernel,
+        out_shape=(
+            jax.ShapeDtypeStruct(q.shape, BF16),
+            jax.ShapeDtypeStruct((rows // UNIT, 8, 2 * UNIT), F32),
+        ),
+        in_specs=[spec_smem(), spec_smem(), spec_vmem(), spec_any(), spec_any(), spec_any()],
+        out_specs=(spec_vmem(), spec_vmem()),
+        scratch_shapes=[
+            pltpu.VMEM((2, seq_len, HEAD_SIZE), BF16),
+            pltpu.VMEM((2, seq_len, 2 * HEAD_SIZE), BF16),
+            pltpu.VMEM((2 * UNIT, 2 * HEAD_SIZE), F32),
+            pltpu.SemaphoreType.DMA((2,)),
+            pltpu.SemaphoreType.DMA((2,)),
+        ],
+        compiler_params=pltpu.CompilerParams(vmem_limit_bytes=VMEM_LIMIT),
+        name="attend",
+    )(order, lens, q, lo, own, hi)
+
+
+def attend_back_kernel(
+    order_ref,
+    lens_ref,
+    q_ref,
+    do_ref,
+    o_ref,
+    lse_ref,
+    lo_ref,
+    own_ref,
+    hi_ref,
+    dq_ref,
+    dlo_ref,
+    down_ref,
+    dhi_ref,
+    keys,
+    values,
+    dkeys,
+    dvalues,
+    dq_acc,
+    key_sem,
+    value_sem,
+):
+    places = Places(order_ref, lens_ref)
+    dkeys[...] = jnp.zeros_like(dkeys)
+    dvalues[...] = jnp.zeros_like(dvalues)
+    places.fetch((lo_ref, own_ref, hi_ref), keys, values, key_sem, value_sem)
+
+    def stacked(ref, rows):
+        both = ref[rows, :]
+        return jnp.concatenate([both[:, :HEAD_SIZE], both[:, HEAD_SIZE:]], axis=0)
+
+    def one_unit(u, carry):
+        seq, slot, position = places.unit(u)
+        length = lens_ref[seq]
+        rows = pl.ds(pl.multiple_of(u * UNIT, UNIT), UNIT)
+        queries = stacked(q_ref, rows)
+        grads = stacked(do_ref, rows)
+        product = grads.astype(F32) * stacked(o_ref, rows).astype(F32)
+        delta = jnp.sum(jnp.transpose(product), axis=0, keepdims=True)
+        lse = lse_ref[u][:1, :]
+        clear = jnp.minimum(position * UNIT, length) // KEYS
+        dq_acc[...] = jnp.zeros_like(dq_acc)
+
+        def part(block, masked):
+            at = pl.ds(pl.multiple_of(block * KEYS, KEYS), KEYS)
+            key = keys[slot, at, :]
+            probs = jnp.exp2(nt(key, queries) - lse)
+            if masked:
+                key_pos = block * KEYS + lax.broadcasted_iota(jnp.int32, probs.shape, 0)
+                query_pos = position * UNIT + lax.rem(
+                    lax.broadcasted_iota(jnp.int32, probs.shape, 1), UNIT
+                )
+                probs = jnp.where((key_pos <= query_pos) & (key_pos < length), probs, 0.0)
+            d_scores = (probs * (nt(values[slot, at, :], grads) - delta)).astype(BF16)
+            dvalues[slot, at, :] += nn(probs.astype(BF16), grads)
+            dkeys[slot, at, :] += nn(d_scores, queries)
+            dq_acc[...] += tn(d_scores, key)
+
+        def full(block, carry):
+            part(block, False)
+            return carry
+
+        lax.fori_loop(0, clear, full, 0)
+        part(clear, True)
+        dq_ref[rows, :] = jnp.concatenate([dq_acc[:UNIT, :], dq_acc[UNIT:, :]], axis=1)
+        return carry
+
+    lax.fori_loop(0, q_ref.shape[0] // UNIT, one_unit, 0)
+    dlo_ref[...] = jnp.zeros_like(dlo_ref)
+    dhi_ref[...] = jnp.zeros_like(dhi_ref)
+
+    def spread(slot, position, away, row):
+        at = pl.ds(pl.multiple_of(position * UNIT, UNIT), UNIT)
+        for n, out in enumerate((dlo_ref, down_ref, dhi_ref)):
+
+            @pl.when(away == n - 1)
+            def _():
+                out[pl.ds(row, UNIT), :HEAD_SIZE] = (dkeys[slot, at, :] * (1.0 / LOG2E)).astype(out.dtype)
+                out[pl.ds(row, UNIT), HEAD_SIZE:] = dvalues[slot, at, :].astype(out.dtype)
+
+    places.each(spread)
+
+
+def attend_back(order, lens, q, d_mixed, mixed, lse, lo, own, hi, seq_len):
+    flat = jax.ShapeDtypeStruct(q.shape, BF16)
+    wide = jax.ShapeDtypeStruct(q.shape, F32)
+    held = pltpu.VMEM((2, seq_len, HEAD_SIZE), BF16)
+    summed = pltpu.VMEM((2, seq_len, HEAD_SIZE), F32)
+    return pl.pallas_call(
+        attend_back_kernel,
+        out_shape=(wide, flat, wide, flat),
+        in_specs=[spec_smem(), spec_smem()] + [spec_vmem()] * 4 + [spec_any()] * 3,
+        out_specs=(spec_vmem(),) * 4,
+        scratch_shapes=[
+            held,
+            held,
+            summed,
+            summed,
+            pltpu.VMEM((2 * UNIT, HEAD_SIZE), F32),
+            pltpu.SemaphoreType.DMA((2,)),
+            pltpu.SemaphoreType.DMA((2,)),
+        ],
+        compiler_params=pltpu.CompilerParams(vmem_limit_bytes=VMEM_LIMIT),
+        name="attend_back",
+    )(order, lens, q, d_mixed, mixed, lse, lo, own, hi)
+
+
+def angles(block_order, ctx_rows, tok_rows):
+    inverse = THETA ** (-jnp.arange(0, HEAD_SIZE, 2, dtype=F32) / HEAD_SIZE)
+    starts = jnp.arange(2 * block_order.shape[1], dtype=jnp.int32) * UNIT
+    coarse = starts.astype(F32)[:, None] * inverse[None, :]
+    fine = jnp.arange(UNIT, dtype=F32)[:, None] * inverse[None, :]
+    units = tok_rows // UNIT
+    g = lax.axis_index("tp") * units + jnp.arange(units, dtype=jnp.int32)
+    seq, quarter = g // 4, g % 4
+    c = jnp.arange(lax.axis_size("ctx"), dtype=jnp.int32)
+    where = 2 * block_order[seq[None, :], 2 * c[:, None] + (quarter // 2)[None, :]] + (quarter % 2)[None, :]
+    where = where.reshape(-1)
+    cos_a, sin_a = jnp.cos(coarse)[where][:, None, :], jnp.sin(coarse)[where][:, None, :]
+    cos_b, sin_b = jnp.cos(fine)[None], jnp.sin(fine)[None]
+    half = HEAD_SIZE // 2
+    cosine = (cos_a * cos_b - sin_a * sin_b).reshape(-1, 1, half)
+    sine = (sin_a * cos_b + cos_a * sin_b).reshape(-1, 1, half)
+    return cosine, sine
+
+
+def from_sibling(parts, core):
+    mine = lax.dynamic_slice_in_dim(parts, 2 * core, 2, 0)
+    other = lax.dynamic_slice_in_dim(parts, 2 - 2 * core, 2, 0)
+    got = lax.ppermute(other, "ctx", SIBLING)
+    low = jnp.where(core == 0, mine, got)
+    high = jnp.where(core == 0, got, mine)
+    return low, high
+
+
+def local_plane(
+    tokens,
+    teacher,
+    seq_lens,
+    block_order,
+    in_gain,
+    w_query,
+    key_weight_matrix,
+    value_weight_matrix,
+    q_gain,
+    k_gain,
+    w_out,
+    post_gain,
+    w_gate,
+    w_up,
+    w_down,
+):
+    me = lax.axis_index("ctx")
+    core = me % 2
+    plane = lax.axis_index("tp")
+    tok_rows, width = tokens.shape
+    plane_rows = 8 * tok_rows
+    seq_len = 2 * 8 * BLK
+    scale_qk = HEAD_SIZE ** (-0.5)
+    deep = width // 8
+    stream = tokens.astype(F32)
+    scale_in = rms_scale(stream)
+    unit_in = stream * scale_in
+    normed_rows = (unit_in * in_gain).astype(BF16)
+
+    def to_heads(home):
+        gathered = lax.all_gather(home, "tp", axis=0, tiled=True)
+        return lax.all_to_all(gathered, "ctx", 0, 0, tiled=True)
+
+    qkv_home = jnp.concatenate(
+        [
+            w_query.reshape(deep, 2, 2 * HEAD_SIZE),
+            key_weight_matrix.reshape(deep, 2, HEAD_SIZE),
+            value_weight_matrix.reshape(deep, 2, HEAD_SIZE),
+        ],
+        axis=2,
+    )
+    w_qkv = to_heads(jnp.transpose(qkv_home, (1, 0, 2))).reshape(width, 4 * HEAD_SIZE)
+    w_o = jnp.transpose(to_heads(w_out.reshape(2, 2 * HEAD_SIZE, deep)), (1, 0, 2)).reshape(
+        2 * HEAD_SIZE, width
+    )
+
+    cols = w_gate.shape[1] // 4
+    gu_home = jnp.transpose(
+        jnp.concatenate([w_gate.reshape(deep, 4, cols), w_up.reshape(deep, 4, cols)], axis=2), (1, 0, 2)
+    )
+    gu_part = lax.all_to_all(gu_home, "ctx", 0, 0, axis_index_groups=CORE_GROUPS, tiled=True)
+    gu_low, gu_high = from_sibling(lax.all_gather(gu_part, "tp", axis=0), core)
+    w_gu = jnp.stack([gu_low, gu_high], axis=2).reshape(2, width, 2 * cols)
+    down_part = lax.all_to_all(
+        w_down.reshape(4, cols, deep), "ctx", 0, 0, axis_index_groups=CORE_GROUPS, tiled=True
+    )
+    down_low, down_high = from_sibling(lax.all_gather(down_part, "tp", axis=0), core)
+    w_d = jnp.transpose(jnp.stack([down_low, down_high], axis=2), (0, 3, 1, 2, 4)).reshape(2 * cols, width)
+
+    normed_all, qkv = gather_qkv(normed_rows, w_qkv)
+    cosine, sine = angles(block_order, plane_rows, tok_rows)
+    query_lin = qkv[:, : 2 * HEAD_SIZE].reshape(plane_rows, 2, HEAD_SIZE)
+    key_lin = qkv[:, 2 * HEAD_SIZE : 3 * HEAD_SIZE].reshape(plane_rows, 1, HEAD_SIZE)
+    query_scale = rms_scale(query_lin)
+    query_unit = query_lin * query_scale
+    key_scale = rms_scale(key_lin)
+    key_unit = key_lin * key_scale
+    queries = (
+        (rotate(query_unit * q_gain, cosine, sine) * (scale_qk * LOG2E))
+        .astype(BF16)
+        .reshape(plane_rows, 2 * HEAD_SIZE)
+    )
+    keys = rotate(key_unit * k_gain, cosine, sine).astype(BF16).reshape(plane_rows, HEAD_SIZE)
+    kv = jnp.concatenate([keys, qkv[:, 3 * HEAD_SIZE :].astype(BF16)], axis=1)
+    upward = [(0, 1), (1, 2), (2, 3)]
+    downward = [(1, 0), (2, 1), (3, 2)]
+    kv_lo = lax.ppermute(kv, "tp", upward)
+    kv_hi = lax.ppermute(kv, "tp", downward)
+    mixed, lse = attend(block_order, seq_lens, queries, kv_lo, kv, kv_hi, seq_len)
+    middle = stream + scatter_sum(product_nn, mixed, w_o, width, 5, "scatter_out")
+    scale_post = rms_scale(middle)
+    unit_post = middle * scale_post
+    post_rows = (unit_post * post_gain).astype(BF16)
+    post_all, slope, active, hidden = gather_up(post_rows, w_gu)
+    result = middle + scatter_sum(product_nn, hidden, w_d, width, 6, "scatter_down")
+    output = result.astype(BF16)
+
+    row = plane * tok_rows + jnp.arange(tok_rows, dtype=jnp.int32)
+    seq, rest = row // (2 * BLK), row % (2 * BLK)
+    position = block_order[seq, 2 * me + rest // BLK] * BLK + rest % BLK
+    valid = (position < seq_lens[seq]).astype(F32)
+    diff = (result - teacher.astype(F32)) * valid[:, None]
+    error_local = jnp.sum(diff * diff)
+    diff_low = diff.astype(BF16)
+    d_gu, grad_wd = gather_down_back(diff_low, w_d, slope, active, hidden)
+    d_post = scatter_sum(product_nt_halves, d_gu, w_gu, width, 7, "scatter_post")
+
+    def home_sum(parts):
+        mine = lax.dynamic_index_in_dim(parts, core, 2, keepdims=False)
+        other = lax.dynamic_index_in_dim(parts, 1 - core, 2, keepdims=False)
+        got = lax.ppermute(other, "ctx", SIBLING)
+        low = jnp.where(core == 0, mine, got)
+        high = jnp.where(core == 0, got, mine)
+        total = lax.psum_scatter(
+            jnp.concatenate([low, high], axis=0), "tp", scatter_dimension=0, tiled=True
+        )
+        return lax.all_to_all(total[0], "ctx", 0, 0, axis_index_groups=CORE_GROUPS, tiled=True)
+
+    grad_down = home_sum(
+        jnp.transpose(grad_wd.astype(BF16).reshape(2, cols, 4, 2, deep), (0, 2, 3, 1, 4))
+    ).reshape(4 * cols, deep)
+    post_flat = post_all.reshape(plane_rows, width)
+    grad_gu = jnp.stack(
+        [matmul_tn(post_flat, d_gu[:, z * 2 * cols : (z + 1) * 2 * cols]).astype(BF16) for z in range(2)]
+    )
+    gu_sum = home_sum(grad_gu.reshape(2, 4, 2, deep, 2 * cols))
+    gu_sum = jnp.transpose(gu_sum, (1, 0, 2))
+    grad_gate = gu_sum[:, :, :cols].reshape(deep, 4 * cols)
+    grad_up = gu_sum[:, :, cols:].reshape(deep, 4 * cols)
+
+    grad_post_local = jnp.sum(d_post * unit_post, axis=0)
+    d_middle = diff + rms_back(middle, scale_post, d_post * post_gain)
+    d_mixed, grad_wo = gather_out_back(d_middle.astype(BF16), w_o, mixed)
+
+    def home_heads(parts):
+        swapped = lax.all_to_all(parts.astype(BF16), "ctx", 0, 0, tiled=True)
+        return lax.psum_scatter(swapped, "tp", scatter_dimension=0, tiled=True)
+
+    grad_out = home_heads(jnp.transpose(grad_wo.reshape(2 * HEAD_SIZE, 8, deep), (1, 0, 2))).reshape(
+        4 * HEAD_SIZE, deep
+    )
+    d_queries, to_lo, d_kv, to_hi = attend_back(
+        block_order, seq_lens, queries, d_mixed, mixed, lse, kv_lo, kv, kv_hi, seq_len
+    )
+    d_kv = (
+        d_kv
+        + lax.ppermute(to_lo, "tp", downward).astype(F32)
+        + lax.ppermute(to_hi, "tp", upward).astype(F32)
+    )
+    query_back = rotate_back(
+        d_queries.reshape(plane_rows, 2, HEAD_SIZE) * scale_qk, cosine, sine
+    )
+    grad_q_local = jnp.sum(query_back * query_unit, axis=(0, 1))
+    d_query_lin = rms_back(query_lin, query_scale, query_back * q_gain).reshape(plane_rows, 2 * HEAD_SIZE)
+    key_back = rotate_back(d_kv[:, :HEAD_SIZE].reshape(plane_rows, 1, HEAD_SIZE), cosine, sine)
+    grad_k_local = jnp.sum(key_back * key_unit, axis=(0, 1))
+    d_key_lin = rms_back(key_lin, key_scale, key_back * k_gain).reshape(plane_rows, HEAD_SIZE)
+    d_qkv = jnp.concatenate([d_query_lin, d_key_lin, d_kv[:, HEAD_SIZE:]], axis=1).astype(BF16)
+    d_normed = scatter_sum(product_nt, d_qkv, w_qkv, width, 8, "scatter_normed")
+    grad_qkv = home_heads(
+        matmul_tn(normed_all.reshape(plane_rows, width), d_qkv).reshape(8, deep, 4 * HEAD_SIZE)
+    )
+    grad_qkv = jnp.transpose(grad_qkv, (1, 0, 2))
+    grad_query = grad_qkv[:, :, : 2 * HEAD_SIZE].reshape(deep, 4 * HEAD_SIZE)
+    grad_key = grad_qkv[:, :, 2 * HEAD_SIZE : 3 * HEAD_SIZE].reshape(deep, 2 * HEAD_SIZE)
+    grad_value = grad_qkv[:, :, 3 * HEAD_SIZE :].reshape(deep, 2 * HEAD_SIZE)
+    grad_in_local = jnp.sum(d_normed * unit_in, axis=0)
+    d_tokens = (d_middle + rms_back(stream, scale_in, d_normed * in_gain)).astype(BF16)
+    totals = lax.psum(
+        (grad_in_local, grad_q_local, grad_k_local, grad_post_local, error_local), ("ctx", "tp")
+    )
+    count_valid = jnp.sum(seq_lens).astype(F32)
+    loss = 0.5 * totals[4] / (count_valid * MODEL_WIDTH)
+    return (
+        output,
+        loss,
+        d_tokens,
+        totals[0],
+        grad_query.astype(F32),
+        grad_key.astype(F32),
+        grad_value.astype(F32),
+        totals[1],
+        totals[2],
+        grad_out.astype(F32),
+        totals[3],
+        grad_gate.astype(F32),
+        grad_up.astype(F32),
+        grad_down.astype(F32),
+    )
+
+
 def solution(mesh):
     in_specs = (
         P(("ctx", "tp"), None),
@@ -417,4 +1388,5 @@
         P("ctx", "tp"),
         P("tp", "ctx"),
     )
-    return jax.shard_map(local, mesh=mesh, in_specs=in_specs, out_specs=out_specs, check_vma=False)
+    body = local_plane if (mesh.shape["ctx"], mesh.shape["tp"]) == (8, 4) else local
+    return jax.shard_map(body, mesh=mesh, in_specs=in_specs, out_specs=out_specs, check_vma=False)

time: 2110 us -> 1210 us (0.57)
  waiting for transfers between devices: 1220 us -> 148 us
  Pallas kernels: 0 us -> 634 us
  matrix products: 529 us -> 39.1 us
  blocking collectives: 41.3 us -> 97.7 us
  other arithmetic: 160 us -> 118 us
  starting transfers between devices: 5.25 us -> 42.6 us
  loops' own time: 27.1 us -> 0 us
    pallas_call x0 -> x10, Pallas kernels: none -> 634 us  [the longest x4 257 us: scatter_sum(): pl.pallas_call(functools.partial(scatter_kernel, product), out_shape=jax....]
    reduce_scatter x11 -> x4, waiting for transfers between devices: 525 us -> 0.05 us  [the longest x2 0.02 us: home_heads(): return lax.psum_scatter(swapped, 'tp', scatter_dimension=0, tiled=True)]
    dot_general x70 -> x0, matrix products: 455 us -> none  [the longest x7 87.9 us: matmul_nt(): lax.dot_general(left, right, (((1,), (1,)), ((), ())), preferred_element_...]
    all_gather x11 -> x4, waiting for transfers between devices: 542 us -> 88.8 us  [the longest x1 71 us: local_plane(): lax.all_gather(down_part, 'tp', axis=0)]
    ppermute x30 -> x8, waiting for transfers between devices: 148 us -> 5.55 us  [the longest x2 5.54 us: home_sum(): got = lax.ppermute(other, 'ctx', SIBLING)]
    all_to_all x0 -> x2, blocking collectives: none -> 55.6 us  [the longest x1 30.7 us: home_heads(): swapped = lax.all_to_all(parts.astype(BF16), 'ctx', 0, 0, tiled=True)]
    all_to_all x0 -> x6, waiting for transfers between devices: none -> 52.9 us  [the longest x2 32.2 us: to_heads(): return lax.all_to_all(gathered, 'ctx', 0, 0, tiled=True)]
    while x172 -> x0, local copies, waits for them, and re-layouts: 47.2 us -> none
  transfers between devices with their start and end apart: 52 -> 22, of which waited for: 38 -> 9; matrix products, arithmetic and copies ran while one was open for 31% -> 18% of each run, Pallas kernels for 0% -> 36%
where the time goes in v1:
time: 1210 us; the launch traced here: 1200 us
  Pallas kernels  634 us (52%)
  waiting for transfers between devices  148 us (12%)
  other arithmetic  118 us (10%)
  local copies, waits for them, and re-layouts  102 us (8%)
  blocking collectives  97.7 us (8%)
  starting transfers between devices  42.6 us (4%)
  matrix products  39.1 us (3%)
  between operations  17.9 us (1%)
    pallas_call x4, Pallas kernels, scatter_sum(): pl.pallas_call(functools.partial(scatter_kernel, product), out_shape=jax....  257 us
    pallas_call x1, Pallas kernels, attend_back(): pl.pallas_call(attend_back_kernel, out_shape=(wide, flat, wide, flat), in...  73.4 us
    all_gather x1, waiting for transfers between devices, local_plane(): lax.all_gather(down_part, 'tp', axis=0)  71 us
    pallas_call x1, Pallas kernels, gather_down_back(): pl.pallas_call(down_back_kernel, out_shape=(jax.ShapeDtypeStruct((8 * row...  69.4 us
    pallas_call x1, Pallas kernels, gather_up(): pl.pallas_call(up_kernel, out_shape=(jax.ShapeDtypeStruct((8, rows, width...  63.6 us
    pallas_call x1, Pallas kernels, gather_out_back(): pl.pallas_call(out_back_kernel, out_shape=(jax.ShapeDtypeStruct((8 * rows...  60.8 us
    pallas_call x1, Pallas kernels, gather_qkv(): pl.pallas_call(qkv_kernel, out_shape=(jax.ShapeDtypeStruct((8, rows, widt...  60 us
    pallas_call x1, Pallas kernels, attend(): pl.pallas_call(attend_kernel, out_shape=(jax.ShapeDtypeStruct(q.shape, BF...  50.1 us
  transfers between devices with their start and end apart: 22, of which 9 were waited for; matrix products, arithmetic and copies ran while one was open for 18% of the time, Pallas kernels for 36%

profile of v1, /device:TPU:0, one launch (start us, length us, event | category | flops | bytes accessed | tf_op | source)
XLA Modules:
  0.0 1199.4 jit_solution(15400428789962524278)
XLA Ops:
  14.7 24.8 %all_to_all.40 = bf16[4,256,768]{2,1,0:T(8,128)(2,1)} all-to-all(bf16[4,256,768]{2,1,0:T(8,128)(2,1)S(1)} %copy.155), channel_id=1, replica_groups={{0,8,16,24},{4,12,20,28},{1,9,17,25},{5,13,21,29},{2,10,18,26},{6,14,22..., dimensions={0} | all-to-all | bytes 3145728 | tf_op jit(solution)/shard_map/all_to_all | solution.py:1226
  48.0 4.7 all-to-all-done.3
  59.3 12.2 %all-to-all-done.1 = bf16[8,256,256]{2,1,0:T(8,128)(2,1)S(1)} async-done(((bf16[8,256,256]{2,1,0:T(8,128)(2,1)}), bf16[8,256,256]{2,1,0:T(8,128)(2,1)S(1)}, u32[]{:S(2)}, u32[]{:S(2)}) %all-to-all-start.1) | async-done | bytes 1048608 | tf_op jit(solution)/shard_map/all_to_all | solution.py:1207
  71.5 16.3 %all-gather.7.cloned.1.call-done = bf16[8,256,512]{2,1,0:T(8,128)(2,1)} async-done(((bf16[2,256,512]{2,1,0:T(8,128)(2,1)}), bf16[8,256,512]{2,1,0:T(8,128)(2,1)}) %all-gather.7.cloned.1.call-update) | async-done | bytes 2097168 | tf_op jit(solution)/shard_map/all_gather | solution.py:1206
  87.9 4.4 all-to-all-start
  99.0 19.9 %all-to-all-done = bf16[8,256,512]{2,1,0:T(8,128)(2,1)} async-done(((bf16[8,256,512]{2,1,0:T(8,128)(2,1)}), bf16[8,256,512]{2,1,0:T(8,128)(2,1)}, u32[]{:S(2)}, u32[]{:S(2)}) %all-to-all-start) | async-done | bytes 2097184 | tf_op jit(solution)/shard_map/all_to_all | solution.py:1207
  118.9 60.0 %gather_qkv.1 = (bf16[8,384,2048]{2,1,0:T(8,128)(2,1)}, f32[3072,512]{1,0:T(8,128)}) custom-call(bf16[384,2048]{1,0:T(8,128)(2,1)} %fusion.12.x_ref, bf16[2048,512]{1,0:T(8,128)(2,1)} %bitcast.4.w_ref), custom_call_target="tpu_custom_call" | custom-call | tf_op jit(solution)/shard_map/gather_qkv/pallas_call | solution.py:587
  178.9 4.0 slice.62
  196.3 6.3 multiply_reduce_fusion.5
  207.7 3.8 constant_dynamic-slice_fusion.3
  211.6 5.4 multiply_multiply_fusion
  217.0 71.0 %all-gather.13.cloned.1.call-done = bf16[16,384,256]{2,1,0:T(8,128)(2,1)} async-done(((bf16[4,384,256]{2,1,0:T(8,128)(2,1)}), bf16[16,384,256]{2,1,0:T(8,128)(2,1)}) %all-gather.13.cloned.1.call-update) | async-done | bytes 3145744 | tf_op jit(solution)/shard_map/all_gather | solution.py:1232
  290.7 6.3 multiply_subtract_fusion.1
  297.0 3.9 fusion.28
  302.2 50.1 %attend.1 = (bf16[3072,256]{1,0:T(8,128)(2,1)}, f32[24,8,256]{2,1,0:T(8,128)}) custom-call(s32[3,16]{1,0:T(4,128)} %order_ref.3, s32[3]{0:T(128)} %lens_ref.3, bf16[3072,256]{1,0:T(8,128)(2,1)} %bitcast.189, bf16[3072,256]{1,0:T(8,128)(2,1)} %collective-permute-done.lo_ref, bf16[3072,256]{1,0:T(8,128)(2,1)} %pad_maximum_fusion.5.own_ref, ...), custom_call_target="tpu_custom_call" | custom-call | tf_op jit(solution)/shard_map/attend/pallas_call | solution.py:1020
  352.4 63.1 %scatter_out.1 = f32[384,2048]{1,0:T(8,128)} custom-call(bf16[3072,256]{1,0:T(8,128)(2,1)} %get-tuple-element.31.a_ref.m_ref.o_ref, bf16[256,2048]{1,0:T(8,128)(2,1)} %bitcast.201), custom_call_target="tpu_custom_call" | custom-call | tf_op jit(solution)/shard_map/scatter_out/pallas_call | solution.py:905
  426.6 4.1 reshape.725.w_ref
  437.2 63.6 %gather_up.1 = (bf16[8,384,2048]{2,1,0:T(8,128)(2,1)}, bf16[3072,768]{1,0:T(8,128)(2,1)}, bf16[3072,768]{1,0:T(8,128)(2,1)}, bf16[3072,768]{1,0:T(8,128)(2,1)}) custom-call(bf16[384,2048]{1,0:T(8,128)(2,1)} %multiply_convert_fusion.x_ref, bf16[2,2048,768]{2,1,0:T(8,128)(2,1)} %bitcast.175), custom_call_target="tpu_custom_call" | custom-call | tf_op jit(solution)/shard_map/gather_up/pallas_call | solution.py:659
  500.9 64.1 %scatter_down.1 = f32[384,2048]{1,0:T(8,128)} custom-call(bf16[3072,768]{1,0:T(8,128)(2,1)} %get-tuple-element.32.a_ref.h_ref, bf16[768,2048]{1,0:T(8,128)(2,1)} %reshape.725.w_ref), custom_call_target="tpu_custom_call" | custom-call | tf_op jit(solution)/shard_map/scatter_down/pallas_call | solution.py:905
  564.9 6.7 fusion.59
  571.7 69.4 %gather_down_back.1 = (bf16[3072,1536]{1,0:T(8,128)(2,1)}, f32[768,2048]{1,0:T(8,128)}) custom-call(bf16[384,2048]{1,0:T(8,128)(2,1)} %get-tuple-element.145.x_ref, bf16[768,2048]{1,0:T(8,128)(2,1)} %reshape.725.w_ref, bf16[3072,768]{1,0:T(8,128)(2,1)} %get-tuple-element.33.a_ref, bf16[3072,768]{1,0:T(8,128)(2,1)} %get-tuple-element.34.b_ref, ...), custom_call_target="tpu_custom_call" | custom-call | tf_op jit(solution)/shard_map/gather_down_back/pallas_call | solution.py:733
  641.1 5.0 convert_element_type.158
  646.0 5.1 reshape.729
  651.2 8.2 constant_dynamic-slice_fusion.1
  660.3 14.7 %fusion.6 = bf16[2048,768]{1,0:T(8,128)(2,1)S(1)} fusion(bf16[3072,2048]{1,0:T(8,128)(2,1)} %bitcast.229, bf16[3072,1536]{1,0:T(8,128)(2,1)} %get-tuple-element.35.a_ref), kind=kOutput, calls=%fused_computation.21 | convolution fusion | flops 9665249280 | bytes 20447232 | tf_op jit(solution)/shard_map/dot_general | solution.py:59
  677.6 14.7 %fusion.9 = bf16[2048,768]{1,0:T(8,128)(2,1)S(1)} fusion(bf16[3072,2048]{1,0:T(8,128)(2,1)} %bitcast.230, bf16[3072,1536]{1,0:T(8,128)(2,1)} %get-tuple-element.35.a_ref), kind=kOutput, calls=%fused_computation.22 | convolution fusion | flops 9665249280 | bytes 20447232 | tf_op jit(solution)/shard_map/dot_general | solution.py:59
  692.8 5.5 collective-permute-done.6
  703.8 16.7 %copy.161 = bf16[2048,3072]{1,0:T(8,128)(2,1)} copy(bf16[2048,3072]{0,1:T(8,128)(2,1)} %bitcast.194) | data formatting | bytes 25165824 | tf_op jit(solution)/shard_map/dot_general | solution.py:59
  720.5 68.0 %scatter_post.1 = f32[384,2048]{1,0:T(8,128)} custom-call(bf16[3072,1536]{1,0:T(8,128)(2,1)} %get-tuple-element.35.a_ref, bf16[2,2048,768]{2,1,0:T(8,128)(2,1)} %bitcast.176), custom_call_target="tpu_custom_call" | custom-call | tf_op jit(solution)/shard_map/scatter_post/pallas_call | solution.py:905
  788.5 3.8 multiply_reduce_fusion
  793.2 6.2 fusion.58
  799.3 60.8 %gather_out_back.1 = (bf16[3072,256]{1,0:T(8,128)(2,1)}, f32[256,2048]{1,0:T(8,128)}) custom-call(bf16[384,2048]{1,0:T(8,128)(2,1)} %get-tuple-element.143.x_ref, bf16[256,2048]{1,0:T(8,128)(2,1)} %bitcast.202, bf16[3072,256]{1,0:T(8,128)(2,1)} %get-tuple-element.31.a_ref.m_ref.o_ref), custom_call_target="tpu_custom_call" | custom-call | tf_op jit(solution)/shard_map/gather_out_back/pallas_call | solution.py:778
  860.1 73.4 %attend_back.1 = (f32[3072,256]{1,0:T(8,128)}, bf16[3072,256]{1,0:T(8,128)(2,1)}, f32[3072,256]{1,0:T(8,128)}, bf16[3072,256]{1,0:T(8,128)(2,1)}) custom-call(s32[3,16]{1,0:T(4,128)} %order_ref.3, s32[3]{0:T(128)} %lens_ref.3, bf16[3072,256]{1,0:T(8,128)(2,1)} %bitcast.190, bf16[3072,256]{1,0:T(8,128)(2,1)} %get-tuple-element.36.do_ref, ...), custom_call_target="tpu_custom_call" | custom-call | tf_op jit(solution)/shard_map/attend_back/pallas_call | solution.py:1128
  933.5 11.3 collective-permute-start.5
  954.1 4.2 all-to-all-start.5
  958.5 7.0 multiply_add_fusion
  965.4 8.6 multiply_reduce_fusion.1
  975.5 3.8 mul.578
  979.3 3.8 mul.659
  983.1 3.8 mul.654
  998.6 9.7 fusion.31
  1008.3 30.7 %all_to_all.41 = bf16[8,256,512]{2,1,0:T(8,128)(2,1)} all-to-all(bf16[8,256,512]{2,1,0:T(8,128)(2,1)S(1)} %fusion.31), channel_id=1, replica_groups=mesh['ctx'=8,'tp'=4] {'ctx'}, dimensions={0} | all-to-all | bytes 4194304 | tf_op jit(solution)/shard_map/all_to_all | solution.py:1301
  1042.3 61.5 %scatter_normed.1 = f32[384,2048]{1,0:T(8,128)} custom-call(bf16[3072,512]{1,0:T(8,128)(2,1)} %pad_maximum_fusion.3.a_ref, bf16[2048,512]{1,0:T(8,128)(2,1)} %bitcast.4.w_ref), custom_call_target="tpu_custom_call" | custom-call | tf_op jit(solution)/shard_map/scatter_normed/pallas_call | solution.py:905
  1106.7 42.1 %all-reduce = (f32[]{:T(128)}, f32[2048]{0:T(1024)}, f32[128]{0:T(128)}, f32[128]{0:T(128)}, f32[2048]{0:T(1024)}) all-reduce(f32[]{:T(128)} %get-tuple-element.170, f32[2048]{0:T(1024)S(1)} %get-tuple-element.134, f32[128]{0:T(128)S(1)} %bitcast_reduce_fusion, ...), channel_id=1, replica_groups=mesh['ctx'=8,'tp'=4] {'ctx','tp'}, use_global_device_ids=true, to_apply=%region_5.6 | all-reduce | flops 4353 | bytes 34824 | tf_op jit(solution)/shard_map/psum | solution.py:1334
  1149.5 5.1 all-to-all-start.7
  1154.6 4.9 fusion.18
  1159.4 5.0 all-to-all-done.7
  1177.2 11.1 all-to-all-done.6
  (231 shorter events, 122.8 us)
Async XLA Ops:
  7.2 5.0 copy-start.27
  7.2 45.4 %all-gather.9.cloned.1.call-start = ((), (), s32[]{:S(2)}) async-start(), calls=%async_computation.13 | async-start | bytes 1310720 | tf_op jit(solution)/shard_map/all_gather | solution.py:1206
  7.9 79.9 %all-gather.7.cloned.1.call-start = ((), (), s32[]{:S(2)}) async-start(), calls=%async_computation.12 | async-start | bytes 2621440 | tf_op jit(solution)/shard_map/all_gather | solution.py:1206
  12.2 195.5 %all-gather.11.cloned.1.call-start = ((), (), s32[]{:S(2)}) async-start(), calls=%async_computation.18 | async-start | bytes 7864320 | tf_op jit(solution)/shard_map/all_gather | solution.py:1227
  14.7 28.7 %copy-start = (s32[3,16]{1,0:T(4,128)S(1)}, s32[3,16]{1,0:T(4,128)}, u32[]{:S(2)}) copy-start(s32[3,16]{1,0:T(4,128)} %order_ref.3) | copy-start | bytes 580
  39.6 13.0 %all-to-all-start.3 = ((bf16[4,384,256]{2,1,0:T(8,128)(2,1)}), bf16[4,384,256]{2,1,0:T(8,128)(2,1)S(1)}, u32[]{:S(2)}, u32[]{:S(2)}) async-start(bf16[4,384,256]{2,1,0:T(8,128)(2,1)} %bitcast.23), calls=%async_computation.3 | async-start | bytes 1572864 | tf_op jit(solution)/shard_map/all_to_all | solution.py:1229
  47.0 9.3 copy-start.36
  47.0 11.9 copy-start.5
  52.6 35.2 %copy-start.22 = (bf16[4,384,256]{2,1,0:T(8,128)(2,1)}, bf16[4,384,256]{2,1,0:T(8,128)(2,1)S(1)}, u32[]{:S(2)}) copy-start(bf16[4,384,256]{2,1,0:T(8,128)(2,1)S(1)} %all-to-all-done.3) | copy-start | bytes 2359300
  52.6 18.9 %all-to-all-start.1 = ((bf16[8,256,256]{2,1,0:T(8,128)(2,1)}), bf16[8,256,256]{2,1,0:T(8,128)(2,1)S(1)}, u32[]{:S(2)}, u32[]{:S(2)}) async-start(bf16[8,256,256]{2,1,0:T(8,128)(2,1)} %all-gather.9.cloned.1.call-done), calls=%async_computation.1 | async-start | bytes 2097152 | tf_op jit(solution)/shard_map/all_to_all | solution.py:1207
  56.2 37.1 %copy-start.31 = (f32[2048]{0:T(1024)S(1)}, f32[2048]{0:T(1024)}, u32[]{:S(2)}) copy-start(f32[2048]{0:T(1024)} %param.19) | copy-start | bytes 24580
  71.5 23.4 %copy-start.20 = (bf16[8,256,256]{2,1,0:T(8,128)(2,1)}, bf16[8,256,256]{2,1,0:T(8,128)(2,1)S(1)}, u32[]{:S(2)}) copy-start(bf16[8,256,256]{2,1,0:T(8,128)(2,1)S(1)} %all-to-all-done.1) | copy-start | bytes 3145732
  87.9 31.0 %all-to-all-start = ((bf16[8,256,512]{2,1,0:T(8,128)(2,1)}), bf16[8,256,512]{2,1,0:T(8,128)(2,1)}, u32[]{:S(2)}, u32[]{:S(2)}) async-start(bf16[8,256,512]{2,1,0:T(8,128)(2,1)} %all-gather.7.cloned.1.call-done), calls=%async_computation | async-start | bytes 4194304 | tf_op jit(solution)/shard_map/all_to_all | solution.py:1207
  92.2 195.7 %all-gather.13.cloned.1.call-start = ((), (), s32[]{:S(2)}) async-start(), calls=%async_computation.19 | async-start | bytes 3932160 | tf_op jit(solution)/shard_map/all_gather | solution.py:1232
  94.9 1054.5 %reduce-scatter.11.cloned.1.call-start = ((), (), s32[]{:S(2)}) async-start(), calls=%async_computation.17 | async-start | bytes 3932160 | tf_op jit(solution)/shard_map/reduce_scatter | solution.py:1279
  97.8 87.9 %copy-start.8 = (f32[24,128,64]{2,1,0:T(8,128)}, f32[24,128,64]{2,1,0:T(8,128)S(1)}, u32[]{:S(2)}) copy-start(f32[24,128,64]{2,1,0:T(8,128)S(1)} %get-tuple-element.175) | copy-start | bytes 2359300
  178.9 4.9 copy-start.14
  188.2 114.0 %collective-permute-start = (bf16[3072,256]{1,0:T(8,128)(2,1)}, bf16[3072,256]{1,0:T(8,128)(2,1)}, u32[]{:S(2)}, u32[]{:S(2)}) collective-permute-start(bf16[3072,256]{1,0:T(8,128)(2,1)} %pad_maximum_fusion.5.own_ref), channel_id=1, source_target_pairs={{0,1},{1,2},{2,3},{4,5},{5,6},{6,7},{8,9},{9,10},{10,11},{12,13},{... | collective-permute-start | bytes 4718600 | tf_op jit(solution)/shard_map/ppermute | solution.py:1252
  191.2 111.0 %collective-permute-start.1 = (bf16[3072,256]{1,0:T(8,128)(2,1)}, bf16[3072,256]{1,0:T(8,128)(2,1)}, u32[]{:S(2)}, u32[]{:S(2)}) collective-permute-start(bf16[3072,256]{1,0:T(8,128)(2,1)} %pad_maximum_fusion.5.own_ref), channel_id=1, source_target_pairs={{1,0},{2,1},{3,2},{5,4},{6,5},{7,6},{9,8},{10,9},{11,10},{13,12},{... | collective-permute-start | bytes 4718600 | tf_op jit(solution)/shard_map/ppermute | solution.py:1253
  196.3 15.3 %copy-start.3 = (f32[3072,2,128]{2,1,0:T(2,128)}, f32[3072,2,128]{2,1,0:T(2,128)S(1)}, u32[]{:S(2)}) copy-start(f32[3072,2,128]{2,1,0:T(2,128)S(1)} %reshape.718) | copy-start | bytes 9437188
  211.5 219.2 %collective-permute-start.2 = (bf16[2,4,256,768]{3,2,1,0:T(8,128)(2,1)}, bf16[2,4,256,768]{3,2,1,0:T(8,128)(2,1)}, u32[]{:S(2)}, u32[]{:S(2)}) collective-permute-start(bf16[2,4,256,768]{3,2,1,0:T(8,128)(2,1)} %constant_dynamic-slice_fusion.3), channel_id=1, source_target_pairs={{0,4},{4,0},{8,12},{12,8},{16,20},{20,16},{24,28},{28,24},{1,5},{5... | collective-permute-start | bytes 9437192 | tf_op jit(solution)/shard_map/ppermute | solution.py:1169
  217.0 73.7 %copy-start.9 = (f32[24,128,64]{2,1,0:T(8,128)S(1)}, f32[24,128,64]{2,1,0:T(8,128)}, u32[]{:S(2)}) copy-start(f32[24,128,64]{2,1,0:T(8,128)} %copy-done.8) | copy-start | bytes 2359300
  217.0 73.7 %copy-start.12 = (f32[24,128,64]{2,1,0:T(8,128)S(1)}, f32[24,128,64]{2,1,0:T(8,128)}, u32[]{:S(2)}) copy-start(f32[24,128,64]{2,1,0:T(8,128)} %get-tuple-element.176) | copy-start | bytes 2359300
  290.7 128.7 %collective-permute-start.3 = (bf16[2,4,384,256]{3,2,1,0:T(8,128)(2,1)}, bf16[2,4,384,256]{3,2,1,0:T(8,128)(2,1)}, u32[]{:S(2)}, u32[]{:S(2)}) collective-permute-start(bf16[2,4,384,256]{3,2,1,0:T(8,128)(2,1)} %constant_dynamic-slice_fusion.2), channel_id=1, source_target_pairs={{0,4},{4,0},{8,12},{12,8},{16,20},{20,16},{24,28},{28,24},{1,5},{5... | collective-permute-start | bytes 4718600 | tf_op jit(solution)/shard_map/ppermute | solution.py:1169
  352.4 63.1 %copy-start.6 = (bf16[384,2048]{1,0:T(8,128)(2,1)S(1)}, bf16[384,2048]{1,0:T(8,128)(2,1)}, u32[]{:S(2)}) copy-start(bf16[384,2048]{1,0:T(8,128)(2,1)} %param.15) | copy-start | bytes 4718596
  417.9 5.2 copy-start.1
  500.8 64.1 %copy-start.26 = (bf16[384,2048]{1,0:T(8,128)(2,1)S(1)}, bf16[384,2048]{1,0:T(8,128)(2,1)}, u32[]{:S(2)}) copy-start(bf16[384,2048]{1,0:T(8,128)(2,1)} %param.16) | copy-start | bytes 4718596
  659.9 15.2 %collective-permute-start.7 = (bf16[2,4,384,256]{3,2,1,0:T(8,128)(2,1)S(1)}, bf16[2,4,384,256]{3,2,1,0:T(8,128)(2,1)S(1)}, u32[]{:S(2)}, u32[]{:S(2)}) collective-permute-start(bf16[2,4,384,256]{3,2,1,0:T(8,128)(2,1)S(1)} %bitcast.219), channel_id=1, source_target_pairs={{0,4},{4,0},{8,12},{12,8},{16,20},{20,16},{24,28},{28,24},{1,5},{5... | collective-permute-start | bytes 4718600 | tf_op jit(solution)/shard_map/ppermute | solution.py:1276
  660.3 14.7 %copy-start.18 = (bf16[2,384,4,1,256]{4,3,2,1,0:T(2,128)(2,1)S(1)}, bf16[2,384,4,1,256]{4,3,2,1,0:T(2,128)(2,1)}, u32[]{:S(2)}) copy-start(bf16[2,384,4,1,256]{4,3,2,1,0:T(2,128)(2,1)} %get-tuple-element.168) | copy-start | bytes 4718596
  677.5 486.9 %reduce-scatter.9.cloned.1.call-start = ((), (), s32[]{:S(2)}) async-start(), calls=%async_computation.16 | async-start | bytes 7864320 | tf_op jit(solution)/shard_map/reduce_scatter | solution.py:1279
  692.6 5.7 collective-permute-start.6
  933.5 54.7 %collective-permute-start.5 = (bf16[3072,256]{1,0:T(8,128)(2,1)}, bf16[3072,256]{1,0:T(8,128)(2,1)}, u32[]{:S(2)}, u32[]{:S(2)}) collective-permute-start(bf16[3072,256]{1,0:T(8,128)(2,1)} %get-tuple-element.41), channel_id=1, source_target_pairs={{0,1},{1,2},{2,3},{4,5},{5,6},{6,7},{8,9},{9,10},{10,11},{12,13},{... | collective-permute-start | bytes 4718600 | tf_op jit(solution)/shard_map/ppermute | solution.py:1313
  944.9 43.4 %collective-permute-start.4 = (bf16[3072,256]{1,0:T(8,128)(2,1)}, bf16[3072,256]{1,0:T(8,128)(2,1)}, u32[]{:S(2)}, u32[]{:S(2)}) collective-permute-start(bf16[3072,256]{1,0:T(8,128)(2,1)} %get-tuple-element.40), channel_id=1, source_target_pairs={{1,0},{2,1},{3,2},{5,4},{6,5},{7,6},{9,8},{10,9},{11,10},{13,12},{... | collective-permute-start | bytes 4718600 | tf_op jit(solution)/shard_map/ppermute | solution.py:1312
  954.1 34.1 %all-to-all-start.5 = ((bf16[8,256,256]{2,1,0:T(8,128)(2,1)}), bf16[8,256,256]{2,1,0:T(8,128)(2,1)}, u32[]{:S(2)}, u32[]{:S(2)}) async-start(bf16[8,256,256]{2,1,0:T(8,128)(2,1)} %bitcast.174), calls=%async_computation.6 | async-start | bytes 2097152 | tf_op jit(solution)/shard_map/all_to_all | solution.py:1301
  958.4 7.0 copy-start.4
  958.4 210.5 %reduce-scatter.7.cloned.1.call-start = ((), (), s32[]{:S(2)}) async-start(), calls=%async_computation.15 | async-start | bytes 1310720 | tf_op jit(solution)/shard_map/reduce_scatter | solution.py:1302
  974.1 12.8 %slice-start = ((s8[6291456]{0:T(1024)(128)(4,1)}), s8[4194304]{0:T(1024)(128)(4,1)S(1)}, s32[]{:S(2)}) async-start(s8[6291456]{0:T(1024)(128)(4,1)} %bitcast.181), calls=%async_computation.20 | async-start | bytes 8388608
  979.3 7.6 slice-start.1
  988.2 182.5 %reduce-scatter.5.cloned.1.call-start = ((), (), s32[]{:S(2)}) async-start(), calls=%async_computation.14 | async-start | bytes 2621440 | tf_op jit(solution)/shard_map/reduce_scatter | solution.py:1302
  988.3 5.8 slice-start.2
  1008.3 30.8 %copy-start.37 = (s32[3]{0:T(128)S(1)}, s32[3]{0:T(128)}, u32[]{:S(2)}) copy-start(s32[3]{0:T(128)} %lens_ref.3) | copy-start | bytes 40
  1042.3 61.5 %copy-start.7 = (bf16[384,2048]{1,0:T(8,128)(2,1)S(1)}, bf16[384,2048]{1,0:T(8,128)(2,1)}, u32[]{:S(2)}) copy-start(bf16[384,2048]{1,0:T(8,128)(2,1)} %param.15) | copy-start | bytes 4718596
  1042.3 61.6 %copy-start.32 = (f32[2048]{0:T(1024)S(1)}, f32[2048]{0:T(1024)}, u32[]{:S(2)}) copy-start(f32[2048]{0:T(1024)} %param.19) | copy-start | bytes 24580
  1042.3 61.6 %copy-start.35 = (f32[384]{0:T(512)S(1)}, f32[384]{0:T(512)}, u32[]{:S(2)}) copy-start(f32[384]{0:T(512)} %copy-done.34) | copy-start | bytes 4612
  1103.8 50.7 %copy-start.38 = (f32[384]{0:T(512)S(1)}, f32[384]{0:T(512)}, u32[]{:S(2)}) copy-start(f32[384]{0:T(512)} %get-tuple-element.181) | copy-start | bytes 4612
  1149.5 14.9 %all-to-all-start.7 = ((bf16[4,384,256]{2,1,0:T(8,128)(2,1)}), bf16[4,384,256]{2,1,0:T(8,128)(2,1)S(1)}, u32[]{:S(2)}, u32[]{:S(2)}) async-start(bf16[4,384,256]{2,1,0:T(8,128)(2,1)} %bitcast.223), calls=%async_computation.11 | async-start | bytes 1572864 | tf_op jit(solution)/shard_map/all_to_all | solution.py:1282
  1165.3 23.0 %all-to-all-start.6 = ((bf16[4,256,768]{2,1,0:T(8,128)(2,1)}), bf16[4,256,768]{2,1,0:T(8,128)(2,1)S(1)}, u32[]{:S(2)}, u32[]{:S(2)}) async-start(bf16[4,256,768]{2,1,0:T(8,128)(2,1)} %bitcast.216), calls=%async_computation.9 | async-start | bytes 3145728 | tf_op jit(solution)/shard_map/all_to_all | solution.py:1282
  1168.8 7.0 copy-start.24
  (20 other events, 49.7 us)
Sparse Core Ops, SparseCore 0:
  9.6 30.6 all-gather.8
  42.4 45.4 all-gather.6
  89.4 118.1 all-gather.10
  209.7 78.2 all-gather.12
  677.7 59.2 reduce-scatter.10
  739.1 110.7 reduce-scatter.8
  988.4 27.7 reduce-scatter.6
  1039.2 42.4 reduce-scatter.4

commit v2 on v1

--- a/solution.py
+++ b/solution.py
@@ -391,6 +391,11 @@
 BF16 = jnp.bfloat16
 MESH = pl.DeviceIdType.MESH
 VMEM_LIMIT = 62 << 20
+
+
+def busy(us):
+    return pl.CostEstimate(flops=0, bytes_accessed=us * 3_000_000, transcendentals=0)
+
 LOG2E = 1.4426950408889634
 UNIT = 128
 KEYS = 512
@@ -439,6 +444,25 @@
 SUBS = 4
 
 
+def on_ctx(device):
+    return {"ctx": device}
+
+
+def on_plane(plane):
+    return {"tp": plane}
+
+
+def send(src, dst, send_sem, recv_sem, where):
+    return pltpu.make_async_remote_copy(
+        src_ref=src,
+        dst_ref=dst,
+        send_sem=send_sem,
+        recv_sem=recv_sem,
+        device_id=where,
+        device_id_type=MESH,
+    )
+
+
 class Gather:
     def __init__(self, x_ref, xs, local_sem, send_sems, recv_sems):
         self.x_ref, self.xs = x_ref, xs
@@ -451,20 +475,14 @@
         return self.xs.at[block, pl.ds(s * self.piece, self.piece)]
 
     def remote(self, src, kind, block, s, device):
-        return pltpu.make_async_remote_copy(
-            src_ref=src,
-            dst_ref=self.part(block, s),
-            send_sem=self.send_sems.at[kind, s],
-            recv_sem=self.recv_sems.at[block, s],
-            device_id={"ctx": device},
-            device_id_type=MESH,
+        return send(
+            src, self.part(block, s), self.send_sems.at[kind, s], self.recv_sems.at[block, s], on_ctx(device)
         )
 
     def own(self, s):
         return self.x_ref.at[pl.ds(s * self.piece, self.piece)]
 
     def start(self):
-        greet((self.sib, self.nx, self.ny))
         for s in range(SUBS):
             t = (s + SUBS // 2) % SUBS
             self.remote(self.own(s), 0, self.me, s, self.nx).start()
@@ -549,6 +567,101 @@
     ]
 
 
+class Scatter:
+    def __init__(self, to_sib, from_sib, own, diag_out, diag_in, x_out, y_out, x_in, y_in, sends, recvs):
+        self.to_sib, self.from_sib, self.own = to_sib, from_sib, own
+        self.diag_out, self.diag_in = diag_out, diag_in
+        self.x_out, self.y_out, self.x_in, self.y_in = x_out, y_out, x_in, y_in
+        self.sends, self.recvs = sends, recvs
+        self.me, self.sib, self.nx, self.ny, self.dg = plane_neighbours()
+        half = diag_out.shape[0] // 2
+        self.first, self.second = first, second = pl.ds(0, half), pl.ds(half, half)
+        nx, ny = self.nx, self.ny
+        self.diag_x = self.remote(diag_out.at[first], diag_in.at[first], 4, nx)
+        self.diag_y = self.remote(diag_out.at[second], diag_in.at[second], 5, ny)
+        self.x_first = self.remote(x_out.at[first], x_in.at[first], 6, nx)
+        self.x_second = self.remote(x_out.at[second], x_in.at[second], 7, nx)
+        self.y_first = self.remote(y_out.at[first], y_in.at[first], 8, ny)
+        self.y_second = self.remote(y_out.at[second], y_in.at[second], 9, ny)
+
+    def remote(self, src, dst, n, device):
+        return send(src, dst, self.sends.at[n], self.recvs.at[n], on_ctx(device))
+
+    def sibling(self, n):
+        return self.remote(self.to_sib.at[n], self.from_sib.at[n], n, self.sib)
+
+    def block(self, step):
+        shift = self.sib - self.me
+        return pick(step, [b + o for b in (self.dg, self.nx, self.ny, self.me) for o in (shift, 0)])
+
+    def chip_sum(self, n, at):
+        return self.own[n, at].astype(F32) + self.from_sib[n, at].astype(F32)
+
+    def step(self, step, product):
+        block = self.block(step)
+        n = step // 2
+        first, second = self.first, self.second
+
+        @pl.when(lax.rem(step, 2) == 0)
+        def _():
+            product(block, self.to_sib, n)
+            self.sibling(n).start()
+
+        @pl.when(lax.rem(step, 2) == 1)
+        def _():
+            product(block, self.own, n)
+            self.sibling(n).wait_recv()
+
+        @pl.when(step == 1)
+        def _():
+            self.diag_out[first] = self.chip_sum(0, first).astype(BF16)
+            self.diag_x.start()
+            self.diag_out[second] = self.chip_sum(0, second).astype(BF16)
+            self.diag_y.start()
+
+        @pl.when(step == 3)
+        def _():
+            self.x_out[first] = self.chip_sum(1, first).astype(BF16)
+            self.x_first.start()
+
+        @pl.when(step == 5)
+        def _():
+            self.y_out[second] = self.chip_sum(2, second).astype(BF16)
+            self.y_second.start()
+            self.diag_x.wait_recv()
+            self.y_out[first] = (self.chip_sum(2, first) + self.diag_in[first].astype(F32)).astype(BF16)
+            self.y_first.start()
+            self.diag_y.wait_recv()
+            self.x_out[second] = (self.chip_sum(1, second) + self.diag_in[second].astype(F32)).astype(BF16)
+            self.x_second.start()
+
+    def finish(self, o_ref):
+        self.x_first.wait_recv()
+        self.y_first.wait_recv()
+        first, second = self.first, self.second
+        o_ref[first] = (
+            self.chip_sum(3, first) + self.x_in[first].astype(F32) + self.y_in[first].astype(F32)
+        ).astype(o_ref.dtype)
+        self.x_second.wait_recv()
+        self.y_second.wait_recv()
+        o_ref[second] = (
+            self.chip_sum(3, second) + self.x_in[second].astype(F32) + self.y_in[second].astype(F32)
+        ).astype(o_ref.dtype)
+        for n in range(4):
+            self.sibling(n).wait_send()
+        for copy in (self.diag_x, self.diag_y, self.x_first, self.x_second, self.y_first, self.y_second):
+            copy.wait_send()
+
+
+def scatter_scratch(rows, width):
+    four = pltpu.VMEM((4, rows, width), BF16)
+    one = pltpu.VMEM((rows, width), BF16)
+    return [four] * 3 + [one] * 6 + [pltpu.SemaphoreType.DMA((10,)), pltpu.SemaphoreType.DMA((10,))]
+
+
+N_SCATTER = 11
+
+
 def nn(left, right):
     return lax.dot_general(left, right, (((1,), (0,)), ((), ())), preferred_element_type=F32)
 
@@ -561,54 +674,344 @@
     return lax.dot_general(left, right, (((0,), (0,)), ((), ())), preferred_element_type=F32)
 
 
-def qkv_kernel(x_ref, w_ref, all_ref, qkv_ref, xs, local_sem, send_sems, recv_sems, keep_sems):
+def comm_params(collective_id):
+    return pltpu.CompilerParams(
+        collective_id=collective_id, has_side_effects=True, vmem_limit_bytes=VMEM_LIMIT
+    )
+
+
+def greet_column(devices):
+    barrier = pltpu.get_barrier_semaphore()
+    plane, planes = lax.axis_index("tp"), lax.axis_size("tp")
+    for device in devices:
+        pl.semaphore_signal(barrier, inc=1, device_id=on_ctx(device), device_id_type=MESH)
+    for step in (1, planes - 1):
+        where = on_plane(lax.rem(plane + step, planes))
+        pl.semaphore_signal(barrier, inc=1, device_id=where, device_id_type=MESH)
+    pl.semaphore_wait(barrier, len(devices) + 2)
+
+
+class Line:
+    def __init__(self, up_src, down_src, from_lo, from_hi, sends, recvs, rows, back):
+        self.up_src, self.down_src, self.from_lo, self.from_hi = up_src, down_src, from_lo, from_hi
+        self.sends, self.recvs = sends, recvs
+        self.units = rows // UNIT
+        self.back = back
+        self.plane, self.planes = lax.axis_index("tp"), lax.axis_size("tp")
+
+    def at(self, block, i):
+        return pl.ds(pl.multiple_of((block * self.units + i) * UNIT, UNIT), UNIT)
+
+    def up(self, block, i):
+        at, n = self.at(block, i), block * self.units + i
+        return send(self.up_src.at[at], self.from_lo.at[at], self.sends.at[0, n], self.recvs.at[0, n], on_plane(self.plane + 1))
+
+    def down(self, block, i):
+        at, n = self.at(block, i), block * self.units + i
+        return send(self.down_src.at[at], self.from_hi.at[at], self.sends.at[1, n], self.recvs.at[1, n], on_plane(self.plane - 1))
+
+    def each(self, block, ups, downs):
+        for i in range(self.units):
+            up = i < self.plane + 1 if self.back else i >= self.plane
+            down = i >= self.plane - 1 if self.back else i < self.plane
+
+            @pl.when(up & (self.plane < self.planes - 1))
+            def _():
+                ups(self.up(block, i))
+
+            @pl.when(down & (self.plane > 0))
+            def _():
+                downs(self.down(block, i))
+
+    def start(self, block):
+        self.each(block, lambda copy: copy.start(), lambda copy: copy.start())
+
+    def sent(self, block):
+        self.each(block, lambda copy: copy.wait_send(), lambda copy: copy.wait_send())
+
+    def arrived(self, block):
+        for i in range(self.units):
+            below = i < self.plane if self.back else i >= self.plane - 1
+            above = i >= self.plane if self.back else i < self.plane + 1
+
+            @pl.when(below & (self.plane > 0))
+            def _():
+                self.up(block, i).wait_recv()
+
+            @pl.when(above & (self.plane < self.planes - 1))
+            def _():
+                self.down(block, i).wait_recv()
+
+
+class Turn:
+    def __init__(self, ca_ref, sa_ref, cb_ref, sb_ref, unit):
+        ca, sa = ca_ref[pl.ds(unit, 1), :], sa_ref[pl.ds(unit, 1), :]
+        cb, sb = cb_ref[...], sb_ref[...]
+        self.cosine = ca * cb - sa * sb
+        sine = sa * cb + ca * sb
+        lane = lax.broadcasted_iota(jnp.int32, sine.shape, 1)
+        self.sine = jnp.where(lane < HEAD_SIZE // 2, -sine, sine)
+
+    def forth(self, v):
+        return v * self.cosine + pltpu.roll(v, HEAD_SIZE // 2, 1) * self.sine
+
+    def back(self, v):
+        return v * self.cosine - pltpu.roll(v, HEAD_SIZE // 2, 1) * self.sine
+
+
+def others(me):
+    _, sib, nx, ny, dg = plane_neighbours()
+    shift = sib - me
+    return (dg, dg + shift, nx, nx + shift, ny, ny + shift, sib)
+
+
+def qkv_kernel(
+    x_ref,
+    slab_ref,
+    qg_ref,
+    kg_ref,
+    ca_ref,
+    sa_ref,
+    cb_ref,
+    sb_ref,
+    all_ref,
+    w_out_ref,
+    q_ref,
+    kv_ref,
+    lo_ref,
+    hi_ref,
+    lin_ref,
+    xs,
+    local_sem,
+    send_sems,
+    recv_sems,
+    keep_sems,
+    w,
+    w_local,
+    w_sends,
+    w_recvs,
+    kv_sends,
+    kv_recvs,
+):
     ring = Gather(x_ref, xs, local_sem, send_sems, recv_sems)
+    me = ring.me
     rows = x_ref.shape[0]
+    deep = slab_ref.shape[1]
+    away = others(me)
+    greet_column(away)
+
+    def weight(device, n):
+        return send(slab_ref.at[device], w.at[pl.ds(me * deep, deep)], w_sends.at[n], w_recvs.at[me], on_ctx(device))
+
+    def weight_from(device):
+        return send(slab_ref.at[device], w.at[pl.ds(device * deep, deep)], w_sends.at[0], w_recvs.at[device], on_ctx(device))
+
+    for n, device in enumerate(away):
+        weight(device, n).start()
+    own_weight = pltpu.make_async_copy(slab_ref.at[me], w.at[pl.ds(me * deep, deep)], w_local)
+    own_weight.start()
     ring.start()
+    own_weight.wait()
+    for device in away:
+        weight_from(device).wait_recv()
+    keep_w = pltpu.make_async_copy(w, w_out_ref, w_local)
+    keep_w.start()
 
     def keep(block):
         return pltpu.make_async_copy(xs.at[block], all_ref.at[block], keep_sems.at[block])
+
+    line = Line(kv_ref, kv_ref, lo_ref, hi_ref, kv_sends, kv_recvs, rows, False)
+
+    def head(v, gain_ref, turn):
+        scale = lax.rsqrt(jnp.mean(v * v, axis=-1, keepdims=True) + EPS)
+        return turn.forth(v * scale * gain_ref[...])
 
     def turn(step, carry):
         ring.before(step)
         block = ring.block(step)
         keep(block).start()
-        qkv_ref[pl.ds(block * rows, rows), :] = nn(xs[block], w_ref[...])
+        lin = nn(xs[block], w[...])
+        lin_ref[pl.ds(pl.multiple_of(block * rows, rows), rows), :] = lin[:, : 3 * HEAD_SIZE]
+        for i in range(rows // UNIT):
+            unit = block * (rows // UNIT) + i
+            rotation = Turn(ca_ref, sa_ref, cb_ref, sb_ref, unit)
+            here = pl.ds(pl.multiple_of(unit * UNIT, UNIT), UNIT)
+            part = lin[i * UNIT : (i + 1) * UNIT]
+            for h in range(2):
+                lanes = slice(h * HEAD_SIZE, (h + 1) * HEAD_SIZE)
+                query = head(part[:, lanes], qg_ref, rotation)
+                q_ref[here, lanes] = (query * (HEAD_SIZE**-0.5 * LOG2E)).astype(BF16)
+            key = head(part[:, 2 * HEAD_SIZE : 3 * HEAD_SIZE], kg_ref, rotation)
+            kv_ref[here, :HEAD_SIZE] = key.astype(BF16)
+            kv_ref[here, HEAD_SIZE:] = part[:, 3 * HEAD_SIZE :].astype(BF16)
+        line.start(block)
         return carry
 
     lax.fori_loop(0, 8, turn, 0)
     ring.finish()
+    keep_w.wait()
+    for n, device in enumerate(away):
+        weight(device, n).wait_send()
     for block in range(8):
         keep(block).wait()
 
-
-def gather_qkv(normed, w_qkv):
+    def settle(block, carry):
+        line.sent(block)
+        line.arrived(block)
+        return carry
+
+    lax.fori_loop(0, 8, settle, 0)
+
+
+def gather_qkv(normed, slab, q_gain, k_gain, tables):
     rows, width = normed.shape
+    _, deep, cols = slab.shape
+    flat = jax.ShapeDtypeStruct((8 * rows, 2 * HEAD_SIZE), BF16)
     return pl.pallas_call(
         qkv_kernel,
         out_shape=(
             jax.ShapeDtypeStruct((8, rows, width), BF16),
-            jax.ShapeDtypeStruct((8 * rows, w_qkv.shape[1]), F32),
+            jax.ShapeDtypeStruct((8 * deep, cols), BF16),
+            flat,
+            flat,
+            flat,
+            flat,
+            jax.ShapeDtypeStruct((8 * rows, 3 * HEAD_SIZE), F32),
         ),
-        in_specs=[spec_vmem(), spec_vmem()],
-        out_specs=(spec_any(), spec_vmem()),
-        scratch_shapes=gather_scratch(rows, width) + [pltpu.SemaphoreType.DMA((8,))],
-        compiler_params=pltpu.CompilerParams(
-            collective_id=1, has_side_effects=True, vmem_limit_bytes=VMEM_LIMIT
-        ),
+        in_specs=[spec_vmem(), spec_any()] + [spec_vmem()] * 6,
+        out_specs=(spec_any(), spec_any(), spec_vmem(), spec_vmem(), spec_any(), spec_any(), spec_vmem()),
+        scratch_shapes=gather_scratch(rows, width)
+        + [
+            pltpu.SemaphoreType.DMA((8,)),
+            pltpu.VMEM((8 * deep, cols), BF16),
+            pltpu.SemaphoreType.DMA,
+            pltpu.SemaphoreType.DMA((7,)),
+            pltpu.SemaphoreType.DMA((8,)),
+            pltpu.SemaphoreType.DMA((2, 8 * rows // UNIT)),
+            pltpu.SemaphoreType.DMA((2, 8 * rows // UNIT)),
+        ],
+        compiler_params=comm_params(1),
+        cost_estimate=busy(80),
         name="gather_qkv",
-    )(normed, w_qkv)
+    )(normed, slab, q_gain.reshape(1, -1), k_gain.reshape(1, -1), *tables)
+
+
+class Halves:
+    def __init__(self, parts, at, local_sems, send_sems, recv_sems):
+        self.parts, self.at = parts, at
+        self.local_sems, self.send_sems, self.recv_sems = local_sems, send_sems, recv_sems
+        self.me, self.sib = plane_neighbours()[:2]
+        self.core = lax.rem(self.me, 2)
+
+    def own(self, z, p):
+        n = 4 * z + p
+        return pltpu.make_async_copy(
+            self.parts.at[2 * self.core + z, p], self.at(z, 2 * p + self.core), self.local_sems.at[n]
+        )
+
+    def swap(self, z, p):
+        n = 4 * z + p
+        return send(
+            self.parts.at[2 - 2 * self.core + z, p],
+            self.at(z, 2 * p + self.core),
+            self.send_sems.at[n],
+            self.recv_sems.at[n],
+            on_ctx(self.sib),
+        )
+
+    def each(self):
+        return [(z, p) for z in range(2) for p in range(4)]
+
+    def start(self):
+        for z, p in self.each():
+            self.swap(z, p).start()
+            self.own(z, p).start()
+
+    def ready(self):
+        for z, p in self.each():
+            self.own(z, p).wait()
+            n = 4 * z + p
+            send(
+                self.parts.at[2 * self.core + z, p],
+                self.at(z, 2 * p + 1 - self.core),
+                self.send_sems.at[n],
+                self.recv_sems.at[n],
+                on_ctx(self.sib),
+            ).wait_recv()
+
+    def finish(self):
+        for z, p in self.each():
+            self.swap(z, p).wait_send()
+
+
+class Shares:
+    def __init__(self, out, local_sems, send_sems, recv_sems):
+        self.out = out
+        self.local_sems, self.send_sems, self.recv_sems = local_sems, send_sems, recv_sems
+        self.me, self.sib = plane_neighbours()[:2]
+        self.core = lax.rem(self.me, 2)
+
+    def own(self, tile, z, p):
+        return pltpu.make_async_copy(tile, self.out.at[2 * self.core + z, p], self.local_sems.at[z, p])
+
+    def other(self, tile, z, p):
+        return send(
+            tile,
+            self.out.at[2 * self.core + z, p],
+            self.send_sems.at[z, p],
+            self.recv_sems.at[z, p],
+            on_ctx(self.sib),
+        )
+
+    def arrive(self):
+        for z in range(2):
+            for p in range(4):
+                there = self.out.at[2 - 2 * self.core + z, p]
+                send(
+                    there, there, self.send_sems.at[z, p], self.recv_sems.at[z, p], on_ctx(self.sib)
+                ).wait_recv()
+
+
+SHARES_SCRATCH = [pltpu.SemaphoreType.DMA((2, 4))] * 3
+HALVES_SCRATCH = [pltpu.SemaphoreType.DMA((8,))] * 3
 
 
 def up_kernel(
-    x_ref, w_ref, all_ref, a_ref, b_ref, h_ref, xs, local_sem, send_sems, recv_sems, keep_sems, stage, stage_sems
+    x_ref,
+    gate_ref,
+    up_ref,
+    all_ref,
+    w_out_ref,
+    a_ref,
+    b_ref,
+    h_ref,
+    xs,
+    local_sem,
+    send_sems,
+    recv_sems,
+    keep_sems,
+    stage,
+    stage_sems,
+    w,
+    w_sem,
+    *w_sems,
 ):
     ring = Gather(x_ref, xs, local_sem, send_sems, recv_sems)
     rows = x_ref.shape[0]
-    halves, _, wide = w_ref.shape
+    halves, width, wide = w.shape
+    deep = width // 8
     cols = wide // 2
     outs = (a_ref, b_ref, h_ref)
+    greet((ring.sib, ring.nx, ring.ny))
     ring.start()
+    gates = Halves(gate_ref, lambda z, c: w.at[z, pl.ds(c * deep, deep), pl.ds(0, cols)], *w_sems[:3])
+    ups = Halves(up_ref, lambda z, c: w.at[z, pl.ds(c * deep, deep), pl.ds(cols, cols)], *w_sems[3:])
+    gates.start()
+    ups.start()
+    gates.ready()
+    ups.ready()
+    keep_w = pltpu.make_async_copy(w, w_out_ref, w_sem)
+    keep_w.start()
 
     def keep(block):
         return pltpu.make_async_copy(xs.at[block], all_ref.at[block], keep_sems.at[block])
@@ -630,7 +1033,7 @@
                 put(slot, n, block).wait()
 
         for z in range(halves):
-            both = nn(xs[block], w_ref[z])
+            both = nn(xs[block], w[z])
             gate, up = both[:, :cols], both[:, cols:]
             sigma = jax.nn.sigmoid(gate)
             active = gate * sigma
@@ -644,6 +1047,9 @@
 
     lax.fori_loop(0, 8, turn, 0)
     ring.finish()
+    gates.finish()
+    ups.finish()
+    keep_w.wait()
     for block in range(8):
         keep(block).wait()
     for slot in range(2):
@@ -651,39 +1057,120 @@
             put(slot, n, 0).wait()
 
 
-def gather_up(post, w_gu):
+def gather_up(post, gate_parts, up_parts):
     rows, width = post.shape
-    halves, _, wide = w_gu.shape
-    ff = halves * wide // 2
-    flat = jax.ShapeDtypeStruct((8 * rows, ff), BF16)
+    wide = 2 * gate_parts.shape[-1]
+    flat = jax.ShapeDtypeStruct((8 * rows, wide), BF16)
     return pl.pallas_call(
         up_kernel,
-        out_shape=(jax.ShapeDtypeStruct((8, rows, width), BF16), flat, flat, flat),
-        in_specs=[spec_vmem(), spec_vmem()],
-        out_specs=(spec_any(),) * 4,
+        out_shape=(
+            jax.ShapeDtypeStruct((8, rows, width), BF16),
+            jax.ShapeDtypeStruct((2, width, wide), BF16),
+            flat,
+            flat,
+            flat,
+        ),
+        in_specs=[spec_vmem(), spec_any(), spec_any()],
+        out_specs=(spec_any(),) * 5,
         scratch_shapes=gather_scratch(rows, width)
         + [
             pltpu.SemaphoreType.DMA((8,)),
-            pltpu.VMEM((2, 3, rows, ff), BF16),
+            pltpu.VMEM((2, 3, rows, wide), BF16),
             pltpu.SemaphoreType.DMA((2, 3)),
-        ],
-        compiler_params=pltpu.CompilerParams(
-            collective_id=2, has_side_effects=True, vmem_limit_bytes=VMEM_LIMIT
-        ),
+            pltpu.VMEM((2, width, wide), BF16),
+            pltpu.SemaphoreType.DMA,
+        ]
+        + HALVES_SCRATCH * 2,
+        compiler_params=comm_params(2),
+        cost_estimate=busy(62),
         name="gather_up",
-    )(post, w_gu)
+    )(post, gate_parts, up_parts)
+
+
+def down_kernel(h_ref, parts_ref, o_ref, w_out_ref, *scratch):
+    rs = Scatter(*scratch[:N_SCATTER])
+    w, w_sem, w_local, w_sends, w_recvs = scratch[N_SCATTER:]
+    rows = o_ref.shape[0]
+    _, _, cols, deep = parts_ref.shape
+    greet((rs.sib, rs.nx, rs.ny))
+    weight = Halves(
+        parts_ref,
+        lambda z, c: w.at[pl.ds(z * cols, cols), pl.ds(pl.multiple_of(c * deep, deep), deep)],
+        w_local,
+        w_sends,
+        w_recvs,
+    )
+    weight.start()
+    weight.ready()
+    keep_w = pltpu.make_async_copy(w, w_out_ref, w_sem)
+    keep_w.start()
+
+    def product(block, out, n):
+        left = h_ref[pl.ds(pl.multiple_of(block * rows, rows), rows), :]
+        for c in range(0, w.shape[1], 512):
+            out[n, :, c : c + 512] = nn(left, w[:, c : c + 512]).astype(BF16)
+
+    def turn(step, carry):
+        rs.step(step, product)
+        return carry
+
+    lax.fori_loop(0, 8, turn, 0)
+    rs.finish(o_ref)
+    weight.finish()
+    keep_w.wait()
+
+
+def scatter_down(hidden, parts):
+    rows = hidden.shape[0] // 8
+    ff = hidden.shape[1]
+    width = 8 * parts.shape[-1]
+    return pl.pallas_call(
+        down_kernel,
+        out_shape=(jax.ShapeDtypeStruct((rows, width), F32), jax.ShapeDtypeStruct((ff, width), BF16)),
+        in_specs=[spec_vmem(), spec_any()],
+        out_specs=(spec_vmem(), spec_any()),
+        scratch_shapes=scatter_scratch(rows, width)
+        + [pltpu.VMEM((ff, width), BF16), pltpu.SemaphoreType.DMA]
+        + HALVES_SCRATCH,
+        compiler_params=comm_params(6),
+        cost_estimate=busy(62),
+        name="scatter_down",
+    )(hidden, parts)
 
 
 def down_back_kernel(
-    x_ref, w_ref, a_ref, b_ref, h_ref, d_ref, gw_ref, xs, local_sem, send_sems, recv_sems, stage, stage_sems
+    x_ref,
+    w_ref,
+    a_ref,
+    b_ref,
+    h_ref,
+    d_ref,
+    gw_ref,
+    xs,
+    local_sem,
+    send_sems,
+    recv_sems,
+    stage,
+    stage_sems,
+    total,
+    low,
+    s_local,
+    s_sends,
+    s_recvs,
 ):
     ring = Gather(x_ref, xs, local_sem, send_sems, recv_sems)
     rows = x_ref.shape[0]
     ff = w_ref.shape[0]
     cols = ff // 2
     width = x_ref.shape[1]
+    greet((ring.sib, ring.nx, ring.ny))
     ring.start()
-    gw_ref[...] = jnp.zeros_like(gw_ref)
+    total[...] = jnp.zeros_like(total)
+    shares = Shares(gw_ref, s_local, s_sends, s_recvs)
+    deep = width // 8
+
+    def tile(z, c):
+        return low.at[pl.ds(z * cols, cols), pl.ds(pl.multiple_of(c * deep, deep), deep)]
 
     def put(slot, block):
         return pltpu.make_async_copy(
@@ -717,14 +1204,25 @@
             hidden = h_ref[pl.ds(pair * 2 * rows, 2 * rows), :]
             for n in range(0, width, 512):
                 seen = xs[pl.ds(pair * 2, 2), :, n : n + 512].reshape(2 * rows, 512)
-                gw_ref[:, n : n + 512] += tn(hidden, seen)
+                total[:, n : n + 512] += tn(hidden, seen)
 
         return carry
 
     lax.fori_loop(0, 8, turn, 0)
     ring.finish()
+    low[...] = total[...].astype(BF16)
+    core = shares.core
+    for z in range(2):
+        for p in range(4):
+            shares.other(tile(z, 2 * p + 1 - core), z, p).start()
+            shares.own(tile(z, 2 * p + core), z, p).start()
     for slot in range(2):
         put(slot, 0).wait()
+    shares.arrive()
+    for z in range(2):
+        for p in range(4):
+            shares.other(tile(z, 2 * p + 1 - core), z, p).wait_send()
+            shares.own(tile(z, 2 * p + core), z, p).wait()
 
 
 def gather_down_back(diff, w_down, a, b, hidden):
@@ -734,187 +1232,702 @@
         down_back_kernel,
         out_shape=(
             jax.ShapeDtypeStruct((8 * rows, 2 * ff), BF16),
-            jax.ShapeDtypeStruct((ff, width), F32),
+            jax.ShapeDtypeStruct((4, 4, ff // 2, width // 8), BF16),
         ),
         in_specs=[spec_vmem()] * 5,
-        out_specs=(spec_any(), spec_vmem()),
+        out_specs=(spec_any(), spec_any()),
         scratch_shapes=gather_scratch(rows, width)
-        + [pltpu.VMEM((2, rows, 2 * ff), BF16), pltpu.SemaphoreType.DMA((2,))],
-        compiler_params=pltpu.CompilerParams(
-            collective_id=3, has_side_effects=True, vmem_limit_bytes=VMEM_LIMIT
-        ),
+        + [
+            pltpu.VMEM((2, rows, 2 * ff), BF16),
+            pltpu.SemaphoreType.DMA((2,)),
+            pltpu.VMEM((ff, width), F32),
+            pltpu.VMEM((ff, width), BF16),
+        ]
+        + SHARES_SCRATCH,
+        compiler_params=comm_params(3),
+        cost_estimate=busy(66),
         name="gather_down_back",
     )(diff, w_down, a, b, hidden)
 
 
-def out_back_kernel(x_ref, w_ref, m_ref, d_ref, gw_ref, xs, local_sem, send_sems, recv_sems):
-    ring = Gather(x_ref, xs, local_sem, send_sems, recv_sems)
-    rows, width = x_ref.shape
-    ring.start()
-    gw_ref[...] = jnp.zeros_like(gw_ref)
-
-    def turn(step, carry):
-        ring.before(step)
-        block = ring.block(step)
-        d_ref[pl.ds(block * rows, rows), :] = nt(xs[block], w_ref[...]).astype(BF16)
-
-        @pl.when(lax.rem(step, 2) == 1)
-        def _():
-            pair = block // 2
-            mixed = m_ref[pl.ds(pair * 2 * rows, 2 * rows), :]
-            for n in range(0, width, 512):
-                seen = xs[pl.ds(pair * 2, 2), :, n : n + 512].reshape(2 * rows, 512)
-                gw_ref[:, n : n + 512] += tn(mixed, seen)
-
-        return carry
-
-    lax.fori_loop(0, 8, turn, 0)
-    ring.finish()
-
-
-def gather_out_back(d_mid, w_out, mixed):
-    rows, width = d_mid.shape
-    heads = w_out.shape[0]
-    return pl.pallas_call(
-        out_back_kernel,
-        out_shape=(
-            jax.ShapeDtypeStruct((8 * rows, heads), BF16),
-            jax.ShapeDtypeStruct((heads, width), F32),
-        ),
-        in_specs=[spec_vmem()] * 3,
-        out_specs=(spec_vmem(), spec_vmem()),
-        scratch_shapes=gather_scratch(rows, width),
-        compiler_params=pltpu.CompilerParams(
-            collective_id=4, has_side_effects=True, vmem_limit_bytes=VMEM_LIMIT
-        ),
-        name="gather_out_back",
-    )(d_mid, w_out, mixed)
-
-
-def scatter_kernel(
-    product, a_ref, w_ref, o_ref, to_sib, from_sib, own, diag_out, diag_in, x_out, y_out, x_in, y_in, sends, recvs
+def mix_kernel(
+    mixed_ref,
+    tokens_ref,
+    gain_ref,
+    w0_ref,
+    w1_ref,
+    w2_ref,
+    w3_ref,
+    middle_ref,
+    post_ref,
+    rows_ref,
+    w_ref,
+    held,
+    w,
+    m_sems,
+    m_sends,
+    m_recvs,
+    w_local,
+    w_sends,
+    w_recvs,
+    keep_sems,
 ):
     me, sib, nx, ny, dg = plane_neighbours()
     shift = sib - me
+    away = others(me)
+    rows, width = held.shape
+    deep = width // 8
+    greet(away)
+
+    def block(c):
+        return pl.ds(pl.multiple_of(c * rows, rows), rows)
+
+    def lanes(c):
+        return pl.ds(pl.multiple_of(c * deep, deep), deep)
+
+    def give(n, c):
+        return send(mixed_ref.at[block(c)], held.at[:, lanes(me)], m_sends.at[n], m_recvs.at[me], on_ctx(c))
+
+    def take(c):
+        return send(mixed_ref.at[block(c)], held.at[:, lanes(c)], m_sends.at[0], m_recvs.at[c], on_ctx(c))
+
+    for n, c in enumerate(away):
+        give(n, c).start()
+    own = pltpu.make_async_copy(mixed_ref.at[block(me)], held.at[:, lanes(me)], m_sems)
+    own.start()
+    parts = ((w0_ref, me), (w1_ref, nx), (w2_ref, ny), (w3_ref, dg))
+
+    def swap(n):
+        part, c = parts[n]
+        return send(part, w.at[:, lanes(c)], w_sends.at[n], w_recvs.at[n], on_ctx(sib))
+
+    def place(n):
+        part, c = parts[n]
+        return pltpu.make_async_copy(part, w.at[:, lanes(c)], w_local.at[n])
+
+    for n in range(4):
+        swap(n).start()
+        place(n).start()
+    for n in range(4):
+        place(n).wait()
+        there = w.at[:, lanes(parts[n][1] + shift)]
+        send(there, there, w_sends.at[n], w_recvs.at[n], on_ctx(sib)).wait_recv()
+    own.wait()
+    for c in away:
+        take(c).wait_recv()
+    keep_rows = pltpu.make_async_copy(held, rows_ref, keep_sems.at[0])
+    keep_rows.start()
+    keep_w = pltpu.make_async_copy(w, w_ref, keep_sems.at[1])
+    keep_w.start()
+    total = jnp.zeros((rows, 1), F32)
+    for n in range(0, width, 512):
+        at = slice(n, n + 512)
+        middle = tokens_ref[:, at].astype(F32) + nn(held[...], w[:, at])
+        middle_ref[:, at] = middle
+        total += jnp.sum(middle * middle, axis=-1, keepdims=True)
+    scale = lax.rsqrt(total / width + EPS)
+    for n in range(0, width, 512):
+        at = slice(n, n + 512)
+        post_ref[:, at] = (middle_ref[:, at] * scale * gain_ref[:, at]).astype(BF16)
+    for n, c in enumerate(away):
+        give(n, c).wait_send()
+    for n in range(4):
+        swap(n).wait_send()
+    keep_rows.wait()
+    keep_w.wait()
+
+
+def mix(mixed, tokens, post_gain, parts):
+    rows, width = tokens.shape
+    dma = pltpu.SemaphoreType.DMA
+    return pl.pallas_call(
+        mix_kernel,
+        out_shape=(
+            jax.ShapeDtypeStruct((rows, width), F32),
+            jax.ShapeDtypeStruct((rows, width), BF16),
+            jax.ShapeDtypeStruct((rows, width), BF16),
+            jax.ShapeDtypeStruct((width, width), BF16),
+        ),
+        in_specs=[spec_any(), spec_vmem(), spec_vmem()] + [spec_any()] * 4,
+        out_specs=(spec_vmem(), spec_vmem(), spec_any(), spec_any()),
+        scratch_shapes=[
+            pltpu.VMEM((rows, width), BF16),
+            pltpu.VMEM((width, width), BF16),
+            dma,
+            dma((7,)),
+            dma((8,)),
+            dma((4,)),
+            dma((4,)),
+            dma((4,)),
+            dma((2,)),
+        ],
+        compiler_params=comm_params(5),
+        cost_estimate=busy(28),
+        name="mix",
+    )(mixed, tokens, post_gain.reshape(1, -1), *parts)
+
+
+def mix_back_kernel(
+    d_ref,
+    w_ref,
+    rows_ref,
+    dm_ref,
+    g0_ref,
+    g1_ref,
+    g2_ref,
+    g3_ref,
+    stage,
+    to_sib,
+    from_sib,
+    own,
+    out_sem,
+    out_sends,
+    out_recvs,
+    s_sends,
+    s_recvs,
+    g_sems,
+):
+    me, sib, nx, ny, dg = plane_neighbours()
+    shift = sib - me
+    away = others(me)
+    rows, width = d_ref.shape
+    deep = width // 8
+    greet(away)
+    outs = (g0_ref, g1_ref, g2_ref, g3_ref)
+    chips = (me, nx, ny, dg)
+
+    def block(c):
+        return pl.ds(pl.multiple_of(c * rows, rows), rows)
+
+    def give(n, c):
+        return send(stage.at[c], dm_ref.at[block(me)], out_sends.at[n], out_recvs.at[me], on_ctx(c))
+
+    def take(c):
+        return send(stage.at[c], dm_ref.at[block(c)], out_sends.at[0], out_recvs.at[c], on_ctx(c))
+
+    def heads(n, carry):
+        c = pick(n, away + (me,))
+        at = pl.ds(pl.multiple_of(c * deep, deep), deep)
+        stage[c] = nt(d_ref[...], w_ref[at, :]).astype(BF16)
+
+        @pl.when(n < 7)
+        def _():
+            give(n, c).start()
+
+        return carry
+
+    lax.fori_loop(0, 8, heads, 0)
+    keep = pltpu.make_async_copy(stage.at[me], dm_ref.at[block(me)], out_sem)
+    keep.start()
+
+    def swap(n):
+        return send(to_sib.at[n], from_sib.at[n], s_sends.at[n], s_recvs.at[n], on_ctx(sib))
+
+    def grad(n, out, c):
+        at = pl.ds(pl.multiple_of(c * deep, deep), deep)
+        out[n] = tn(rows_ref[...], d_ref[:, at]).astype(BF16)
+
+    def theirs(n, carry):
+        grad(n, to_sib, pick(n, chips) + shift)
+        swap(n).start()
+        return carry
+
+    def ours(n, carry):
+        grad(n, own, pick(n, chips))
+        return carry
+
+    lax.fori_loop(0, 4, theirs, 0)
+    lax.fori_loop(0, 4, ours, 0)
+    for n in range(4):
+        swap(n).wait_recv()
+        own[n] = (own[n].astype(F32) + from_sib[n].astype(F32)).astype(BF16)
+        pltpu.make_async_copy(own.at[n], outs[n], g_sems.at[n]).start()
+    for c in away:
+        take(c).wait_recv()
+    keep.wait()
+    for n, c in enumerate(away):
+        give(n, c).wait_send()
+    for n in range(4):
+        swap(n).wait_send()
+        pltpu.make_async_copy(own.at[n], outs[n], g_sems.at[n]).wait()
+
+
+def mix_back(d_mid, w, mixed_rows):
+    rows, width = d_mid.shape
+    deep = width // 8
+    dma = pltpu.SemaphoreType.DMA
+    four = pltpu.VMEM((4, width, deep), BF16)
+    return pl.pallas_call(
+        mix_back_kernel,
+        out_shape=(jax.ShapeDtypeStruct((8 * rows, deep), BF16),)
+        + (jax.ShapeDtypeStruct((width, deep), BF16),) * 4,
+        in_specs=[spec_vmem()] * 3,
+        out_specs=(spec_any(),) * 5,
+        scratch_shapes=[
+            pltpu.VMEM((8, rows, deep), BF16),
+            four,
+            four,
+            four,
+            dma,
+            dma((7,)),
+            dma((8,)),
+            dma((4,)),
+            dma((4,)),
+            dma((4,)),
+        ],
+        compiler_params=comm_params(4),
+        cost_estimate=busy(26),
+        name="mix_back",
+    )(d_mid, w, mixed_rows)
+
+
+def columns(all_ref, slices, sems, c, slot):
+    deep = slices.shape[-1]
+    return pltpu.make_async_copy(
+        all_ref.at[:, :, pl.ds(pl.multiple_of(c * deep, deep), deep)], slices.at[slot], sems.at[slot]
+    )
+
+
+def post_back_kernel(d_ref, w_ref, all_ref, o_ref, gw_ref, *scratch):
+    rs = Scatter(*scratch[:N_SCATTER])
+    slices, slice_sems, tile, s_local, s_sends, s_recvs = scratch[N_SCATTER:]
+    shares = Shares(gw_ref, s_local, s_sends, s_recvs)
+    rows = o_ref.shape[0]
+    _, width, wide = w_ref.shape
+    plane_rows = d_ref.shape[0]
+    deep = width // 8
+    greet((rs.sib, rs.nx, rs.ny))
+    columns(all_ref, slices, slice_sems, 0, 0).start()
+
+    def product(block, out, n):
+        here = pl.ds(pl.multiple_of(block * rows, rows), rows)
+        for c in range(0, width, 512):
+            total = nt(d_ref[here, :wide], w_ref[0, c : c + 512, :])
+            total += nt(d_ref[here, wide:], w_ref[1, c : c + 512, :])
+            out[n, :, c : c + 512] = total.astype(BF16)
+
+    def put(slot, p, act):
+        @pl.when(slot == shares.core)
+        def _():
+            for z in range(2):
+                copy = shares.own(tile.at[slot, z], z, p)
+                copy.start() if act == "start" else copy.wait()
+
+        @pl.when(slot != shares.core)
+        def _():
+            for z in range(2):
+                copy = shares.other(tile.at[slot, z], z, p)
+                copy.start() if act == "start" else copy.wait_send()
+
+    def grad(c):
+        slot = lax.rem(c, 2)
+        columns(all_ref, slices, slice_sems, c, slot).wait()
+
+        @pl.when(c < 7)
+        def _():
+            columns(all_ref, slices, slice_sems, c + 1, 1 - slot).start()
+
+        @pl.when(c >= 2)
+        def _():
+            put(slot, c // 2 - 1, "wait")
+
+        seen = slices[slot].reshape(plane_rows, deep)
+        for z in range(2):
+            tile[slot, z] = tn(seen, d_ref[:, z * wide : (z + 1) * wide]).astype(BF16)
+        put(slot, c // 2, "start")
+
+    def turn(t, carry):
+        is_grad = ((t >= 5) & (t < 8)) | (t >= 11)
+
+        @pl.when(is_grad)
+        def _():
+            grad(jnp.where(t < 8, t - 5, t - 8))
+
+        @pl.when(jnp.logical_not(is_grad))
+        def _():
+            rs.step(jnp.where(t < 5, t, t - 3), product)
+
+        return carry
+
+    lax.fori_loop(0, 16, turn, 0)
+    rs.finish(o_ref)
+    for slot in range(2):
+        put(slot, 3, "wait")
+    shares.arrive()
+
+
+def scatter_post(d_gu, w_gu, post_all):
+    _, rows, width = post_all.shape
+    wide = w_gu.shape[-1]
+    deep = width // 8
+    return pl.pallas_call(
+        post_back_kernel,
+        out_shape=(
+            jax.ShapeDtypeStruct((rows, width), F32),
+            jax.ShapeDtypeStruct((4, 4, deep, wide), BF16),
+        ),
+        in_specs=[spec_vmem(), spec_vmem(), spec_any()],
+        out_specs=(spec_vmem(), spec_any()),
+        scratch_shapes=scatter_scratch(rows, width)
+        + [
+            pltpu.VMEM((2, 8, rows, deep), BF16),
+            pltpu.SemaphoreType.DMA((2,)),
+            pltpu.VMEM((2, 2, deep, wide), BF16),
+        ]
+        + SHARES_SCRATCH,
+        compiler_params=comm_params(7),
+        cost_estimate=busy(66),
+        name="scatter_post",
+    )(d_gu, w_gu, post_all)
+
+
+def normed_back_kernel(
+    dq_ref,
+    dkv_ref,
+    to_lo_ref,
+    to_hi_ref,
+    lin_ref,
+    w_ref,
+    all_ref,
+    swap_a_ref,
+    swap_b_ref,
+    qg_ref,
+    kg_ref,
+    ca_ref,
+    sa_ref,
+    cb_ref,
+    sb_ref,
+    o_ref,
+    gw_ref,
+    gains_ref,
+    swapped_a_ref,
+    swapped_b_ref,
+    *scratch,
+):
+    rs = Scatter(*scratch[:N_SCATTER])
+    (
+        from_lo,
+        from_hi,
+        d_lin,
+        slices,
+        slice_sems,
+        tiles,
+        tiles_in,
+        planes_in,
+        z_sends,
+        z_recvs,
+        t_sends,
+        t_recvs,
+        p_sends,
+        p_recvs,
+        c_local,
+        c_sends,
+        c_recvs,
+    ) = scratch[N_SCATTER:]
+    me = rs.me
+    plane, planes = lax.axis_index("tp"), lax.axis_size("tp")
     rows, width = o_ref.shape
-    half = rows // 2
-    first, second = pl.ds(0, half), pl.ds(half, half)
-    greet((sib, nx, ny))
-
-    def remote(src, dst, n, device):
-        return pltpu.make_async_remote_copy(
-            src_ref=src,
-            dst_ref=dst,
-            send_sem=sends.at[n],
-            recv_sem=recvs.at[n],
-            device_id={"ctx": device},
-            device_id_type=MESH,
+    deep = width // 8
+    plane_rows = dq_ref.shape[0]
+    units = rows // UNIT
+    wide = 2 * HEAD_SIZE
+    away = others(me)
+    order = [b + o for b in (rs.dg, rs.nx, rs.ny, me) for o in (rs.sib - me, 0)]
+    far = [lax.rem(plane + step, planes) for step in range(1, planes)]
+
+    from_lo[...] = jnp.zeros_like(from_lo)
+    from_hi[...] = jnp.zeros_like(from_hi)
+    line = Line(to_hi_ref, to_lo_ref, from_lo, from_hi, z_sends, z_recvs, rows, True)
+    barrier = pltpu.get_barrier_semaphore()
+    for where in [on_ctx(c) for c in away] + [on_plane(p) for p in far]:
+        pl.semaphore_signal(barrier, inc=1, device_id=where, device_id_type=MESH)
+    pl.semaphore_wait(barrier, len(away) + len(far))
+
+    def at_block(block):
+        return pl.ds(pl.multiple_of(block * rows, rows), rows)
+
+    for block in order:
+        line.start(block)
+    columns(all_ref, slices, slice_sems, order[0], 0).start()
+    gains_ref[...] = jnp.zeros_like(gains_ref)
+
+    def head_back(grad, lin, gain_ref, rotation):
+        back = rotation.back(grad)
+        scale = lax.rsqrt(jnp.mean(lin * lin, axis=-1, keepdims=True) + EPS)
+        normal = lin * scale
+        gained = back * gain_ref[...]
+        d = scale * (gained - normal * jnp.mean(gained * normal, axis=-1, keepdims=True))
+        return d.astype(BF16), jnp.sum(back * normal, axis=0, keepdims=True)
+
+    def rotation_of(unit):
+        return Turn(ca_ref, sa_ref, cb_ref, sb_ref, unit)
+
+    def prepare_queries(unit, carry):
+        rotation = rotation_of(unit)
+        here = pl.ds(pl.multiple_of(unit * UNIT, UNIT), UNIT)
+        for h in range(2):
+            lanes = slice(h * HEAD_SIZE, (h + 1) * HEAD_SIZE)
+            d, gain = head_back(dq_ref[here, lanes] * HEAD_SIZE**-0.5, lin_ref[here, lanes], qg_ref, rotation)
+            d_lin[here, lanes] = d
+            gains_ref[0:1, :] += gain
+        return carry
+
+    def prepare_keys(block):
+        line.arrived(block)
+        for i in range(units):
+            unit = block * units + i
+            here = pl.ds(pl.multiple_of(unit * UNIT, UNIT), UNIT)
+            d_kv = dkv_ref[here, :] + from_lo[here, :].astype(F32) + from_hi[here, :].astype(F32)
+            lanes = slice(2 * HEAD_SIZE, 3 * HEAD_SIZE)
+            d, gain = head_back(d_kv[:, :HEAD_SIZE], lin_ref[here, lanes], kg_ref, rotation_of(unit))
+            d_lin[here, lanes] = d
+            gains_ref[1:2, :] += gain
+            d_lin[here, 3 * HEAD_SIZE :] = d_kv[:, HEAD_SIZE:].astype(BF16)
+
+    def tile_to(part, n, device):
+        return send(
+            tiles.at[part, device],
+            tiles_in.at[part, me],
+            t_sends.at[part, n],
+            t_recvs.at[part, me],
+            on_ctx(device),
         )
 
-    def sibling(n):
-        return remote(to_sib.at[n], from_sib.at[n], n, sib)
-
-    diag_x = remote(diag_out.at[first], diag_in.at[first], 4, nx)
-    diag_y = remote(diag_out.at[second], diag_in.at[second], 5, ny)
-    x_first = remote(x_out.at[first], x_in.at[first], 6, nx)
-    x_second = remote(x_out.at[second], x_in.at[second], 7, nx)
-    y_first = remote(y_out.at[first], y_in.at[first], 8, ny)
-    y_second = remote(y_out.at[second], y_in.at[second], 9, ny)
-    order = [b + o for b in (dg, nx, ny, me) for o in (shift, 0)]
-
-    def chip_sum(n, at):
-        return own[n, at].astype(F32) + from_sib[n, at].astype(F32)
+    def tile_from(part, device):
+        return send(
+            tiles.at[part, device],
+            tiles_in.at[part, device],
+            t_sends.at[part, 0],
+            t_recvs.at[part, device],
+            on_ctx(device),
+        )
+
+    def grads(part):
+        def grad(n, carry):
+            c = pick(n, order)
+            slot = lax.rem(n, 2)
+            columns(all_ref, slices, slice_sems, c, slot).wait()
+
+            @pl.when((n < 7) | (part == 0))
+            def _():
+                columns(all_ref, slices, slice_sems, pick(lax.rem(n + 1, 8), order), 1 - slot).start()
+
+            lanes = slice(part * wide, (part + 1) * wide)
+            value = tn(slices[slot].reshape(plane_rows, deep), d_lin[:, lanes]).astype(BF16)
+
+            @pl.when(n < 7)
+            def _():
+                tiles[part, c] = value
+                tile_to(part, n, c).start()
+
+            @pl.when(n == 7)
+            def _():
+                tiles_in[part, me] = value
+
+            return carry
+
+        lax.fori_loop(0, 8, grad, 0)
+
+    def pair(part, p):
+        return tiles_in.at[part, pl.ds(2 * p, 2)]
+
+    def to_plane(part, n):
+        return send(
+            pair(part, far[n]),
+            planes_in.at[part, plane],
+            p_sends.at[part, n],
+            p_recvs.at[part, plane],
+            on_plane(far[n]),
+        )
+
+    def from_plane(part, p):
+        return send(pair(part, p), planes_in.at[part, p], p_sends.at[part, 0], p_recvs.at[part, p], on_plane(p))
+
+    def spread(part):
+        for device in away:
+            tile_from(part, device).wait_recv()
+        for n in range(len(far)):
+            to_plane(part, n).start()
+
+    def collect(part):
+        total = tiles_in[part, pl.ds(2 * plane, 2)].astype(F32)
+        for p in far:
+            from_plane(part, p).wait_recv()
+            total += planes_in[part, p].astype(F32)
+        gw_ref[part] = total
+
+    def product(block, out, n):
+        left = d_lin[at_block(block), :]
+        for c in range(0, width, 512):
+            out[n, :, c : c + 512] = nt(left, w_ref[c : c + 512, :]).astype(BF16)
 
     def turn(step, carry):
-        block = pick(step, order)
-        n = step // 2
-
-        @pl.when(lax.rem(step, 2) == 0)
-        def _():
-            product(a_ref, w_ref, block, rows, to_sib, n)
-            sibling(n).start()
-
-        @pl.when(lax.rem(step, 2) == 1)
-        def _():
-            product(a_ref, w_ref, block, rows, own, n)
-            sibling(n).wait_recv()
-
-        @pl.when(step == 1)
-        def _():
-            diag_out[first] = chip_sum(0, first).astype(BF16)
-            diag_x.start()
-            diag_out[second] = chip_sum(0, second).astype(BF16)
-            diag_y.start()
-
-        @pl.when(step == 3)
-        def _():
-            x_out[first] = chip_sum(1, first).astype(BF16)
-            x_first.start()
-
-        @pl.when(step == 5)
-        def _():
-            y_out[second] = chip_sum(2, second).astype(BF16)
-            y_second.start()
-            diag_x.wait_recv()
-            y_out[first] = (chip_sum(2, first) + diag_in[first].astype(F32)).astype(BF16)
-            y_first.start()
-            diag_y.wait_recv()
-            x_out[second] = (chip_sum(1, second) + diag_in[second].astype(F32)).astype(BF16)
-            x_second.start()
-
+        prepare_keys(rs.block(step))
+        rs.step(step, product)
         return carry
 
+    lax.fori_loop(0, plane_rows // UNIT, prepare_queries, 0)
+    grads(0)
     lax.fori_loop(0, 8, turn, 0)
-    x_first.wait_recv()
-    y_second.wait_recv()
-    x_second.wait_recv()
-    y_first.wait_recv()
-    for at in (first, second):
-        o_ref[at] = chip_sum(3, at) + x_in[at].astype(F32) + y_in[at].astype(F32)
-    for n in range(4):
-        sibling(n).wait_send()
-    for copy in (diag_x, diag_y, x_first, x_second, y_first, y_second):
-        copy.wait_send()
-
-
-def product_nn(a_ref, w_ref, block, rows, out, n):
-    left = a_ref[pl.ds(block * rows, rows), :]
-    for c in range(0, w_ref.shape[1], 512):
-        out[n, :, c : c + 512] = nn(left, w_ref[:, c : c + 512]).astype(BF16)
-
-
-def product_nt(a_ref, w_ref, block, rows, out, n):
-    left = a_ref[pl.ds(block * rows, rows), :]
-    for c in range(0, w_ref.shape[0], 512):
-        out[n, :, c : c + 512] = nt(left, w_ref[c : c + 512, :]).astype(BF16)
-
-
-def product_nt_halves(a_ref, w_ref, block, rows, out, n):
-    wide = w_ref.shape[2]
-    here = pl.ds(block * rows, rows)
-    for c in range(0, w_ref.shape[1], 512):
-        total = nt(a_ref[here, :wide], w_ref[0, c : c + 512, :])
-        total += nt(a_ref[here, wide:], w_ref[1, c : c + 512, :])
-        out[n, :, c : c + 512] = total.astype(BF16)
-
-
-def scatter_sum(product, a, w, width, collective_id, name):
-    rows = a.shape[0] // 8
-    four = pltpu.VMEM((4, rows, width), BF16)
-    one = pltpu.VMEM((rows, width), BF16)
+    grads(1)
+    chip = me // 2
+    chips = (rs.dg, rs.nx, rs.ny)
+    swaps = ((swap_a_ref, swapped_a_ref), (swap_b_ref, swapped_b_ref))
+
+    def swap_own(i):
+        return pltpu.make_async_copy(swaps[i][0].at[chip], swaps[i][1].at[chip], c_local.at[i])
+
+    def swap_to(i, n):
+        there = chips[n]
+        return send(
+            swaps[i][0].at[there // 2], swaps[i][1].at[chip], c_sends.at[i, n], c_recvs.at[i, chip], on_ctx(there)
+        )
+
+    def swap_from(i, n):
+        there = chips[n] // 2
+        return send(
+            swaps[i][0].at[there], swaps[i][1].at[there], c_sends.at[i, n], c_recvs.at[i, there], on_ctx(chips[n])
+        )
+
+    for i in range(2):
+        swap_own(i).start()
+        for n in range(3):
+            swap_to(i, n).start()
+    spread(0)
+    rs.finish(o_ref)
+    spread(1)
+    collect(0)
+    collect(1)
+    for i in range(2):
+        swap_own(i).wait()
+        for n in range(3):
+            swap_from(i, n).wait_recv()
+            swap_to(i, n).wait_send()
+    for part in range(2):
+        for n, device in enumerate(order[:7]):
+            tile_to(part, n, device).wait_send()
+        for n in range(len(far)):
+            to_plane(part, n).wait_send()
+
+    def settle(block, carry):
+        line.sent(block)
+        return carry
+
+    lax.fori_loop(0, 8, settle, 0)
+
+
+def scatter_normed(d_queries, d_kv, to_lo, to_hi, lin, w_qkv, normed_all, swaps, q_gain, k_gain, tables):
+    _, rows, width = normed_all.shape
+    deep = width // 8
+    cols = w_qkv.shape[1]
+    half = pltpu.VMEM(to_lo.shape, BF16)
+    tiles = pltpu.VMEM((2, 8, deep, cols // 2), BF16)
+    dma = pltpu.SemaphoreType.DMA
     return pl.pallas_call(
-        functools.partial(scatter_kernel, product),
-        out_shape=jax.ShapeDtypeStruct((rows, width), F32),
-        in_specs=[spec_vmem(), spec_vmem()],
+        normed_back_kernel,
+        out_shape=(
+            jax.ShapeDtypeStruct((rows, width), F32),
+            jax.ShapeDtypeStruct((2, 2, deep, cols // 2), F32),
+            jax.ShapeDtypeStruct((8, HEAD_SIZE), F32),
+            jax.ShapeDtypeStruct(swaps[0].shape, BF16),
+            jax.ShapeDtypeStruct(swaps[1].shape, BF16),
+        ),
+        in_specs=[spec_vmem()] * 2
+        + [spec_any()] * 2
+        + [spec_vmem()] * 2
+        + [spec_any()] * 3
+        + [spec_vmem()] * 6,
+        out_specs=(spec_vmem(),) * 3 + (spec_any(),) * 2,
+        scratch_shapes=scatter_scratch(rows, width)
+        + [
+            half,
+            half,
+            pltpu.VMEM((8 * rows, cols), BF16),
+            pltpu.VMEM((2, 8, rows, deep), BF16),
+            dma((2,)),
+            tiles,
+            tiles,
+            pltpu.VMEM((2, 4, 2, deep, cols // 2), BF16),
+            dma((2, 8 * rows // UNIT)),
+            dma((2, 8 * rows // UNIT)),
+            dma((2, 7)),
+            dma((2, 8)),
+            dma((2, 3)),
+            dma((2, 4)),
+            dma((2,)),
+            dma((2, 3)),
+            dma((2, 4)),
+        ],
+        compiler_params=comm_params(8),
+        cost_estimate=busy(110),
+        name="scatter_normed",
+    )(
+        d_queries,
+        d_kv,
+        to_lo,
+        to_hi,
+        lin,
+        w_qkv,
+        normed_all,
+        *swaps,
+        q_gain.reshape(1, -1),
+        k_gain.reshape(1, -1),
+        *tables,
+    )
+
+
+def total_kernel(v_ref, o_ref, held, held_planes, sends, recvs):
+    me = lax.axis_index("ctx")
+    plane, planes = lax.axis_index("tp"), lax.axis_size("tp")
+    away = others(me)
+    far = [lax.rem(plane + step, planes) for step in range(1, planes)]
+    barrier = pltpu.get_barrier_semaphore()
+    for where in [on_ctx(c) for c in away] + [on_plane(p) for p in far]:
+        pl.semaphore_signal(barrier, inc=1, device_id=where, device_id_type=MESH)
+    pl.semaphore_wait(barrier, len(away) + len(far))
+    held[me] = v_ref[...]
+    for n, c in enumerate(away):
+        send(held.at[me], held.at[me], sends.at[n], recvs.at[me], on_ctx(c)).start()
+    for c in away:
+        send(held.at[c], held.at[c], sends.at[0], recvs.at[c], on_ctx(c)).wait_recv()
+    value = held[0]
+    for c in range(1, 8):
+        value += held[c]
+    held_planes[plane] = value
+    for n, p in enumerate(far):
+        send(
+            held_planes.at[plane], held_planes.at[plane], sends.at[7 + n], recvs.at[8 + plane], on_plane(p)
+        ).start()
+    for p in far:
+        send(held_planes.at[p], held_planes.at[p], sends.at[0], recvs.at[8 + p], on_plane(p)).wait_recv()
+    value = held_planes[0]
+    for p in range(1, 4):
+        value += held_planes[p]
+    o_ref[...] = value
+    for n, c in enumerate(away):
+        send(held.at[me], held.at[me], sends.at[n], recvs.at[me], on_ctx(c)).wait_send()
+    for n, p in enumerate(far):
+        send(
+            held_planes.at[plane], held_planes.at[plane], sends.at[7 + n], recvs.at[8 + plane], on_plane(p)
+        ).wait_send()
+
+
+def total_of(values):
+    return pl.pallas_call(
+        total_kernel,
+        out_shape=jax.ShapeDtypeStruct(values.shape, F32),
+        in_specs=[spec_vmem()],
         out_specs=spec_vmem(),
-        scratch_shapes=[four, four, four]
-        + [one] * 6
-        + [pltpu.SemaphoreType.DMA((10,)), pltpu.SemaphoreType.DMA((10,))],
-        compiler_params=pltpu.CompilerParams(
-            collective_id=collective_id, has_side_effects=True, vmem_limit_bytes=VMEM_LIMIT
-        ),
-        name=name,
-    )(a, w)
+        scratch_shapes=[
+            pltpu.VMEM((8,) + values.shape, F32),
+            pltpu.VMEM((4,) + values.shape, F32),
+            pltpu.SemaphoreType.DMA((10,)),
+            pltpu.SemaphoreType.DMA((12,)),
+        ],
+        compiler_params=pltpu.CompilerParams(collective_id=9, has_side_effects=True),
+        cost_estimate=busy(12),
+        name="total_of",
+    )(values)
 
 
 class Places:
@@ -1033,6 +2046,7 @@
             pltpu.SemaphoreType.DMA((2,)),
         ],
         compiler_params=pltpu.CompilerParams(vmem_limit_bytes=VMEM_LIMIT),
+        cost_estimate=busy(50),
         name="attend",
     )(order, lens, q, lo, own, hi)
 
@@ -1140,36 +2154,27 @@
             pltpu.SemaphoreType.DMA((2,)),
         ],
         compiler_params=pltpu.CompilerParams(vmem_limit_bytes=VMEM_LIMIT),
+        cost_estimate=busy(75),
         name="attend_back",
     )(order, lens, q, d_mixed, mixed, lse, lo, own, hi)
 
 
-def angles(block_order, ctx_rows, tok_rows):
+def angles(block_order, tok_rows):
     inverse = THETA ** (-jnp.arange(0, HEAD_SIZE, 2, dtype=F32) / HEAD_SIZE)
-    starts = jnp.arange(2 * block_order.shape[1], dtype=jnp.int32) * UNIT
-    coarse = starts.astype(F32)[:, None] * inverse[None, :]
-    fine = jnp.arange(UNIT, dtype=F32)[:, None] * inverse[None, :]
+    inverse = jnp.concatenate([inverse, inverse])
     units = tok_rows // UNIT
     g = lax.axis_index("tp") * units + jnp.arange(units, dtype=jnp.int32)
     seq, quarter = g // 4, g % 4
     c = jnp.arange(lax.axis_size("ctx"), dtype=jnp.int32)
     where = 2 * block_order[seq[None, :], 2 * c[:, None] + (quarter // 2)[None, :]] + (quarter % 2)[None, :]
-    where = where.reshape(-1)
-    cos_a, sin_a = jnp.cos(coarse)[where][:, None, :], jnp.sin(coarse)[where][:, None, :]
-    cos_b, sin_b = jnp.cos(fine)[None], jnp.sin(fine)[None]
-    half = HEAD_SIZE // 2
-    cosine = (cos_a * cos_b - sin_a * sin_b).reshape(-1, 1, half)
-    sine = (sin_a * cos_b + cos_a * sin_b).reshape(-1, 1, half)
-    return cosine, sine
-
-
-def from_sibling(parts, core):
-    mine = lax.dynamic_slice_in_dim(parts, 2 * core, 2, 0)
-    other = lax.dynamic_slice_in_dim(parts, 2 - 2 * core, 2, 0)
-    got = lax.ppermute(other, "ctx", SIBLING)
-    low = jnp.where(core == 0, mine, got)
-    high = jnp.where(core == 0, got, mine)
-    return low, high
+    starts = (where.reshape(-1) * UNIT).astype(F32)
+    coarse = starts[:, None] * inverse[None, :]
+    fine = jnp.arange(UNIT, dtype=F32)[:, None] * inverse[None, :]
+    return jnp.cos(coarse), jnp.sin(coarse), jnp.cos(fine), jnp.sin(fine)
+
+
+def after(value, *earlier):
+    return lax.optimization_barrier((value,) + earlier)[0]
 
 
 def local_plane(
@@ -1195,16 +2200,12 @@
     tok_rows, width = tokens.shape
     plane_rows = 8 * tok_rows
     seq_len = 2 * 8 * BLK
-    scale_qk = HEAD_SIZE ** (-0.5)
     deep = width // 8
+    cols = w_gate.shape[1] // 4
     stream = tokens.astype(F32)
     scale_in = rms_scale(stream)
     unit_in = stream * scale_in
     normed_rows = (unit_in * in_gain).astype(BF16)
-
-    def to_heads(home):
-        gathered = lax.all_gather(home, "tp", axis=0, tiled=True)
-        return lax.all_to_all(gathered, "ctx", 0, 0, tiled=True)
 
     qkv_home = jnp.concatenate(
         [
@@ -1214,50 +2215,28 @@
         ],
         axis=2,
     )
-    w_qkv = to_heads(jnp.transpose(qkv_home, (1, 0, 2))).reshape(width, 4 * HEAD_SIZE)
-    w_o = jnp.transpose(to_heads(w_out.reshape(2, 2 * HEAD_SIZE, deep)), (1, 0, 2)).reshape(
-        2 * HEAD_SIZE, width
-    )
-
-    cols = w_gate.shape[1] // 4
-    gu_home = jnp.transpose(
-        jnp.concatenate([w_gate.reshape(deep, 4, cols), w_up.reshape(deep, 4, cols)], axis=2), (1, 0, 2)
-    )
-    gu_part = lax.all_to_all(gu_home, "ctx", 0, 0, axis_index_groups=CORE_GROUPS, tiled=True)
-    gu_low, gu_high = from_sibling(lax.all_gather(gu_part, "tp", axis=0), core)
-    w_gu = jnp.stack([gu_low, gu_high], axis=2).reshape(2, width, 2 * cols)
-    down_part = lax.all_to_all(
-        w_down.reshape(4, cols, deep), "ctx", 0, 0, axis_index_groups=CORE_GROUPS, tiled=True
-    )
-    down_low, down_high = from_sibling(lax.all_gather(down_part, "tp", axis=0), core)
-    w_d = jnp.transpose(jnp.stack([down_low, down_high], axis=2), (0, 3, 1, 2, 4)).reshape(2 * cols, width)
-
-    normed_all, qkv = gather_qkv(normed_rows, w_qkv)
-    cosine, sine = angles(block_order, plane_rows, tok_rows)
-    query_lin = qkv[:, : 2 * HEAD_SIZE].reshape(plane_rows, 2, HEAD_SIZE)
-    key_lin = qkv[:, 2 * HEAD_SIZE : 3 * HEAD_SIZE].reshape(plane_rows, 1, HEAD_SIZE)
-    query_scale = rms_scale(query_lin)
-    query_unit = query_lin * query_scale
-    key_scale = rms_scale(key_lin)
-    key_unit = key_lin * key_scale
-    queries = (
-        (rotate(query_unit * q_gain, cosine, sine) * (scale_qk * LOG2E))
-        .astype(BF16)
-        .reshape(plane_rows, 2 * HEAD_SIZE)
-    )
-    keys = rotate(key_unit * k_gain, cosine, sine).astype(BF16).reshape(plane_rows, HEAD_SIZE)
-    kv = jnp.concatenate([keys, qkv[:, 3 * HEAD_SIZE :].astype(BF16)], axis=1)
-    upward = [(0, 1), (1, 2), (2, 3)]
-    downward = [(1, 0), (2, 1), (3, 2)]
-    kv_lo = lax.ppermute(kv, "tp", upward)
-    kv_hi = lax.ppermute(kv, "tp", downward)
-    mixed, lse = attend(block_order, seq_lens, queries, kv_lo, kv, kv_hi, seq_len)
-    middle = stream + scatter_sum(product_nn, mixed, w_o, width, 5, "scatter_out")
-    scale_post = rms_scale(middle)
-    unit_post = middle * scale_post
-    post_rows = (unit_post * post_gain).astype(BF16)
-    post_all, slope, active, hidden = gather_up(post_rows, w_gu)
-    result = middle + scatter_sum(product_nn, hidden, w_d, width, 6, "scatter_down")
+    qkv_slab = lax.all_gather(jnp.transpose(qkv_home, (1, 0, 2)), "tp", axis=0, tiled=True)
+
+    def to_chips(home):
+        return lax.all_to_all(home, "ctx", 0, 0, axis_index_groups=CORE_GROUPS, tiled=True)
+
+    gate_part = to_chips(jnp.transpose(w_gate.reshape(deep, 4, cols), (1, 0, 2)))
+    up_part = to_chips(jnp.transpose(w_up.reshape(deep, 4, cols), (1, 0, 2)))
+    down_part = to_chips(w_down.reshape(4, cols, deep))
+    gate_parts = lax.all_gather(after(gate_part, up_part, down_part), "tp", axis=0)
+    tables = angles(block_order, tok_rows)
+    normed_all, w_qkv, queries, kv, kv_lo, kv_hi, lin = gather_qkv(
+        normed_rows, after(qkv_slab, gate_part, up_part, down_part), q_gain, k_gain, tables
+    )
+    out_part = lax.all_gather(after(w_out, gate_part, up_part, down_part), "tp", axis=0, tiled=True)
+    out_parts = [out_part] + [lax.ppermute(out_part, "ctx", [(i, i ^ n) for i in range(8)]) for n in (2, 4, 6)]
+    up_parts = lax.all_gather(after(up_part, kv), "tp", axis=0)
+    mixed, lse = attend(block_order, seq_lens, after(queries, gate_parts, out_part), kv_lo, kv, kv_hi, seq_len)
+    down_parts = lax.all_gather(after(down_part, kv), "tp", axis=0)
+    middle, post_rows, mixed_rows, w_o = mix(mixed, tokens, post_gain, out_parts)
+    post_all, w_gu, slope, active, hidden = gather_up(post_rows, gate_parts, up_parts)
+    summed, w_d = scatter_down(hidden, down_parts)
+    result = middle + summed
     output = result.astype(BF16)
 
     row = plane * tok_rows + jnp.arange(tok_rows, dtype=jnp.int32)
@@ -1268,86 +2247,86 @@
     error_local = jnp.sum(diff * diff)
     diff_low = diff.astype(BF16)
     d_gu, grad_wd = gather_down_back(diff_low, w_d, slope, active, hidden)
-    d_post = scatter_sum(product_nt_halves, d_gu, w_gu, width, 7, "scatter_post")
+    d_post, grad_gu = scatter_post(d_gu, w_gu, post_all)
 
     def home_sum(parts):
-        mine = lax.dynamic_index_in_dim(parts, core, 2, keepdims=False)
-        other = lax.dynamic_index_in_dim(parts, 1 - core, 2, keepdims=False)
-        got = lax.ppermute(other, "ctx", SIBLING)
-        low = jnp.where(core == 0, mine, got)
-        high = jnp.where(core == 0, got, mine)
-        total = lax.psum_scatter(
-            jnp.concatenate([low, high], axis=0), "tp", scatter_dimension=0, tiled=True
-        )
-        return lax.all_to_all(total[0], "ctx", 0, 0, axis_index_groups=CORE_GROUPS, tiled=True)
-
-    grad_down = home_sum(
-        jnp.transpose(grad_wd.astype(BF16).reshape(2, cols, 4, 2, deep), (0, 2, 3, 1, 4))
-    ).reshape(4 * cols, deep)
-    post_flat = post_all.reshape(plane_rows, width)
-    grad_gu = jnp.stack(
-        [matmul_tn(post_flat, d_gu[:, z * 2 * cols : (z + 1) * 2 * cols]).astype(BF16) for z in range(2)]
-    )
-    gu_sum = home_sum(grad_gu.reshape(2, 4, 2, deep, 2 * cols))
+        return lax.psum_scatter(parts, "tp", scatter_dimension=0, tiled=True)[0]
+
+    grad_down = home_sum(grad_wd)
+    grad_gu = home_sum(grad_gu)
+    scale_post = rms_scale(middle)
+    unit_post = middle * scale_post
+    grad_post_local = jnp.sum(d_post * unit_post, axis=0)
+    d_middle = diff + rms_back(middle, scale_post, d_post * post_gain)
+    d_mixed, *grad_wo = mix_back(d_middle.astype(BF16), w_o, mixed_rows)
+    grad_wo = [grad_wo[0]] + [
+        lax.ppermute(grad_wo[m], "ctx", [(i, i ^ n) for i in range(8)]) for m, n in ((1, 2), (2, 4), (3, 6))
+    ]
+
+    d_queries, to_lo, d_kv, to_hi = attend_back(
+        block_order,
+        seq_lens,
+        queries,
+        d_mixed,
+        mixed,
+        lse,
+        kv_lo,
+        kv,
+        kv_hi,
+        seq_len,
+    )
+    grad_out = lax.psum_scatter(
+        sum(after(g, d_queries).astype(F32) for g in grad_wo).astype(BF16), "tp", scatter_dimension=0, tiled=True
+    )
+    d_normed, grad_qkv, grad_gains, gu_sum, grad_down = scatter_normed(
+        d_queries,
+        d_kv,
+        to_lo,
+        to_hi,
+        lin,
+        w_qkv,
+        normed_all,
+        (grad_gu, grad_down),
+        q_gain,
+        k_gain,
+        tables,
+    )
+    grad_down = grad_down.reshape(4 * cols, deep)
     gu_sum = jnp.transpose(gu_sum, (1, 0, 2))
     grad_gate = gu_sum[:, :, :cols].reshape(deep, 4 * cols)
     grad_up = gu_sum[:, :, cols:].reshape(deep, 4 * cols)
-
-    grad_post_local = jnp.sum(d_post * unit_post, axis=0)
-    d_middle = diff + rms_back(middle, scale_post, d_post * post_gain)
-    d_mixed, grad_wo = gather_out_back(d_middle.astype(BF16), w_o, mixed)
-
-    def home_heads(parts):
-        swapped = lax.all_to_all(parts.astype(BF16), "ctx", 0, 0, tiled=True)
-        return lax.psum_scatter(swapped, "tp", scatter_dimension=0, tiled=True)
-
-    grad_out = home_heads(jnp.transpose(grad_wo.reshape(2 * HEAD_SIZE, 8, deep), (1, 0, 2))).reshape(
-        4 * HEAD_SIZE, deep
-    )
-    d_queries, to_lo, d_kv, to_hi = attend_back(
-        block_order, seq_lens, queries, d_mixed, mixed, lse, kv_lo, kv, kv_hi, seq_len
-    )
-    d_kv = (
-        d_kv
-        + lax.ppermute(to_lo, "tp", downward).astype(F32)
-        + lax.ppermute(to_hi, "tp", upward).astype(F32)
-    )
-    query_back = rotate_back(
-        d_queries.reshape(plane_rows, 2, HEAD_SIZE) * scale_qk, cosine, sine
-    )
-    grad_q_local = jnp.sum(query_back * query_unit, axis=(0, 1))
-    d_query_lin = rms_back(query_lin, query_scale, query_back * q_gain).reshape(plane_rows, 2 * HEAD_SIZE)
-    key_back = rotate_back(d_kv[:, :HEAD_SIZE].reshape(plane_rows, 1, HEAD_SIZE), cosine, sine)
-    grad_k_local = jnp.sum(key_back * key_unit, axis=(0, 1))
-    d_key_lin = rms_back(key_lin, key_scale, key_back * k_gain).reshape(plane_rows, HEAD_SIZE)
-    d_qkv = jnp.concatenate([d_query_lin, d_key_lin, d_kv[:, HEAD_SIZE:]], axis=1).astype(BF16)
-    d_normed = scatter_sum(product_nt, d_qkv, w_qkv, width, 8, "scatter_normed")
-    grad_qkv = home_heads(
-        matmul_tn(normed_all.reshape(plane_rows, width), d_qkv).reshape(8, deep, 4 * HEAD_SIZE)
-    )
-    grad_qkv = jnp.transpose(grad_qkv, (1, 0, 2))
-    grad_query = grad_qkv[:, :, : 2 * HEAD_SIZE].reshape(deep, 4 * HEAD_SIZE)
-    grad_key = grad_qkv[:, :, 2 * HEAD_SIZE : 3 * HEAD_SIZE].reshape(deep, 2 * HEAD_SIZE)
-    grad_value = grad_qkv[:, :, 3 * HEAD_SIZE :].reshape(deep, 2 * HEAD_SIZE)
+    grad_qkv = jnp.transpose(grad_qkv, (0, 2, 1, 3))
+    grad_query = grad_qkv[0].reshape(deep, 4 * HEAD_SIZE)
+    grad_key = grad_qkv[1, :, :, :HEAD_SIZE].reshape(deep, 2 * HEAD_SIZE)
+    grad_value = grad_qkv[1, :, :, HEAD_SIZE:].reshape(deep, 2 * HEAD_SIZE)
     grad_in_local = jnp.sum(d_normed * unit_in, axis=0)
     d_tokens = (d_middle + rms_back(stream, scale_in, d_normed * in_gain)).astype(BF16)
-    totals = lax.psum(
-        (grad_in_local, grad_q_local, grad_k_local, grad_post_local, error_local), ("ctx", "tp")
+    lanes = width // HEAD_SIZE
+    totals = total_of(
+        jnp.concatenate(
+            [
+                grad_in_local.reshape(lanes, HEAD_SIZE),
+                grad_post_local.reshape(lanes, HEAD_SIZE),
+                grad_gains[:2],
+                jnp.full((6, HEAD_SIZE), error_local),
+            ],
+            axis=0,
+        )
     )
     count_valid = jnp.sum(seq_lens).astype(F32)
-    loss = 0.5 * totals[4] / (count_valid * MODEL_WIDTH)
+    loss = 0.5 * totals[2 * lanes + 2, 0] / (count_valid * MODEL_WIDTH)
     return (
         output,
         loss,
         d_tokens,
-        totals[0],
-        grad_query.astype(F32),
-        grad_key.astype(F32),
-        grad_value.astype(F32),
-        totals[1],
-        totals[2],
-        grad_out.astype(F32),
-        totals[3],
+        totals[:lanes].reshape(width),
+        grad_query,
+        grad_key,
+        grad_value,
+        totals[2 * lanes],
+        totals[2 * lanes + 1],
+        after(grad_out, d_normed).astype(F32),
+        totals[lanes : 2 * lanes].reshape(width),
         grad_gate.astype(F32),
         grad_up.astype(F32),
         grad_down.astype(F32),

time: 1210 us -> 871 us (0.72)
  waiting for transfers between devices: 148 us -> 33.8 us
  other arithmetic: 118 us -> 39.3 us
  blocking collectives: 97.7 us -> 29.8 us
  local copies, waits for them, and re-layouts: 102 us -> 41.5 us
  Pallas kernels: 634 us -> 693 us
  matrix products: 39.1 us -> 0 us
  starting transfers between devices: 42.6 us -> 10.9 us
    all_gather x4 -> x5, waiting for transfers between devices: 88.8 us -> 0.08 us  [the longest x1 0.02 us: local_plane(): up_parts = lax.all_gather(after(up_part, kv), 'tp', axis=0)]
    pallas_call x1, Pallas kernels: 60 us -> 119 us  [gather_qkv(): pl.pallas_call(qkv_kernel, out_shape=(jax.ShapeDtypeStruct((8, rows, widt...]
    all_to_all x6 -> x1, waiting for transfers between devices: 52.9 us -> 9.18 us  [to_chips(): lax.all_to_all(home, 'ctx', 0, 0, axis_index_groups=CORE_GROUPS, tiled=True)]
    psum x1 -> x0, blocking collectives: 42.1 us -> none  [local_plane(): lax.psum((grad_in_local, grad_q_local, grad_k_local, grad_post_local, err...]
    dot_general x3 -> x0, matrix products: 39.1 us -> none  [matmul_tn(): lax.dot_general(left, right, (((0,), (0,)), ((), ())), preferred_element_...]
    pallas_call x5 -> x6, Pallas kernels: 317 us -> 345 us  [the longest x1 139 us: scatter_normed(): pl.pallas_call(normed_back_kernel, out_shape=(jax.ShapeDtypeStruct((rows,...]
    all_to_all x2, blocking collectives: 55.6 us -> 29.8 us  [to_chips(): lax.all_to_all(home, 'ctx', 0, 0, axis_index_groups=CORE_GROUPS, tiled=True)]
    reduce_scatter x4 -> x3, waiting for transfers between devices: 0.05 us -> 23.9 us  [the longest x2 23.9 us: home_sum(): return lax.psum_scatter(parts, 'tp', scatter_dimension=0, tiled=True)[0]]
  transfers between devices with their start and end apart: 22 -> 15, of which waited for: 9 -> 2; matrix products, arithmetic and copies ran while one was open for 18% -> 4% of each run, Pallas kernels for 36% -> 64%
where the time goes in v2:
time: 871 us; the launch traced here: 866 us
  Pallas kernels  693 us (80%)
  local copies, waits for them, and re-layouts  41.5 us (5%)
  other arithmetic  39.3 us (5%)
  waiting for transfers between devices  33.8 us (4%)
  blocking collectives  29.8 us (3%)
  between operations  17.3 us (2%)
  starting transfers between devices  10.9 us (1%)
    pallas_call x1, Pallas kernels, scatter_normed(): pl.pallas_call(normed_back_kernel, out_shape=(jax.ShapeDtypeStruct((rows,...  139 us
    pallas_call x1, Pallas kernels, gather_qkv(): pl.pallas_call(qkv_kernel, out_shape=(jax.ShapeDtypeStruct((8, rows, widt...  119 us
    pallas_call x1, Pallas kernels, scatter_post(): pl.pallas_call(post_back_kernel, out_shape=(jax.ShapeDtypeStruct((rows, w...  70.9 us
    pallas_call x1, Pallas kernels, gather_down_back(): pl.pallas_call(down_back_kernel, out_shape=(jax.ShapeDtypeStruct((8 * row...  70.1 us
    pallas_call x1, Pallas kernels, scatter_down(): pl.pallas_call(down_kernel, out_shape=(jax.ShapeDtypeStruct((rows, width)...  66.8 us
    pallas_call x1, Pallas kernels, gather_up(): pl.pallas_call(up_kernel, out_shape=(jax.ShapeDtypeStruct((8, rows, width...  63 us
    pallas_call x1, Pallas kernels, attend_back(): pl.pallas_call(attend_back_kernel, out_shape=(wide, flat, wide, flat), in...  57.8 us
    pallas_call x1, Pallas kernels, attend(): pl.pallas_call(attend_kernel, out_shape=(jax.ShapeDtypeStruct(q.shape, BF...  38.9 us
  transfers between devices with their start and end apart: 15, of which 2 were waited for; matrix products, arithmetic and copies ran while one was open for 4% of the time, Pallas kernels for 64%

profile of v2, /device:TPU:0, one launch (start us, length us, event | category | flops | bytes accessed | tf_op | source)
XLA Modules:
  0.0 866.0 jit_solution(5804939665006613466)
XLA Ops:
  7.2 1.1 copy.63
  10.5 1.0 copy.66
  11.8 16.4 %all_to_all.15 = bf16[4,256,384]{1,2,0:T(8,128)(2,1)} all-to-all(bf16[4,256,384]{1,2,0:T(8,128)(2,1)S(1)} %bitcast.49), channel_id=1, replica_groups={{0,8,16,24},{4,12,20,28},{1,9,17,25},{5,13,21,29},{2,10,18,26},{6,14,22..., dimensions={0} | all-to-all | bytes 1572864 | tf_op jit(solution)/shard_map/all_to_all | solution.py:2221
  28.2 3.5 all-to-all-start.2
  32.0 9.2 %all-to-all-done.2 = bf16[4,384,256]{2,1,0:T(8,128)(2,1)S(1)} async-done(((bf16[4,384,256]{2,1,0:T(8,128)(2,1)}), bf16[4,384,256]{2,1,0:T(8,128)(2,1)S(1)}, u32[]{:S(2)}, u32[]{:S(2)}) %all-to-all-start.2) | async-done | bytes 786464 | tf_op jit(solution)/shard_map/all_to_all | solution.py:2221
  41.2 13.4 %all_to_all.16 = bf16[4,256,384]{1,2,0:T(8,128)(2,1)} all-to-all(bf16[4,256,384]{1,2,0:T(8,128)(2,1)S(1)} %bitcast.48), channel_id=1, replica_groups={{0,8,16,24},{4,12,20,28},{1,9,17,25},{5,13,21,29},{2,10,18,26},{6,14,22..., dimensions={0} | all-to-all | bytes 1572864 | tf_op jit(solution)/shard_map/all_to_all | solution.py:2221
  54.7 2.4 copy.69
  60.6 1.6 fusion.2.x_ref
  62.2 118.6 %gather_qkv.1 = (bf16[8,384,2048]{2,1,0:T(8,128)(2,1)}, bf16[2048,512]{1,0:T(8,128)(2,1)}, bf16[3072,256]{1,0:T(8,128)(2,1)}, bf16[3072,256]{1,0:T(8,128)(2,1)},...) custom-call(bf16[384,2048]{1,0:T(8,128)(2,1)} %fusion.2.x_ref, ...), custom_call_target="tpu_custom_call" | custom-call | bytes 240000000 | tf_op jit(solution)/shard_map/gather_qkv/pallas_call | solution.py:870
  180.8 1.2 copy.70
  182.7 1.4 collective-permute-start
  184.1 1.4 collective-permute-start.1
  186.3 3.6 gather_fusion.1
  190.5 2.0 fusion.20
  192.6 38.9 %attend.1 = (bf16[3072,256]{1,0:T(8,128)(2,1)}, f32[24,8,256]{2,1,0:T(8,128)}) custom-call(s32[3,16]{1,0:T(4,128)} %order_ref.3, s32[3]{0:T(128)} %lens_ref.3, bf16[3072,256]{1,0:T(8,128)(2,1)} %get-tuple-element.67.q_ref, bf16[3072,256]{1,0:T(8,128)(2,1)} %get-tuple-element.68.lo_ref, bf16[3072,256]{1,0:T(8,128)(2,1)} %get-tuple-element.69.own_ref, ...), custom_call_target="tpu_custom_call" | custom-call | bytes 150000000 | tf_op jit(solution)/shard_map/attend/pallas_call | solution.py:2033
  232.4 28.3 %mix.1 = (f32[384,2048]{1,0:T(8,128)}, bf16[384,2048]{1,0:T(8,128)(2,1)}, bf16[384,2048]{1,0:T(8,128)(2,1)}, bf16[2048,2048]{1,0:T(8,128)(2,1)}) custom-call(bf16[3072,256]{1,0:T(8,128)(2,1)} %get-tuple-element.71.mixed_ref.o_ref, bf16[384,2048]{1,0:T(8,128)(2,1)} %tokens_ref.1, f32[1,2048]{1,0:T(1,128)} %bitcast.65, ...), custom_call_target="tpu_custom_call" | custom-call | bytes 84000000 | tf_op jit(solution)/shard_map/mix/pallas_call | solution.py:1343
  260.8 63.0 %gather_up.1 = (bf16[8,384,2048]{2,1,0:T(8,128)(2,1)}, bf16[2,2048,768]{2,1,0:T(8,128)(2,1)}, bf16[3072,768]{1,0:T(8,128)(2,1)}, bf16[3072,768]{1,0:T(8,128)(2,1)}, bf16[3072,768]{1,0:T(8,128)(2,1)}) custom-call(bf16[384,2048]{1,0:T(8,128)(2,1)} %get-tuple-element.73.x_ref, bf16[4,4,256,384]{3,2,1,0:T(8,128)(2,1)} %bitcast.50, bf16[4,4,256,384]{3,2,1,0:T(8,128)(2,1)} %bitcast.52), custom_call_target="tpu_custom_call" | custom-call | bytes 186000000 | tf_op jit(solution)/shard_map/gather_up/pallas_call | solution.py:1064
  323.8 66.8 %scatter_down.1 = (f32[384,2048]{1,0:T(8,128)}, bf16[768,2048]{1,0:T(8,128)(2,1)}) custom-call(bf16[3072,768]{1,0:T(8,128)(2,1)} %get-tuple-element.75.h_ref, bf16[4,4,384,256]{3,2,1,0:T(8,128)(2,1)} %bitcast.51), custom_call_target="tpu_custom_call" | custom-call | bytes 186000000 | tf_op jit(solution)/shard_map/scatter_down/pallas_call | solution.py:1127
  390.7 6.4 multiply_reduce_fusion
  397.0 1.7 copy-done.4
  398.7 1.4 convert_element_type.84.x_ref
  400.1 70.1 %gather_down_back.1 = (bf16[3072,1536]{1,0:T(8,128)(2,1)}, bf16[4,4,384,256]{3,2,1,0:T(8,128)(2,1)}) custom-call(bf16[384,2048]{1,0:T(8,128)(2,1)} %convert_element_type.84.x_ref, bf16[768,2048]{1,0:T(8,128)(2,1)} %get-tuple-element.78.w_ref, bf16[3072,768]{1,0:T(8,128)(2,1)} %get-tuple-element.79.a_ref, bf16[3072,768]{1,0:T(8,128)(2,1)} %get-tuple-element.80.b_ref, ...), custom_call_target="tpu_custom_call" | custom-call | bytes 198000000 | tf_op jit(solution)/shard_map/gather_down_back/pallas_call | solution.py:1231
  470.3 70.9 %scatter_post.1 = (f32[384,2048]{1,0:T(8,128)}, bf16[4,4,256,768]{3,2,1,0:T(8,128)(2,1)}) custom-call(bf16[3072,1536]{1,0:T(8,128)(2,1)} %get-tuple-element.81.d_ref, bf16[2,2048,768]{2,1,0:T(8,128)(2,1)} %get-tuple-element.82.w_ref, bf16[8,384,2048]{2,1,0:T(8,128)(2,1)} %get-tuple-element.83.all_ref), custom_call_target="tpu_custom_call" | custom-call | bytes 198000000 | tf_op jit(solution)/shard_map/scatter_post/pallas_call | solution.py:1563
  541.3 1.8 copy-done.3
  543.1 2.8 multiply_reduce_fusion.1
  546.9 3.0 fusion.27
  550.0 26.1 %mix_back.1 = (bf16[3072,256]{1,0:T(8,128)(2,1)}, bf16[2048,256]{1,0:T(8,128)(2,1)}, bf16[2048,256]{1,0:T(8,128)(2,1)}, bf16[2048,256]{1,0:T(8,128)(2,1)}, bf16[2048,256]{1,0:T(8,128)(2,1)}) custom-call(bf16[384,2048]{1,0:T(8,128)(2,1)} %get-tuple-element.160.d_ref, bf16[2048,2048]{1,0:T(8,128)(2,1)} %get-tuple-element.85.w_ref, ...), custom_call_target="tpu_custom_call" | custom-call | bytes 78000000 | tf_op jit(solution)/shard_map/mix_back/pallas_call | solution.py:1460
  576.1 1.4 collective-permute-start.3
  578.2 1.5 collective-permute-start.5
  579.6 57.8 %attend_back.1 = (f32[3072,256]{1,0:T(8,128)}, bf16[3072,256]{1,0:T(8,128)(2,1)}, f32[3072,256]{1,0:T(8,128)}, bf16[3072,256]{1,0:T(8,128)(2,1)}) custom-call(s32[3,16]{1,0:T(4,128)} %order_ref.3, s32[3]{0:T(128)} %lens_ref.3, bf16[3072,256]{1,0:T(8,128)(2,1)} %get-tuple-element.67.q_ref, bf16[3072,256]{1,0:T(8,128)(2,1)} %get-tuple-element.87.do_ref, ...), custom_call_target="tpu_custom_call" | custom-call | bytes 225000000 | tf_op jit(solution)/shard_map/attend_back/pallas_call | solution.py:2142
  637.5 3.3 add_convert_fusion
  642.9 23.9 %reduce-scatter.4.cloned.1.call-done = bf16[1,4,256,768]{3,2,1,0:T(8,128)(2,1)} async-done(((bf16[4,4,256,768]{3,2,1,0:T(8,128)(2,1)}), bf16[1,4,256,768]{3,2,1,0:T(8,128)(2,1)}) %reduce-scatter.4.cloned.1.call-update) | async-done | bytes 1572880 | tf_op jit(solution)/shard_map/reduce_scatter | solution.py:2253
  666.8 139.3 %scatter_normed.1 = (f32[384,2048]{1,0:T(8,128)}, f32[2,2,256,256]{3,2,1,0:T(8,128)}, f32[8,128]{1,0:T(8,128)}, bf16[4,256,768]{2,1,0:T(8,128)(2,1)}, bf16[4,384,256]{2,1,0:T(8,128)(2,1)}) custom-call(f32[3072,256]{1,0:T(8,128)} %get-tuple-element.89.dq_ref, f32[3072,256]{1,0:T(8,128)} %get-tuple-element.90.dkv_ref, ...), custom_call_target="tpu_custom_call" | custom-call | bytes 330000000 | tf_op jit(solution)/shard_map/scatter_normed/pallas_call | solution.py:1826
  806.1 1.1 slice.52
  807.9 2.8 fusion.9
  811.3 13.4 %total_of.1 = f32[40,128]{1,0:T(8,128)} custom-call(f32[40,128]{1,0:T(8,128)} %maximum_maximum_fusion.v_ref), custom_call_target="tpu_custom_call" | custom-call | bytes 36000000 | tf_op jit(solution)/shard_map/total_of/pallas_call | solution.py:1916
  824.7 1.2 slice.34
  825.9 1.3 slice_bitcast_fusion.2
  827.2 1.3 slice_bitcast_fusion
  828.5 1.1 fusion.28
  829.6 1.8 convert_element_type.93
  831.4 3.2 slice_convert_fusion
  834.6 3.0 copy.74
  837.6 3.0 copy.79
  840.7 3.0 copy.75
  843.7 3.0 copy.80
  846.7 2.4 bitcast_convert_fusion
  852.9 4.9 fusion.8
  (103 shorter events, 17.0 us)
Async XLA Ops:
  7.2 4.3 copy-start.12
  7.2 55.0 %all-gather.9.cloned.1.call-start = ((), (), s32[]{:S(2)}) async-start(), calls=%async_computation.6 | async-start | bytes 2621440 | tf_op jit(solution)/shard_map/all_gather | solution.py:2218
  10.5 21.3 %copy-start.13 = (bf16[256,1536]{1,0:T(8,128)(2,1)S(1)}, bf16[256,1536]{1,0:T(8,128)(2,1)}, u32[]{:S(2)}) copy-start(bf16[256,1536]{1,0:T(8,128)(2,1)} %param.27) | copy-start | bytes 2359300
  28.2 13.0 %all-to-all-start.2 = ((bf16[4,384,256]{2,1,0:T(8,128)(2,1)}), bf16[4,384,256]{2,1,0:T(8,128)(2,1)S(1)}, u32[]{:S(2)}, u32[]{:S(2)}) async-start(bf16[4,384,256]{2,1,0:T(8,128)(2,1)} %bitcast.61), calls=%async_computation.2 | async-start | bytes 1572864 | tf_op jit(solution)/shard_map/all_to_all | solution.py:2221
  31.7 25.7 %copy-start = (s32[3,16]{1,0:T(4,128)S(1)}, s32[3,16]{1,0:T(4,128)}, u32[]{:S(2)}) copy-start(s32[3,16]{1,0:T(4,128)} %order_ref.3) | copy-start | bytes 580
  31.7 151.0 %all-gather.11.cloned.1.call-start = ((), (), s32[]{:S(2)}) async-start(), calls=%async_computation.7 | async-start | bytes 1310720 | tf_op jit(solution)/shard_map/all_gather | solution.py:2231
  41.2 17.0 %copy-start.7 = (bf16[4,384,256]{2,1,0:T(8,128)(2,1)}, bf16[4,384,256]{2,1,0:T(8,128)(2,1)S(1)}, u32[]{:S(2)}) copy-start(bf16[4,384,256]{2,1,0:T(8,128)(2,1)S(1)} %all-to-all-done.2) | copy-start | bytes 2359300
  54.6 3.9 copy-start.1
  54.7 137.9 %all-gather.13.cloned.1.call-start = ((), (), s32[]{:S(2)}) async-start(), calls=%async_computation.11 | async-start | bytes 3932160 | tf_op jit(solution)/shard_map/all_gather | solution.py:2226
  57.1 3.5 copy-start.15
  57.1 203.6 %all-gather.15.cloned.1.call-start = ((), (), s32[]{:S(2)}) async-start(), calls=%async_computation.12 | async-start | bytes 3932160 | tf_op jit(solution)/shard_map/all_gather | solution.py:2233
  62.2 118.7 %copy-start.8 = (bf16[4,256,384]{1,2,0:T(8,128)(2,1)S(1)}, bf16[4,256,384]{1,2,0:T(8,128)(2,1)}, u32[]{:S(2)}) copy-start(bf16[4,256,384]{1,2,0:T(8,128)(2,1)} %all_to_all.15) | copy-start | bytes 2359300
  180.8 9.1 %copy-start.16 = (s32[3]{0:T(128)S(1)}, s32[3]{0:T(128)}, u32[]{:S(2)}) copy-start(s32[3]{0:T(128)} %lens_ref.3) | copy-start | bytes 40
  182.0 141.7 %all-gather.17.cloned.1.call-start = ((), (), s32[]{:S(2)}) async-start(), calls=%async_computation.13 | async-start | bytes 3932160 | tf_op jit(solution)/shard_map/all_gather | solution.py:2235
  182.6 460.3 %reduce-scatter.6.cloned.1.call-start = ((), (), s32[]{:S(2)}) async-start(), calls=%async_computation.9 | async-start | bytes 3932160 | tf_op jit(solution)/shard_map/reduce_scatter | solution.py:2253
  182.7 48.8 %collective-permute-start = (bf16[2048,256]{1,0:T(8,128)(2,1)}, bf16[2048,256]{1,0:T(8,128)(2,1)S(1)}, u32[]{:S(2)}, u32[]{:S(2)}) collective-permute-start(bf16[2048,256]{1,0:T(8,128)(2,1)} %all-gather.11.cloned.1.call-done.w0_ref), channel_id=1, source_target_pairs={{0,8},{4,12},{8,0},{12,4},{16,24},{20,28},{24,16},{28,20},{1,9},{5... | collective-permute-start | bytes 3145736 | tf_op jit(solution)/shard_map/ppermute | solution.py:2232
  184.1 47.4 %collective-permute-start.1 = (bf16[2048,256]{1,0:T(8,128)(2,1)}, bf16[2048,256]{1,0:T(8,128)(2,1)}, u32[]{:S(2)}, u32[]{:S(2)}) collective-permute-start(bf16[2048,256]{1,0:T(8,128)(2,1)} %all-gather.11.cloned.1.call-done.w0_ref), channel_id=1, source_target_pairs={{0,16},{4,20},{8,24},{12,28},{16,0},{20,4},{24,8},{28,12},{1,17},{... | collective-permute-start | bytes 3145736 | tf_op jit(solution)/shard_map/ppermute | solution.py:2232
  185.5 46.0 %collective-permute-start.2 = (bf16[2048,256]{1,0:T(8,128)(2,1)}, bf16[2048,256]{1,0:T(8,128)(2,1)}, u32[]{:S(2)}, u32[]{:S(2)}) collective-permute-start(bf16[2048,256]{1,0:T(8,128)(2,1)} %all-gather.11.cloned.1.call-done.w0_ref), channel_id=1, source_target_pairs={{0,24},{4,28},{8,16},{12,20},{16,8},{20,12},{24,0},{28,4},{1,25},{... | collective-permute-start | bytes 3145736 | tf_op jit(solution)/shard_map/ppermute | solution.py:2232
  231.4 1.0 copy-start.11
  323.8 66.9 %copy-start.9 = (bf16[384,2048]{1,0:T(8,128)(2,1)S(1)}, bf16[384,2048]{1,0:T(8,128)(2,1)}, u32[]{:S(2)}) copy-start(bf16[384,2048]{1,0:T(8,128)(2,1)} %param.16) | copy-start | bytes 4718596
  397.0 1.7 copy-start.4
  470.2 196.6 %reduce-scatter.4.cloned.1.call-start = ((), (), s32[]{:S(2)}) async-start(), calls=%async_computation.8 | async-start | bytes 7864320 | tf_op jit(solution)/shard_map/reduce_scatter | solution.py:2253
  541.2 1.9 copy-start.3
  541.2 1.9 copy-start.14
  541.2 288.4 %reduce-scatter.8.cloned.1.call-start = ((), (), s32[]{:S(2)}) async-start(), calls=%async_computation.10 | async-start | bytes 1310720 | tf_op jit(solution)/shard_map/reduce_scatter | solution.py:2278
  543.1 2.9 copy-start.5
  543.1 3.9 copy-start.6
  576.1 61.4 %collective-permute-start.3 = (bf16[2048,256]{1,0:T(8,128)(2,1)}, bf16[2048,256]{1,0:T(8,128)(2,1)}, u32[]{:S(2)}, u32[]{:S(2)}) collective-permute-start(bf16[2048,256]{1,0:T(8,128)(2,1)} %get-tuple-element.103), channel_id=1, source_target_pairs={{0,8},{4,12},{8,0},{12,4},{16,24},{20,28},{24,16},{28,20},{1,9},{5... | collective-permute-start | bytes 3145736 | tf_op jit(solution)/shard_map/ppermute | solution.py:2263
  577.4 60.1 %collective-permute-start.4 = (bf16[2048,256]{1,0:T(8,128)(2,1)}, bf16[2048,256]{1,0:T(8,128)(2,1)}, u32[]{:S(2)}, u32[]{:S(2)}) collective-permute-start(bf16[2048,256]{1,0:T(8,128)(2,1)} %get-tuple-element.105), channel_id=1, source_target_pairs={{0,16},{4,20},{8,24},{12,28},{16,0},{20,4},{24,8},{28,12},{1,17},{... | collective-permute-start | bytes 3145736 | tf_op jit(solution)/shard_map/ppermute | solution.py:2263
  578.2 59.4 %collective-permute-start.5 = (bf16[2048,256]{1,0:T(8,128)(2,1)}, bf16[2048,256]{1,0:T(8,128)(2,1)}, u32[]{:S(2)}, u32[]{:S(2)}) collective-permute-start(bf16[2048,256]{1,0:T(8,128)(2,1)} %get-tuple-element.107), channel_id=1, source_target_pairs={{0,24},{4,28},{8,16},{12,20},{16,8},{20,12},{24,0},{28,4},{1,25},{... | collective-permute-start | bytes 3145736 | tf_op jit(solution)/shard_map/ppermute | solution.py:2263
  579.6 57.9 %copy-start.10 = (bf16[2048,256]{1,0:T(8,128)(2,1)S(1)}, bf16[2048,256]{1,0:T(8,128)(2,1)}, u32[]{:S(2)}) copy-start(bf16[2048,256]{1,0:T(8,128)(2,1)} %get-tuple-element.102) | copy-start | bytes 3145732
  637.5 3.4 copy-start.17
  666.8 141.1 %copy-start.2 = (bf16[384,2048]{1,0:T(8,128)(2,1)S(1)}, bf16[384,2048]{1,0:T(8,128)(2,1)}, u32[]{:S(2)}) copy-start(bf16[384,2048]{1,0:T(8,128)(2,1)} %tokens_ref.1) | copy-start | bytes 4718596
Sparse Core Ops, SparseCore 0:
  11.6 48.6 all-gather.8
  61.9 26.6 all-gather.10
  90.7 84.5 all-gather.12
  182.1 65.6 all-gather.14
  249.8 62.1 all-gather.16
  470.4 74.3 reduce-scatter.5
  547.0 119.7 reduce-scatter.3
  669.7 46.7 reduce-scatter.7

commit v3 on v2

--- a/solution.py
+++ b/solution.py
@@ -597,7 +597,7 @@
     def chip_sum(self, n, at):
         return self.own[n, at].astype(F32) + self.from_sib[n, at].astype(F32)
 
-    def step(self, step, product):
+    def step(self, step, product, late=False):
         block = self.block(step)
         n = step // 2
         first, second = self.first, self.second
@@ -628,12 +628,17 @@
         def _():
             self.y_out[second] = self.chip_sum(2, second).astype(BF16)
             self.y_second.start()
-            self.diag_x.wait_recv()
-            self.y_out[first] = (self.chip_sum(2, first) + self.diag_in[first].astype(F32)).astype(BF16)
-            self.y_first.start()
-            self.diag_y.wait_recv()
-            self.x_out[second] = (self.chip_sum(1, second) + self.diag_in[second].astype(F32)).astype(BF16)
-            self.x_second.start()
+            if not late:
+                self.second_wave()
+
+    def second_wave(self):
+        first, second = self.first, self.second
+        self.diag_x.wait_recv()
+        self.y_out[first] = (self.chip_sum(2, first) + self.diag_in[first].astype(F32)).astype(BF16)
+        self.y_first.start()
+        self.diag_y.wait_recv()
+        self.x_out[second] = (self.chip_sum(1, second) + self.diag_in[second].astype(F32)).astype(BF16)
+        self.x_second.start()
 
     def finish(self, o_ref):
         self.x_first.wait_recv()
@@ -743,6 +748,69 @@
                 self.down(block, i).wait_recv()
 
 
+class LineGather:
+    def __init__(self, src, dst, local_sem, send_sems, recv_sems):
+        self.src, self.dst = src, dst
+        self.local_sem, self.send_sems, self.recv_sems = local_sem, send_sems, recv_sems
+        self.plane, self.planes = lax.axis_index("tp"), lax.axis_size("tp")
+        self.pieces = src.shape[0]
+
+    def own(self):
+        return pltpu.make_async_copy(self.src, self.dst.at[self.plane], self.local_sem)
+
+    def copy(self, way, hop, n, origin):
+        src = self.src.at[n] if hop == 0 else self.dst.at[origin, n]
+        return send(
+            src,
+            self.dst.at[origin, n],
+            self.send_sems.at[way, hop, n],
+            self.recv_sems.at[origin, n],
+            on_plane(self.plane + 1 - 2 * way),
+        )
+
+    def each(self, hop, visit):
+        for way in range(2):
+            origin = self.plane - hop if way == 0 else self.plane + hop
+            inside = origin >= 0 if way == 0 else origin < self.planes
+            going = self.plane < self.planes - 1 if way == 0 else self.plane > 0
+
+            @pl.when(inside & going)
+            def _():
+                for n in range(self.pieces):
+                    visit(self.copy(way, hop, n, origin))
+
+    def hop(self, hop):
+        if hop == 0:
+            self.own().start()
+
+        def go(copy):
+            if hop > 0:
+                copy.wait_recv()
+            copy.start()
+
+        self.each(hop, go)
+
+    def finish(self):
+        self.own().wait()
+        for way in range(2):
+            last = self.plane == self.planes - 1 if way == 0 else self.plane == 0
+
+            @pl.when(last)
+            def _():
+                for hop in range(1, 4):
+                    origin = self.plane - hop if way == 0 else self.plane + hop
+                    for n in range(self.pieces):
+                        self.copy(way, 0, n, origin).wait_recv()
+
+        for hop in range(3):
+            self.each(hop, lambda copy: copy.wait_send())
+
+
+def line_scratch(pieces):
+    dma = pltpu.SemaphoreType.DMA
+    return [dma, dma((2, 3, pieces)), dma((4, pieces))]
+
+
 class Turn:
     def __init__(self, ca_ref, sa_ref, cb_ref, sb_ref, unit):
         ca, sa = ca_ref[pl.ds(unit, 1), :], sa_ref[pl.ds(unit, 1), :]
@@ -774,6 +842,8 @@
     sa_ref,
     cb_ref,
     sb_ref,
+    gate_ref,
+    out_ref,
     all_ref,
     w_out_ref,
     q_ref,
@@ -781,6 +851,8 @@
     lo_ref,
     hi_ref,
     lin_ref,
+    gates_ref,
+    outs_ref,
     xs,
     local_sem,
     send_sems,
@@ -792,6 +864,7 @@
     w_recvs,
     kv_sends,
     kv_recvs,
+    *line_sems,
 ):
     ring = Gather(x_ref, xs, local_sem, send_sems, recv_sems)
     me = ring.me
@@ -806,8 +879,14 @@
     def weight_from(device):
         return send(slab_ref.at[device], w.at[pl.ds(device * deep, deep)], w_sends.at[0], w_recvs.at[device], on_ctx(device))
 
+    gathers = (
+        LineGather(out_ref, outs_ref, *line_sems[:3]),
+        LineGather(gate_ref, gates_ref, *line_sems[3:]),
+    )
     for n, device in enumerate(away):
         weight(device, n).start()
+    for gather in gathers:
+        gather.hop(0)
     own_weight = pltpu.make_async_copy(slab_ref.at[me], w.at[pl.ds(me * deep, deep)], w_local)
     own_weight.start()
     ring.start()
@@ -827,6 +906,13 @@
         return turn.forth(v * scale * gain_ref[...])
 
     def turn(step, carry):
+        for hop in (1, 2):
+
+            @pl.when(step == 2 * hop)
+            def _():
+                for gather in gathers:
+                    gather.hop(hop)
+
         ring.before(step)
         block = ring.block(step)
         keep(block).start()
@@ -861,9 +947,11 @@
         return carry
 
     lax.fori_loop(0, 8, settle, 0)
-
-
-def gather_qkv(normed, slab, q_gain, k_gain, tables):
+    for gather in gathers:
+        gather.finish()
+
+
+def gather_qkv(normed, slab, q_gain, k_gain, tables, gate, out):
     rows, width = normed.shape
     _, deep, cols = slab.shape
     flat = jax.ShapeDtypeStruct((8 * rows, 2 * HEAD_SIZE), BF16)
@@ -877,9 +965,12 @@
             flat,
             flat,
             jax.ShapeDtypeStruct((8 * rows, 3 * HEAD_SIZE), F32),
+            jax.ShapeDtypeStruct((4,) + gate.shape, BF16),
+            jax.ShapeDtypeStruct((4,) + out.shape, BF16),
         ),
-        in_specs=[spec_vmem(), spec_any()] + [spec_vmem()] * 6,
-        out_specs=(spec_any(), spec_any(), spec_vmem(), spec_vmem(), spec_any(), spec_any(), spec_vmem()),
+        in_specs=[spec_vmem(), spec_any()] + [spec_vmem()] * 6 + [spec_any()] * 2,
+        out_specs=(spec_any(), spec_any(), spec_vmem(), spec_vmem(), spec_any(), spec_any(), spec_vmem())
+        + (spec_any(),) * 2,
         scratch_shapes=gather_scratch(rows, width)
         + [
             pltpu.SemaphoreType.DMA((8,)),
@@ -889,11 +980,13 @@
             pltpu.SemaphoreType.DMA((8,)),
             pltpu.SemaphoreType.DMA((2, 8 * rows // UNIT)),
             pltpu.SemaphoreType.DMA((2, 8 * rows // UNIT)),
-        ],
+        ]
+        + line_scratch(out.shape[0])
+        + line_scratch(gate.shape[0]),
         compiler_params=comm_params(1),
         cost_estimate=busy(80),
         name="gather_qkv",
-    )(normed, slab, q_gain.reshape(1, -1), k_gain.reshape(1, -1), *tables)
+    )(normed, slab, q_gain.reshape(1, -1), k_gain.reshape(1, -1), *tables, gate, out)
 
 
 class Halves:
@@ -1087,7 +1180,7 @@
     )(post, gate_parts, up_parts)
 
 
-def down_kernel(h_ref, parts_ref, o_ref, w_out_ref, *scratch):
+def down_kernel(h_ref, parts_ref, middle_ref, teacher_ref, valid_ref, o_ref, low_ref, diff_ref, error_ref, w_out_ref, *scratch):
     rs = Scatter(*scratch[:N_SCATTER])
     w, w_sem, w_local, w_sends, w_recvs = scratch[N_SCATTER:]
     rows = o_ref.shape[0]
@@ -1115,27 +1208,43 @@
         return carry
 
     lax.fori_loop(0, 8, turn, 0)
-    rs.finish(o_ref)
+    rs.finish(diff_ref)
+    error = jnp.zeros((rows, HEAD_SIZE), F32)
+    for n in range(0, diff_ref.shape[1], HEAD_SIZE):
+        at = slice(n, n + HEAD_SIZE)
+        result = middle_ref[:, at] + diff_ref[:, at]
+        o_ref[:, at] = result.astype(BF16)
+        diff = (result - teacher_ref[:, at].astype(F32)) * valid_ref[...]
+        diff_ref[:, at] = diff
+        low_ref[:, at] = diff.astype(BF16)
+        error += diff * diff
+    error_ref[...] = jnp.sum(error, axis=0, keepdims=True)
     weight.finish()
     keep_w.wait()
 
 
-def scatter_down(hidden, parts):
-    rows = hidden.shape[0] // 8
+def scatter_down(hidden, parts, middle, teacher, valid):
+    rows, width = middle.shape
     ff = hidden.shape[1]
-    width = 8 * parts.shape[-1]
+    low = jax.ShapeDtypeStruct((rows, width), BF16)
     return pl.pallas_call(
         down_kernel,
-        out_shape=(jax.ShapeDtypeStruct((rows, width), F32), jax.ShapeDtypeStruct((ff, width), BF16)),
-        in_specs=[spec_vmem(), spec_any()],
-        out_specs=(spec_vmem(), spec_any()),
+        out_shape=(
+            low,
+            low,
+            jax.ShapeDtypeStruct((rows, width), F32),
+            jax.ShapeDtypeStruct((1, HEAD_SIZE), F32),
+            jax.ShapeDtypeStruct((ff, width), BF16),
+        ),
+        in_specs=[spec_vmem(), spec_any()] + [spec_vmem()] * 3,
+        out_specs=(spec_vmem(),) * 4 + (spec_any(),),
         scratch_shapes=scatter_scratch(rows, width)
         + [pltpu.VMEM((ff, width), BF16), pltpu.SemaphoreType.DMA]
         + HALVES_SCRATCH,
         compiler_params=comm_params(6),
         cost_estimate=busy(62),
         name="scatter_down",
-    )(hidden, parts)
+    )(hidden, parts, middle, teacher, valid)
 
 
 def down_back_kernel(
@@ -1368,14 +1477,22 @@
 
 
 def mix_back_kernel(
-    d_ref,
+    post_ref,
+    middle_ref,
+    diff_ref,
+    gain_ref,
     w_ref,
     rows_ref,
+    swap_ref,
     dm_ref,
+    d_middle_ref,
+    gp_ref,
     g0_ref,
     g1_ref,
     g2_ref,
     g3_ref,
+    swapped_ref,
+    d_ref,
     stage,
     to_sib,
     from_sib,
@@ -1386,6 +1503,7 @@
     s_sends,
     s_recvs,
     g_sems,
+    *c_sems,
 ):
     me, sib, nx, ny, dg = plane_neighbours()
     shift = sib - me
@@ -1393,6 +1511,23 @@
     rows, width = d_ref.shape
     deep = width // 8
     greet(away)
+    weight_swap = ChipSwap(swap_ref, swapped_ref, *c_sems)
+    weight_swap.start()
+    squares = jnp.zeros((rows, HEAD_SIZE), F32)
+    dots = jnp.zeros((rows, HEAD_SIZE), F32)
+    cuts = [slice(n, n + HEAD_SIZE) for n in range(0, width, HEAD_SIZE)]
+    for at in cuts:
+        middle = middle_ref[:, at]
+        squares += middle * middle
+        dots += post_ref[:, at] * gain_ref[:, at] * middle
+    scale = lax.rsqrt(jnp.sum(squares, axis=-1, keepdims=True) / width + EPS)
+    pull = scale * scale * scale * (jnp.sum(dots, axis=-1, keepdims=True) / width)
+    for at in cuts:
+        middle, post = middle_ref[:, at], post_ref[:, at]
+        gp_ref[:, at] = jnp.sum(post * (middle * scale), axis=0, keepdims=True)
+        d_middle = diff_ref[:, at] + scale * (post * gain_ref[:, at]) - middle * pull
+        d_middle_ref[:, at] = d_middle
+        d_ref[:, at] = d_middle.astype(BF16)
     outs = (g0_ref, g1_ref, g2_ref, g3_ref)
     chips = (me, nx, ny, dg)
 
@@ -1450,20 +1585,27 @@
     for n in range(4):
         swap(n).wait_send()
         pltpu.make_async_copy(own.at[n], outs[n], g_sems.at[n]).wait()
-
-
-def mix_back(d_mid, w, mixed_rows):
-    rows, width = d_mid.shape
+    weight_swap.finish()
+
+
+def mix_back(d_post, middle, diff, post_gain, w, mixed_rows, swap):
+    rows, width = middle.shape
     deep = width // 8
     dma = pltpu.SemaphoreType.DMA
     four = pltpu.VMEM((4, width, deep), BF16)
     return pl.pallas_call(
         mix_back_kernel,
-        out_shape=(jax.ShapeDtypeStruct((8 * rows, deep), BF16),)
-        + (jax.ShapeDtypeStruct((width, deep), BF16),) * 4,
-        in_specs=[spec_vmem()] * 3,
-        out_specs=(spec_any(),) * 5,
+        out_shape=(
+            jax.ShapeDtypeStruct((8 * rows, deep), BF16),
+            jax.ShapeDtypeStruct((rows, width), F32),
+            jax.ShapeDtypeStruct((1, width), F32),
+        )
+        + (jax.ShapeDtypeStruct((width, deep), BF16),) * 4
+        + (jax.ShapeDtypeStruct(swap.shape, BF16),),
+        in_specs=[spec_vmem()] * 6 + [spec_any()],
+        out_specs=(spec_any(), spec_vmem(), spec_vmem()) + (spec_any(),) * 5,
         scratch_shapes=[
+            pltpu.VMEM((rows, width), BF16),
             pltpu.VMEM((8, rows, deep), BF16),
             four,
             four,
@@ -1474,11 +1616,46 @@
             dma((4,)),
             dma((4,)),
             dma((4,)),
-        ],
+        ]
+        + SWAP_SCRATCH,
         compiler_params=comm_params(4),
         cost_estimate=busy(26),
         name="mix_back",
-    )(d_mid, w, mixed_rows)
+    )(d_post, middle, diff, post_gain.reshape(1, -1), w, mixed_rows, swap)
+
+
+class ChipSwap:
+    def __init__(self, src, dst, local_sem, send_sems, recv_sems):
+        self.src, self.dst = src, dst
+        self.local_sem, self.send_sems, self.recv_sems = local_sem, send_sems, recv_sems
+        me, _, nx, ny, dg = plane_neighbours()
+        self.chip, self.away = me // 2, (dg, nx, ny)
+
+    def own(self):
+        return pltpu.make_async_copy(self.src.at[self.chip], self.dst.at[self.chip], self.local_sem)
+
+    def to(self, n):
+        there = self.away[n]
+        return send(
+            self.src.at[there // 2], self.dst.at[self.chip], self.send_sems.at[n], self.recv_sems.at[self.chip], on_ctx(there)
+        )
+
+    def start(self):
+        self.own().start()
+        for n in range(3):
+            self.to(n).start()
+
+    def finish(self):
+        self.own().wait()
+        for n in range(3):
+            there = self.away[n] // 2
+            send(
+                self.src.at[there], self.dst.at[there], self.send_sems.at[n], self.recv_sems.at[there], on_ctx(self.away[n])
+            ).wait_recv()
+            self.to(n).wait_send()
+
+
+SWAP_SCRATCH = [pltpu.SemaphoreType.DMA, pltpu.SemaphoreType.DMA((3,)), pltpu.SemaphoreType.DMA((4,))]
 
 
 def columns(all_ref, slices, sems, c, slot):
@@ -1589,8 +1766,8 @@
     lin_ref,
     w_ref,
     all_ref,
-    swap_a_ref,
-    swap_b_ref,
+    swap_ref,
+    wo_ref,
     qg_ref,
     kg_ref,
     ca_ref,
@@ -1600,8 +1777,8 @@
     o_ref,
     gw_ref,
     gains_ref,
-    swapped_a_ref,
-    swapped_b_ref,
+    swapped_ref,
+    wo_planes_ref,
     *scratch,
 ):
     rs = Scatter(*scratch[:N_SCATTER])
@@ -1620,9 +1797,10 @@
         t_recvs,
         p_sends,
         p_recvs,
-        c_local,
-        c_sends,
-        c_recvs,
+        o_local,
+        o_sends,
+        o_recvs,
+        *c_sems,
     ) = scratch[N_SCATTER:]
     me = rs.me
     plane, planes = lax.axis_index("tp"), lax.axis_size("tp")
@@ -1667,7 +1845,7 @@
         here = pl.ds(pl.multiple_of(unit * UNIT, UNIT), UNIT)
         for h in range(2):
             lanes = slice(h * HEAD_SIZE, (h + 1) * HEAD_SIZE)
-            d, gain = head_back(dq_ref[here, lanes] * HEAD_SIZE**-0.5, lin_ref[here, lanes], qg_ref, rotation)
+            d, gain = head_back(dq_ref[here, lanes].astype(F32) * HEAD_SIZE**-0.5, lin_ref[here, lanes], qg_ref, rotation)
             d_lin[here, lanes] = d
             gains_ref[0:1, :] += gain
         return carry
@@ -1677,7 +1855,7 @@
         for i in range(units):
             unit = block * units + i
             here = pl.ds(pl.multiple_of(unit * UNIT, UNIT), UNIT)
-            d_kv = dkv_ref[here, :] + from_lo[here, :].astype(F32) + from_hi[here, :].astype(F32)
+            d_kv = dkv_ref[here, :].astype(F32) + from_lo[here, :].astype(F32) + from_hi[here, :].astype(F32)
             lanes = slice(2 * HEAD_SIZE, 3 * HEAD_SIZE)
             d, gain = head_back(d_kv[:, :HEAD_SIZE], lin_ref[here, lanes], kg_ref, rotation_of(unit))
             d_lin[here, lanes] = d
@@ -1763,46 +1941,37 @@
 
     def turn(step, carry):
         prepare_keys(rs.block(step))
-        rs.step(step, product)
+        rs.step(step, product, late=True)
         return carry
 
+    def out_to(n):
+        return send(
+            wo_ref.at[far[n]], wo_planes_ref.at[plane], o_sends.at[n], o_recvs.at[plane], on_plane(far[n])
+        )
+
+    out_own = pltpu.make_async_copy(wo_ref.at[plane], wo_planes_ref.at[plane], o_local)
     lax.fori_loop(0, plane_rows // UNIT, prepare_queries, 0)
     grads(0)
     lax.fori_loop(0, 8, turn, 0)
+    out_own.start()
+    for n in range(len(far)):
+        out_to(n).start()
     grads(1)
-    chip = me // 2
-    chips = (rs.dg, rs.nx, rs.ny)
-    swaps = ((swap_a_ref, swapped_a_ref), (swap_b_ref, swapped_b_ref))
-
-    def swap_own(i):
-        return pltpu.make_async_copy(swaps[i][0].at[chip], swaps[i][1].at[chip], c_local.at[i])
-
-    def swap_to(i, n):
-        there = chips[n]
-        return send(
-            swaps[i][0].at[there // 2], swaps[i][1].at[chip], c_sends.at[i, n], c_recvs.at[i, chip], on_ctx(there)
-        )
-
-    def swap_from(i, n):
-        there = chips[n] // 2
-        return send(
-            swaps[i][0].at[there], swaps[i][1].at[there], c_sends.at[i, n], c_recvs.at[i, there], on_ctx(chips[n])
-        )
-
-    for i in range(2):
-        swap_own(i).start()
-        for n in range(3):
-            swap_to(i, n).start()
+    rs.second_wave()
+    swap = ChipSwap(swap_ref, swapped_ref, *c_sems)
+    swap.start()
     spread(0)
     rs.finish(o_ref)
     spread(1)
     collect(0)
     collect(1)
-    for i in range(2):
-        swap_own(i).wait()
-        for n in range(3):
-            swap_from(i, n).wait_recv()
-            swap_to(i, n).wait_send()
+    swap.finish()
+    out_own.wait()
+    for n, p in enumerate(far):
+        send(
+            wo_ref.at[p], wo_planes_ref.at[p], o_sends.at[n], o_recvs.at[p], on_plane(p)
+        ).wait_recv()
+        out_to(n).wait_send()
     for part in range(2):
         for n, device in enumerate(order[:7]):
             tile_to(part, n, device).wait_send()
@@ -1816,7 +1985,7 @@
     lax.fori_loop(0, 8, settle, 0)
 
 
-def scatter_normed(d_queries, d_kv, to_lo, to_hi, lin, w_qkv, normed_all, swaps, q_gain, k_gain, tables):
+def scatter_normed(d_queries, d_kv, to_lo, to_hi, lin, w_qkv, normed_all, swap, wo, q_gain, k_gain, tables):
     _, rows, width = normed_all.shape
     deep = width // 8
     cols = w_qkv.shape[1]
@@ -1829,8 +1998,8 @@
             jax.ShapeDtypeStruct((rows, width), F32),
             jax.ShapeDtypeStruct((2, 2, deep, cols // 2), F32),
             jax.ShapeDtypeStruct((8, HEAD_SIZE), F32),
-            jax.ShapeDtypeStruct(swaps[0].shape, BF16),
-            jax.ShapeDtypeStruct(swaps[1].shape, BF16),
+            jax.ShapeDtypeStruct(swap.shape, BF16),
+            jax.ShapeDtypeStruct(wo.shape, BF16),
         ),
         in_specs=[spec_vmem()] * 2
         + [spec_any()] * 2
@@ -1854,10 +2023,11 @@
             dma((2, 8)),
             dma((2, 3)),
             dma((2, 4)),
-            dma((2,)),
-            dma((2, 3)),
-            dma((2, 4)),
-        ],
+            dma,
+            dma((3,)),
+            dma((4,)),
+        ]
+        + SWAP_SCRATCH,
         compiler_params=comm_params(8),
         cost_estimate=busy(110),
         name="scatter_normed",
@@ -1869,7 +2039,8 @@
         lin,
         w_qkv,
         normed_all,
-        *swaps,
+        swap,
+        wo,
         q_gain.reshape(1, -1),
         k_gain.reshape(1, -1),
         *tables,
@@ -1930,6 +2101,76 @@
     )(values)
 
 
+def finish_kernel(
+    d_ref, tokens_ref, middle_ref, gain_ref, gu_ref, down_ref, qkv_ref, out_ref,
+    dt_ref, gin_ref, gate_ref, up_ref, dw_ref, wq_ref, wk_ref, wv_ref, wo_ref,
+):
+    width = d_ref.shape[1]
+
+    @pl.when(pl.program_id(0) == 0)
+    def _():
+        gin_ref[...] = jnp.zeros_like(gin_ref)
+
+    stream = tokens_ref[...].astype(F32)
+    scale = lax.rsqrt(jnp.mean(stream * stream, axis=-1, keepdims=True) + EPS)
+    grad = d_ref[...]
+    gin_ref[...] += jnp.sum(grad * (stream * scale), axis=0, keepdims=True)
+    gained = grad * gain_ref[...]
+    pull = scale * scale * scale * jnp.mean(gained * stream, axis=-1, keepdims=True)
+    dt_ref[...] = (middle_ref[...] + (scale * gained - stream * pull)).astype(BF16)
+    cols = gu_ref.shape[2] // 2
+    for p in range(4):
+        here = slice(p * cols, (p + 1) * cols)
+        gate_ref[:, here] = gu_ref[p, :, :cols].astype(F32)
+        up_ref[:, here] = gu_ref[p, :, cols:].astype(F32)
+    dw_ref[...] = down_ref[...].astype(F32)
+    wide = 2 * HEAD_SIZE
+    for k in range(2):
+        wq_ref[:, k * wide : (k + 1) * wide] = qkv_ref[0, k]
+        wk_ref[:, k * HEAD_SIZE : (k + 1) * HEAD_SIZE] = qkv_ref[1, k, :, :HEAD_SIZE]
+        wv_ref[:, k * HEAD_SIZE : (k + 1) * HEAD_SIZE] = qkv_ref[1, k, :, HEAD_SIZE:]
+    wo_ref[...] = sum(out_ref[p].astype(F32) for p in range(4))
+
+
+def finish(d_normed, tokens, d_middle, in_gain, gu, down, qkv, out):
+    steps = 8
+
+    def piece(shape, axis):
+        block = list(shape)
+        block[axis] //= steps
+        return pl.BlockSpec(
+            tuple(block), lambda i, axis=axis, n=len(shape): tuple(i if d == axis else 0 for d in range(n))
+        )
+
+    rows, width = tokens.shape
+    deep, ff = gu.shape[1], 2 * gu.shape[2]
+    one = (1, width)
+    whole = pl.BlockSpec(one, lambda i: (0, 0))
+    flat, square = (rows, width), (deep, 2 * HEAD_SIZE)
+    ins = [(flat, 0), (flat, 0), (flat, 0), None, (gu.shape, 1), (down.shape, 1), (qkv.shape, 2), (out.shape, 1)]
+    outs = [
+        (flat, 0, BF16),
+        None,
+        ((deep, ff), 0, F32),
+        ((deep, ff), 0, F32),
+        (down.shape, 1, F32),
+        ((deep, 4 * HEAD_SIZE), 0, F32),
+        (square, 0, F32),
+        (square, 0, F32),
+        (out.shape[1:], 0, F32),
+    ]
+    return pl.pallas_call(
+        finish_kernel,
+        grid=(steps,),
+        out_shape=tuple(jax.ShapeDtypeStruct(o[0], o[2]) if o else jax.ShapeDtypeStruct(one, F32) for o in outs),
+        in_specs=[piece(*i) if i else whole for i in ins],
+        out_specs=tuple(piece(o[0], o[1]) if o else whole for o in outs),
+        compiler_params=pltpu.CompilerParams(vmem_limit_bytes=VMEM_LIMIT),
+        cost_estimate=busy(8),
+        name="finish",
+    )(d_normed, tokens, d_middle, in_gain.reshape(1, -1), gu, down, qkv, out)
+
+
 class Places:
     def __init__(self, order_ref, lens_ref):
         self.order, self.lens = order_ref, lens_ref
@@ -1986,6 +2227,29 @@
                 pltpu.make_async_copy(keys.at[slot], keys.at[slot], value_sem.at[slot]).wait()
 
 
+def sweep(clear, part):
+    def four(i, carry):
+        part(i * 4 * KEYS, 4 * KEYS, False)
+        return carry
+
+    lax.fori_loop(0, clear // 4, four, 0)
+
+    @pl.when(lax.rem(clear, 4) >= 2)
+    def _():
+        part(clear // 4 * 4 * KEYS, 2 * KEYS, False)
+
+
+    odd = lax.rem(clear, 2)
+
+    @pl.when(odd == 1)
+    def _():
+        part((clear - 1) * KEYS, 2 * KEYS, True)
+
+    @pl.when(odd == 0)
+    def _():
+        part(clear * KEYS, KEYS, True)
+
+
 def attend_kernel(
     order_ref, lens_ref, q_ref, lo_ref, own_ref, hi_ref, o_ref, lse_ref, keys, values, acc, key_sem, value_sem
 ):
@@ -2001,28 +2265,25 @@
         queries = jnp.concatenate([both[:, :HEAD_SIZE], both[:, HEAD_SIZE:]], axis=0)
         clear = jnp.minimum(position * UNIT, length) // KEYS
         acc[...] = jnp.zeros_like(acc)
-
-        def part(block, masked):
-            at = pl.ds(pl.multiple_of(block * KEYS, KEYS), KEYS)
+        row = lax.rem(lax.broadcasted_iota(jnp.int32, (2 * UNIT, 1), 0), UNIT)
+
+        def part(start, size, masked):
+            at = pl.ds(pl.multiple_of(start, KEYS), size)
             weights = jnp.exp2(nt(queries, keys[slot, at, :]))
             if masked:
-                key_pos = block * KEYS + lax.broadcasted_iota(jnp.int32, weights.shape, 1)
-                query_pos = position * UNIT + lax.rem(
-                    lax.broadcasted_iota(jnp.int32, weights.shape, 0), UNIT
-                )
-                weights = jnp.where((key_pos <= query_pos) & (key_pos < length), weights, 0.0)
-            acc[...] += nn(weights.astype(BF16), values[slot, at, :])
-
-        def full(block, carry):
-            part(block, False)
-            return carry
-
-        lax.fori_loop(0, clear, full, 0)
-        part(clear, True)
-        total = acc[:, HEAD_SIZE:]
+                last = jnp.minimum(row + (position * UNIT - start), length - 1 - start)
+                weights = jnp.where(lax.broadcasted_iota(jnp.int32, weights.shape, 1) <= last, weights, 0.0)
+            acc[:, :HEAD_SIZE] += nn(weights.astype(BF16), values[slot, at, :HEAD_SIZE])
+            part_sum = weights[:, :HEAD_SIZE]
+            for n in range(HEAD_SIZE, size, HEAD_SIZE):
+                part_sum += weights[:, n : n + HEAD_SIZE]
+            acc[:, HEAD_SIZE:] += part_sum
+
+        sweep(clear, part)
+        total = jnp.sum(acc[:, HEAD_SIZE:], axis=-1, keepdims=True)
         mixed = (acc[:, :HEAD_SIZE] / total).astype(BF16)
         o_ref[rows, :] = jnp.concatenate([mixed[:UNIT], mixed[UNIT:]], axis=1)
-        lse_ref[u] = jnp.transpose(jnp.log2(total))[:8, :]
+        lse_ref[u] = jnp.transpose(jnp.broadcast_to(jnp.log2(total), (2 * UNIT, HEAD_SIZE)))[:8, :]
         return carry
 
     lax.fori_loop(0, q_ref.shape[0] // UNIT, one_unit, 0)
@@ -2093,29 +2354,22 @@
         lse = lse_ref[u][:1, :]
         clear = jnp.minimum(position * UNIT, length) // KEYS
         dq_acc[...] = jnp.zeros_like(dq_acc)
-
-        def part(block, masked):
-            at = pl.ds(pl.multiple_of(block * KEYS, KEYS), KEYS)
+        row = lax.rem(lax.broadcasted_iota(jnp.int32, (1, 2 * UNIT), 1), UNIT)
+
+        def part(start, size, masked):
+            at = pl.ds(pl.multiple_of(start, KEYS), size)
             key = keys[slot, at, :]
             probs = jnp.exp2(nt(key, queries) - lse)
             if masked:
-                key_pos = block * KEYS + lax.broadcasted_iota(jnp.int32, probs.shape, 0)
-                query_pos = position * UNIT + lax.rem(
-                    lax.broadcasted_iota(jnp.int32, probs.shape, 1), UNIT
-                )
-                probs = jnp.where((key_pos <= query_pos) & (key_pos < length), probs, 0.0)
+                last = jnp.minimum(row + (position * UNIT - start), length - 1 - start)
+                probs = jnp.where(lax.broadcasted_iota(jnp.int32, probs.shape, 0) <= last, probs, 0.0)
             d_scores = (probs * (nt(values[slot, at, :], grads) - delta)).astype(BF16)
             dvalues[slot, at, :] += nn(probs.astype(BF16), grads)
             dkeys[slot, at, :] += nn(d_scores, queries)
             dq_acc[...] += tn(d_scores, key)
 
-        def full(block, carry):
-            part(block, False)
-            return carry
-
-        lax.fori_loop(0, clear, full, 0)
-        part(clear, True)
-        dq_ref[rows, :] = jnp.concatenate([dq_acc[:UNIT, :], dq_acc[UNIT:, :]], axis=1)
+        sweep(clear, part)
+        dq_ref[rows, :] = jnp.concatenate([dq_acc[:UNIT, :], dq_acc[UNIT:, :]], axis=1).astype(BF16)
         return carry
 
     lax.fori_loop(0, q_ref.shape[0] // UNIT, one_unit, 0)
@@ -2136,12 +2390,11 @@
 
 def attend_back(order, lens, q, d_mixed, mixed, lse, lo, own, hi, seq_len):
     flat = jax.ShapeDtypeStruct(q.shape, BF16)
-    wide = jax.ShapeDtypeStruct(q.shape, F32)
     held = pltpu.VMEM((2, seq_len, HEAD_SIZE), BF16)
     summed = pltpu.VMEM((2, seq_len, HEAD_SIZE), F32)
     return pl.pallas_call(
         attend_back_kernel,
-        out_shape=(wide, flat, wide, flat),
+        out_shape=(flat,) * 4,
         in_specs=[spec_smem(), spec_smem()] + [spec_vmem()] * 4 + [spec_any()] * 3,
         out_specs=(spec_vmem(),) * 4,
         scratch_shapes=[
@@ -2203,9 +2456,12 @@
     deep = width // 8
     cols = w_gate.shape[1] // 4
     stream = tokens.astype(F32)
-    scale_in = rms_scale(stream)
-    unit_in = stream * scale_in
-    normed_rows = (unit_in * in_gain).astype(BF16)
+    normed_rows = (stream * rms_scale(stream) * in_gain).astype(BF16)
+    unit = plane * (tok_rows // UNIT) + jnp.arange(tok_rows // UNIT, dtype=jnp.int32)
+    seq, quarter = unit // 4, unit % 4
+    start = block_order[seq, 2 * me + quarter // 2] * BLK + (quarter % 2) * UNIT
+    position = start[:, None] + jnp.arange(UNIT, dtype=jnp.int32)
+    valid = (position < seq_lens[seq][:, None]).astype(F32).reshape(tok_rows, 1)
 
     qkv_home = jnp.concatenate(
         [
@@ -2223,29 +2479,24 @@
     gate_part = to_chips(jnp.transpose(w_gate.reshape(deep, 4, cols), (1, 0, 2)))
     up_part = to_chips(jnp.transpose(w_up.reshape(deep, 4, cols), (1, 0, 2)))
     down_part = to_chips(w_down.reshape(4, cols, deep))
-    gate_parts = lax.all_gather(after(gate_part, up_part, down_part), "tp", axis=0)
     tables = angles(block_order, tok_rows)
-    normed_all, w_qkv, queries, kv, kv_lo, kv_hi, lin = gather_qkv(
-        normed_rows, after(qkv_slab, gate_part, up_part, down_part), q_gain, k_gain, tables
-    )
-    out_part = lax.all_gather(after(w_out, gate_part, up_part, down_part), "tp", axis=0, tiled=True)
+    normed_all, w_qkv, queries, kv, kv_lo, kv_hi, lin, gate_parts, out_part = gather_qkv(
+        normed_rows,
+        after(qkv_slab, up_part, down_part),
+        q_gain,
+        k_gain,
+        tables,
+        gate_part,
+        w_out.reshape(2, 2 * HEAD_SIZE, deep),
+    )
+    out_part = out_part.reshape(width, deep)
     out_parts = [out_part] + [lax.ppermute(out_part, "ctx", [(i, i ^ n) for i in range(8)]) for n in (2, 4, 6)]
-    up_parts = lax.all_gather(after(up_part, kv), "tp", axis=0)
-    mixed, lse = attend(block_order, seq_lens, after(queries, gate_parts, out_part), kv_lo, kv, kv_hi, seq_len)
-    down_parts = lax.all_gather(after(down_part, kv), "tp", axis=0)
+    up_parts = lax.all_gather(after(up_part, kv[:8]), "tp", axis=0)
+    mixed, lse = attend(block_order, seq_lens, queries, kv_lo, kv, kv_hi, seq_len)
+    down_parts = lax.all_gather(after(down_part, kv[:8]), "tp", axis=0)
     middle, post_rows, mixed_rows, w_o = mix(mixed, tokens, post_gain, out_parts)
     post_all, w_gu, slope, active, hidden = gather_up(post_rows, gate_parts, up_parts)
-    summed, w_d = scatter_down(hidden, down_parts)
-    result = middle + summed
-    output = result.astype(BF16)
-
-    row = plane * tok_rows + jnp.arange(tok_rows, dtype=jnp.int32)
-    seq, rest = row // (2 * BLK), row % (2 * BLK)
-    position = block_order[seq, 2 * me + rest // BLK] * BLK + rest % BLK
-    valid = (position < seq_lens[seq]).astype(F32)
-    diff = (result - teacher.astype(F32)) * valid[:, None]
-    error_local = jnp.sum(diff * diff)
-    diff_low = diff.astype(BF16)
+    output, diff_low, diff, error, w_d = scatter_down(hidden, down_parts, middle, teacher, valid)
     d_gu, grad_wd = gather_down_back(diff_low, w_d, slope, active, hidden)
     d_post, grad_gu = scatter_post(d_gu, w_gu, post_all)
 
@@ -2254,11 +2505,9 @@
 
     grad_down = home_sum(grad_wd)
     grad_gu = home_sum(grad_gu)
-    scale_post = rms_scale(middle)
-    unit_post = middle * scale_post
-    grad_post_local = jnp.sum(d_post * unit_post, axis=0)
-    d_middle = diff + rms_back(middle, scale_post, d_post * post_gain)
-    d_mixed, *grad_wo = mix_back(d_middle.astype(BF16), w_o, mixed_rows)
+    d_mixed, d_middle, grad_post, *grad_wo, grad_down = mix_back(
+        d_post, middle, diff, post_gain, w_o, mixed_rows, grad_down
+    )
     grad_wo = [grad_wo[0]] + [
         lax.ppermute(grad_wo[m], "ctx", [(i, i ^ n) for i in range(8)]) for m, n in ((1, 2), (2, 4), (3, 6))
     ]
@@ -2275,10 +2524,8 @@
         kv_hi,
         seq_len,
     )
-    grad_out = lax.psum_scatter(
-        sum(after(g, d_queries).astype(F32) for g in grad_wo).astype(BF16), "tp", scatter_dimension=0, tiled=True
-    )
-    d_normed, grad_qkv, grad_gains, gu_sum, grad_down = scatter_normed(
+    out_sum = sum(after(g, d_queries[:8]).astype(F32) for g in grad_wo).astype(BF16)
+    d_normed, grad_qkv, grad_gains, gu_sum, grad_out = scatter_normed(
         d_queries,
         d_kv,
         to_lo,
@@ -2286,35 +2533,29 @@
         lin,
         w_qkv,
         normed_all,
-        (grad_gu, grad_down),
+        grad_gu,
+        out_sum.reshape(4, 4 * HEAD_SIZE, deep),
         q_gain,
         k_gain,
         tables,
     )
-    grad_down = grad_down.reshape(4 * cols, deep)
-    gu_sum = jnp.transpose(gu_sum, (1, 0, 2))
-    grad_gate = gu_sum[:, :, :cols].reshape(deep, 4 * cols)
-    grad_up = gu_sum[:, :, cols:].reshape(deep, 4 * cols)
-    grad_qkv = jnp.transpose(grad_qkv, (0, 2, 1, 3))
-    grad_query = grad_qkv[0].reshape(deep, 4 * HEAD_SIZE)
-    grad_key = grad_qkv[1, :, :, :HEAD_SIZE].reshape(deep, 2 * HEAD_SIZE)
-    grad_value = grad_qkv[1, :, :, HEAD_SIZE:].reshape(deep, 2 * HEAD_SIZE)
-    grad_in_local = jnp.sum(d_normed * unit_in, axis=0)
-    d_tokens = (d_middle + rms_back(stream, scale_in, d_normed * in_gain)).astype(BF16)
+    d_tokens, grad_in, grad_gate, grad_up, grad_down, grad_query, grad_key, grad_value, grad_out = finish(
+        d_normed, tokens, d_middle, in_gain, gu_sum, grad_down, grad_qkv, grad_out
+    )
     lanes = width // HEAD_SIZE
     totals = total_of(
         jnp.concatenate(
             [
-                grad_in_local.reshape(lanes, HEAD_SIZE),
-                grad_post_local.reshape(lanes, HEAD_SIZE),
+                grad_in.reshape(lanes, HEAD_SIZE),
+                grad_post.reshape(lanes, HEAD_SIZE),
                 grad_gains[:2],
-                jnp.full((6, HEAD_SIZE), error_local),
+                jnp.broadcast_to(error, (6, HEAD_SIZE)),
             ],
             axis=0,
         )
     )
     count_valid = jnp.sum(seq_lens).astype(F32)
-    loss = 0.5 * totals[2 * lanes + 2, 0] / (count_valid * MODEL_WIDTH)
+    loss = 0.5 * jnp.sum(totals[2 * lanes + 2]) / (count_valid * MODEL_WIDTH)
     return (
         output,
         loss,
@@ -2325,11 +2566,11 @@
         grad_value,
         totals[2 * lanes],
         totals[2 * lanes + 1],
-        after(grad_out, d_normed).astype(F32),
+        grad_out,
         totals[lanes : 2 * lanes].reshape(width),
-        grad_gate.astype(F32),
-        grad_up.astype(F32),
-        grad_down.astype(F32),
+        grad_gate,
+        grad_up,
+        grad_down.reshape(4 * cols, deep),
     )
 
 

time: 871 us -> 790 us (0.907)
  blocking collectives: 29.8 us -> 0 us
  other arithmetic: 39.3 us -> 11.2 us
  local copies, waits for them, and re-layouts: 41.5 us -> 17.7 us
  Pallas kernels: 693 us -> 681 us
    all_to_all x2 -> x0, blocking collectives: 29.8 us -> none  [to_chips(): lax.all_to_all(home, 'ctx', 0, 0, axis_index_groups=CORE_GROUPS, tiled=True)]
    pallas_call x1, Pallas kernels: 139 us -> 117 us  [scatter_normed(): pl.pallas_call(normed_back_kernel, out_shape=(jax.ShapeDtypeStruct((rows,...]
    reduce_scatter x2, waiting for transfers between devices: 23.9 us -> 2.9 us  [home_sum(): return lax.psum_scatter(parts, 'tp', scatter_dimension=0, tiled=True)[0]]
    convert_element_type x9 -> x2, other arithmetic: 21.6 us -> 4.91 us  [the longest x1 3.34 us: local_plane(): sum((after(g, d_queries[:8]).astype(F32) for g in grad_wo)).astype(BF16)]
    pallas_call x1, Pallas kernels: 119 us -> 102 us  [gather_qkv(): pl.pallas_call(qkv_kernel, out_shape=(jax.ShapeDtypeStruct((8, rows, widt...]
    pallas_call x2 -> x3, Pallas kernels: 125 us -> 140 us  [the longest x1 70.4 us: scatter_down(): pl.pallas_call(down_kernel, out_shape=(low, low, jax.ShapeDtypeStruct((ro...]
    pallas_call x1, Pallas kernels: 26.1 us -> 38.3 us  [mix_back(): pl.pallas_call(mix_back_kernel, out_shape=(jax.ShapeDtypeStruct((8 * rows...]
    reduce_sum x3 -> x0, other arithmetic: 12 us -> none  [the longest x1 6.37 us: local_plane(): error_local = jnp.sum(diff * diff)]
  transfers between devices with their start and end apart: 15 -> 14, of which waited for: 2 -> 6; matrix products, arithmetic and copies ran while one was open for 4% -> 2% of each run, Pallas kernels for 64% -> 38%
where the time goes in v3:
time: 790 us; the launch traced here: 783 us
  Pallas kernels  681 us (86%)
  waiting for transfers between devices  37.1 us (5%)
  starting transfers between devices  19.5 us (2%)
  local copies, waits for them, and re-layouts  17.7 us (2%)
  between operations  16.9 us (2%)
  other arithmetic  11.2 us (1%)
    pallas_call x1, Pallas kernels, scatter_normed(): pl.pallas_call(normed_back_kernel, out_shape=(jax.ShapeDtypeStruct((rows,...  117 us
    pallas_call x1, Pallas kernels, gather_qkv(): pl.pallas_call(qkv_kernel, out_shape=(jax.ShapeDtypeStruct((8, rows, widt...  102 us
    pallas_call x1, Pallas kernels, scatter_post(): pl.pallas_call(post_back_kernel, out_shape=(jax.ShapeDtypeStruct((rows, w...  71.3 us
    pallas_call x1, Pallas kernels, scatter_down(): pl.pallas_call(down_kernel, out_shape=(low, low, jax.ShapeDtypeStruct((ro...  70.4 us
    pallas_call x1, Pallas kernels, gather_down_back(): pl.pallas_call(down_back_kernel, out_shape=(jax.ShapeDtypeStruct((8 * row...  70 us
    pallas_call x1, Pallas kernels, gather_up(): pl.pallas_call(up_kernel, out_shape=(jax.ShapeDtypeStruct((8, rows, width...  62.8 us
    pallas_call x1, Pallas kernels, attend_back(): pl.pallas_call(attend_back_kernel, out_shape=(flat,) * 4, in_specs=[spec_...  59.9 us
    pallas_call x1, Pallas kernels, mix_back(): pl.pallas_call(mix_back_kernel, out_shape=(jax.ShapeDtypeStruct((8 * rows...  38.3 us
  transfers between devices with their start and end apart: 14, of which 6 were waited for; matrix products, arithmetic and copies ran while one was open for 2% of the time, Pallas kernels for 38%

profile of v3, /device:TPU:0, one launch (start us, length us, event | category | flops | bytes accessed | tf_op | source)
XLA Modules:
  0.0 783.5 jit_solution(12701345874962972805)
XLA Ops:
  7.2 1.1 copy.47
  8.4 1.0 copy.48
  9.4 1.0 copy.49
  10.5 1.0 copy.50
  11.5 1.2 copy.51
  12.6 5.2 all-to-all-start
  18.7 0.8 gather_fusion
  20.5 8.1 %all-to-all-done = bf16[4,256,384]{1,2,0:T(8,128)(2,1)S(1)} async-done(((bf16[4,256,384]{1,2,0:T(8,128)(2,1)}), bf16[4,256,384]{1,2,0:T(8,128)(2,1)S(1)}, u32[]{:S(2)}, u32[]{:S(2)}) %all-to-all-start) | async-done | bytes 786464 | tf_op jit(solution)/shard_map/all_to_all | solution.py:2477
  28.6 0.9 copy-done.5
  29.5 3.5 all-to-all-start.1
  33.1 1.4 copy.52
  34.6 1.2 copy.53
  35.8 0.7 multiply_sine_fusion
  36.5 0.9 fusion.3
  37.4 6.0 all-to-all-done.1
  43.4 3.5 all-to-all-start.2
  47.0 1.6 fusion.2.x_ref
  48.5 11.8 %all-gather.6.cloned.1.call-done.slab_ref = bf16[8,256,512]{2,1,0:T(8,128)(2,1)} async-done(((bf16[2,256,512]{2,1,0:T(8,128)(2,1)}), bf16[8,256,512]{2,1,0:T(8,128)(2,1)}) %all-gather.6.cloned.1.call-update) | async-done | bytes 2097168 | tf_op jit(solution)/shard_map/all_gather | solution.py:2474
  60.3 0.9 copy-done.7
  61.2 102.0 %gather_qkv.1 = (bf16[8,384,2048]{2,1,0:T(8,128)(2,1)}, bf16[2048,512]{1,0:T(8,128)(2,1)}, bf16[3072,256]{1,0:T(8,128)(2,1)}, bf16[3072,256]{1,0:T(8,128)(2,1)},...) custom-call(bf16[384,2048]{1,0:T(8,128)(2,1)} %fusion.2.x_ref, ...), custom_call_target="tpu_custom_call" | custom-call | bytes 240000000 | tf_op jit(solution)/shard_map/gather_qkv/pallas_call | solution.py:958
  163.2 1.2 copy.54
  164.5 0.7 all-gather.10.cloned.1.call-update
  165.2 0.8 collective-permute-start
  166.0 1.4 collective-permute-start.1
  167.5 1.3 collective-permute-start.2
  169.5 0.8 copy.57
  170.4 35.6 %attend.1 = (bf16[3072,256]{1,0:T(8,128)(2,1)}, f32[24,8,256]{2,1,0:T(8,128)}) custom-call(s32[3,16]{1,0:T(4,128)} %order_ref.3, s32[3]{0:T(128)} %lens_ref.3, bf16[3072,256]{1,0:T(8,128)(2,1)} %get-tuple-element.77.q_ref, bf16[3072,256]{1,0:T(8,128)(2,1)} %get-tuple-element.78.lo_ref, bf16[3072,256]{1,0:T(8,128)(2,1)} %get-tuple-element.79.own_ref, ...), custom_call_target="tpu_custom_call" | custom-call | bytes 150000000 | tf_op jit(solution)/shard_map/attend/pallas_call | solution.py:2294
  206.0 5.9 collective-permute-done.1.w2_ref
  211.9 1.6 collective-permute-done.2.w3_ref
  213.5 27.7 %mix.1 = (f32[384,2048]{1,0:T(8,128)}, bf16[384,2048]{1,0:T(8,128)(2,1)}, bf16[384,2048]{1,0:T(8,128)(2,1)}, bf16[2048,2048]{1,0:T(8,128)(2,1)}) custom-call(bf16[3072,256]{1,0:T(8,128)(2,1)} %get-tuple-element.81.mixed_ref.o_ref, bf16[384,2048]{1,0:T(8,128)(2,1)} %tokens_ref.3, f32[1,2048]{1,0:T(1,128)} %bitcast.62, bf16[2048,256]{1,0:T(8,128)(2,1)} %bitcast.53, ...), custom_call_target="tpu_custom_call" | custom-call | bytes 84000000 | tf_op jit(solution)/shard_map/mix/pallas_call | solution.py:1452
  241.3 62.8 %gather_up.1 = (bf16[8,384,2048]{2,1,0:T(8,128)(2,1)}, bf16[2,2048,768]{2,1,0:T(8,128)(2,1)}, bf16[3072,768]{1,0:T(8,128)(2,1)}, bf16[3072,768]{1,0:T(8,128)(2,1)}, bf16[3072,768]{1,0:T(8,128)(2,1)}) custom-call(bf16[384,2048]{1,0:T(8,128)(2,1)} %get-tuple-element.83.x_ref, bf16[4,4,256,384]{3,2,1,0:T(8,128)(2,1)} %get-tuple-element.84.gate_ref, ...), custom_call_target="tpu_custom_call" | custom-call | bytes 186000000 | tf_op jit(solution)/shard_map/gather_up/pallas_call | solution.py:1157
  304.2 70.4 %scatter_down.1 = (bf16[384,2048]{1,0:T(8,128)(2,1)}, bf16[384,2048]{1,0:T(8,128)(2,1)}, f32[384,2048]{1,0:T(8,128)}, f32[1,128]{1,0:T(1,128)}, bf16[768,2048]{1,0:T(8,128)(2,1)}) custom-call(bf16[3072,768]{1,0:T(8,128)(2,1)} %get-tuple-element.86.h_ref, bf16[4,4,384,256]{3,2,1,0:T(8,128)(2,1)} %bitcast.49, f32[384,2048]{1,0:T(8,128)} %get-tuple-element.88.middle_ref, ...), custom_call_target="tpu_custom_call" | custom-call | bytes 186000000 | tf_op jit(solution)/shard_map/scatter_down/pallas_call | solution.py:1230
  374.6 70.0 %gather_down_back.1 = (bf16[3072,1536]{1,0:T(8,128)(2,1)}, bf16[4,4,384,256]{3,2,1,0:T(8,128)(2,1)}) custom-call(bf16[384,2048]{1,0:T(8,128)(2,1)} %get-tuple-element.90.x_ref, bf16[768,2048]{1,0:T(8,128)(2,1)} %get-tuple-element.91.w_ref, bf16[3072,768]{1,0:T(8,128)(2,1)} %get-tuple-element.92.a_ref, bf16[3072,768]{1,0:T(8,128)(2,1)} %get-tuple-element.93.b_ref, ...), custom_call_target="tpu_custom_call" | custom-call | bytes 198000000 | tf_op jit(solution)/shard_map/gather_down_back/pallas_call | solution.py:1340
  444.7 71.3 %scatter_post.1 = (f32[384,2048]{1,0:T(8,128)}, bf16[4,4,256,768]{3,2,1,0:T(8,128)(2,1)}) custom-call(bf16[3072,1536]{1,0:T(8,128)(2,1)} %get-tuple-element.94.d_ref, bf16[2,2048,768]{2,1,0:T(8,128)(2,1)} %get-tuple-element.95.w_ref, bf16[8,384,2048]{2,1,0:T(8,128)(2,1)} %get-tuple-element.96.all_ref), custom_call_target="tpu_custom_call" | custom-call | bytes 198000000 | tf_op jit(solution)/shard_map/scatter_post/pallas_call | solution.py:1740
  516.1 38.3 %mix_back.1 = (bf16[3072,256]{1,0:T(8,128)(2,1)}, f32[384,2048]{1,0:T(8,128)}, f32[1,2048]{1,0:T(1,128)}, bf16[2048,256]{1,0:T(8,128)(2,1)}, bf16[2048,256]{1,0:...) custom-call(f32[384,2048]{1,0:T(8,128)} %get-tuple-element.97.post_ref, ...), custom_call_target="tpu_custom_call" | custom-call | bytes 78000000 | tf_op jit(solution)/shard_map/mix_back/pallas_call | solution.py:1596
  554.4 1.3 collective-permute-start.3
  555.7 0.9 collective-permute-start.4
  556.5 1.4 collective-permute-start.5
  559.3 59.9 %attend_back.1 = (bf16[3072,256]{1,0:T(8,128)(2,1)}, bf16[3072,256]{1,0:T(8,128)(2,1)}, bf16[3072,256]{1,0:T(8,128)(2,1)}, bf16[3072,256]{1,0:T(8,128)(2,1)}) custom-call(s32[3,16]{1,0:T(4,128)} %order_ref.3, s32[3]{0:T(128)} %lens_ref.3, bf16[3072,256]{1,0:T(8,128)(2,1)} %get-tuple-element.77.q_ref, bf16[3072,256]{1,0:T(8,128)(2,1)} %get-tuple-element.102.do_ref, ...), custom_call_target="tpu_custom_call" | custom-call | bytes 225000000 | tf_op jit(solution)/shard_map/attend_back/pallas_call | solution.py:2395
  619.2 3.3 add_convert_fusion
  622.5 2.9 reduce-scatter.5.cloned.1.call-done
  625.4 116.9 %scatter_normed.1 = (f32[384,2048]{1,0:T(8,128)}, f32[2,2,256,256]{3,2,1,0:T(8,128)}, f32[8,128]{1,0:T(8,128)}, bf16[4,256,768]{2,1,0:T(8,128)(2,1)}, bf16[4,512,256]{2,1,0:T(8,128)(2,1)}) custom-call(bf16[3072,256]{1,0:T(8,128)(2,1)} %get-tuple-element.104.dq_ref, bf16[3072,256]{1,0:T(8,128)(2,1)} %get-tuple-element.105.dkv_ref, ...), custom_call_target="tpu_custom_call" | custom-call | bytes 330000000 | tf_op jit(solution)/shard_map/scatter_normed/pallas_call | solution.py:1995
  743.0 10.1 %finish.1 = (bf16[384,2048]{1,0:T(8,128)(2,1)}, f32[1,2048]{1,0:T(1,128)}, f32[256,1536]{1,0:T(8,128)}, f32[256,1536]{1,0:T(8,128)}, f32[4,384,256]{2,1,0:T(8,12...) custom-call(f32[384,2048]{1,0:T(8,128)} %get-tuple-element.120.d_ref, ...), custom_call_target="tpu_custom_call" | custom-call | bytes 24000000 | tf_op jit(solution)/shard_map/finish/pallas_call | solution.py:2162
  753.1 1.3 pad_maximum_fusion.v_ref
  754.4 16.1 %total_of.1 = f32[40,128]{1,0:T(8,128)} custom-call(f32[40,128]{1,0:T(8,128)} %pad_maximum_fusion.v_ref), custom_call_target="tpu_custom_call" | custom-call | bytes 36000000 | tf_op jit(solution)/shard_map/total_of/pallas_call | solution.py:2087
  770.6 1.3 slice_bitcast_fusion
  771.9 1.9 slice_bitcast_fusion.2
  774.5 1.1 copy.61
  (69 shorter events, 4.5 us)
Async XLA Ops:
  7.2 4.3 copy-start.11
  7.2 53.1 %all-gather.6.cloned.1.call-start = ((), (), s32[]{:S(2)}) async-start(), calls=%async_computation.5 | async-start | bytes 2621440 | tf_op jit(solution)/shard_map/all_gather | solution.py:2474
  11.5 6.4 copy-start
  12.6 16.0 %all-to-all-start = ((bf16[4,256,384]{1,2,0:T(8,128)(2,1)}), bf16[4,256,384]{1,2,0:T(8,128)(2,1)S(1)}, u32[]{:S(2)}, u32[]{:S(2)}) async-start(bf16[4,256,384]{1,2,0:T(8,128)(2,1)} %bitcast.5), calls=%async_computation | async-start | bytes 1572864 | tf_op jit(solution)/shard_map/all_to_all | solution.py:2477
  18.7 1.4 copy-start.3
  28.6 0.9 copy-start.5
  29.5 13.9 %all-to-all-start.1 = ((bf16[4,384,256]{2,1,0:T(8,128)(2,1)}), bf16[4,384,256]{2,1,0:T(8,128)(2,1)S(1)}, u32[]{:S(2)}, u32[]{:S(2)}) async-start(bf16[4,384,256]{2,1,0:T(8,128)(2,1)} %bitcast.6), calls=%async_computation.1 | async-start | bytes 1572864 | tf_op jit(solution)/shard_map/all_to_all | solution.py:2477
  33.1 13.8 %copy-start.12 = (f32[2048]{0:T(1024)S(1)}, f32[2048]{0:T(1024)}, u32[]{:S(2)}) copy-start(f32[2048]{0:T(1024)} %param.19) | copy-start | bytes 24580
  43.4 5.2 copy-start.4
  43.4 16.9 %all-to-all-start.2 = ((bf16[4,256,384]{2,1,0:T(8,128)(2,1)}), bf16[4,256,384]{2,1,0:T(8,128)(2,1)S(1)}, u32[]{:S(2)}, u32[]{:S(2)}) async-start(bf16[4,256,384]{2,1,0:T(8,128)(2,1)} %bitcast.10), calls=%async_computation.2 | async-start | bytes 1572864 | tf_op jit(solution)/shard_map/all_to_all | solution.py:2477
  46.9 194.4 %all-gather.8.cloned.1.call-start = ((), (), s32[]{:S(2)}) async-start(), calls=%async_computation.8 | async-start | bytes 3932160 | tf_op jit(solution)/shard_map/all_gather | solution.py:2494
  60.3 0.9 copy-start.7
  61.2 102.1 %copy-start.6 = (bf16[4,256,384]{1,2,0:T(8,128)(2,1)S(1)}, bf16[4,256,384]{1,2,0:T(8,128)(2,1)}, u32[]{:S(2)}) copy-start(bf16[4,256,384]{1,2,0:T(8,128)(2,1)} %copy-done.5) | copy-start | bytes 2359300
  163.2 2.0 copy-start.10
  163.2 5.6 copy-start.1
  164.4 139.7 %all-gather.10.cloned.1.call-start = ((), (), s32[]{:S(2)}) async-start(), calls=%async_computation.9 | async-start | bytes 3932160 | tf_op jit(solution)/shard_map/all_gather | solution.py:2496
  165.2 350.9 %reduce-scatter.3.cloned.1.call-start = ((), (), s32[]{:S(2)}) async-start(), calls=%async_computation.6 | async-start | bytes 3932160 | tf_op jit(solution)/shard_map/reduce_scatter | solution.py:2504
  165.2 40.8 %collective-permute-start = (bf16[2048,256]{1,0:T(8,128)(2,1)S(1)}, bf16[2048,256]{1,0:T(8,128)(2,1)}, u32[]{:S(2)}, u32[]{:S(2)}) collective-permute-start(bf16[2048,256]{1,0:T(8,128)(2,1)S(1)} %bitcast.54), channel_id=1, source_target_pairs={{0,8},{4,12},{8,0},{12,4},{16,24},{20,28},{24,16},{28,20},{1,9},{5... | collective-permute-start | bytes 3145736 | tf_op jit(solution)/shard_map/ppermute | solution.py:2493
  166.0 45.9 %collective-permute-start.1 = (bf16[2048,256]{1,0:T(8,128)(2,1)S(1)}, bf16[2048,256]{1,0:T(8,128)(2,1)}, u32[]{:S(2)}, u32[]{:S(2)}) collective-permute-start(bf16[2048,256]{1,0:T(8,128)(2,1)S(1)} %bitcast.55), channel_id=1, source_target_pairs={{0,16},{4,20},{8,24},{12,28},{16,0},{20,4},{24,8},{28,12},{1,17},{... | collective-permute-start | bytes 3145736 | tf_op jit(solution)/shard_map/ppermute | solution.py:2493
  167.5 46.1 %collective-permute-start.2 = (bf16[2048,256]{1,0:T(8,128)(2,1)S(1)}, bf16[2048,256]{1,0:T(8,128)(2,1)}, u32[]{:S(2)}, u32[]{:S(2)}) collective-permute-start(bf16[2048,256]{1,0:T(8,128)(2,1)S(1)} %bitcast.56), channel_id=1, source_target_pairs={{0,24},{4,28},{8,16},{12,20},{16,8},{20,12},{24,0},{28,4},{1,25},{... | collective-permute-start | bytes 3145736 | tf_op jit(solution)/shard_map/ppermute | solution.py:2493
  444.6 180.8 %reduce-scatter.5.cloned.1.call-start = ((), (), s32[]{:S(2)}) async-start(), calls=%async_computation.7 | async-start | bytes 7864320 | tf_op jit(solution)/shard_map/reduce_scatter | solution.py:2504
  516.1 41.9 %copy-start.2 = (s32[3]{0:T(128)S(1)}, s32[3]{0:T(128)}, u32[]{:S(2)}) copy-start(s32[3]{0:T(128)} %lens_ref.3) | copy-start | bytes 40
  554.4 64.8 %collective-permute-start.3 = (bf16[2048,256]{1,0:T(8,128)(2,1)}, bf16[2048,256]{1,0:T(8,128)(2,1)}, u32[]{:S(2)}, u32[]{:S(2)}) collective-permute-start(bf16[2048,256]{1,0:T(8,128)(2,1)} %get-tuple-element.114), channel_id=1, source_target_pairs={{0,8},{4,12},{8,0},{12,4},{16,24},{20,28},{24,16},{28,20},{1,9},{5... | collective-permute-start | bytes 3145736 | tf_op jit(solution)/shard_map/ppermute | solution.py:2512
  555.7 63.5 %collective-permute-start.4 = (bf16[2048,256]{1,0:T(8,128)(2,1)}, bf16[2048,256]{1,0:T(8,128)(2,1)}, u32[]{:S(2)}, u32[]{:S(2)}) collective-permute-start(bf16[2048,256]{1,0:T(8,128)(2,1)} %get-tuple-element.116), channel_id=1, source_target_pairs={{0,16},{4,20},{8,24},{12,28},{16,0},{20,4},{24,8},{28,12},{1,17},{... | collective-permute-start | bytes 3145736 | tf_op jit(solution)/shard_map/ppermute | solution.py:2512
  556.5 62.6 %collective-permute-start.5 = (bf16[2048,256]{1,0:T(8,128)(2,1)}, bf16[2048,256]{1,0:T(8,128)(2,1)}, u32[]{:S(2)}, u32[]{:S(2)}) collective-permute-start(bf16[2048,256]{1,0:T(8,128)(2,1)} %get-tuple-element.118), channel_id=1, source_target_pairs={{0,24},{4,28},{8,16},{12,20},{16,8},{20,12},{24,0},{28,4},{1,25},{... | collective-permute-start | bytes 3145736 | tf_op jit(solution)/shard_map/ppermute | solution.py:2512
  559.2 60.0 %copy-start.9 = (bf16[2048,256]{1,0:T(8,128)(2,1)S(1)}, bf16[2048,256]{1,0:T(8,128)(2,1)}, u32[]{:S(2)}) copy-start(bf16[2048,256]{1,0:T(8,128)(2,1)} %get-tuple-element.113) | copy-start | bytes 3145732
  743.0 10.1 %copy-start.14 = (f32[1,128]{1,0:T(1,128)S(1)}, f32[1,128]{1,0:T(1,128)}, u32[]{:S(2)}) copy-start(f32[1,128]{1,0:T(1,128)} %get-tuple-element.129) | copy-start | bytes 1540
  743.0 10.1 %copy-start.13 = (f32[1,2048]{1,0:T(1,128)S(1)}, f32[1,2048]{1,0:T(1,128)}, u32[]{:S(2)}) copy-start(f32[1,2048]{1,0:T(1,128)} %get-tuple-element.127) | copy-start | bytes 24580
  743.0 31.5 %copy-start.8 = (bf16[384,2048]{1,0:T(8,128)(2,1)S(1)}, bf16[384,2048]{1,0:T(8,128)(2,1)}, u32[]{:S(2)}) copy-start(bf16[384,2048]{1,0:T(8,128)(2,1)} %get-tuple-element.165) | copy-start | bytes 4718596
Sparse Core Ops, SparseCore 0:
  11.6 48.6 all-gather.5
  164.5 62.2 all-gather.7
  229.0 62.1 all-gather.9
  444.8 59.1 reduce-scatter.2
  516.2 109.2 reduce-scatter.4

commit v4 on v3

--- a/solution.py
+++ b/solution.py
@@ -499,7 +499,19 @@
     def relay(self, kind, block, s, device):
         self.remote(self.part(block, s), kind, block, s, device).start()
 
-    def before(self, step):
+    def pass_on(self, i):
+        half = SUBS // 2
+        s, t = i, (i + half) % SUBS
+        self.arrived(self.nx, s)
+        if s < half:
+            self.relay(3, self.nx, s, self.ny)
+        self.relay(4, self.nx, s, self.sib)
+        self.arrived(self.ny, t)
+        if t >= half:
+            self.relay(3, self.ny, t, self.nx)
+        self.relay(5, self.ny, t, self.sib)
+
+    def before(self, step, passing=True):
         half = SUBS // 2
 
         @pl.when(step == 1)
@@ -507,18 +519,12 @@
             for s in range(SUBS):
                 self.arrived(self.sib, s)
 
-        @pl.when(step == 2)
-        def _():
-            for s in range(SUBS):
-                self.arrived(self.nx, s)
-                if s < half:
-                    self.relay(3, self.nx, s, self.ny)
-                self.relay(4, self.nx, s, self.sib)
-                t = (s + half) % SUBS
-                self.arrived(self.ny, t)
-                if t >= half:
-                    self.relay(3, self.ny, t, self.nx)
-                self.relay(5, self.ny, t, self.sib)
+        if passing:
+
+            @pl.when(step == 2)
+            def _():
+                for i in range(SUBS):
+                    self.pass_on(i)
 
         @pl.when(step == 3)
         def _():
@@ -574,94 +580,115 @@
         self.x_out, self.y_out, self.x_in, self.y_in = x_out, y_out, x_in, y_in
         self.sends, self.recvs = sends, recvs
         self.me, self.sib, self.nx, self.ny, self.dg = plane_neighbours()
-        half = diag_out.shape[0] // 2
-        self.first, self.second = first, second = pl.ds(0, half), pl.ds(half, half)
-        nx, ny = self.nx, self.ny
-        self.diag_x = self.remote(diag_out.at[first], diag_in.at[first], 4, nx)
-        self.diag_y = self.remote(diag_out.at[second], diag_in.at[second], 5, ny)
-        self.x_first = self.remote(x_out.at[first], x_in.at[first], 6, nx)
-        self.x_second = self.remote(x_out.at[second], x_in.at[second], 7, nx)
-        self.y_first = self.remote(y_out.at[first], y_in.at[first], 8, ny)
-        self.y_second = self.remote(y_out.at[second], y_in.at[second], 9, ny)
-
-    def remote(self, src, dst, n, device):
-        return send(src, dst, self.sends.at[n], self.recvs.at[n], on_ctx(device))
-
-    def sibling(self, n):
-        return self.remote(self.to_sib.at[n], self.from_sib.at[n], n, self.sib)
+        self.rows = diag_out.shape[0]
+
+    def round(self, i):
+        return pl.ds(i * (self.rows // 2), self.rows // 2)
+
+    def piece(self, i, half):
+        quarter = self.rows // 4
+        return pl.ds((2 * i + half) * quarter, quarter)
+
+    def remote(self, src, dst, kind, i, device):
+        return send(src, dst, self.sends.at[kind, i], self.recvs.at[kind, i], on_ctx(device))
+
+    def sibling(self, n, i):
+        at = self.round(i)
+        return self.remote(self.to_sib.at[n, at], self.from_sib.at[n, at], n, i, self.sib)
+
+    def hop(self, kind, i):
+        out, into, half, device = (
+            (self.diag_out, self.diag_in, 0, self.nx),
+            (self.diag_out, self.diag_in, 1, self.ny),
+            (self.x_out, self.x_in, 0, self.nx),
+            (self.x_out, self.x_in, 1, self.nx),
+            (self.y_out, self.y_in, 0, self.ny),
+            (self.y_out, self.y_in, 1, self.ny),
+        )[kind]
+        at = self.piece(i, half)
+        return self.remote(out.at[at], into.at[at], 4 + kind, i, device)
+
+    def blocks(self):
+        shift = self.sib - self.me
+        return [b + o for b in (self.dg, self.nx, self.ny, self.me) for o in (shift, 0)]
 
     def block(self, step):
-        shift = self.sib - self.me
-        return pick(step, [b + o for b in (self.dg, self.nx, self.ny, self.me) for o in (shift, 0)])
+        return pick(2 * (step // 4) + lax.rem(step, 2), self.blocks())
 
     def chip_sum(self, n, at):
         return self.own[n, at].astype(F32) + self.from_sib[n, at].astype(F32)
 
     def step(self, step, product, late=False):
         block = self.block(step)
-        n = step // 2
-        first, second = self.first, self.second
+        n = step // 4
+        i = lax.rem(step, 4) // 2
+        at = self.round(pl.multiple_of(i, 1))
 
         @pl.when(lax.rem(step, 2) == 0)
         def _():
-            product(block, self.to_sib, n)
-            self.sibling(n).start()
+            product(block, at, self.to_sib, n)
+            self.sibling(n, i).start()
 
         @pl.when(lax.rem(step, 2) == 1)
         def _():
-            product(block, self.own, n)
-            self.sibling(n).wait_recv()
-
-        @pl.when(step == 1)
-        def _():
-            self.diag_out[first] = self.chip_sum(0, first).astype(BF16)
-            self.diag_x.start()
-            self.diag_out[second] = self.chip_sum(0, second).astype(BF16)
-            self.diag_y.start()
-
-        @pl.when(step == 3)
-        def _():
-            self.x_out[first] = self.chip_sum(1, first).astype(BF16)
-            self.x_first.start()
-
-        @pl.when(step == 5)
-        def _():
-            self.y_out[second] = self.chip_sum(2, second).astype(BF16)
-            self.y_second.start()
-            if not late:
+            product(block, at, self.own, n)
+            self.sibling(n, i).wait_recv()
+
+        for r in range(2):
+            first, second = self.piece(r, 0), self.piece(r, 1)
+
+            @pl.when(step == 1 + 2 * r)
+            def _():
+                self.diag_out[first] = self.chip_sum(0, first).astype(BF16)
+                self.hop(0, r).start()
+                self.diag_out[second] = self.chip_sum(0, second).astype(BF16)
+                self.hop(1, r).start()
+
+            @pl.when(step == 5 + 2 * r)
+            def _():
+                self.x_out[first] = self.chip_sum(1, first).astype(BF16)
+                self.hop(2, r).start()
+
+            @pl.when(step == 9 + 2 * r)
+            def _():
+                self.y_out[second] = self.chip_sum(2, second).astype(BF16)
+                self.hop(5, r).start()
+
+        if not late:
+
+            @pl.when(step == 11)
+            def _():
                 self.second_wave()
 
     def second_wave(self):
-        first, second = self.first, self.second
-        self.diag_x.wait_recv()
-        self.y_out[first] = (self.chip_sum(2, first) + self.diag_in[first].astype(F32)).astype(BF16)
-        self.y_first.start()
-        self.diag_y.wait_recv()
-        self.x_out[second] = (self.chip_sum(1, second) + self.diag_in[second].astype(F32)).astype(BF16)
-        self.x_second.start()
+        for i in range(2):
+            first, second = self.piece(i, 0), self.piece(i, 1)
+            self.hop(0, i).wait_recv()
+            self.y_out[first] = (self.chip_sum(2, first) + self.diag_in[first].astype(F32)).astype(BF16)
+            self.hop(4, i).start()
+            self.hop(1, i).wait_recv()
+            self.x_out[second] = (self.chip_sum(1, second) + self.diag_in[second].astype(F32)).astype(BF16)
+            self.hop(3, i).start()
 
     def finish(self, o_ref):
-        self.x_first.wait_recv()
-        self.y_first.wait_recv()
-        first, second = self.first, self.second
-        o_ref[first] = (
-            self.chip_sum(3, first) + self.x_in[first].astype(F32) + self.y_in[first].astype(F32)
-        ).astype(o_ref.dtype)
-        self.x_second.wait_recv()
-        self.y_second.wait_recv()
-        o_ref[second] = (
-            self.chip_sum(3, second) + self.x_in[second].astype(F32) + self.y_in[second].astype(F32)
-        ).astype(o_ref.dtype)
-        for n in range(4):
-            self.sibling(n).wait_send()
-        for copy in (self.diag_x, self.diag_y, self.x_first, self.x_second, self.y_first, self.y_second):
-            copy.wait_send()
+        for i in range(2):
+            for kind in range(2, 6):
+                self.hop(kind, i).wait_recv()
+            at = self.round(i)
+            o_ref[at] = (
+                self.chip_sum(3, at) + self.x_in[at].astype(F32) + self.y_in[at].astype(F32)
+            ).astype(o_ref.dtype)
+        for i in range(2):
+            for n in range(4):
+                self.sibling(n, i).wait_send()
+            for kind in range(6):
+                self.hop(kind, i).wait_send()
 
 
 def scatter_scratch(rows, width):
     four = pltpu.VMEM((4, rows, width), BF16)
     one = pltpu.VMEM((rows, width), BF16)
-    return [four] * 3 + [one] * 6 + [pltpu.SemaphoreType.DMA((10,)), pltpu.SemaphoreType.DMA((10,))]
+    return [four] * 3 + [one] * 6 + [pltpu.SemaphoreType.DMA((10, 2)), pltpu.SemaphoreType.DMA((10, 2))]
 
 
 N_SCATTER = 11
@@ -748,6 +775,47 @@
                 self.down(block, i).wait_recv()
 
 
+class ChipSwap:
+    def __init__(self, src, dst, local_sem, send_sems, recv_sems):
+        self.src, self.dst = src, dst
+        self.local_sem, self.send_sems, self.recv_sems = local_sem, send_sems, recv_sems
+        me, _, nx, ny, dg = plane_neighbours()
+        self.chip, self.away = me // 2, (dg, nx, ny)
+
+    def own(self):
+        return pltpu.make_async_copy(self.src.at[self.chip], self.dst.at[self.chip], self.local_sem)
+
+    def to(self, n):
+        there = self.away[n]
+        return send(
+            self.src.at[there // 2], self.dst.at[self.chip], self.send_sems.at[n], self.recv_sems.at[self.chip], on_ctx(there)
+        )
+
+    def start(self):
+        self.own().start()
+        for n in range(3):
+            self.to(n).start()
+
+    def arrive(self):
+        self.own().wait()
+        for n in range(3):
+            there = self.away[n] // 2
+            send(
+                self.src.at[there], self.dst.at[there], self.send_sems.at[n], self.recv_sems.at[there], on_ctx(self.away[n])
+            ).wait_recv()
+
+    def sent(self):
+        for n in range(3):
+            self.to(n).wait_send()
+
+    def finish(self):
+        self.arrive()
+        self.sent()
+
+
+SWAP_SCRATCH = [pltpu.SemaphoreType.DMA, pltpu.SemaphoreType.DMA((3,)), pltpu.SemaphoreType.DMA((4,))]
+
+
 class LineGather:
     def __init__(self, src, dst, local_sem, send_sems, recv_sems):
         self.src, self.dst = src, dst
@@ -768,47 +836,108 @@
             on_plane(self.plane + 1 - 2 * way),
         )
 
-    def each(self, hop, visit):
-        for way in range(2):
-            origin = self.plane - hop if way == 0 else self.plane + hop
-            inside = origin >= 0 if way == 0 else origin < self.planes
-            going = self.plane < self.planes - 1 if way == 0 else self.plane > 0
-
-            @pl.when(inside & going)
+    def ways(self, hop):
+        up, down = self.plane - hop, self.plane + hop
+        yield 0, up, up >= 0, self.plane < self.planes - 1
+        yield 1, down, down < self.planes, self.plane > 0
+
+    def start(self):
+        self.own().start()
+        for way, origin, _, goes_on in self.ways(0):
+
+            @pl.when(goes_on)
             def _():
                 for n in range(self.pieces):
-                    visit(self.copy(way, hop, n, origin))
-
-    def hop(self, hop):
-        if hop == 0:
-            self.own().start()
-
-        def go(copy):
-            if hop > 0:
-                copy.wait_recv()
-            copy.start()
-
-        self.each(hop, go)
+                    self.copy(way, 0, n, origin).start()
+
+    def arrive(self, hop, then=None):
+        for way, origin, there, goes_on in self.ways(hop):
+
+            @pl.when(there)
+            def _():
+                for n in range(self.pieces):
+                    self.copy(way, 0, n, origin).wait_recv()
+                    if hop == self.planes - 1:
+                        continue
+
+                    @pl.when(goes_on)
+                    def _():
+                        self.copy(way, hop, n, origin).start()
+
+                if then is not None:
+                    then(origin)
 
     def finish(self):
         self.own().wait()
-        for way in range(2):
-            last = self.plane == self.planes - 1 if way == 0 else self.plane == 0
-
-            @pl.when(last)
-            def _():
-                for hop in range(1, 4):
-                    origin = self.plane - hop if way == 0 else self.plane + hop
+        self.sent()
+
+    def sent(self):
+        for hop in range(self.planes - 1):
+            for way, origin, there, goes_on in self.ways(hop):
+
+                @pl.when(there & goes_on)
+                def _():
                     for n in range(self.pieces):
-                        self.copy(way, 0, n, origin).wait_recv()
-
-        for hop in range(3):
-            self.each(hop, lambda copy: copy.wait_send())
+                        self.copy(way, hop, n, origin).wait_send()
 
 
 def line_scratch(pieces):
     dma = pltpu.SemaphoreType.DMA
     return [dma, dma((2, 3, pieces)), dma((4, pieces))]
+
+
+class LineSum:
+    def __init__(self, own, up_in, down_in, send_sems, recv_sems):
+        self.own, self.into = own, (up_in, down_in)
+        self.send_sems, self.recv_sems = send_sems, recv_sems
+        self.plane, self.planes = lax.axis_index("tp"), lax.axis_size("tp")
+
+    def copy(self, way, p, first):
+        into = self.into[way]
+        return send(
+            self.own(p) if first else into.at[p],
+            into.at[p],
+            self.send_sems.at[way, p],
+            self.recv_sems.at[way, p],
+            on_plane(self.plane + 1 - 2 * way),
+        )
+
+    def moves(self, k):
+        last = self.planes - 1
+        for way in range(2):
+            z = last - k if way else k
+            yield way, z, (range(z) if way else range(last, z, -1))
+
+    def stage(self, k):
+        for way, z, ends in self.moves(k):
+
+            @pl.when(self.plane == z)
+            def _():
+                for p in ends:
+                    copy = self.copy(way, p, k == 0)
+                    if k > 0:
+                        copy.wait_recv()
+                        into = self.into[way]
+                        into[p] = (self.own(p)[...].astype(F32) + into[p].astype(F32)).astype(BF16)
+                    copy.start()
+
+    def collect(self, out):
+        out[...] = self.own(self.plane)[...].astype(F32)
+        for way in range(2):
+
+            @pl.when(self.plane < self.planes - 1 if way else self.plane > 0)
+            def _():
+                self.copy(way, self.plane, False).wait_recv()
+                out[...] += self.into[way][self.plane].astype(F32)
+
+    def finish(self):
+        for k in range(self.planes - 1):
+            for way, z, ends in self.moves(k):
+
+                @pl.when(self.plane == z)
+                def _():
+                    for p in ends:
+                        self.copy(way, p, k == 0).wait_send()
 
 
 class Turn:
@@ -835,7 +964,7 @@
 
 def qkv_kernel(
     x_ref,
-    slab_ref,
+    home_ref,
     qg_ref,
     kg_ref,
     ca_ref,
@@ -843,6 +972,8 @@
     cb_ref,
     sb_ref,
     gate_ref,
+    up_ref,
+    down_ref,
     out_ref,
     all_ref,
     w_out_ref,
@@ -852,6 +983,8 @@
     hi_ref,
     lin_ref,
     gates_ref,
+    ups_ref,
+    downs_ref,
     outs_ref,
     xs,
     local_sem,
@@ -862,58 +995,87 @@
     w_local,
     w_sends,
     w_recvs,
+    slab,
+    gate_part,
     kv_sends,
     kv_recvs,
-    *line_sems,
+    *sems,
 ):
     ring = Gather(x_ref, xs, local_sem, send_sems, recv_sems)
     me = ring.me
     rows = x_ref.shape[0]
-    deep = slab_ref.shape[1]
-    away = others(me)
-    greet_column(away)
-
-    def weight(device, n):
-        return send(slab_ref.at[device], w.at[pl.ds(me * deep, deep)], w_sends.at[n], w_recvs.at[me], on_ctx(device))
-
-    def weight_from(device):
-        return send(slab_ref.at[device], w.at[pl.ds(device * deep, deep)], w_sends.at[0], w_recvs.at[device], on_ctx(device))
-
-    gathers = (
-        LineGather(out_ref, outs_ref, *line_sems[:3]),
-        LineGather(gate_ref, gates_ref, *line_sems[3:]),
-    )
-    for n, device in enumerate(away):
-        weight(device, n).start()
-    for gather in gathers:
-        gather.hop(0)
-    own_weight = pltpu.make_async_copy(slab_ref.at[me], w.at[pl.ds(me * deep, deep)], w_local)
-    own_weight.start()
+    deep = home_ref.shape[1]
+    slabs = LineGather(home_ref, slab, *sems[0:3])
+    outs = LineGather(out_ref, outs_ref, *sems[3:6])
+    gates = LineGather(gate_part, gates_ref, *sems[6:9])
+    gate_swap = ChipSwap(gate_ref, gate_part, *sems[9:12])
+    late_swaps = (ChipSwap(up_ref, ups_ref, *sems[12:15]), ChipSwap(down_ref, downs_ref, *sems[15:18]))
+    line = Line(kv_ref, kv_ref, lo_ref, hi_ref, kv_sends, kv_recvs, rows, False)
+
+    def weight(source, origin, k):
+        return send(
+            slab.at[origin, k],
+            w.at[pl.ds(source * deep, deep)],
+            w_sends.at[2 * origin + k],
+            w_recvs.at[source],
+            on_ctx(2 * origin + k),
+        )
+
+    own_weight = pltpu.make_async_copy(
+        slab.at[me // 2, lax.rem(me, 2)], w.at[pl.ds(me * deep, deep)], w_local
+    )
+
+    def hand_out(origin):
+        for k in range(2):
+
+            @pl.when(2 * origin + k == me)
+            def _():
+                own_weight.start()
+
+            @pl.when(2 * origin + k != me)
+            def _():
+                weight(me, origin, k).start()
+
+    greet_column(others(me))
+    gate_swap.start()
+    slabs.start()
     ring.start()
+    outs.start()
+    slabs.own().wait()
+    hand_out(slabs.plane)
+    slabs.arrive(1, hand_out)
+    gate_swap.arrive()
+    gates.start()
+    ring.pass_on(0)
+    ring.pass_on(1)
+    slabs.arrive(2, hand_out)
+    ring.pass_on(2)
+    ring.pass_on(3)
+    slabs.arrive(3, hand_out)
+    for swap in late_swaps:
+        swap.start()
+    outs.arrive(1)
+    gates.arrive(1)
     own_weight.wait()
-    for device in away:
-        weight_from(device).wait_recv()
+    for device in others(me):
+        weight(device, 0, 0).wait_recv()
     keep_w = pltpu.make_async_copy(w, w_out_ref, w_local)
     keep_w.start()
 
     def keep(block):
         return pltpu.make_async_copy(xs.at[block], all_ref.at[block], keep_sems.at[block])
-
-    line = Line(kv_ref, kv_ref, lo_ref, hi_ref, kv_sends, kv_recvs, rows, False)
 
     def head(v, gain_ref, turn):
         scale = lax.rsqrt(jnp.mean(v * v, axis=-1, keepdims=True) + EPS)
         return turn.forth(v * scale * gain_ref[...])
 
     def turn(step, carry):
-        for hop in (1, 2):
-
-            @pl.when(step == 2 * hop)
-            def _():
-                for gather in gathers:
-                    gather.hop(hop)
-
-        ring.before(step)
+        @pl.when(step == 4)
+        def _():
+            outs.arrive(2)
+            gates.arrive(2)
+
+        ring.before(step, passing=False)
         block = ring.block(step)
         keep(block).start()
         lin = nn(xs[block], w[...])
@@ -930,14 +1092,20 @@
             key = head(part[:, 2 * HEAD_SIZE : 3 * HEAD_SIZE], kg_ref, rotation)
             kv_ref[here, :HEAD_SIZE] = key.astype(BF16)
             kv_ref[here, HEAD_SIZE:] = part[:, 3 * HEAD_SIZE :].astype(BF16)
+
         line.start(block)
         return carry
 
     lax.fori_loop(0, 8, turn, 0)
     ring.finish()
     keep_w.wait()
-    for n, device in enumerate(away):
-        weight(device, n).wait_send()
+    for origin in range(4):
+        for k in range(2):
+
+            @pl.when(2 * origin + k != me)
+            def _():
+                weight(me, origin, k).wait_send()
+
     for block in range(8):
         keep(block).wait()
 
@@ -947,14 +1115,20 @@
         return carry
 
     lax.fori_loop(0, 8, settle, 0)
-    for gather in gathers:
-        gather.finish()
-
-
-def gather_qkv(normed, slab, q_gain, k_gain, tables, gate, out):
+    for gather in (outs, gates):
+        gather.arrive(3)
+    for gather in (slabs, outs, gates):
+        gather.finish() if gather is not slabs else gather.sent()
+    gate_swap.sent()
+    for swap in late_swaps:
+        swap.finish()
+
+
+def gather_qkv(normed, home, q_gain, k_gain, tables, gate, up, down, out):
     rows, width = normed.shape
-    _, deep, cols = slab.shape
+    _, deep, cols = home.shape
     flat = jax.ShapeDtypeStruct((8 * rows, 2 * HEAD_SIZE), BF16)
+    dma = pltpu.SemaphoreType.DMA
     return pl.pallas_call(
         qkv_kernel,
         out_shape=(
@@ -966,27 +1140,33 @@
             flat,
             jax.ShapeDtypeStruct((8 * rows, 3 * HEAD_SIZE), F32),
             jax.ShapeDtypeStruct((4,) + gate.shape, BF16),
+            jax.ShapeDtypeStruct(up.shape, BF16),
+            jax.ShapeDtypeStruct(down.shape, BF16),
             jax.ShapeDtypeStruct((4,) + out.shape, BF16),
         ),
-        in_specs=[spec_vmem(), spec_any()] + [spec_vmem()] * 6 + [spec_any()] * 2,
+        in_specs=[spec_any()] * 2 + [spec_vmem()] * 6 + [spec_any()] * 4,
         out_specs=(spec_any(), spec_any(), spec_vmem(), spec_vmem(), spec_any(), spec_any(), spec_vmem())
-        + (spec_any(),) * 2,
+        + (spec_any(),) * 4,
         scratch_shapes=gather_scratch(rows, width)
         + [
-            pltpu.SemaphoreType.DMA((8,)),
+            dma((8,)),
             pltpu.VMEM((8 * deep, cols), BF16),
-            pltpu.SemaphoreType.DMA,
-            pltpu.SemaphoreType.DMA((7,)),
-            pltpu.SemaphoreType.DMA((8,)),
-            pltpu.SemaphoreType.DMA((2, 8 * rows // UNIT)),
-            pltpu.SemaphoreType.DMA((2, 8 * rows // UNIT)),
+            dma,
+            dma((8,)),
+            dma((8,)),
+            pltpu.VMEM((4,) + home.shape, BF16),
+            pltpu.VMEM(gate.shape, BF16),
+            dma((2, 8 * rows // UNIT)),
+            dma((2, 8 * rows // UNIT)),
         ]
+        + line_scratch(home.shape[0])
         + line_scratch(out.shape[0])
-        + line_scratch(gate.shape[0]),
+        + line_scratch(gate.shape[0])
+        + SWAP_SCRATCH * 3,
         compiler_params=comm_params(1),
-        cost_estimate=busy(80),
+        cost_estimate=busy(100),
         name="gather_qkv",
-    )(normed, slab, q_gain.reshape(1, -1), k_gain.reshape(1, -1), *tables, gate, out)
+    )(normed, home, q_gain.reshape(1, -1), k_gain.reshape(1, -1), *tables, gate, up, down, out)
 
 
 class Halves:
@@ -1163,7 +1343,7 @@
             flat,
             flat,
         ),
-        in_specs=[spec_vmem(), spec_any(), spec_any()],
+        in_specs=[spec_any()] * 3,
         out_specs=(spec_any(),) * 5,
         scratch_shapes=gather_scratch(rows, width)
         + [
@@ -1180,12 +1360,11 @@
     )(post, gate_parts, up_parts)
 
 
-def down_kernel(h_ref, parts_ref, middle_ref, teacher_ref, valid_ref, o_ref, low_ref, diff_ref, error_ref, w_out_ref, *scratch):
+def down_kernel(h_any, parts_ref, middle_any, teacher_any, valid_ref, o_ref, low_ref, diff_ref, error_ref, w_out_ref, *scratch):
     rs = Scatter(*scratch[:N_SCATTER])
-    w, w_sem, w_local, w_sends, w_recvs = scratch[N_SCATTER:]
+    (w, w_sem, h_ref, h_sems, middle_ref, teacher_ref, row_sems, w_local, w_sends, w_recvs) = scratch[N_SCATTER:]
     rows = o_ref.shape[0]
     _, _, cols, deep = parts_ref.shape
-    greet((rs.sib, rs.nx, rs.ny))
     weight = Halves(
         parts_ref,
         lambda z, c: w.at[pl.ds(z * cols, cols), pl.ds(pl.multiple_of(c * deep, deep), deep)],
@@ -1193,21 +1372,40 @@
         w_sends,
         w_recvs,
     )
+    def fetch(block):
+        here = pl.ds(pl.multiple_of(block * rows, rows), rows)
+        return pltpu.make_async_copy(h_any.at[here], h_ref.at[here], h_sems.at[block])
+
+    for block in rs.blocks():
+        fetch(block).start()
+    late = (
+        pltpu.make_async_copy(middle_any, middle_ref, row_sems.at[0]),
+        pltpu.make_async_copy(teacher_any, teacher_ref, row_sems.at[1]),
+    )
+    greet((rs.sib, rs.nx, rs.ny))
     weight.start()
+    for copy in late:
+        copy.start()
     weight.ready()
     keep_w = pltpu.make_async_copy(w, w_out_ref, w_sem)
     keep_w.start()
 
-    def product(block, out, n):
-        left = h_ref[pl.ds(pl.multiple_of(block * rows, rows), rows), :]
+    def product(block, at, out, n):
+        left = h_ref[pl.ds(pl.multiple_of(block * rows + at.start, rows // 2), rows // 2), :]
         for c in range(0, w.shape[1], 512):
-            out[n, :, c : c + 512] = nn(left, w[:, c : c + 512]).astype(BF16)
+            out[n, at, c : c + 512] = nn(left, w[:, c : c + 512]).astype(BF16)
 
     def turn(step, carry):
+        @pl.when(lax.rem(step, 4) < 2)
+        def _():
+            fetch(rs.block(step)).wait()
+
         rs.step(step, product)
         return carry
 
-    lax.fori_loop(0, 8, turn, 0)
+    lax.fori_loop(0, 16, turn, 0)
+    for copy in late:
+        copy.wait()
     rs.finish(diff_ref)
     error = jnp.zeros((rows, HEAD_SIZE), F32)
     for n in range(0, diff_ref.shape[1], HEAD_SIZE):
@@ -1236,10 +1434,18 @@
             jax.ShapeDtypeStruct((1, HEAD_SIZE), F32),
             jax.ShapeDtypeStruct((ff, width), BF16),
         ),
-        in_specs=[spec_vmem(), spec_any()] + [spec_vmem()] * 3,
+        in_specs=[spec_any()] * 4 + [spec_vmem()],
         out_specs=(spec_vmem(),) * 4 + (spec_any(),),
         scratch_shapes=scatter_scratch(rows, width)
-        + [pltpu.VMEM((ff, width), BF16), pltpu.SemaphoreType.DMA]
+        + [
+            pltpu.VMEM((ff, width), BF16),
+            pltpu.SemaphoreType.DMA,
+            pltpu.VMEM(hidden.shape, BF16),
+            pltpu.SemaphoreType.DMA((8,)),
+            pltpu.VMEM((rows, width), F32),
+            pltpu.VMEM((rows, width), BF16),
+            pltpu.SemaphoreType.DMA((2,)),
+        ]
         + HALVES_SCRATCH,
         compiler_params=comm_params(6),
         cost_estimate=busy(62),
@@ -1263,19 +1469,24 @@
     stage_sems,
     total,
     low,
+    w,
+    w_sem,
+    factors,
+    factor_sems,
+    hidden,
+    hidden_sems,
     s_local,
     s_sends,
     s_recvs,
 ):
     ring = Gather(x_ref, xs, local_sem, send_sems, recv_sems)
-    rows = x_ref.shape[0]
+    rows, width = x_ref.shape
     ff = w_ref.shape[0]
     cols = ff // 2
-    width = x_ref.shape[1]
-    greet((ring.sib, ring.nx, ring.ny))
-    ring.start()
-    total[...] = jnp.zeros_like(total)
+    fetch_w = pltpu.make_async_copy(w_ref, w, w_sem)
+    fetch_w.start()
     shares = Shares(gw_ref, s_local, s_sends, s_recvs)
+    core = shares.core
     deep = width // 8
 
     def tile(z, c):
@@ -1286,45 +1497,78 @@
             stage.at[slot], d_ref.at[pl.ds(block * rows, rows)], stage_sems.at[slot]
         )
 
+    def factor(n, slot, block):
+        ref = (a_ref, b_ref)[n]
+        return pltpu.make_async_copy(
+            ref.at[pl.ds(block * rows, rows)], factors.at[slot, n], factor_sems.at[slot, n]
+        )
+
+    def chip_hidden(slot, block):
+        return pltpu.make_async_copy(
+            h_ref.at[pl.ds(block // 2 * 2 * rows, 2 * rows)], hidden.at[slot], hidden_sems.at[slot]
+        )
+
+    def fetch(step):
+        block = ring.block(step)
+        for n in range(2):
+            factor(n, lax.rem(step, 2), block).start()
+
+        @pl.when(lax.rem(step, 2) == 0)
+        def _():
+            chip_hidden(lax.rem(step // 2, 2), block).start()
+
+    fetch(jnp.int32(0))
+    greet((ring.sib, ring.nx, ring.ny))
+    ring.start()
+    total[...] = jnp.zeros_like(total)
+    fetch_w.wait()
+
     def turn(step, carry):
         ring.before(step)
         block = ring.block(step)
         slot = lax.rem(step, 2)
+        pair_slot = lax.rem(step // 2, 2)
 
         @pl.when(step >= 2)
         def _():
             put(slot, block).wait()
 
-        here = pl.ds(block * rows, rows)
+        for n in range(2):
+            factor(n, slot, block).wait()
+
+        @pl.when(step < 7)
+        def _():
+            fetch(step + 1)
+
         for z in range(2):
             part = slice(z * cols, (z + 1) * cols)
-            grad = nt(xs[block], w_ref[part, :])
-            stage[slot, :, 2 * z * cols : (2 * z + 1) * cols] = (
-                grad * a_ref[here, part].astype(F32)
-            ).astype(BF16)
-            stage[slot, :, (2 * z + 1) * cols : (2 * z + 2) * cols] = (
-                grad * b_ref[here, part].astype(F32)
-            ).astype(BF16)
+            grad = nt(xs[block], w[part, :])
+            for n in range(2):
+                stage[slot, :, (2 * z + n) * cols : (2 * z + n + 1) * cols] = (
+                    grad * factors[slot, n, :, part].astype(F32)
+                ).astype(BF16)
         put(slot, block).start()
 
         @pl.when(slot == 1)
         def _():
+            chip_hidden(pair_slot, block).wait()
             pair = block // 2
-            hidden = h_ref[pl.ds(pair * 2 * rows, 2 * rows), :]
-            for n in range(0, width, 512):
-                seen = xs[pl.ds(pair * 2, 2), :, n : n + 512].reshape(2 * rows, 512)
-                total[:, n : n + 512] += tn(hidden, seen)
+            for p in range(4):
+                at = slice(p * 2 * deep, (p + 1) * 2 * deep)
+                seen = xs[pl.ds(pair * 2, 2), :, at].reshape(2 * rows, 2 * deep)
+                total[:, at] += tn(hidden[pair_slot], seen)
+
+                @pl.when(step == 7)
+                def _():
+                    low[:, at] = total[:, at].astype(BF16)
+                    for z in range(2):
+                        shares.other(tile(z, 2 * p + 1 - core), z, p).start()
+                        shares.own(tile(z, 2 * p + core), z, p).start()
 
         return carry
 
     lax.fori_loop(0, 8, turn, 0)
     ring.finish()
-    low[...] = total[...].astype(BF16)
-    core = shares.core
-    for z in range(2):
-        for p in range(4):
-            shares.other(tile(z, 2 * p + 1 - core), z, p).start()
-            shares.own(tile(z, 2 * p + core), z, p).start()
     for slot in range(2):
         put(slot, 0).wait()
     shares.arrive()
@@ -1337,20 +1581,27 @@
 def gather_down_back(diff, w_down, a, b, hidden):
     rows, width = diff.shape
     ff = w_down.shape[0]
+    dma = pltpu.SemaphoreType.DMA
     return pl.pallas_call(
         down_back_kernel,
         out_shape=(
             jax.ShapeDtypeStruct((8 * rows, 2 * ff), BF16),
             jax.ShapeDtypeStruct((4, 4, ff // 2, width // 8), BF16),
         ),
-        in_specs=[spec_vmem()] * 5,
+        in_specs=[spec_any()] * 5,
         out_specs=(spec_any(), spec_any()),
         scratch_shapes=gather_scratch(rows, width)
         + [
             pltpu.VMEM((2, rows, 2 * ff), BF16),
-            pltpu.SemaphoreType.DMA((2,)),
+            dma((2,)),
             pltpu.VMEM((ff, width), F32),
             pltpu.VMEM((ff, width), BF16),
+            pltpu.VMEM((ff, width), BF16),
+            dma,
+            pltpu.VMEM((2, 2, rows, ff), BF16),
+            dma((2, 2)),
+            pltpu.VMEM((2, 2 * rows, ff), BF16),
+            dma((2,)),
         ]
         + SHARES_SCRATCH,
         compiler_params=comm_params(3),
@@ -1481,8 +1732,8 @@
     middle_ref,
     diff_ref,
     gain_ref,
-    w_ref,
-    rows_ref,
+    w_any,
+    rows_any,
     swap_ref,
     dm_ref,
     d_middle_ref,
@@ -1492,6 +1743,9 @@
     g2_ref,
     g3_ref,
     swapped_ref,
+    w_ref,
+    rows_ref,
+    fetch_sems,
     d_ref,
     stage,
     to_sib,
@@ -1510,6 +1764,10 @@
     away = others(me)
     rows, width = d_ref.shape
     deep = width // 8
+    fetch_w = pltpu.make_async_copy(w_any, w_ref, fetch_sems.at[0])
+    fetch_w.start()
+    fetch_rows = pltpu.make_async_copy(rows_any, rows_ref, fetch_sems.at[1])
+    fetch_rows.start()
     greet(away)
     weight_swap = ChipSwap(swap_ref, swapped_ref, *c_sems)
     weight_swap.start()
@@ -1530,6 +1788,8 @@
         d_ref[:, at] = d_middle.astype(BF16)
     outs = (g0_ref, g1_ref, g2_ref, g3_ref)
     chips = (me, nx, ny, dg)
+    fetch_w.wait()
+    fetch_rows.wait()
 
     def block(c):
         return pl.ds(pl.multiple_of(c * rows, rows), rows)
@@ -1602,9 +1862,12 @@
         )
         + (jax.ShapeDtypeStruct((width, deep), BF16),) * 4
         + (jax.ShapeDtypeStruct(swap.shape, BF16),),
-        in_specs=[spec_vmem()] * 6 + [spec_any()],
+        in_specs=[spec_vmem()] * 4 + [spec_any()] * 3,
         out_specs=(spec_any(), spec_vmem(), spec_vmem()) + (spec_any(),) * 5,
         scratch_shapes=[
+            pltpu.VMEM((width, width), BF16),
+            pltpu.VMEM((rows, width), BF16),
+            dma((2,)),
             pltpu.VMEM((rows, width), BF16),
             pltpu.VMEM((8, rows, deep), BF16),
             four,
@@ -1624,40 +1887,6 @@
     )(d_post, middle, diff, post_gain.reshape(1, -1), w, mixed_rows, swap)
 
 
-class ChipSwap:
-    def __init__(self, src, dst, local_sem, send_sems, recv_sems):
-        self.src, self.dst = src, dst
-        self.local_sem, self.send_sems, self.recv_sems = local_sem, send_sems, recv_sems
-        me, _, nx, ny, dg = plane_neighbours()
-        self.chip, self.away = me // 2, (dg, nx, ny)
-
-    def own(self):
-        return pltpu.make_async_copy(self.src.at[self.chip], self.dst.at[self.chip], self.local_sem)
-
-    def to(self, n):
-        there = self.away[n]
-        return send(
-            self.src.at[there // 2], self.dst.at[self.chip], self.send_sems.at[n], self.recv_sems.at[self.chip], on_ctx(there)
-        )
-
-    def start(self):
-        self.own().start()
-        for n in range(3):
-            self.to(n).start()
-
-    def finish(self):
-        self.own().wait()
-        for n in range(3):
-            there = self.away[n] // 2
-            send(
-                self.src.at[there], self.dst.at[there], self.send_sems.at[n], self.recv_sems.at[there], on_ctx(self.away[n])
-            ).wait_recv()
-            self.to(n).wait_send()
-
-
-SWAP_SCRATCH = [pltpu.SemaphoreType.DMA, pltpu.SemaphoreType.DMA((3,)), pltpu.SemaphoreType.DMA((4,))]
-
-
 def columns(all_ref, slices, sems, c, slot):
     deep = slices.shape[-1]
     return pltpu.make_async_copy(
@@ -1665,23 +1894,40 @@
     )
 
 
-def post_back_kernel(d_ref, w_ref, all_ref, o_ref, gw_ref, *scratch):
+EARLY = 1
+
+
+def post_back_kernel(d_any, w_any, all_ref, o_ref, gw_ref, *scratch):
     rs = Scatter(*scratch[:N_SCATTER])
-    slices, slice_sems, tile, s_local, s_sends, s_recvs = scratch[N_SCATTER:]
+    slices, slice_sems, tile, d_ref, d_sems, w_ref, w_sems, s_local, s_sends, s_recvs = scratch[N_SCATTER:]
     shares = Shares(gw_ref, s_local, s_sends, s_recvs)
     rows = o_ref.shape[0]
     _, width, wide = w_ref.shape
     plane_rows = d_ref.shape[0]
     deep = width // 8
+    fetch_w = [pltpu.make_async_copy(w_any.at[z], w_ref.at[z], w_sems.at[z]) for z in range(2)]
+
+    def fetch(block):
+        here = pl.ds(pl.multiple_of(block * rows, rows), rows)
+        return pltpu.make_async_copy(d_any.at[here], d_ref.at[here], d_sems.at[block])
+
+    order = rs.blocks()
+    fetch(order[0]).start()
+    for copy in fetch_w:
+        copy.start()
+    for block in order[1:]:
+        fetch(block).start()
+    columns(all_ref, slices, slice_sems, 0, 0).start()
     greet((rs.sib, rs.nx, rs.ny))
-    columns(all_ref, slices, slice_sems, 0, 0).start()
-
-    def product(block, out, n):
-        here = pl.ds(pl.multiple_of(block * rows, rows), rows)
+    for copy in fetch_w:
+        copy.wait()
+
+    def product(block, at, out, n):
+        here = pl.ds(pl.multiple_of(block * rows + at.start, rows // 2), rows // 2)
         for c in range(0, width, 512):
             total = nt(d_ref[here, :wide], w_ref[0, c : c + 512, :])
             total += nt(d_ref[here, wide:], w_ref[1, c : c + 512, :])
-            out[n, :, c : c + 512] = total.astype(BF16)
+            out[n, at, c : c + 512] = total.astype(BF16)
 
     def put(slot, p, act):
         @pl.when(slot == shares.core)
@@ -1714,19 +1960,30 @@
         put(slot, c // 2, "start")
 
     def turn(t, carry):
-        is_grad = ((t >= 5) & (t < 8)) | (t >= 11)
+        is_grad = ((t >= 10) & (t < 10 + EARLY)) | (t >= 16 + EARLY)
+
+        for n in range(2):
+
+            @pl.when(t == n)
+            def _():
+                fetch(order[n]).wait()
+
+        @pl.when(t == 4)
+        def _():
+            for block in order[2:]:
+                fetch(block).wait()
 
         @pl.when(is_grad)
         def _():
-            grad(jnp.where(t < 8, t - 5, t - 8))
+            grad(jnp.where(t < 10 + EARLY, t - 10, t - 16))
 
         @pl.when(jnp.logical_not(is_grad))
         def _():
-            rs.step(jnp.where(t < 5, t, t - 3), product)
+            rs.step(jnp.where(t < 10, t, t - EARLY), product)
 
         return carry
 
-    lax.fori_loop(0, 16, turn, 0)
+    lax.fori_loop(0, 24, turn, 0)
     rs.finish(o_ref)
     for slot in range(2):
         put(slot, 3, "wait")
@@ -1743,13 +2000,17 @@
             jax.ShapeDtypeStruct((rows, width), F32),
             jax.ShapeDtypeStruct((4, 4, deep, wide), BF16),
         ),
-        in_specs=[spec_vmem(), spec_vmem(), spec_any()],
+        in_specs=[spec_any()] * 3,
         out_specs=(spec_vmem(), spec_any()),
         scratch_shapes=scatter_scratch(rows, width)
         + [
             pltpu.VMEM((2, 8, rows, deep), BF16),
             pltpu.SemaphoreType.DMA((2,)),
             pltpu.VMEM((2, 2, deep, wide), BF16),
+            pltpu.VMEM(d_gu.shape, BF16),
+            pltpu.SemaphoreType.DMA((8,)),
+            pltpu.VMEM(w_gu.shape, BF16),
+            pltpu.SemaphoreType.DMA((2,)),
         ]
         + SHARES_SCRATCH,
         compiler_params=comm_params(7),
@@ -1778,7 +2039,7 @@
     gw_ref,
     gains_ref,
     swapped_ref,
-    wo_planes_ref,
+    wo_sum_ref,
     *scratch,
 ):
     rs = Scatter(*scratch[:N_SCATTER])
@@ -1790,14 +2051,16 @@
         slice_sems,
         tiles,
         tiles_in,
-        planes_in,
+        up_in,
+        down_in,
+        wo_up,
+        wo_down,
         z_sends,
         z_recvs,
         t_sends,
         t_recvs,
         p_sends,
         p_recvs,
-        o_local,
         o_sends,
         o_recvs,
         *c_sems,
@@ -1810,20 +2073,12 @@
     units = rows // UNIT
     wide = 2 * HEAD_SIZE
     away = others(me)
-    order = [b + o for b in (rs.dg, rs.nx, rs.ny, me) for o in (rs.sib - me, 0)]
-    far = [lax.rem(plane + step, planes) for step in range(1, planes)]
+    order = rs.blocks()
 
     from_lo[...] = jnp.zeros_like(from_lo)
     from_hi[...] = jnp.zeros_like(from_hi)
     line = Line(to_hi_ref, to_lo_ref, from_lo, from_hi, z_sends, z_recvs, rows, True)
-    barrier = pltpu.get_barrier_semaphore()
-    for where in [on_ctx(c) for c in away] + [on_plane(p) for p in far]:
-        pl.semaphore_signal(barrier, inc=1, device_id=where, device_id_type=MESH)
-    pl.semaphore_wait(barrier, len(away) + len(far))
-
-    def at_block(block):
-        return pl.ds(pl.multiple_of(block * rows, rows), rows)
-
+    greet_column(away)
     for block in order:
         line.start(block)
     columns(all_ref, slices, slice_sems, order[0], 0).start()
@@ -1906,77 +2161,75 @@
 
         lax.fori_loop(0, 8, grad, 0)
 
-    def pair(part, p):
-        return tiles_in.at[part, pl.ds(2 * p, 2)]
-
-    def to_plane(part, n):
-        return send(
-            pair(part, far[n]),
-            planes_in.at[part, plane],
-            p_sends.at[part, n],
-            p_recvs.at[part, plane],
-            on_plane(far[n]),
+    sums = [
+        LineSum(
+            lambda p, part=part: tiles_in.at[part, pl.ds(2 * p, 2)],
+            up_in.at[part],
+            down_in.at[part],
+            p_sends.at[part],
+            p_recvs.at[part],
         )
-
-    def from_plane(part, p):
-        return send(pair(part, p), planes_in.at[part, p], p_sends.at[part, 0], p_recvs.at[part, p], on_plane(p))
-
-    def spread(part):
+        for part in range(2)
+    ]
+    out_sum = LineSum(lambda p: wo_ref.at[p], wo_up, wo_down, o_sends, o_recvs)
+
+    def tiles_there(part):
         for device in away:
             tile_from(part, device).wait_recv()
-        for n in range(len(far)):
-            to_plane(part, n).start()
-
-    def collect(part):
-        total = tiles_in[part, pl.ds(2 * plane, 2)].astype(F32)
-        for p in far:
-            from_plane(part, p).wait_recv()
-            total += planes_in[part, p].astype(F32)
-        gw_ref[part] = total
-
-    def product(block, out, n):
-        left = d_lin[at_block(block), :]
+
+    def product(block, at, out, n):
+        left = d_lin[pl.ds(pl.multiple_of(block * rows + at.start, rows // 2), rows // 2), :]
         for c in range(0, width, 512):
-            out[n, :, c : c + 512] = nt(left, w_ref[c : c + 512, :]).astype(BF16)
+            out[n, at, c : c + 512] = nt(left, w_ref[c : c + 512, :]).astype(BF16)
 
     def turn(step, carry):
-        prepare_keys(rs.block(step))
+        @pl.when(lax.rem(step, 4) < 2)
+        def _():
+            prepare_keys(rs.block(step))
+
         rs.step(step, product, late=True)
+
+        @pl.when(step == 4)
+        def _():
+            out_sum.stage(1)
+
+        @pl.when(step == 7)
+        def _():
+            tiles_there(0)
+            sums[0].stage(0)
+
+        @pl.when(step == 9)
+        def _():
+            out_sum.stage(2)
+
+        @pl.when(step == 12)
+        def _():
+            sums[0].stage(1)
+
         return carry
 
-    def out_to(n):
-        return send(
-            wo_ref.at[far[n]], wo_planes_ref.at[plane], o_sends.at[n], o_recvs.at[plane], on_plane(far[n])
-        )
-
-    out_own = pltpu.make_async_copy(wo_ref.at[plane], wo_planes_ref.at[plane], o_local)
+    swap = ChipSwap(swap_ref, swapped_ref, *c_sems)
+    swap.start()
+    out_sum.stage(0)
     lax.fori_loop(0, plane_rows // UNIT, prepare_queries, 0)
     grads(0)
-    lax.fori_loop(0, 8, turn, 0)
-    out_own.start()
-    for n in range(len(far)):
-        out_to(n).start()
+    lax.fori_loop(0, 16, turn, 0)
     grads(1)
     rs.second_wave()
-    swap = ChipSwap(swap_ref, swapped_ref, *c_sems)
-    swap.start()
-    spread(0)
+    sums[0].stage(2)
+    tiles_there(1)
+    for k in range(3):
+        sums[1].stage(k)
     rs.finish(o_ref)
-    spread(1)
-    collect(0)
-    collect(1)
+    out_sum.collect(wo_sum_ref)
+    for part in range(2):
+        sums[part].collect(gw_ref.at[part])
     swap.finish()
-    out_own.wait()
-    for n, p in enumerate(far):
-        send(
-            wo_ref.at[p], wo_planes_ref.at[p], o_sends.at[n], o_recvs.at[p], on_plane(p)
-        ).wait_recv()
-        out_to(n).wait_send()
+    for line_sum in (out_sum, *sums):
+        line_sum.finish()
     for part in range(2):
         for n, device in enumerate(order[:7]):
             tile_to(part, n, device).wait_send()
-        for n in range(len(far)):
-            to_plane(part, n).wait_send()
 
     def settle(block, carry):
         line.sent(block)
@@ -1999,14 +2252,14 @@
             jax.ShapeDtypeStruct((2, 2, deep, cols // 2), F32),
             jax.ShapeDtypeStruct((8, HEAD_SIZE), F32),
             jax.ShapeDtypeStruct(swap.shape, BF16),
-            jax.ShapeDtypeStruct(wo.shape, BF16),
+            jax.ShapeDtypeStruct(wo.shape[1:], F32),
         ),
         in_specs=[spec_vmem()] * 2
         + [spec_any()] * 2
         + [spec_vmem()] * 2
-        + [spec_any()] * 3
-        + [spec_vmem()] * 6,
-        out_specs=(spec_vmem(),) * 3 + (spec_any(),) * 2,
+        + [spec_any()] * 2
+        + [spec_vmem()] * 7,
+        out_specs=(spec_vmem(),) * 3 + (spec_any(), spec_vmem()),
         scratch_shapes=scatter_scratch(rows, width)
         + [
             half,
@@ -2017,15 +2270,17 @@
             tiles,
             tiles,
             pltpu.VMEM((2, 4, 2, deep, cols // 2), BF16),
+            pltpu.VMEM((2, 4, 2, deep, cols // 2), BF16),
+            pltpu.VMEM(wo.shape, BF16),
+            pltpu.VMEM(wo.shape, BF16),
             dma((2, 8 * rows // UNIT)),
             dma((2, 8 * rows // UNIT)),
             dma((2, 7)),
             dma((2, 8)),
-            dma((2, 3)),
+            dma((2, 2, 4)),
+            dma((2, 2, 4)),
             dma((2, 4)),
-            dma,
-            dma((3,)),
-            dma((4,)),
+            dma((2, 4)),
         ]
         + SWAP_SCRATCH,
         compiler_params=comm_params(8),
@@ -2129,7 +2384,7 @@
         wq_ref[:, k * wide : (k + 1) * wide] = qkv_ref[0, k]
         wk_ref[:, k * HEAD_SIZE : (k + 1) * HEAD_SIZE] = qkv_ref[1, k, :, :HEAD_SIZE]
         wv_ref[:, k * HEAD_SIZE : (k + 1) * HEAD_SIZE] = qkv_ref[1, k, :, HEAD_SIZE:]
-    wo_ref[...] = sum(out_ref[p].astype(F32) for p in range(4))
+    wo_ref[...] = out_ref[...]
 
 
 def finish(d_normed, tokens, d_middle, in_gain, gu, down, qkv, out):
@@ -2147,7 +2402,7 @@
     one = (1, width)
     whole = pl.BlockSpec(one, lambda i: (0, 0))
     flat, square = (rows, width), (deep, 2 * HEAD_SIZE)
-    ins = [(flat, 0), (flat, 0), (flat, 0), None, (gu.shape, 1), (down.shape, 1), (qkv.shape, 2), (out.shape, 1)]
+    ins = [(flat, 0), (flat, 0), (flat, 0), None, (gu.shape, 1), (down.shape, 1), (qkv.shape, 2), (out.shape, 0)]
     outs = [
         (flat, 0, BF16),
         None,
@@ -2157,7 +2412,7 @@
         ((deep, 4 * HEAD_SIZE), 0, F32),
         (square, 0, F32),
         (square, 0, F32),
-        (out.shape[1:], 0, F32),
+        (out.shape, 0, F32),
     ]
     return pl.pallas_call(
         finish_kernel,
@@ -2471,29 +2726,23 @@
         ],
         axis=2,
     )
-    qkv_slab = lax.all_gather(jnp.transpose(qkv_home, (1, 0, 2)), "tp", axis=0, tiled=True)
-
-    def to_chips(home):
-        return lax.all_to_all(home, "ctx", 0, 0, axis_index_groups=CORE_GROUPS, tiled=True)
-
-    gate_part = to_chips(jnp.transpose(w_gate.reshape(deep, 4, cols), (1, 0, 2)))
-    up_part = to_chips(jnp.transpose(w_up.reshape(deep, 4, cols), (1, 0, 2)))
-    down_part = to_chips(w_down.reshape(4, cols, deep))
     tables = angles(block_order, tok_rows)
-    normed_all, w_qkv, queries, kv, kv_lo, kv_hi, lin, gate_parts, out_part = gather_qkv(
+    normed_all, w_qkv, queries, kv, kv_lo, kv_hi, lin, gate_parts, up_part, down_part, out_part = gather_qkv(
         normed_rows,
-        after(qkv_slab, up_part, down_part),
+        jnp.transpose(qkv_home, (1, 0, 2)),
         q_gain,
         k_gain,
         tables,
-        gate_part,
+        jnp.transpose(w_gate.reshape(deep, 4, cols), (1, 0, 2)),
+        jnp.transpose(w_up.reshape(deep, 4, cols), (1, 0, 2)),
+        w_down.reshape(4, cols, deep),
         w_out.reshape(2, 2 * HEAD_SIZE, deep),
     )
     out_part = out_part.reshape(width, deep)
     out_parts = [out_part] + [lax.ppermute(out_part, "ctx", [(i, i ^ n) for i in range(8)]) for n in (2, 4, 6)]
-    up_parts = lax.all_gather(after(up_part, kv[:8]), "tp", axis=0)
+    up_parts = lax.all_gather(up_part, "tp", axis=0)
     mixed, lse = attend(block_order, seq_lens, queries, kv_lo, kv, kv_hi, seq_len)
-    down_parts = lax.all_gather(after(down_part, kv[:8]), "tp", axis=0)
+    down_parts = lax.all_gather(down_part, "tp", axis=0)
     middle, post_rows, mixed_rows, w_o = mix(mixed, tokens, post_gain, out_parts)
     post_all, w_gu, slope, active, hidden = gather_up(post_rows, gate_parts, up_parts)
     output, diff_low, diff, error, w_d = scatter_down(hidden, down_parts, middle, teacher, valid)

time: 790 us -> 744 us (0.942)
  waiting for transfers between devices: 37.1 us -> 14.8 us
  starting transfers between devices: 19.5 us -> 8.09 us
    pallas_call x1, Pallas kernels: 102 us -> 126 us  [gather_qkv(): pl.pallas_call(qkv_kernel, out_shape=(jax.ShapeDtypeStruct((8, rows, widt...]
    all_to_all x3 -> x0, waiting for transfers between devices: 14.1 us -> none  [to_chips(): lax.all_to_all(home, 'ctx', 0, 0, axis_index_groups=CORE_GROUPS, tiled=True)]
    all_to_all x3 -> x0, starting transfers between devices: 12.2 us -> none  [to_chips(): lax.all_to_all(home, 'ctx', 0, 0, axis_index_groups=CORE_GROUPS, tiled=True)]
    all_gather x3 -> x2, waiting for transfers between devices: 11.8 us -> 0.04 us  [the longest x1 0.02 us: local_plane(): up_parts = lax.all_gather(up_part, 'tp', axis=0)]
    pallas_call x1, Pallas kernels: 117 us -> 108 us  [scatter_normed(): pl.pallas_call(normed_back_kernel, out_shape=(jax.ShapeDtypeStruct((rows,...]
  transfers between devices with their start and end apart: 14 -> 10, of which waited for: 6 -> 2; matrix products, arithmetic and copies ran while one was open for 2% -> 1% of each run, Pallas kernels for 38% -> 39%
where the time goes in v4:
time: 744 us; the launch traced here: 737 us
  Pallas kernels  674 us (91%)
  between operations  17.2 us (2%)
  waiting for transfers between devices  14.8 us (2%)
  other arithmetic  12 us (2%)
  local copies, waits for them, and re-layouts  10.7 us (1%)
  starting transfers between devices  8.09 us (1%)
    pallas_call x1, Pallas kernels, gather_qkv(): pl.pallas_call(qkv_kernel, out_shape=(jax.ShapeDtypeStruct((8, rows, widt...  126 us
    pallas_call x1, Pallas kernels, scatter_normed(): pl.pallas_call(normed_back_kernel, out_shape=(jax.ShapeDtypeStruct((rows,...  108 us
    pallas_call x1, Pallas kernels, scatter_post(): pl.pallas_call(post_back_kernel, out_shape=(jax.ShapeDtypeStruct((rows, w...  66.2 us
    pallas_call x1, Pallas kernels, scatter_down(): pl.pallas_call(down_kernel, out_shape=(low, low, jax.ShapeDtypeStruct((ro...  65.1 us
    pallas_call x1, Pallas kernels, gather_down_back(): pl.pallas_call(down_back_kernel, out_shape=(jax.ShapeDtypeStruct((8 * row...  63.3 us
    pallas_call x1, Pallas kernels, gather_up(): pl.pallas_call(up_kernel, out_shape=(jax.ShapeDtypeStruct((8, rows, width...  61.9 us
    pallas_call x1, Pallas kernels, attend_back(): pl.pallas_call(attend_back_kernel, out_shape=(flat,) * 4, in_specs=[spec_...  60.9 us
    pallas_call x1, Pallas kernels, attend(): pl.pallas_call(attend_kernel, out_shape=(jax.ShapeDtypeStruct(q.shape, BF...  36 us
  transfers between devices with their start and end apart: 10, of which 2 were waited for; matrix products, arithmetic and copies ran while one was open for 1% of the time, Pallas kernels for 39%

profile of v4, /device:TPU:0, one launch (start us, length us, event | category | flops | bytes accessed | tf_op | source)
XLA Modules:
  0.0 736.9 jit_solution(10426999590444979557)
XLA Ops:
  7.3 1.3 gather_fusion.1
  8.8 0.1 reshape.438
  8.9 0.8 gather_fusion
  9.8 0.1 convert_element_type.50
  10.0 0.9 fusion.3
  10.9 0.7 multiply_sine_fusion
  11.6 0.4 fusion
  12.0 0.3 copy.46
  12.3 1.2 copy.47
  13.5 0.3 copy.48
  13.8 1.2 copy.49
  14.9 0.1 copy.40
  15.1 0.1 copy.43
  15.2 0.1 copy.41
  15.3 0.1 copy.44
  15.5 0.1 copy.42
  15.6 0.1 copy.45
  15.7 1.6 fusion.2.x_ref
  17.3 0.8 maximum_bitcast_fusion.home_ref
  18.1 125.9 %gather_qkv.1 = (bf16[8,384,2048]{2,1,0:T(8,128)(2,1)}, bf16[2048,512]{1,0:T(8,128)(2,1)}, bf16[3072,256]{1,0:T(8,128)(2,1)}, bf16[3072,256]{1,0:T(8,128)(2,1)},...) custom-call(bf16[384,2048]{1,0:T(8,128)(2,1)} %fusion.2.x_ref, ...), custom_call_target="tpu_custom_call" | custom-call | bytes 300000000 | tf_op jit(solution)/shard_map/gather_qkv/pallas_call | solution.py:1132
  144.2 0.7 all-gather.7.cloned.1.call-update
  144.9 0.7 collective-permute-start
  145.6 3.7 collective-permute-start.1
  149.3 0.6 gather_fusion.2
  150.0 0.8 copy.52
  150.9 36.0 %attend.1 = (bf16[3072,256]{1,0:T(8,128)(2,1)}, f32[24,8,256]{2,1,0:T(8,128)}) custom-call(s32[3,16]{1,0:T(4,128)} %order_ref.3, s32[3]{0:T(128)} %lens_ref.3, bf16[3072,256]{1,0:T(8,128)(2,1)} %get-tuple-element.75.q_ref, bf16[3072,256]{1,0:T(8,128)(2,1)} %get-tuple-element.76.lo_ref, bf16[3072,256]{1,0:T(8,128)(2,1)} %get-tuple-element.77.own_ref, ...), custom_call_target="tpu_custom_call" | custom-call | bytes 150000000 | tf_op jit(solution)/shard_map/attend/pallas_call | solution.py:2549
  186.9 7.4 collective-permute-done.1.w2_ref
  194.3 30.2 %mix.1 = (f32[384,2048]{1,0:T(8,128)}, bf16[384,2048]{1,0:T(8,128)(2,1)}, bf16[384,2048]{1,0:T(8,128)(2,1)}, bf16[2048,2048]{1,0:T(8,128)(2,1)}) custom-call(bf16[3072,256]{1,0:T(8,128)(2,1)} %get-tuple-element.79.mixed_ref.o_ref, bf16[384,2048]{1,0:T(8,128)(2,1)} %tokens_ref.3, f32[1,2048]{1,0:T(1,128)} %bitcast.66, bf16[2048,256]{1,0:T(8,128)(2,1)} %bitcast.58, ...), custom_call_target="tpu_custom_call" | custom-call | bytes 84000000 | tf_op jit(solution)/shard_map/mix/pallas_call | solution.py:1703
  224.5 61.9 %gather_up.1 = (bf16[8,384,2048]{2,1,0:T(8,128)(2,1)}, bf16[2,2048,768]{2,1,0:T(8,128)(2,1)}, bf16[3072,768]{1,0:T(8,128)(2,1)}, bf16[3072,768]{1,0:T(8,128)(2,1)}, bf16[3072,768]{1,0:T(8,128)(2,1)}) custom-call(bf16[384,2048]{1,0:T(8,128)(2,1)} %get-tuple-element.81.x_ref, bf16[4,4,256,384]{3,2,1,0:T(8,128)(2,1)} %get-tuple-element.82.gate_ref, ...), custom_call_target="tpu_custom_call" | custom-call | bytes 186000000 | tf_op jit(solution)/shard_map/gather_up/pallas_call | solution.py:1337
  286.4 65.1 %scatter_down.1 = (bf16[384,2048]{1,0:T(8,128)(2,1)}, bf16[384,2048]{1,0:T(8,128)(2,1)}, f32[384,2048]{1,0:T(8,128)}, f32[1,128]{1,0:T(1,128)}, bf16[768,2048]{1,0:T(8,128)(2,1)}) custom-call(bf16[3072,768]{1,0:T(8,128)(2,1)} %get-tuple-element.84.h_any.h_ref, bf16[4,4,384,256]{3,2,1,0:T(8,128)(2,1)} %bitcast.49, ...), custom_call_target="tpu_custom_call" | custom-call | bytes 186000000 | tf_op jit(solution)/shard_map/scatter_down/pallas_call | solution.py:1428
  351.6 63.3 %gather_down_back.1 = (bf16[3072,1536]{1,0:T(8,128)(2,1)}, bf16[4,4,384,256]{3,2,1,0:T(8,128)(2,1)}) custom-call(bf16[384,2048]{1,0:T(8,128)(2,1)} %get-tuple-element.88.x_ref, bf16[768,2048]{1,0:T(8,128)(2,1)} %get-tuple-element.89.w_ref, bf16[3072,768]{1,0:T(8,128)(2,1)} %get-tuple-element.90.a_ref, bf16[3072,768]{1,0:T(8,128)(2,1)} %get-tuple-element.91.b_ref, ...), custom_call_target="tpu_custom_call" | custom-call | bytes 198000000 | tf_op jit(solution)/shard_map/gather_down_back/pallas_call | solution.py:1585
  415.0 66.2 %scatter_post.1 = (f32[384,2048]{1,0:T(8,128)}, bf16[4,4,256,768]{3,2,1,0:T(8,128)(2,1)}) custom-call(bf16[3072,1536]{1,0:T(8,128)(2,1)} %get-tuple-element.92.d_any, bf16[2,2048,768]{2,1,0:T(8,128)(2,1)} %get-tuple-element.93.w_any, bf16[8,384,2048]{2,1,0:T(8,128)(2,1)} %get-tuple-element.94.all_ref), custom_call_target="tpu_custom_call" | custom-call | bytes 198000000 | tf_op jit(solution)/shard_map/scatter_post/pallas_call | solution.py:1997
  481.3 34.3 %mix_back.1 = (bf16[3072,256]{1,0:T(8,128)(2,1)}, f32[384,2048]{1,0:T(8,128)}, f32[1,2048]{1,0:T(1,128)}, bf16[2048,256]{1,0:T(8,128)(2,1)}, bf16[2048,256]{1,0:...) custom-call(f32[384,2048]{1,0:T(8,128)} %get-tuple-element.95.post_ref, ...), custom_call_target="tpu_custom_call" | custom-call | bytes 78000000 | tf_op jit(solution)/shard_map/mix_back/pallas_call | solution.py:1856
  515.6 1.4 collective-permute-start.3
  517.0 0.7 collective-permute-start.4
  517.7 1.5 collective-permute-start.5
  519.1 0.6 reduce_sum.29
  520.4 60.9 %attend_back.1 = (bf16[3072,256]{1,0:T(8,128)(2,1)}, bf16[3072,256]{1,0:T(8,128)(2,1)}, bf16[3072,256]{1,0:T(8,128)(2,1)}, bf16[3072,256]{1,0:T(8,128)(2,1)}) custom-call(s32[3,16]{1,0:T(4,128)} %order_ref.3, s32[3]{0:T(128)} %lens_ref.3, bf16[3072,256]{1,0:T(8,128)(2,1)} %get-tuple-element.75.q_ref, bf16[3072,256]{1,0:T(8,128)(2,1)} %get-tuple-element.100.do_ref, ...), custom_call_target="tpu_custom_call" | custom-call | bytes 225000000 | tf_op jit(solution)/shard_map/attend_back/pallas_call | solution.py:2650
  581.4 3.4 add_convert_fusion
  584.8 6.6 reduce-scatter.5.cloned.1.call-done
  591.3 108.2 %scatter_normed.1 = (f32[384,2048]{1,0:T(8,128)}, f32[2,2,256,256]{3,2,1,0:T(8,128)}, f32[8,128]{1,0:T(8,128)}, bf16[4,256,768]{2,1,0:T(8,128)(2,1)}, f32[512,256]{1,0:T(8,128)}) custom-call(bf16[3072,256]{1,0:T(8,128)(2,1)} %get-tuple-element.102.dq_ref, bf16[3072,256]{1,0:T(8,128)(2,1)} %get-tuple-element.103.dkv_ref, ...), custom_call_target="tpu_custom_call" | custom-call | bytes 330000000 | tf_op jit(solution)/shard_map/scatter_normed/pallas_call | solution.py:2248
  699.6 0.7 slice.25
  700.3 10.0 %finish.1 = (bf16[384,2048]{1,0:T(8,128)(2,1)}, f32[1,2048]{1,0:T(1,128)}, f32[256,1536]{1,0:T(8,128)}, f32[256,1536]{1,0:T(8,128)}, f32[4,384,256]{2,1,0:T(8,12...) custom-call(f32[384,2048]{1,0:T(8,128)} %get-tuple-element.118.d_ref, ...), custom_call_target="tpu_custom_call" | custom-call | bytes 24000000 | tf_op jit(solution)/shard_map/finish/pallas_call | solution.py:2417
  710.3 1.3 pad_maximum_fusion.v_ref
  711.6 12.0 %total_of.1 = f32[40,128]{1,0:T(8,128)} custom-call(f32[40,128]{1,0:T(8,128)} %pad_maximum_fusion.v_ref), custom_call_target="tpu_custom_call" | custom-call | bytes 36000000 | tf_op jit(solution)/shard_map/total_of/pallas_call | solution.py:2342
  723.6 1.3 slice_bitcast_fusion
  724.9 1.9 slice_bitcast_fusion.2
  727.5 1.1 copy.56
  (62 shorter events, 0.8 us)
Async XLA Ops:
  7.2 1.7 copy-start
  7.2 217.3 %all-gather.5.cloned.1.call-start = ((), (), s32[]{:S(2)}) async-start(), calls=%async_computation.4 | async-start | bytes 3932160 | tf_op jit(solution)/shard_map/all_gather | solution.py:2743
  8.9 2.8 copy-start.3
  8.9 3.1 copy-start.7
  12.3 1.2 copy-start.8
  12.3 2.6 copy-start.9
  13.5 1.7 copy-start.10
  13.7 1.7 copy-start.11
  13.8 1.9 copy-start.12
  18.1 131.2 %copy-start.1 = (s32[3]{0:T(128)S(1)}, s32[3]{0:T(128)}, u32[]{:S(2)}) copy-start(s32[3]{0:T(128)} %lens_ref.3) | copy-start | bytes 40
  144.1 142.3 %all-gather.7.cloned.1.call-start = ((), (), s32[]{:S(2)}) async-start(), calls=%async_computation.5 | async-start | bytes 3932160 | tf_op jit(solution)/shard_map/all_gather | solution.py:2745
  144.9 336.4 %reduce-scatter.3.cloned.1.call-start = ((), (), s32[]{:S(2)}) async-start(), calls=%async_computation.2 | async-start | bytes 3932160 | tf_op jit(solution)/shard_map/reduce_scatter | solution.py:2753
  144.9 42.0 %collective-permute-start = (bf16[2048,256]{1,0:T(8,128)(2,1)}, bf16[2048,256]{1,0:T(8,128)(2,1)S(1)}, u32[]{:S(2)}, u32[]{:S(2)}) collective-permute-start(bf16[2048,256]{1,0:T(8,128)(2,1)} %bitcast.55), channel_id=1, source_target_pairs={{0,8},{4,12},{8,0},{12,4},{16,24},{20,28},{24,16},{28,20},{1,9},{5... | collective-permute-start | bytes 3145736 | tf_op jit(solution)/shard_map/ppermute | solution.py:2742
  145.6 48.7 %collective-permute-start.1 = (bf16[2048,256]{1,0:T(8,128)(2,1)}, bf16[2048,256]{1,0:T(8,128)(2,1)}, u32[]{:S(2)}, u32[]{:S(2)}) collective-permute-start(bf16[2048,256]{1,0:T(8,128)(2,1)} %bitcast.56), channel_id=1, source_target_pairs={{0,16},{4,20},{8,24},{12,28},{16,0},{20,4},{24,8},{28,12},{1,17},{... | collective-permute-start | bytes 3145736 | tf_op jit(solution)/shard_map/ppermute | solution.py:2742
  149.3 45.0 %collective-permute-start.2 = (bf16[2048,256]{1,0:T(8,128)(2,1)}, bf16[2048,256]{1,0:T(8,128)(2,1)}, u32[]{:S(2)}, u32[]{:S(2)}) collective-permute-start(bf16[2048,256]{1,0:T(8,128)(2,1)} %bitcast.57), channel_id=1, source_target_pairs={{0,24},{4,28},{8,16},{12,20},{16,8},{20,12},{24,0},{28,4},{1,25},{... | collective-permute-start | bytes 3145736 | tf_op jit(solution)/shard_map/ppermute | solution.py:2742
  186.9 7.4 %copy-start.6 = (bf16[2048,256]{1,0:T(8,128)(2,1)}, bf16[2048,256]{1,0:T(8,128)(2,1)S(1)}, u32[]{:S(2)}) copy-start(bf16[2048,256]{1,0:T(8,128)(2,1)S(1)} %collective-permute-done.w1_ref) | copy-start | bytes 3145732
  414.9 176.4 %reduce-scatter.5.cloned.1.call-start = ((), (), s32[]{:S(2)}) async-start(), calls=%async_computation.3 | async-start | bytes 7864320 | tf_op jit(solution)/shard_map/reduce_scatter | solution.py:2753
  481.3 37.8 %copy-start.2 = (s32[3]{0:T(128)S(1)}, s32[3]{0:T(128)}, u32[]{:S(2)}) copy-start(s32[3]{0:T(128)} %lens_ref.3) | copy-start | bytes 40
  515.6 65.7 %collective-permute-start.3 = (bf16[2048,256]{1,0:T(8,128)(2,1)}, bf16[2048,256]{1,0:T(8,128)(2,1)}, u32[]{:S(2)}, u32[]{:S(2)}) collective-permute-start(bf16[2048,256]{1,0:T(8,128)(2,1)} %get-tuple-element.112), channel_id=1, source_target_pairs={{0,8},{4,12},{8,0},{12,4},{16,24},{20,28},{24,16},{28,20},{1,9},{5... | collective-permute-start | bytes 3145736 | tf_op jit(solution)/shard_map/ppermute | solution.py:2761
  517.0 64.4 %collective-permute-start.4 = (bf16[2048,256]{1,0:T(8,128)(2,1)}, bf16[2048,256]{1,0:T(8,128)(2,1)}, u32[]{:S(2)}, u32[]{:S(2)}) collective-permute-start(bf16[2048,256]{1,0:T(8,128)(2,1)} %get-tuple-element.114), channel_id=1, source_target_pairs={{0,16},{4,20},{8,24},{12,28},{16,0},{20,4},{24,8},{28,12},{1,17},{... | collective-permute-start | bytes 3145736 | tf_op jit(solution)/shard_map/ppermute | solution.py:2761
  517.7 63.7 %collective-permute-start.5 = (bf16[2048,256]{1,0:T(8,128)(2,1)}, bf16[2048,256]{1,0:T(8,128)(2,1)}, u32[]{:S(2)}, u32[]{:S(2)}) collective-permute-start(bf16[2048,256]{1,0:T(8,128)(2,1)} %get-tuple-element.116), channel_id=1, source_target_pairs={{0,24},{4,28},{8,16},{12,20},{16,8},{20,12},{24,0},{28,4},{1,25},{... | collective-permute-start | bytes 3145736 | tf_op jit(solution)/shard_map/ppermute | solution.py:2761
  520.4 60.9 %copy-start.5 = (bf16[2048,256]{1,0:T(8,128)(2,1)S(1)}, bf16[2048,256]{1,0:T(8,128)(2,1)}, u32[]{:S(2)}) copy-start(bf16[2048,256]{1,0:T(8,128)(2,1)} %get-tuple-element.111) | copy-start | bytes 3145732
  700.2 10.0 %copy-start.14 = (f32[1,128]{1,0:T(1,128)S(1)}, f32[1,128]{1,0:T(1,128)}, u32[]{:S(2)}) copy-start(f32[1,128]{1,0:T(1,128)} %get-tuple-element.127) | copy-start | bytes 1540
  700.3 10.0 %copy-start.13 = (f32[1,2048]{1,0:T(1,128)S(1)}, f32[1,2048]{1,0:T(1,128)}, u32[]{:S(2)}) copy-start(f32[1,2048]{1,0:T(1,128)} %get-tuple-element.125) | copy-start | bytes 24580
  700.3 27.3 %copy-start.4 = (bf16[384,2048]{1,0:T(8,128)(2,1)S(1)}, bf16[384,2048]{1,0:T(8,128)(2,1)}, u32[]{:S(2)}) copy-start(bf16[384,2048]{1,0:T(8,128)(2,1)} %get-tuple-element.163) | copy-start | bytes 4718596
Sparse Core Ops, SparseCore 0:
  144.2 66.2 all-gather.4
  212.1 62.1 all-gather.6
  415.1 59.4 reduce-scatter.2
  481.4 109.8 reduce-scatter.4

commit v5 on v4

--- a/solution.py
+++ b/solution.py
@@ -442,6 +442,7 @@
 
 
 SUBS = 4
+BY_X, BY_Y = (0, 2, 1, 3), (1, 3, 0, 2)
 
 
 def on_ctx(device):
@@ -483,8 +484,7 @@
         return self.x_ref.at[pl.ds(s * self.piece, self.piece)]
 
     def start(self):
-        for s in range(SUBS):
-            t = (s + SUBS // 2) % SUBS
+        for s, t in zip(BY_X, BY_Y):
             self.remote(self.own(s), 0, self.me, s, self.nx).start()
             self.remote(self.own(t), 1, self.me, t, self.ny).start()
         for s in range(SUBS):
@@ -500,63 +500,62 @@
         self.remote(self.part(block, s), kind, block, s, device).start()
 
     def pass_on(self, i):
-        half = SUBS // 2
-        s, t = i, (i + half) % SUBS
+        s, t = BY_X[i], BY_Y[i]
         self.arrived(self.nx, s)
-        if s < half:
+        if s % 2 == 0:
             self.relay(3, self.nx, s, self.ny)
         self.relay(4, self.nx, s, self.sib)
         self.arrived(self.ny, t)
-        if t >= half:
+        if t % 2 == 1:
             self.relay(3, self.ny, t, self.nx)
         self.relay(5, self.ny, t, self.sib)
 
+    def far_half(self, h):
+        for s in (2 * h, 2 * h + 1):
+            self.arrived(self.dg, s)
+            self.relay(6, self.dg, s, self.sib)
+
+    def all_of(self, block, pieces=range(SUBS)):
+        for s in pieces:
+            self.arrived(block, s)
+
+    def pass_all(self):
+        for i in range(SUBS):
+            self.pass_on(i)
+
     def before(self, step, passing=True):
-        half = SUBS // 2
-
-        @pl.when(step == 1)
-        def _():
-            for s in range(SUBS):
-                self.arrived(self.sib, s)
-
-        if passing:
-
-            @pl.when(step == 2)
-            def _():
-                for i in range(SUBS):
-                    self.pass_on(i)
-
-        @pl.when(step == 3)
-        def _():
-            for s in range(SUBS):
-                self.arrived(self.nx + self.shift, s)
-
-        @pl.when(step == 4)
-        def _():
-            for s in (0, half):
-                self.arrived(self.dg, s)
-                self.relay(6, self.dg, s, self.sib)
-
-        @pl.when(step == 5)
-        def _():
-            for s in range(SUBS):
-                self.arrived(self.ny + self.shift, s)
-
-        @pl.when(step == 6)
-        def _():
-            for s in range(SUBS):
-                if s % half:
-                    self.arrived(self.dg, s)
-                    self.relay(6, self.dg, s, self.sib)
-
-        @pl.when(step == 7)
-        def _():
-            for s in range(SUBS):
-                self.arrived(self.dg + self.shift, s)
+        for at, act in (
+            (1, lambda: self.all_of(self.sib)),
+            (2, self.pass_all if passing else lambda: None),
+            (3, lambda: self.all_of(self.nx + self.shift)),
+            (4, lambda: self.far_half(0)),
+            (5, lambda: self.all_of(self.ny + self.shift)),
+            (6, lambda: self.far_half(1)),
+            (7, lambda: self.all_of(self.dg + self.shift)),
+        ):
+            pl.when(step == at)(act)
+
+    def before_half(self, step):
+        for at, act in (
+            (2, lambda: self.all_of(self.sib)),
+            (4, self.pass_all),
+            (6, lambda: self.all_of(self.nx + self.shift)),
+            (8, lambda: self.far_half(0)),
+            (10, lambda: self.all_of(self.ny + self.shift)),
+            (13, lambda: self.all_of(self.dg + self.shift, (0, 1))),
+            (14, lambda: self.far_half(1)),
+            (15, lambda: self.all_of(self.dg + self.shift, (2, 3))),
+        ):
+            pl.when(step == at)(act)
 
     def block(self, step):
         near = (self.me, self.nx, self.ny, self.dg)
         return pick(step, [b + o for b in near for o in (0, self.shift)])
+
+    def half_block(self, step):
+        last = step >= 12
+        n = jnp.where(last, 6 + lax.rem(step, 2), step // 2)
+        return self.block(n), jnp.where(last, (step - 12) // 2, lax.rem(step, 2))
 
     def finish(self):
         for s in range(SUBS):
@@ -782,13 +781,19 @@
         me, _, nx, ny, dg = plane_neighbours()
         self.chip, self.away = me // 2, (dg, nx, ny)
 
+    def part(self, chip):
+        if len(self.src.shape) == 3:
+            return self.src.at[chip]
+        cols = self.src.shape[1] // 4
+        return self.src.at[:, pl.ds(pl.multiple_of(chip * cols, HEAD_SIZE), cols)]
+
     def own(self):
-        return pltpu.make_async_copy(self.src.at[self.chip], self.dst.at[self.chip], self.local_sem)
+        return pltpu.make_async_copy(self.part(self.chip), self.dst.at[self.chip], self.local_sem)
 
     def to(self, n):
         there = self.away[n]
         return send(
-            self.src.at[there // 2], self.dst.at[self.chip], self.send_sems.at[n], self.recv_sems.at[self.chip], on_ctx(there)
+            self.part(there // 2), self.dst.at[self.chip], self.send_sems.at[n], self.recv_sems.at[self.chip], on_ctx(there)
         )
 
     def start(self):
@@ -801,7 +806,7 @@
         for n in range(3):
             there = self.away[n] // 2
             send(
-                self.src.at[there], self.dst.at[there], self.send_sems.at[n], self.recv_sems.at[there], on_ctx(self.away[n])
+                self.part(there), self.dst.at[there], self.send_sems.at[n], self.recv_sems.at[there], on_ctx(self.away[n])
             ).wait_recv()
 
     def sent(self):
@@ -938,6 +943,49 @@
                 def _():
                     for p in ends:
                         self.copy(way, p, k == 0).wait_send()
+
+
+class Total:
+    def __init__(self, held, held_planes, sends, recvs):
+        self.held, self.held_planes, self.sends, self.recvs = held, held_planes, sends, recvs
+        self.me = lax.axis_index("ctx")
+        self.plane, self.planes = lax.axis_index("tp"), lax.axis_size("tp")
+        self.away = others(self.me)
+        self.far = [lax.rem(self.plane + step, self.planes) for step in range(1, self.planes)]
+
+    def here(self, c, n):
+        ref = self.held.at[c]
+        return send(ref, ref, self.sends.at[n], self.recvs.at[c], on_ctx(self.away[n]))
+
+    def there(self, p, n):
+        ref = self.held_planes.at[p]
+        return send(ref, ref, self.sends.at[7 + n], self.recvs.at[8 + p], on_plane(self.far[n]))
+
+    def start(self):
+        for n in range(7):
+            self.here(self.me, n).start()
+
+    def middle(self):
+        for n, c in enumerate(self.away):
+            self.here(c, n).wait_recv()
+        value = self.held[0]
+        for c in range(1, 8):
+            value += self.held[c]
+        self.held_planes[self.plane] = value
+        for n in range(len(self.far)):
+            self.there(self.plane, n).start()
+
+    def finish(self, out):
+        for n, p in enumerate(self.far):
+            self.there(p, n).wait_recv()
+        value = self.held_planes[0]
+        for p in range(1, 4):
+            value += self.held_planes[p]
+        out[...] = value
+        for n in range(7):
+            self.here(self.me, n).wait_send()
+        for n in range(len(self.far)):
+            self.there(self.plane, n).wait_send()
 
 
 class Turn:
@@ -1007,9 +1055,9 @@
     deep = home_ref.shape[1]
     slabs = LineGather(home_ref, slab, *sems[0:3])
     outs = LineGather(out_ref, outs_ref, *sems[3:6])
-    gates = LineGather(gate_part, gates_ref, *sems[6:9])
+    gates = LineGather(gate_part.at[pl.ds(0, 3)], gates_ref, *sems[6:9])
     gate_swap = ChipSwap(gate_ref, gate_part, *sems[9:12])
-    late_swaps = (ChipSwap(up_ref, ups_ref, *sems[12:15]), ChipSwap(down_ref, downs_ref, *sems[15:18]))
+    late_swaps = (ChipSwap(up_ref, ups_ref.at[pl.ds(0, 4)], *sems[12:15]), ChipSwap(down_ref, downs_ref, *sems[15:18]))
     line = Line(kv_ref, kv_ref, lo_ref, hi_ref, kv_sends, kv_recvs, rows, False)
 
     def weight(source, origin, k):
@@ -1046,6 +1094,8 @@
     slabs.arrive(1, hand_out)
     gate_swap.arrive()
     gates.start()
+    keep_last = pltpu.make_async_copy(gate_part.at[3], ups_ref.at[4], sems[18])
+    keep_last.start()
     ring.pass_on(0)
     ring.pass_on(1)
     slabs.arrive(2, hand_out)
@@ -1120,6 +1170,7 @@
     for gather in (slabs, outs, gates):
         gather.finish() if gather is not slabs else gather.sent()
     gate_swap.sent()
+    keep_last.wait()
     for swap in late_swaps:
         swap.finish()
 
@@ -1127,6 +1178,7 @@
 def gather_qkv(normed, home, q_gain, k_gain, tables, gate, up, down, out):
     rows, width = normed.shape
     _, deep, cols = home.shape
+    part = (4, gate.shape[0], gate.shape[1] // 4)
     flat = jax.ShapeDtypeStruct((8 * rows, 2 * HEAD_SIZE), BF16)
     dma = pltpu.SemaphoreType.DMA
     return pl.pallas_call(
@@ -1139,8 +1191,8 @@
             flat,
             flat,
             jax.ShapeDtypeStruct((8 * rows, 3 * HEAD_SIZE), F32),
-            jax.ShapeDtypeStruct((4,) + gate.shape, BF16),
-            jax.ShapeDtypeStruct(up.shape, BF16),
+            jax.ShapeDtypeStruct((4, 3) + part[1:], BF16),
+            jax.ShapeDtypeStruct((5,) + part[1:], BF16),
             jax.ShapeDtypeStruct(down.shape, BF16),
             jax.ShapeDtypeStruct((4,) + out.shape, BF16),
         ),
@@ -1155,14 +1207,15 @@
             dma((8,)),
             dma((8,)),
             pltpu.VMEM((4,) + home.shape, BF16),
-            pltpu.VMEM(gate.shape, BF16),
+            pltpu.VMEM(part, BF16),
             dma((2, 8 * rows // UNIT)),
             dma((2, 8 * rows // UNIT)),
         ]
         + line_scratch(home.shape[0])
         + line_scratch(out.shape[0])
-        + line_scratch(gate.shape[0])
-        + SWAP_SCRATCH * 3,
+        + line_scratch(3)
+        + SWAP_SCRATCH * 3
+        + [dma],
         compiler_params=comm_params(1),
         cost_estimate=busy(100),
         name="gather_qkv",
@@ -1179,13 +1232,13 @@
     def own(self, z, p):
         n = 4 * z + p
         return pltpu.make_async_copy(
-            self.parts.at[2 * self.core + z, p], self.at(z, 2 * p + self.core), self.local_sems.at[n]
+            self.parts(2 * self.core + z, p), self.at(z, 2 * p + self.core), self.local_sems.at[n]
         )
 
     def swap(self, z, p):
         n = 4 * z + p
         return send(
-            self.parts.at[2 - 2 * self.core + z, p],
+            self.parts(2 - 2 * self.core + z, p),
             self.at(z, 2 * p + self.core),
             self.send_sems.at[n],
             self.recv_sems.at[n],
@@ -1205,7 +1258,7 @@
             self.own(z, p).wait()
             n = 4 * z + p
             send(
-                self.parts.at[2 * self.core + z, p],
+                self.parts(2 * self.core + z, p),
                 self.at(z, 2 * p + 1 - self.core),
                 self.send_sems.at[n],
                 self.recv_sems.at[n],
@@ -1277,8 +1330,16 @@
     outs = (a_ref, b_ref, h_ref)
     greet((ring.sib, ring.nx, ring.ny))
     ring.start()
-    gates = Halves(gate_ref, lambda z, c: w.at[z, pl.ds(c * deep, deep), pl.ds(0, cols)], *w_sems[:3])
-    ups = Halves(up_ref, lambda z, c: w.at[z, pl.ds(c * deep, deep), pl.ds(cols, cols)], *w_sems[3:])
+    gates = Halves(
+        lambda plane, p: gate_ref.at[plane, p] if p < 3 else up_ref.at[plane, 4],
+        lambda z, c: w.at[z, pl.ds(c * deep, deep), pl.ds(0, cols)],
+        *w_sems[:3],
+    )
+    ups = Halves(
+        lambda plane, p: up_ref.at[plane, p],
+        lambda z, c: w.at[z, pl.ds(c * deep, deep), pl.ds(cols, cols)],
+        *w_sems[3:],
+    )
     gates.start()
     ups.start()
     gates.ready()
@@ -1289,24 +1350,30 @@
     def keep(block):
         return pltpu.make_async_copy(xs.at[block], all_ref.at[block], keep_sems.at[block])
 
-    def put(slot, n, block):
-        return pltpu.make_async_copy(
-            stage.at[slot, n], outs[n].at[pl.ds(block * rows, rows)], stage_sems.at[slot, n]
-        )
+    part = rows // 2
+
+    def put(slot, n, at):
+        return pltpu.make_async_copy(stage.at[slot, n], outs[n].at[at], stage_sems.at[slot, n])
 
     def turn(step, carry):
-        ring.before(step)
-        block = ring.block(step)
-        keep(block).start()
+        ring.before_half(step)
+        block, h = ring.half_block(step)
+        seen = xs[block, pl.ds(pl.multiple_of(h * part, part), part), :]
+        at = pl.ds(pl.multiple_of(block * rows + h * part, part), part)
+
+        @pl.when(h == 1)
+        def _():
+            keep(block).start()
+
         slot = lax.rem(step, 2)
 
         @pl.when(step >= 2)
         def _():
             for n in range(3):
-                put(slot, n, block).wait()
+                put(slot, n, at).wait()
 
         for z in range(halves):
-            both = nn(xs[block], w[z])
+            both = nn(seen, w[z])
             gate, up = both[:, :cols], both[:, cols:]
             sigma = jax.nn.sigmoid(gate)
             active = gate * sigma
@@ -1315,10 +1382,10 @@
             stage[slot, 1, :, here] = active.astype(BF16)
             stage[slot, 2, :, here] = (active * up).astype(BF16)
         for n in range(3):
-            put(slot, n, block).start()
+            put(slot, n, at).start()
         return carry
 
-    lax.fori_loop(0, 8, turn, 0)
+    lax.fori_loop(0, 16, turn, 0)
     ring.finish()
     gates.finish()
     ups.finish()
@@ -1327,7 +1394,7 @@
         keep(block).wait()
     for slot in range(2):
         for n in range(3):
-            put(slot, n, 0).wait()
+            put(slot, n, pl.ds(0, part)).wait()
 
 
 def gather_up(post, gate_parts, up_parts):
@@ -1348,7 +1415,7 @@
         scratch_shapes=gather_scratch(rows, width)
         + [
             pltpu.SemaphoreType.DMA((8,)),
-            pltpu.VMEM((2, 3, rows, wide), BF16),
+            pltpu.VMEM((2, 3, rows // 2, wide), BF16),
             pltpu.SemaphoreType.DMA((2, 3)),
             pltpu.VMEM((2, width, wide), BF16),
             pltpu.SemaphoreType.DMA,
@@ -1366,7 +1433,7 @@
     rows = o_ref.shape[0]
     _, _, cols, deep = parts_ref.shape
     weight = Halves(
-        parts_ref,
+        lambda plane, p: parts_ref.at[plane, p],
         lambda z, c: w.at[pl.ds(z * cols, cols), pl.ds(pl.multiple_of(c * deep, deep), deep)],
         w_local,
         w_sends,
@@ -2029,6 +2096,9 @@
     all_ref,
     swap_ref,
     wo_ref,
+    tokens_ref,
+    gp_ref,
+    error_ref,
     qg_ref,
     kg_ref,
     ca_ref,
@@ -2037,7 +2107,7 @@
     sb_ref,
     o_ref,
     gw_ref,
-    gains_ref,
+    totals_ref,
     swapped_ref,
     wo_sum_ref,
     *scratch,
@@ -2063,6 +2133,11 @@
         p_recvs,
         o_sends,
         o_recvs,
+        gains_ref,
+        held,
+        held_planes,
+        v_sends,
+        v_recvs,
         *c_sems,
     ) = scratch[N_SCATTER:]
     me = rs.me
@@ -2078,7 +2153,11 @@
     from_lo[...] = jnp.zeros_like(from_lo)
     from_hi[...] = jnp.zeros_like(from_hi)
     line = Line(to_hi_ref, to_lo_ref, from_lo, from_hi, z_sends, z_recvs, rows, True)
-    greet_column(away)
+    barrier = pltpu.get_barrier_semaphore()
+    far = [lax.rem(plane + step, planes) for step in range(1, planes)]
+    for where in [on_ctx(c) for c in away] + [on_plane(p) for p in far]:
+        pl.semaphore_signal(barrier, inc=1, device_id=where, device_id_type=MESH)
+    pl.semaphore_wait(barrier, len(away) + len(far))
     for block in order:
         line.start(block)
     columns(all_ref, slices, slice_sems, order[0], 0).start()
@@ -2215,16 +2294,42 @@
     grads(0)
     lax.fori_loop(0, 16, turn, 0)
     grads(1)
+    for c in range(8):
+        pltpu.make_async_copy(
+            tokens_ref.at[:, pl.ds(c * deep, deep)], slices.at[0, c], slice_sems.at[0]
+        ).start()
     rs.second_wave()
     sums[0].stage(2)
     tiles_there(1)
     for k in range(3):
         sums[1].stage(k)
     rs.finish(o_ref)
+    total = Total(held, held_planes, v_sends, v_recvs)
+    vector = held.at[me]
+    pltpu.make_async_copy(slices.at[0], slices.at[0], slice_sems.at[0]).wait()
+    squares = jnp.zeros((rows, deep), F32)
+    for c in range(8):
+        stream = slices[0, c].astype(F32)
+        squares += stream * stream
+    scale = lax.rsqrt(jnp.sum(squares, axis=-1, keepdims=True) / width + EPS)
+    lanes_of = width // HEAD_SIZE
+    for c in range(8):
+        at = slice(c * deep, (c + 1) * deep)
+        unit_in = slices[0, c].astype(F32) * scale
+        gain = jnp.sum(o_ref[:, at].astype(F32) * unit_in, axis=0, keepdims=True)
+        for i in range(2):
+            n, lanes = 2 * c + i, slice(i * HEAD_SIZE, (i + 1) * HEAD_SIZE)
+            vector[n : n + 1, :] = gain[:, lanes]
+            vector[lanes_of + n : lanes_of + n + 1, :] = gp_ref[:, n * HEAD_SIZE : (n + 1) * HEAD_SIZE]
+    vector[2 * lanes_of : 2 * lanes_of + 2, :] = gains_ref[0:2, :]
+    vector[2 * lanes_of + 2 : 2 * lanes_of + 8, :] = jnp.broadcast_to(error_ref[...], (6, HEAD_SIZE))
+    total.start()
     out_sum.collect(wo_sum_ref)
     for part in range(2):
         sums[part].collect(gw_ref.at[part])
+    total.middle()
     swap.finish()
+    total.finish(totals_ref)
     for line_sum in (out_sum, *sums):
         line_sum.finish()
     for part in range(2):
@@ -2238,7 +2343,7 @@
     lax.fori_loop(0, 8, settle, 0)
 
 
-def scatter_normed(d_queries, d_kv, to_lo, to_hi, lin, w_qkv, normed_all, swap, wo, q_gain, k_gain, tables):
+def scatter_normed(d_queries, d_kv, to_lo, to_hi, lin, w_qkv, normed_all, swap, wo, tokens, gp, error, q_gain, k_gain, tables):
     _, rows, width = normed_all.shape
     deep = width // 8
     cols = w_qkv.shape[1]
@@ -2248,9 +2353,9 @@
     return pl.pallas_call(
         normed_back_kernel,
         out_shape=(
-            jax.ShapeDtypeStruct((rows, width), F32),
+            jax.ShapeDtypeStruct((rows, width), BF16),
             jax.ShapeDtypeStruct((2, 2, deep, cols // 2), F32),
-            jax.ShapeDtypeStruct((8, HEAD_SIZE), F32),
+            jax.ShapeDtypeStruct((2 * width // HEAD_SIZE + 8, HEAD_SIZE), F32),
             jax.ShapeDtypeStruct(swap.shape, BF16),
             jax.ShapeDtypeStruct(wo.shape[1:], F32),
         ),
@@ -2258,7 +2363,8 @@
         + [spec_any()] * 2
         + [spec_vmem()] * 2
         + [spec_any()] * 2
-        + [spec_vmem()] * 7,
+        + [spec_vmem(), spec_any()]
+        + [spec_vmem()] * 8,
         out_specs=(spec_vmem(),) * 3 + (spec_any(), spec_vmem()),
         scratch_shapes=scatter_scratch(rows, width)
         + [
@@ -2281,6 +2387,11 @@
             dma((2, 2, 4)),
             dma((2, 4)),
             dma((2, 4)),
+            pltpu.VMEM((8, HEAD_SIZE), F32),
+            pltpu.VMEM((8, 2 * width // HEAD_SIZE + 8, HEAD_SIZE), F32),
+            pltpu.VMEM((4, 2 * width // HEAD_SIZE + 8, HEAD_SIZE), F32),
+            dma((10,)),
+            dma((12,)),
         ]
         + SWAP_SCRATCH,
         compiler_params=comm_params(8),
@@ -2296,81 +2407,22 @@
         normed_all,
         swap,
         wo,
+        tokens,
+        gp,
+        error,
         q_gain.reshape(1, -1),
         k_gain.reshape(1, -1),
         *tables,
     )
 
 
-def total_kernel(v_ref, o_ref, held, held_planes, sends, recvs):
-    me = lax.axis_index("ctx")
-    plane, planes = lax.axis_index("tp"), lax.axis_size("tp")
-    away = others(me)
-    far = [lax.rem(plane + step, planes) for step in range(1, planes)]
-    barrier = pltpu.get_barrier_semaphore()
-    for where in [on_ctx(c) for c in away] + [on_plane(p) for p in far]:
-        pl.semaphore_signal(barrier, inc=1, device_id=where, device_id_type=MESH)
-    pl.semaphore_wait(barrier, len(away) + len(far))
-    held[me] = v_ref[...]
-    for n, c in enumerate(away):
-        send(held.at[me], held.at[me], sends.at[n], recvs.at[me], on_ctx(c)).start()
-    for c in away:
-        send(held.at[c], held.at[c], sends.at[0], recvs.at[c], on_ctx(c)).wait_recv()
-    value = held[0]
-    for c in range(1, 8):
-        value += held[c]
-    held_planes[plane] = value
-    for n, p in enumerate(far):
-        send(
-            held_planes.at[plane], held_planes.at[plane], sends.at[7 + n], recvs.at[8 + plane], on_plane(p)
-        ).start()
-    for p in far:
-        send(held_planes.at[p], held_planes.at[p], sends.at[0], recvs.at[8 + p], on_plane(p)).wait_recv()
-    value = held_planes[0]
-    for p in range(1, 4):
-        value += held_planes[p]
-    o_ref[...] = value
-    for n, c in enumerate(away):
-        send(held.at[me], held.at[me], sends.at[n], recvs.at[me], on_ctx(c)).wait_send()
-    for n, p in enumerate(far):
-        send(
-            held_planes.at[plane], held_planes.at[plane], sends.at[7 + n], recvs.at[8 + plane], on_plane(p)
-        ).wait_send()
-
-
-def total_of(values):
-    return pl.pallas_call(
-        total_kernel,
-        out_shape=jax.ShapeDtypeStruct(values.shape, F32),
-        in_specs=[spec_vmem()],
-        out_specs=spec_vmem(),
-        scratch_shapes=[
-            pltpu.VMEM((8,) + values.shape, F32),
-            pltpu.VMEM((4,) + values.shape, F32),
-            pltpu.SemaphoreType.DMA((10,)),
-            pltpu.SemaphoreType.DMA((12,)),
-        ],
-        compiler_params=pltpu.CompilerParams(collective_id=9, has_side_effects=True),
-        cost_estimate=busy(12),
-        name="total_of",
-    )(values)
-
-
 def finish_kernel(
     d_ref, tokens_ref, middle_ref, gain_ref, gu_ref, down_ref, qkv_ref, out_ref,
-    dt_ref, gin_ref, gate_ref, up_ref, dw_ref, wq_ref, wk_ref, wv_ref, wo_ref,
+    dt_ref, gate_ref, up_ref, dw_ref, wq_ref, wk_ref, wv_ref, wo_ref,
 ):
-    width = d_ref.shape[1]
-
-    @pl.when(pl.program_id(0) == 0)
-    def _():
-        gin_ref[...] = jnp.zeros_like(gin_ref)
-
     stream = tokens_ref[...].astype(F32)
     scale = lax.rsqrt(jnp.mean(stream * stream, axis=-1, keepdims=True) + EPS)
-    grad = d_ref[...]
-    gin_ref[...] += jnp.sum(grad * (stream * scale), axis=0, keepdims=True)
-    gained = grad * gain_ref[...]
+    gained = d_ref[...].astype(F32) * gain_ref[...]
     pull = scale * scale * scale * jnp.mean(gained * stream, axis=-1, keepdims=True)
     dt_ref[...] = (middle_ref[...] + (scale * gained - stream * pull)).astype(BF16)
     cols = gu_ref.shape[2] // 2
@@ -2405,7 +2457,6 @@
     ins = [(flat, 0), (flat, 0), (flat, 0), None, (gu.shape, 1), (down.shape, 1), (qkv.shape, 2), (out.shape, 0)]
     outs = [
         (flat, 0, BF16),
-        None,
         ((deep, ff), 0, F32),
         ((deep, ff), 0, F32),
         (down.shape, 1, F32),
@@ -2417,9 +2468,9 @@
     return pl.pallas_call(
         finish_kernel,
         grid=(steps,),
-        out_shape=tuple(jax.ShapeDtypeStruct(o[0], o[2]) if o else jax.ShapeDtypeStruct(one, F32) for o in outs),
+        out_shape=tuple(jax.ShapeDtypeStruct(o[0], o[2]) for o in outs),
         in_specs=[piece(*i) if i else whole for i in ins],
-        out_specs=tuple(piece(o[0], o[1]) if o else whole for o in outs),
+        out_specs=tuple(piece(o[0], o[1]) for o in outs),
         compiler_params=pltpu.CompilerParams(vmem_limit_bytes=VMEM_LIMIT),
         cost_estimate=busy(8),
         name="finish",
@@ -2727,17 +2778,18 @@
         axis=2,
     )
     tables = angles(block_order, tok_rows)
-    normed_all, w_qkv, queries, kv, kv_lo, kv_hi, lin, gate_parts, up_part, down_part, out_part = gather_qkv(
+    normed_all, w_qkv, queries, kv, kv_lo, kv_hi, lin, gate_parts, *parts = gather_qkv(
         normed_rows,
         jnp.transpose(qkv_home, (1, 0, 2)),
         q_gain,
         k_gain,
         tables,
-        jnp.transpose(w_gate.reshape(deep, 4, cols), (1, 0, 2)),
-        jnp.transpose(w_up.reshape(deep, 4, cols), (1, 0, 2)),
+        w_gate,
+        w_up,
         w_down.reshape(4, cols, deep),
         w_out.reshape(2, 2 * HEAD_SIZE, deep),
     )
+    up_part, down_part, out_part = parts
     out_part = out_part.reshape(width, deep)
     out_parts = [out_part] + [lax.ppermute(out_part, "ctx", [(i, i ^ n) for i in range(8)]) for n in (2, 4, 6)]
     up_parts = lax.all_gather(up_part, "tp", axis=0)
@@ -2774,7 +2826,7 @@
         seq_len,
     )
     out_sum = sum(after(g, d_queries[:8]).astype(F32) for g in grad_wo).astype(BF16)
-    d_normed, grad_qkv, grad_gains, gu_sum, grad_out = scatter_normed(
+    d_normed, grad_qkv, totals, gu_sum, grad_out = scatter_normed(
         d_queries,
         d_kv,
         to_lo,
@@ -2784,25 +2836,17 @@
         normed_all,
         grad_gu,
         out_sum.reshape(4, 4 * HEAD_SIZE, deep),
+        tokens,
+        grad_post,
+        error,
         q_gain,
         k_gain,
         tables,
     )
-    d_tokens, grad_in, grad_gate, grad_up, grad_down, grad_query, grad_key, grad_value, grad_out = finish(
+    d_tokens, grad_gate, grad_up, grad_down, grad_query, grad_key, grad_value, grad_out = finish(
         d_normed, tokens, d_middle, in_gain, gu_sum, grad_down, grad_qkv, grad_out
     )
     lanes = width // HEAD_SIZE
-    totals = total_of(
-        jnp.concatenate(
-            [
-                grad_in.reshape(lanes, HEAD_SIZE),
-                grad_post.reshape(lanes, HEAD_SIZE),
-                grad_gains[:2],
-                jnp.broadcast_to(error, (6, HEAD_SIZE)),
-            ],
-            axis=0,
-        )
-    )
     count_valid = jnp.sum(seq_lens).astype(F32)
     loss = 0.5 * jnp.sum(totals[2 * lanes + 2]) / (count_valid * MODEL_WIDTH)
     return (

time: 744 us -> 728 us (0.978)
  Pallas kernels: 674 us -> 651 us
  starting transfers between devices: 8.09 us -> 16.5 us
    pallas_call x1, Pallas kernels: 126 us -> 113 us  [gather_qkv(): pl.pallas_call(qkv_kernel, out_shape=(jax.ShapeDtypeStruct((8, rows, widt...]
    pallas_call x1 -> x0, Pallas kernels: 12 us -> none  [total_of(): pl.pallas_call(total_kernel, out_shape=jax.ShapeDtypeStruct(values.shape,...]
    ppermute x3, starting transfers between devices: 4.38 us -> 12.8 us  [local_plane(): lax.ppermute(out_part, 'ctx', [(i, i ^ n) for i in range(8)])]
  transfers between devices with their start and end apart: 10 -> 10, of which waited for: 2 -> 4; matrix products, arithmetic and copies ran while one was open for 1% -> 1% of each run, Pallas kernels for 39% -> 40%
where the time goes in v5:
time: 728 us; the launch traced here: 722 us
  Pallas kernels  651 us (89%)
  waiting for transfers between devices  19.5 us (3%)
  between operations  16.8 us (2%)
  starting transfers between devices  16.5 us (2%)
  other arithmetic  10.6 us (1%)
    pallas_call x1, Pallas kernels, scatter_normed(): pl.pallas_call(normed_back_kernel, out_shape=(jax.ShapeDtypeStruct((rows,...  113 us
    pallas_call x1, Pallas kernels, gather_qkv(): pl.pallas_call(qkv_kernel, out_shape=(jax.ShapeDtypeStruct((8, rows, widt...  113 us
    pallas_call x1, Pallas kernels, scatter_post(): pl.pallas_call(post_back_kernel, out_shape=(jax.ShapeDtypeStruct((rows, w...  66.4 us
    pallas_call x1, Pallas kernels, scatter_down(): pl.pallas_call(down_kernel, out_shape=(low, low, jax.ShapeDtypeStruct((ro...  66.3 us
    pallas_call x1, Pallas kernels, gather_down_back(): pl.pallas_call(down_back_kernel, out_shape=(jax.ShapeDtypeStruct((8 * row...  63 us
    pallas_call x1, Pallas kernels, gather_up(): pl.pallas_call(up_kernel, out_shape=(jax.ShapeDtypeStruct((8, rows, width...  61.5 us
    pallas_call x1, Pallas kernels, attend_back(): pl.pallas_call(attend_back_kernel, out_shape=(flat,) * 4, in_specs=[spec_...  57.8 us
    pallas_call x1, Pallas kernels, mix_back(): pl.pallas_call(mix_back_kernel, out_shape=(jax.ShapeDtypeStruct((8 * rows...  34.6 us
  transfers between devices with their start and end apart: 10, of which 4 were waited for; matrix products, arithmetic and copies ran while one was open for 1% of the time, Pallas kernels for 40%

profile of v5, /device:TPU:0, one launch (start us, length us, event | category | flops | bytes accessed | tf_op | source)
XLA Modules:
  0.0 721.6 jit_solution(10781066932306326220)
XLA Ops:
  7.3 1.3 gather_fusion.1
  8.7 0.1 fusion.7
  8.8 0.1 reshape.422
  8.9 0.8 gather_fusion
  9.7 0.1 reshape.445
  9.8 0.1 convert_element_type.50
  9.9 0.1 pad_maximum_fusion
  10.0 0.9 fusion.3
  10.9 0.7 multiply_sine_fusion
  11.6 0.4 fusion
  12.0 0.1 copy.36
  12.2 0.1 copy.39
  12.3 0.1 copy.37
  12.4 0.1 copy.40
  12.6 0.1 copy.38
  12.7 0.1 copy.41
  12.8 1.6 fusion.2.x_ref
  14.4 0.8 maximum_bitcast_fusion.home_ref
  15.2 113.2 %gather_qkv.1 = (bf16[8,384,2048]{2,1,0:T(8,128)(2,1)}, bf16[2048,512]{1,0:T(8,128)(2,1)}, bf16[3072,256]{1,0:T(8,128)(2,1)}, bf16[3072,256]{1,0:T(8,128)(2,1)},...) custom-call(bf16[384,2048]{1,0:T(8,128)(2,1)} %fusion.2.x_ref, ...), custom_call_target="tpu_custom_call" | custom-call | bytes 300000000 | tf_op jit(solution)/shard_map/gather_qkv/pallas_call | solution.py:1184
  128.5 0.7 all-gather.7.cloned.1.call-update
  129.2 0.7 collective-permute-start
  129.9 12.1 %collective-permute-start.1 = (bf16[2048,256]{1,0:T(8,128)(2,1)}, bf16[2048,256]{1,0:T(8,128)(2,1)}, u32[]{:S(2)}, u32[]{:S(2)}) collective-permute-start(bf16[2048,256]{1,0:T(8,128)(2,1)} %bitcast.45), channel_id=1, source_target_pairs={{0,16},{4,20},{8,24},{12,28},{16,0},{20,4},{24,8},{28,12},{1,17},{... | collective-permute-start | bytes 3145736 | tf_op jit(solution)/shard_map/ppermute | solution.py:2794
  142.1 0.6 gather_fusion.2
  142.7 0.1 convert_bitcast_fusion
  142.8 0.8 copy.44
  143.6 34.5 %attend.1 = (bf16[3072,256]{1,0:T(8,128)(2,1)}, f32[24,8,256]{2,1,0:T(8,128)}) custom-call(s32[3,16]{1,0:T(4,128)} %order_ref.3, s32[3]{0:T(128)} %lens_ref.3, bf16[3072,256]{1,0:T(8,128)(2,1)} %get-tuple-element.74.q_ref, bf16[3072,256]{1,0:T(8,128)(2,1)} %get-tuple-element.75.lo_ref, bf16[3072,256]{1,0:T(8,128)(2,1)} %get-tuple-element.76.own_ref, ...), custom_call_target="tpu_custom_call" | custom-call | bytes 150000000 | tf_op jit(solution)/shard_map/attend/pallas_call | solution.py:2600
  178.2 7.8 %collective-permute-done.1.w2_ref = bf16[2048,256]{1,0:T(8,128)(2,1)} collective-permute-done((bf16[2048,256]{1,0:T(8,128)(2,1)}, bf16[2048,256]{1,0:T(8,128)(2,1)}, u32[]{:S(2)}, u32[]{:S(2)}) %collective-permute-start.1) | collective-permute-done | bytes 1048608 | tf_op jit(solution)/shard_map/ppermute | solution.py:2794
  186.0 31.2 %mix.1 = (f32[384,2048]{1,0:T(8,128)}, bf16[384,2048]{1,0:T(8,128)(2,1)}, bf16[384,2048]{1,0:T(8,128)(2,1)}, bf16[2048,2048]{1,0:T(8,128)(2,1)}) custom-call(bf16[3072,256]{1,0:T(8,128)(2,1)} %get-tuple-element.78.mixed_ref.o_ref, bf16[384,2048]{1,0:T(8,128)(2,1)} %tokens_ref.5, f32[1,2048]{1,0:T(1,128)} %bitcast.54, bf16[2048,256]{1,0:T(8,128)(2,1)} %bitcast.47, ...), custom_call_target="tpu_custom_call" | custom-call | bytes 84000000 | tf_op jit(solution)/shard_map/mix/pallas_call | solution.py:1770
  217.2 0.7 all-gather.5.cloned.1.call-done
  217.9 61.5 %gather_up.1 = (bf16[8,384,2048]{2,1,0:T(8,128)(2,1)}, bf16[2,2048,768]{2,1,0:T(8,128)(2,1)}, bf16[3072,768]{1,0:T(8,128)(2,1)}, bf16[3072,768]{1,0:T(8,128)(2,1)}, bf16[3072,768]{1,0:T(8,128)(2,1)}) custom-call(bf16[384,2048]{1,0:T(8,128)(2,1)} %get-tuple-element.80.x_ref, bf16[4,3,256,384]{3,2,1,0:T(8,128)(2,1)} %get-tuple-element.81.gate_ref, ...), custom_call_target="tpu_custom_call" | custom-call | bytes 186000000 | tf_op jit(solution)/shard_map/gather_up/pallas_call | solution.py:1404
  279.5 2.2 all-gather.7.cloned.1.call-done
  281.6 66.3 %scatter_down.1 = (bf16[384,2048]{1,0:T(8,128)(2,1)}, bf16[384,2048]{1,0:T(8,128)(2,1)}, f32[384,2048]{1,0:T(8,128)}, f32[1,128]{1,0:T(1,128)}, bf16[768,2048]{1,0:T(8,128)(2,1)}) custom-call(bf16[3072,768]{1,0:T(8,128)(2,1)} %get-tuple-element.83.h_any.h_ref, bf16[4,4,384,256]{3,2,1,0:T(8,128)(2,1)} %bitcast.41, ...), custom_call_target="tpu_custom_call" | custom-call | bytes 186000000 | tf_op jit(solution)/shard_map/scatter_down/pallas_call | solution.py:1495
  347.9 63.0 %gather_down_back.1 = (bf16[3072,1536]{1,0:T(8,128)(2,1)}, bf16[4,4,384,256]{3,2,1,0:T(8,128)(2,1)}) custom-call(bf16[384,2048]{1,0:T(8,128)(2,1)} %get-tuple-element.87.x_ref, bf16[768,2048]{1,0:T(8,128)(2,1)} %get-tuple-element.88.w_ref, bf16[3072,768]{1,0:T(8,128)(2,1)} %get-tuple-element.89.a_ref, bf16[3072,768]{1,0:T(8,128)(2,1)} %get-tuple-element.90.b_ref, ...), custom_call_target="tpu_custom_call" | custom-call | bytes 198000000 | tf_op jit(solution)/shard_map/gather_down_back/pallas_call | solution.py:1652
  410.9 0.0 reduce-scatter.5.cloned.1.call-start
  411.0 66.4 %scatter_post.1 = (f32[384,2048]{1,0:T(8,128)}, bf16[4,4,256,768]{3,2,1,0:T(8,128)(2,1)}) custom-call(bf16[3072,1536]{1,0:T(8,128)(2,1)} %get-tuple-element.91.d_any, bf16[2,2048,768]{2,1,0:T(8,128)(2,1)} %get-tuple-element.92.w_any, bf16[8,384,2048]{2,1,0:T(8,128)(2,1)} %get-tuple-element.93.all_ref), custom_call_target="tpu_custom_call" | custom-call | bytes 198000000 | tf_op jit(solution)/shard_map/scatter_post/pallas_call | solution.py:2064
  477.5 34.6 %mix_back.1 = (bf16[3072,256]{1,0:T(8,128)(2,1)}, f32[384,2048]{1,0:T(8,128)}, f32[1,2048]{1,0:T(1,128)}, bf16[2048,256]{1,0:T(8,128)(2,1)}, bf16[2048,256]{1,0:...) custom-call(f32[384,2048]{1,0:T(8,128)} %get-tuple-element.94.post_ref, ...), custom_call_target="tpu_custom_call" | custom-call | bytes 78000000 | tf_op jit(solution)/shard_map/mix_back/pallas_call | solution.py:1923
  512.1 1.0 collective-permute-start.3
  513.1 1.0 collective-permute-start.4
  514.2 1.5 collective-permute-start.5
  515.6 0.6 reduce_sum.29
  516.9 57.8 %attend_back.1 = (bf16[3072,256]{1,0:T(8,128)(2,1)}, bf16[3072,256]{1,0:T(8,128)(2,1)}, bf16[3072,256]{1,0:T(8,128)(2,1)}, bf16[3072,256]{1,0:T(8,128)(2,1)}) custom-call(s32[3,16]{1,0:T(4,128)} %order_ref.3, s32[3]{0:T(128)} %lens_ref.3, bf16[3072,256]{1,0:T(8,128)(2,1)} %get-tuple-element.74.q_ref, bf16[3072,256]{1,0:T(8,128)(2,1)} %get-tuple-element.99.do_ref, ...), custom_call_target="tpu_custom_call" | custom-call | bytes 225000000 | tf_op jit(solution)/shard_map/attend_back/pallas_call | solution.py:2701
  574.8 3.3 add_convert_fusion
  578.1 8.1 %reduce-scatter.5.cloned.1.call-done = bf16[1,4,256,768]{3,2,1,0:T(8,128)(2,1)} async-done(((bf16[4,4,256,768]{3,2,1,0:T(8,128)(2,1)}), bf16[1,4,256,768]{3,2,1,0:T(8,128)(2,1)}) %reduce-scatter.5.cloned.1.call-update) | async-done | bytes 1572880 | tf_op jit(solution)/shard_map/reduce_scatter | solution.py:2805
  586.2 113.2 %scatter_normed.1 = (bf16[384,2048]{1,0:T(8,128)(2,1)}, f32[2,2,256,256]{3,2,1,0:T(8,128)}, f32[40,128]{1,0:T(8,128)}, bf16[4,256,768]{2,1,0:T(8,128)(2,1)}, f32[512,256]{1,0:T(8,128)}) custom-call(bf16[3072,256]{1,0:T(8,128)(2,1)} %get-tuple-element.101.dq_ref, bf16[3072,256]{1,0:T(8,128)(2,1)} %get-tuple-element.102.dkv_ref, ...), custom_call_target="tpu_custom_call" | custom-call | bytes 330000000 | tf_op jit(solution)/shard_map/scatter_normed/pallas_call | solution.py:2353
  699.4 1.3 slice_bitcast_fusion
  700.8 1.9 slice_bitcast_fusion.2
  703.4 9.2 %finish.1 = (bf16[384,2048]{1,0:T(8,128)(2,1)}, f32[256,1536]{1,0:T(8,128)}, f32[256,1536]{1,0:T(8,128)}, f32[4,384,256]{2,1,0:T(8,128)}, f32[256,512]{1,0:T(8,1...) custom-call(bf16[384,2048]{1,0:T(8,128)(2,1)} %get-tuple-element.120.d_ref, ...), custom_call_target="tpu_custom_call" | custom-call | bytes 24000000 | tf_op jit(solution)/shard_map/finish/pallas_call | solution.py:2468
  712.6 1.1 copy.48
  (46 shorter events, 0.4 us)
Async XLA Ops:
  7.2 1.7 copy-start
  7.2 210.8 %all-gather.5.cloned.1.call-start = ((), (), s32[]{:S(2)}) async-start(), calls=%async_computation.4 | async-start | bytes 4915200 | tf_op jit(solution)/shard_map/all_gather | solution.py:2795
  8.9 2.8 copy-start.3
  8.9 3.2 copy-start.7
  9.7 2.6 copy-start.8
  9.7 2.8 copy-start.9
  9.7 3.1 copy-start.10
  128.4 13.7 %copy-start.1 = (s32[3]{0:T(128)S(1)}, s32[3]{0:T(128)}, u32[]{:S(2)}) copy-start(s32[3]{0:T(128)} %lens_ref.3) | copy-start | bytes 40
  128.4 153.2 %all-gather.7.cloned.1.call-start = ((), (), s32[]{:S(2)}) async-start(), calls=%async_computation.5 | async-start | bytes 3932160 | tf_op jit(solution)/shard_map/all_gather | solution.py:2797
  129.2 348.3 %reduce-scatter.3.cloned.1.call-start = ((), (), s32[]{:S(2)}) async-start(), calls=%async_computation.2 | async-start | bytes 3932160 | tf_op jit(solution)/shard_map/reduce_scatter | solution.py:2805
  129.2 48.9 %collective-permute-start = (bf16[2048,256]{1,0:T(8,128)(2,1)}, bf16[2048,256]{1,0:T(8,128)(2,1)S(1)}, u32[]{:S(2)}, u32[]{:S(2)}) collective-permute-start(bf16[2048,256]{1,0:T(8,128)(2,1)} %bitcast.44), channel_id=1, source_target_pairs={{0,8},{4,12},{8,0},{12,4},{16,24},{20,28},{24,16},{28,20},{1,9},{5... | collective-permute-start | bytes 3145736 | tf_op jit(solution)/shard_map/ppermute | solution.py:2794
  129.9 56.1 %collective-permute-start.1 = (bf16[2048,256]{1,0:T(8,128)(2,1)}, bf16[2048,256]{1,0:T(8,128)(2,1)}, u32[]{:S(2)}, u32[]{:S(2)}) collective-permute-start(bf16[2048,256]{1,0:T(8,128)(2,1)} %bitcast.45), channel_id=1, source_target_pairs={{0,16},{4,20},{8,24},{12,28},{16,0},{20,4},{24,8},{28,12},{1,17},{... | collective-permute-start | bytes 3145736 | tf_op jit(solution)/shard_map/ppermute | solution.py:2794
  142.0 43.9 %collective-permute-start.2 = (bf16[2048,256]{1,0:T(8,128)(2,1)}, bf16[2048,256]{1,0:T(8,128)(2,1)}, u32[]{:S(2)}, u32[]{:S(2)}) collective-permute-start(bf16[2048,256]{1,0:T(8,128)(2,1)} %bitcast.46), channel_id=1, source_target_pairs={{0,24},{4,28},{8,16},{12,20},{16,8},{20,12},{24,0},{28,4},{1,25},{... | collective-permute-start | bytes 3145736 | tf_op jit(solution)/shard_map/ppermute | solution.py:2794
  178.2 7.8 %copy-start.6 = (bf16[2048,256]{1,0:T(8,128)(2,1)}, bf16[2048,256]{1,0:T(8,128)(2,1)S(1)}, u32[]{:S(2)}) copy-start(bf16[2048,256]{1,0:T(8,128)(2,1)S(1)} %collective-permute-done.w1_ref) | copy-start | bytes 3145732
  410.9 175.3 %reduce-scatter.5.cloned.1.call-start = ((), (), s32[]{:S(2)}) async-start(), calls=%async_computation.3 | async-start | bytes 7864320 | tf_op jit(solution)/shard_map/reduce_scatter | solution.py:2805
  477.5 38.2 %copy-start.2 = (s32[3]{0:T(128)S(1)}, s32[3]{0:T(128)}, u32[]{:S(2)}) copy-start(s32[3]{0:T(128)} %lens_ref.3) | copy-start | bytes 40
  512.1 62.7 %collective-permute-start.3 = (bf16[2048,256]{1,0:T(8,128)(2,1)}, bf16[2048,256]{1,0:T(8,128)(2,1)}, u32[]{:S(2)}, u32[]{:S(2)}) collective-permute-start(bf16[2048,256]{1,0:T(8,128)(2,1)} %get-tuple-element.111), channel_id=1, source_target_pairs={{0,8},{4,12},{8,0},{12,4},{16,24},{20,28},{24,16},{28,20},{1,9},{5... | collective-permute-start | bytes 3145736 | tf_op jit(solution)/shard_map/ppermute | solution.py:2813
  513.1 61.6 %collective-permute-start.4 = (bf16[2048,256]{1,0:T(8,128)(2,1)}, bf16[2048,256]{1,0:T(8,128)(2,1)}, u32[]{:S(2)}, u32[]{:S(2)}) collective-permute-start(bf16[2048,256]{1,0:T(8,128)(2,1)} %get-tuple-element.113), channel_id=1, source_target_pairs={{0,16},{4,20},{8,24},{12,28},{16,0},{20,4},{24,8},{28,12},{1,17},{... | collective-permute-start | bytes 3145736 | tf_op jit(solution)/shard_map/ppermute | solution.py:2813
  514.2 60.6 %collective-permute-start.5 = (bf16[2048,256]{1,0:T(8,128)(2,1)}, bf16[2048,256]{1,0:T(8,128)(2,1)}, u32[]{:S(2)}, u32[]{:S(2)}) collective-permute-start(bf16[2048,256]{1,0:T(8,128)(2,1)} %get-tuple-element.115), channel_id=1, source_target_pairs={{0,24},{4,28},{8,16},{12,20},{16,8},{20,12},{24,0},{28,4},{1,25},{... | collective-permute-start | bytes 3145736 | tf_op jit(solution)/shard_map/ppermute | solution.py:2813
  516.9 57.9 %copy-start.5 = (bf16[2048,256]{1,0:T(8,128)(2,1)S(1)}, bf16[2048,256]{1,0:T(8,128)(2,1)}, u32[]{:S(2)}) copy-start(bf16[2048,256]{1,0:T(8,128)(2,1)} %get-tuple-element.110) | copy-start | bytes 3145732
  703.4 9.2 %copy-start.4 = (bf16[384,2048]{1,0:T(8,128)(2,1)S(1)}, bf16[384,2048]{1,0:T(8,128)(2,1)}, u32[]{:S(2)}) copy-start(bf16[384,2048]{1,0:T(8,128)(2,1)} %get-tuple-element.161) | copy-start | bytes 4718596
Sparse Core Ops, SparseCore 0:
  128.6 89.3 all-gather.4
  219.5 62.0 all-gather.6
  411.0 58.0 reduce-scatter.2
  477.6 108.5 reduce-scatter.4

commit v6 on v5

--- a/solution.py
+++ b/solution.py
@@ -1088,7 +1088,6 @@
     gate_swap.start()
     slabs.start()
     ring.start()
-    outs.start()
     slabs.own().wait()
     hand_out(slabs.plane)
     slabs.arrive(1, hand_out)
@@ -1096,12 +1095,12 @@
     gates.start()
     keep_last = pltpu.make_async_copy(gate_part.at[3], ups_ref.at[4], sems[18])
     keep_last.start()
+    slabs.arrive(2, hand_out)
+    outs.start()
     ring.pass_on(0)
-    ring.pass_on(1)
-    slabs.arrive(2, hand_out)
-    ring.pass_on(2)
-    ring.pass_on(3)
     slabs.arrive(3, hand_out)
+    for i in range(1, SUBS):
+        ring.pass_on(i)
     for swap in late_swaps:
         swap.start()
     outs.arrive(1)

time: 728 us -> 719 us (0.988)
  starting transfers between devices: 16.5 us -> 7.27 us
    ppermute x3, starting transfers between devices: 12.8 us -> 3.55 us  [local_plane(): lax.ppermute(out_part, 'ctx', [(i, i ^ n) for i in range(8)])]
  transfers between devices with their start and end apart: 10 -> 10, of which waited for: 4 -> 5; matrix products, arithmetic and copies ran while one was open for 1% -> 1% of each run, Pallas kernels for 40% -> 40%
where the time goes in v6:
time: 719 us; the launch traced here: 713 us
  Pallas kernels  649 us (90%)
  waiting for transfers between devices  22.7 us (3%)
  between operations  16.8 us (2%)
  other arithmetic  10.6 us (1%)
  starting transfers between devices  7.27 us (1%)
    pallas_call x1, Pallas kernels, gather_qkv(): pl.pallas_call(qkv_kernel, out_shape=(jax.ShapeDtypeStruct((8, rows, widt...  114 us
    pallas_call x1, Pallas kernels, scatter_normed(): pl.pallas_call(normed_back_kernel, out_shape=(jax.ShapeDtypeStruct((rows,...  113 us
    pallas_call x1, Pallas kernels, scatter_post(): pl.pallas_call(post_back_kernel, out_shape=(jax.ShapeDtypeStruct((rows, w...  66.4 us
    pallas_call x1, Pallas kernels, scatter_down(): pl.pallas_call(down_kernel, out_shape=(low, low, jax.ShapeDtypeStruct((ro...  66.3 us
    pallas_call x1, Pallas kernels, gather_down_back(): pl.pallas_call(down_back_kernel, out_shape=(jax.ShapeDtypeStruct((8 * row...  63 us
    pallas_call x1, Pallas kernels, gather_up(): pl.pallas_call(up_kernel, out_shape=(jax.ShapeDtypeStruct((8, rows, width...  61.5 us
    pallas_call x1, Pallas kernels, attend_back(): pl.pallas_call(attend_back_kernel, out_shape=(flat,) * 4, in_specs=[spec_...  55.8 us
    pallas_call x1, Pallas kernels, mix_back(): pl.pallas_call(mix_back_kernel, out_shape=(jax.ShapeDtypeStruct((8 * rows...  34.6 us
  transfers between devices with their start and end apart: 10, of which 5 were waited for; matrix products, arithmetic and copies ran while one was open for 1% of the time, Pallas kernels for 40%

profile of v6, /device:TPU:0, one launch (start us, length us, event | category | flops | bytes accessed | tf_op | source)
XLA Modules:
  0.0 713.2 jit_solution(2361755655899689915)
XLA Ops:
  7.3 1.3 gather_fusion.1
  8.7 0.1 fusion.7
  8.8 0.1 reshape.422
  8.9 0.8 gather_fusion
  9.7 0.1 reshape.445
  9.8 0.1 convert_element_type.50
  9.9 0.1 pad_maximum_fusion
  10.0 0.9 fusion.3
  10.9 0.7 multiply_sine_fusion
  11.6 0.4 fusion
  12.0 0.1 copy.36
  12.2 0.1 copy.39
  12.3 0.1 copy.37
  12.4 0.1 copy.40
  12.6 0.1 copy.38
  12.7 0.1 copy.41
  12.8 1.6 fusion.2.x_ref
  14.4 0.8 maximum_bitcast_fusion.home_ref
  15.2 114.0 %gather_qkv.1 = (bf16[8,384,2048]{2,1,0:T(8,128)(2,1)}, bf16[2048,512]{1,0:T(8,128)(2,1)}, bf16[3072,256]{1,0:T(8,128)(2,1)}, bf16[3072,256]{1,0:T(8,128)(2,1)},...) custom-call(bf16[384,2048]{1,0:T(8,128)(2,1)} %fusion.2.x_ref, ...), custom_call_target="tpu_custom_call" | custom-call | bytes 300000000 | tf_op jit(solution)/shard_map/gather_qkv/pallas_call | solution.py:1183
  129.3 0.7 all-gather.7.cloned.1.call-update
  130.1 1.5 collective-permute-start
  131.6 1.7 collective-permute-start.1
  133.3 0.3 collective-permute-start.2
  133.7 0.6 gather_fusion.2
  134.4 0.8 copy.44
  135.2 33.5 %attend.1 = (bf16[3072,256]{1,0:T(8,128)(2,1)}, f32[24,8,256]{2,1,0:T(8,128)}) custom-call(s32[3,16]{1,0:T(4,128)} %order_ref.3, s32[3]{0:T(128)} %lens_ref.3, bf16[3072,256]{1,0:T(8,128)(2,1)} %get-tuple-element.74.q_ref, bf16[3072,256]{1,0:T(8,128)(2,1)} %get-tuple-element.75.lo_ref, bf16[3072,256]{1,0:T(8,128)(2,1)} %get-tuple-element.76.own_ref, ...), custom_call_target="tpu_custom_call" | custom-call | bytes 150000000 | tf_op jit(solution)/shard_map/attend/pallas_call | solution.py:2599
  168.7 8.2 %collective-permute-done.1.w2_ref = bf16[2048,256]{1,0:T(8,128)(2,1)} collective-permute-done((bf16[2048,256]{1,0:T(8,128)(2,1)}, bf16[2048,256]{1,0:T(8,128)(2,1)}, u32[]{:S(2)}, u32[]{:S(2)}) %collective-permute-start.1) | collective-permute-done | bytes 1048608 | tf_op jit(solution)/shard_map/ppermute | solution.py:2793
  176.9 0.4 collective-permute-done.2.w3_ref
  177.3 31.2 %mix.1 = (f32[384,2048]{1,0:T(8,128)}, bf16[384,2048]{1,0:T(8,128)(2,1)}, bf16[384,2048]{1,0:T(8,128)(2,1)}, bf16[2048,2048]{1,0:T(8,128)(2,1)}) custom-call(bf16[3072,256]{1,0:T(8,128)(2,1)} %get-tuple-element.78.mixed_ref.o_ref, bf16[384,2048]{1,0:T(8,128)(2,1)} %tokens_ref.5, f32[1,2048]{1,0:T(1,128)} %bitcast.54, bf16[2048,256]{1,0:T(8,128)(2,1)} %bitcast.47, ...), custom_call_target="tpu_custom_call" | custom-call | bytes 84000000 | tf_op jit(solution)/shard_map/mix/pallas_call | solution.py:1769
  208.5 1.0 all-gather.5.cloned.1.call-done
  209.5 61.5 %gather_up.1 = (bf16[8,384,2048]{2,1,0:T(8,128)(2,1)}, bf16[2,2048,768]{2,1,0:T(8,128)(2,1)}, bf16[3072,768]{1,0:T(8,128)(2,1)}, bf16[3072,768]{1,0:T(8,128)(2,1)}, bf16[3072,768]{1,0:T(8,128)(2,1)}) custom-call(bf16[384,2048]{1,0:T(8,128)(2,1)} %get-tuple-element.80.x_ref, bf16[4,3,256,384]{3,2,1,0:T(8,128)(2,1)} %get-tuple-element.81.gate_ref, ...), custom_call_target="tpu_custom_call" | custom-call | bytes 186000000 | tf_op jit(solution)/shard_map/gather_up/pallas_call | solution.py:1403
  271.0 2.2 all-gather.7.cloned.1.call-done
  273.2 66.3 %scatter_down.1 = (bf16[384,2048]{1,0:T(8,128)(2,1)}, bf16[384,2048]{1,0:T(8,128)(2,1)}, f32[384,2048]{1,0:T(8,128)}, f32[1,128]{1,0:T(1,128)}, bf16[768,2048]{1,0:T(8,128)(2,1)}) custom-call(bf16[3072,768]{1,0:T(8,128)(2,1)} %get-tuple-element.83.h_any.h_ref, bf16[4,4,384,256]{3,2,1,0:T(8,128)(2,1)} %bitcast.41, ...), custom_call_target="tpu_custom_call" | custom-call | bytes 186000000 | tf_op jit(solution)/shard_map/scatter_down/pallas_call | solution.py:1494
  339.5 63.0 %gather_down_back.1 = (bf16[3072,1536]{1,0:T(8,128)(2,1)}, bf16[4,4,384,256]{3,2,1,0:T(8,128)(2,1)}) custom-call(bf16[384,2048]{1,0:T(8,128)(2,1)} %get-tuple-element.87.x_ref, bf16[768,2048]{1,0:T(8,128)(2,1)} %get-tuple-element.88.w_ref, bf16[3072,768]{1,0:T(8,128)(2,1)} %get-tuple-element.89.a_ref, bf16[3072,768]{1,0:T(8,128)(2,1)} %get-tuple-element.90.b_ref, ...), custom_call_target="tpu_custom_call" | custom-call | bytes 198000000 | tf_op jit(solution)/shard_map/gather_down_back/pallas_call | solution.py:1651
  402.6 66.4 %scatter_post.1 = (f32[384,2048]{1,0:T(8,128)}, bf16[4,4,256,768]{3,2,1,0:T(8,128)(2,1)}) custom-call(bf16[3072,1536]{1,0:T(8,128)(2,1)} %get-tuple-element.91.d_any, bf16[2,2048,768]{2,1,0:T(8,128)(2,1)} %get-tuple-element.92.w_any, bf16[8,384,2048]{2,1,0:T(8,128)(2,1)} %get-tuple-element.93.all_ref), custom_call_target="tpu_custom_call" | custom-call | bytes 198000000 | tf_op jit(solution)/shard_map/scatter_post/pallas_call | solution.py:2063
  469.1 34.6 %mix_back.1 = (bf16[3072,256]{1,0:T(8,128)(2,1)}, f32[384,2048]{1,0:T(8,128)}, f32[1,2048]{1,0:T(1,128)}, bf16[2048,256]{1,0:T(8,128)(2,1)}, bf16[2048,256]{1,0:...) custom-call(f32[384,2048]{1,0:T(8,128)} %get-tuple-element.94.post_ref, ...), custom_call_target="tpu_custom_call" | custom-call | bytes 78000000 | tf_op jit(solution)/shard_map/mix_back/pallas_call | solution.py:1922
  503.6 1.1 collective-permute-start.3
  504.7 1.0 collective-permute-start.4
  505.7 1.5 collective-permute-start.5
  507.2 0.6 reduce_sum.29
  508.5 55.8 %attend_back.1 = (bf16[3072,256]{1,0:T(8,128)(2,1)}, bf16[3072,256]{1,0:T(8,128)(2,1)}, bf16[3072,256]{1,0:T(8,128)(2,1)}, bf16[3072,256]{1,0:T(8,128)(2,1)}) custom-call(s32[3,16]{1,0:T(4,128)} %order_ref.3, s32[3]{0:T(128)} %lens_ref.3, bf16[3072,256]{1,0:T(8,128)(2,1)} %get-tuple-element.74.q_ref, bf16[3072,256]{1,0:T(8,128)(2,1)} %get-tuple-element.99.do_ref, ...), custom_call_target="tpu_custom_call" | custom-call | bytes 225000000 | tf_op jit(solution)/shard_map/attend_back/pallas_call | solution.py:2700
  564.3 3.3 add_convert_fusion
  567.6 10.2 %reduce-scatter.5.cloned.1.call-done = bf16[1,4,256,768]{3,2,1,0:T(8,128)(2,1)} async-done(((bf16[4,4,256,768]{3,2,1,0:T(8,128)(2,1)}), bf16[1,4,256,768]{3,2,1,0:T(8,128)(2,1)}) %reduce-scatter.5.cloned.1.call-update) | async-done | bytes 1572880 | tf_op jit(solution)/shard_map/reduce_scatter | solution.py:2804
  577.8 113.2 %scatter_normed.1 = (bf16[384,2048]{1,0:T(8,128)(2,1)}, f32[2,2,256,256]{3,2,1,0:T(8,128)}, f32[40,128]{1,0:T(8,128)}, bf16[4,256,768]{2,1,0:T(8,128)(2,1)}, f32[512,256]{1,0:T(8,128)}) custom-call(bf16[3072,256]{1,0:T(8,128)(2,1)} %get-tuple-element.101.dq_ref, bf16[3072,256]{1,0:T(8,128)(2,1)} %get-tuple-element.102.dkv_ref, ...), custom_call_target="tpu_custom_call" | custom-call | bytes 330000000 | tf_op jit(solution)/shard_map/scatter_normed/pallas_call | solution.py:2352
  691.0 1.3 slice_bitcast_fusion
  692.4 1.9 slice_bitcast_fusion.2
  695.0 9.2 %finish.1 = (bf16[384,2048]{1,0:T(8,128)(2,1)}, f32[256,1536]{1,0:T(8,128)}, f32[256,1536]{1,0:T(8,128)}, f32[4,384,256]{2,1,0:T(8,128)}, f32[256,512]{1,0:T(8,1...) custom-call(bf16[384,2048]{1,0:T(8,128)(2,1)} %get-tuple-element.120.d_ref, ...), custom_call_target="tpu_custom_call" | custom-call | bytes 24000000 | tf_op jit(solution)/shard_map/finish/pallas_call | solution.py:2467
  704.2 1.1 copy.48
  (46 shorter events, 0.5 us)
Async XLA Ops:
  7.2 1.7 copy-start
  7.2 202.3 %all-gather.5.cloned.1.call-start = ((), (), s32[]{:S(2)}) async-start(), calls=%async_computation.4 | async-start | bytes 4915200 | tf_op jit(solution)/shard_map/all_gather | solution.py:2794
  8.9 2.8 copy-start.3
  8.9 3.2 copy-start.7
  9.7 2.6 copy-start.8
  9.7 2.8 copy-start.9
  9.7 3.1 copy-start.10
  129.2 4.4 copy-start.1
  129.3 143.9 %all-gather.7.cloned.1.call-start = ((), (), s32[]{:S(2)}) async-start(), calls=%async_computation.5 | async-start | bytes 3932160 | tf_op jit(solution)/shard_map/all_gather | solution.py:2796
  130.0 339.0 %reduce-scatter.3.cloned.1.call-start = ((), (), s32[]{:S(2)}) async-start(), calls=%async_computation.2 | async-start | bytes 3932160 | tf_op jit(solution)/shard_map/reduce_scatter | solution.py:2804
  130.1 38.6 %collective-permute-start = (bf16[2048,256]{1,0:T(8,128)(2,1)}, bf16[2048,256]{1,0:T(8,128)(2,1)S(1)}, u32[]{:S(2)}, u32[]{:S(2)}) collective-permute-start(bf16[2048,256]{1,0:T(8,128)(2,1)} %bitcast.44), channel_id=1, source_target_pairs={{0,8},{4,12},{8,0},{12,4},{16,24},{20,28},{24,16},{28,20},{1,9},{5... | collective-permute-start | bytes 3145736 | tf_op jit(solution)/shard_map/ppermute | solution.py:2793
  131.6 45.3 %collective-permute-start.1 = (bf16[2048,256]{1,0:T(8,128)(2,1)}, bf16[2048,256]{1,0:T(8,128)(2,1)}, u32[]{:S(2)}, u32[]{:S(2)}) collective-permute-start(bf16[2048,256]{1,0:T(8,128)(2,1)} %bitcast.45), channel_id=1, source_target_pairs={{0,16},{4,20},{8,24},{12,28},{16,0},{20,4},{24,8},{28,12},{1,17},{... | collective-permute-start | bytes 3145736 | tf_op jit(solution)/shard_map/ppermute | solution.py:2793
  133.3 44.0 %collective-permute-start.2 = (bf16[2048,256]{1,0:T(8,128)(2,1)}, bf16[2048,256]{1,0:T(8,128)(2,1)}, u32[]{:S(2)}, u32[]{:S(2)}) collective-permute-start(bf16[2048,256]{1,0:T(8,128)(2,1)} %bitcast.46), channel_id=1, source_target_pairs={{0,24},{4,28},{8,16},{12,20},{16,8},{20,12},{24,0},{28,4},{1,25},{... | collective-permute-start | bytes 3145736 | tf_op jit(solution)/shard_map/ppermute | solution.py:2793
  168.7 8.6 %copy-start.6 = (bf16[2048,256]{1,0:T(8,128)(2,1)}, bf16[2048,256]{1,0:T(8,128)(2,1)S(1)}, u32[]{:S(2)}) copy-start(bf16[2048,256]{1,0:T(8,128)(2,1)S(1)} %collective-permute-done.w1_ref) | copy-start | bytes 3145732
  402.5 175.3 %reduce-scatter.5.cloned.1.call-start = ((), (), s32[]{:S(2)}) async-start(), calls=%async_computation.3 | async-start | bytes 7864320 | tf_op jit(solution)/shard_map/reduce_scatter | solution.py:2804
  469.1 38.1 %copy-start.2 = (s32[3]{0:T(128)S(1)}, s32[3]{0:T(128)}, u32[]{:S(2)}) copy-start(s32[3]{0:T(128)} %lens_ref.3) | copy-start | bytes 40
  503.6 60.6 %collective-permute-start.3 = (bf16[2048,256]{1,0:T(8,128)(2,1)}, bf16[2048,256]{1,0:T(8,128)(2,1)}, u32[]{:S(2)}, u32[]{:S(2)}) collective-permute-start(bf16[2048,256]{1,0:T(8,128)(2,1)} %get-tuple-element.111), channel_id=1, source_target_pairs={{0,8},{4,12},{8,0},{12,4},{16,24},{20,28},{24,16},{28,20},{1,9},{5... | collective-permute-start | bytes 3145736 | tf_op jit(solution)/shard_map/ppermute | solution.py:2812
  504.7 59.6 %collective-permute-start.4 = (bf16[2048,256]{1,0:T(8,128)(2,1)}, bf16[2048,256]{1,0:T(8,128)(2,1)}, u32[]{:S(2)}, u32[]{:S(2)}) collective-permute-start(bf16[2048,256]{1,0:T(8,128)(2,1)} %get-tuple-element.113), channel_id=1, source_target_pairs={{0,16},{4,20},{8,24},{12,28},{16,0},{20,4},{24,8},{28,12},{1,17},{... | collective-permute-start | bytes 3145736 | tf_op jit(solution)/shard_map/ppermute | solution.py:2812
  505.7 58.6 %collective-permute-start.5 = (bf16[2048,256]{1,0:T(8,128)(2,1)}, bf16[2048,256]{1,0:T(8,128)(2,1)}, u32[]{:S(2)}, u32[]{:S(2)}) collective-permute-start(bf16[2048,256]{1,0:T(8,128)(2,1)} %get-tuple-element.115), channel_id=1, source_target_pairs={{0,24},{4,28},{8,16},{12,20},{16,8},{20,12},{24,0},{28,4},{1,25},{... | collective-permute-start | bytes 3145736 | tf_op jit(solution)/shard_map/ppermute | solution.py:2812
  508.5 55.8 %copy-start.5 = (bf16[2048,256]{1,0:T(8,128)(2,1)S(1)}, bf16[2048,256]{1,0:T(8,128)(2,1)}, u32[]{:S(2)}) copy-start(bf16[2048,256]{1,0:T(8,128)(2,1)} %get-tuple-element.110) | copy-start | bytes 3145732
  695.0 9.2 %copy-start.4 = (bf16[384,2048]{1,0:T(8,128)(2,1)S(1)}, bf16[384,2048]{1,0:T(8,128)(2,1)}, u32[]{:S(2)}) copy-start(bf16[384,2048]{1,0:T(8,128)(2,1)} %get-tuple-element.161) | copy-start | bytes 4718596
Sparse Core Ops, SparseCore 0:
  129.4 80.0 all-gather.4
  211.1 62.0 all-gather.6
  402.6 58.0 reduce-scatter.2
  469.1 108.6 reduce-scatter.4

commit v7 on v6

--- a/solution.py
+++ b/solution.py
@@ -1074,7 +1074,8 @@
     )
 
     def hand_out(origin):
-        for k in range(2):
+        for first in range(2):
+            k = lax.rem(me + first, 2)
 
             @pl.when(2 * origin + k == me)
             def _():
@@ -2439,7 +2440,7 @@
 
 
 def finish(d_normed, tokens, d_middle, in_gain, gu, down, qkv, out):
-    steps = 8
+    steps = 4
 
     def piece(shape, axis):
         block = list(shape)

time: 719 us -> 723 us (level)
  transfers between devices with their start and end apart: 10 -> 10, of which waited for: 5 -> 3; matrix products, arithmetic and copies ran while one was open for 1% -> 1% of each run, Pallas kernels for 40% -> 40%
where the time goes in v7:
time: 723 us; the launch traced here: 717 us
  Pallas kernels  652 us (90%)
  waiting for transfers between devices  18.4 us (3%)
  between operations  16.8 us (2%)
  starting transfers between devices  12.1 us (2%)
  other arithmetic  10.6 us (1%)
    pallas_call x1, Pallas kernels, gather_qkv(): pl.pallas_call(qkv_kernel, out_shape=(jax.ShapeDtypeStruct((8, rows, widt...  114 us
    pallas_call x1, Pallas kernels, scatter_normed(): pl.pallas_call(normed_back_kernel, out_shape=(jax.ShapeDtypeStruct((rows,...  113 us
    pallas_call x1, Pallas kernels, scatter_post(): pl.pallas_call(post_back_kernel, out_shape=(jax.ShapeDtypeStruct((rows, w...  66.4 us
    pallas_call x1, Pallas kernels, scatter_down(): pl.pallas_call(down_kernel, out_shape=(low, low, jax.ShapeDtypeStruct((ro...  66.3 us
    pallas_call x1, Pallas kernels, gather_down_back(): pl.pallas_call(down_back_kernel, out_shape=(jax.ShapeDtypeStruct((8 * row...  63 us
    pallas_call x1, Pallas kernels, gather_up(): pl.pallas_call(up_kernel, out_shape=(jax.ShapeDtypeStruct((8, rows, width...  61 us
    pallas_call x1, Pallas kernels, attend_back(): pl.pallas_call(attend_back_kernel, out_shape=(flat,) * 4, in_specs=[spec_...  60.2 us
    pallas_call x1, Pallas kernels, attend(): pl.pallas_call(attend_kernel, out_shape=(jax.ShapeDtypeStruct(q.shape, BF...  35.7 us
  transfers between devices with their start and end apart: 10, of which 3 were waited for; matrix products, arithmetic and copies ran while one was open for 1% of the time, Pallas kernels for 40%

profile of v7, /device:TPU:0, one launch (start us, length us, event | category | flops | bytes accessed | tf_op | source)
XLA Modules:
  0.0 716.7 jit_solution(1207158445360037530)
XLA Ops:
  7.3 1.3 gather_fusion.1
  8.7 0.1 fusion.7
  8.8 0.1 reshape.422
  8.9 0.8 gather_fusion
  9.7 0.1 reshape.445
  9.8 0.1 convert_element_type.50
  9.9 0.1 pad_maximum_fusion
  10.0 0.9 fusion.3
  10.9 0.7 multiply_sine_fusion
  11.6 0.4 fusion
  12.0 0.1 copy.36
  12.2 0.1 copy.39
  12.3 0.1 copy.37
  12.4 0.1 copy.40
  12.6 0.1 copy.38
  12.7 0.1 copy.41
  12.8 1.6 fusion.2.x_ref
  14.4 0.8 maximum_bitcast_fusion.home_ref
  15.2 114.0 %gather_qkv.1 = (bf16[8,384,2048]{2,1,0:T(8,128)(2,1)}, bf16[2048,512]{1,0:T(8,128)(2,1)}, bf16[3072,256]{1,0:T(8,128)(2,1)}, bf16[3072,256]{1,0:T(8,128)(2,1)},...) custom-call(bf16[384,2048]{1,0:T(8,128)(2,1)} %fusion.2.x_ref, ...), custom_call_target="tpu_custom_call" | custom-call | bytes 300000000 | tf_op jit(solution)/shard_map/gather_qkv/pallas_call | solution.py:1184
  129.3 0.0 all-gather.7.cloned.1.call-start
  129.3 0.7 all-gather.7.cloned.1.call-update
  130.1 1.8 collective-permute-start
  131.9 6.5 collective-permute-start.1
  138.5 0.6 gather_fusion.2
  139.1 0.1 convert_bitcast_fusion
  139.2 0.8 copy.44
  140.1 35.7 %attend.1 = (bf16[3072,256]{1,0:T(8,128)(2,1)}, f32[24,8,256]{2,1,0:T(8,128)}) custom-call(s32[3,16]{1,0:T(4,128)} %order_ref.3, s32[3]{0:T(128)} %lens_ref.3, bf16[3072,256]{1,0:T(8,128)(2,1)} %get-tuple-element.74.q_ref, bf16[3072,256]{1,0:T(8,128)(2,1)} %get-tuple-element.75.lo_ref, bf16[3072,256]{1,0:T(8,128)(2,1)} %get-tuple-element.76.own_ref, ...), custom_call_target="tpu_custom_call" | custom-call | bytes 150000000 | tf_op jit(solution)/shard_map/attend/pallas_call | solution.py:2600
  175.7 8.3 %collective-permute-done.1.w2_ref = bf16[2048,256]{1,0:T(8,128)(2,1)} collective-permute-done((bf16[2048,256]{1,0:T(8,128)(2,1)}, bf16[2048,256]{1,0:T(8,128)(2,1)}, u32[]{:S(2)}, u32[]{:S(2)}) %collective-permute-start.1) | collective-permute-done | bytes 1048608 | tf_op jit(solution)/shard_map/ppermute | solution.py:2794
  184.0 29.6 %mix.1 = (f32[384,2048]{1,0:T(8,128)}, bf16[384,2048]{1,0:T(8,128)(2,1)}, bf16[384,2048]{1,0:T(8,128)(2,1)}, bf16[2048,2048]{1,0:T(8,128)(2,1)}) custom-call(bf16[3072,256]{1,0:T(8,128)(2,1)} %get-tuple-element.78.mixed_ref.o_ref, bf16[384,2048]{1,0:T(8,128)(2,1)} %tokens_ref.5, f32[1,2048]{1,0:T(1,128)} %bitcast.54, bf16[2048,256]{1,0:T(8,128)(2,1)} %bitcast.47, ...), custom_call_target="tpu_custom_call" | custom-call | bytes 84000000 | tf_op jit(solution)/shard_map/mix/pallas_call | solution.py:1770
  213.7 61.0 %gather_up.1 = (bf16[8,384,2048]{2,1,0:T(8,128)(2,1)}, bf16[2,2048,768]{2,1,0:T(8,128)(2,1)}, bf16[3072,768]{1,0:T(8,128)(2,1)}, bf16[3072,768]{1,0:T(8,128)(2,1)}, bf16[3072,768]{1,0:T(8,128)(2,1)}) custom-call(bf16[384,2048]{1,0:T(8,128)(2,1)} %get-tuple-element.80.x_ref, bf16[4,3,256,384]{3,2,1,0:T(8,128)(2,1)} %get-tuple-element.81.gate_ref, ...), custom_call_target="tpu_custom_call" | custom-call | bytes 186000000 | tf_op jit(solution)/shard_map/gather_up/pallas_call | solution.py:1404
  274.7 2.2 all-gather.7.cloned.1.call-done
  276.9 66.3 %scatter_down.1 = (bf16[384,2048]{1,0:T(8,128)(2,1)}, bf16[384,2048]{1,0:T(8,128)(2,1)}, f32[384,2048]{1,0:T(8,128)}, f32[1,128]{1,0:T(1,128)}, bf16[768,2048]{1,0:T(8,128)(2,1)}) custom-call(bf16[3072,768]{1,0:T(8,128)(2,1)} %get-tuple-element.83.h_any.h_ref, bf16[4,4,384,256]{3,2,1,0:T(8,128)(2,1)} %bitcast.41, ...), custom_call_target="tpu_custom_call" | custom-call | bytes 186000000 | tf_op jit(solution)/shard_map/scatter_down/pallas_call | solution.py:1495
  343.1 63.0 %gather_down_back.1 = (bf16[3072,1536]{1,0:T(8,128)(2,1)}, bf16[4,4,384,256]{3,2,1,0:T(8,128)(2,1)}) custom-call(bf16[384,2048]{1,0:T(8,128)(2,1)} %get-tuple-element.87.x_ref, bf16[768,2048]{1,0:T(8,128)(2,1)} %get-tuple-element.88.w_ref, bf16[3072,768]{1,0:T(8,128)(2,1)} %get-tuple-element.89.a_ref, bf16[3072,768]{1,0:T(8,128)(2,1)} %get-tuple-element.90.b_ref, ...), custom_call_target="tpu_custom_call" | custom-call | bytes 198000000 | tf_op jit(solution)/shard_map/gather_down_back/pallas_call | solution.py:1652
  406.2 0.0 reduce-scatter.5.cloned.1.call-start
  406.2 66.4 %scatter_post.1 = (f32[384,2048]{1,0:T(8,128)}, bf16[4,4,256,768]{3,2,1,0:T(8,128)(2,1)}) custom-call(bf16[3072,1536]{1,0:T(8,128)(2,1)} %get-tuple-element.91.d_any, bf16[2,2048,768]{2,1,0:T(8,128)(2,1)} %get-tuple-element.92.w_any, bf16[8,384,2048]{2,1,0:T(8,128)(2,1)} %get-tuple-element.93.all_ref), custom_call_target="tpu_custom_call" | custom-call | bytes 198000000 | tf_op jit(solution)/shard_map/scatter_post/pallas_call | solution.py:2064
  472.7 34.6 %mix_back.1 = (bf16[3072,256]{1,0:T(8,128)(2,1)}, f32[384,2048]{1,0:T(8,128)}, f32[1,2048]{1,0:T(1,128)}, bf16[2048,256]{1,0:T(8,128)(2,1)}, bf16[2048,256]{1,0:...) custom-call(f32[384,2048]{1,0:T(8,128)} %get-tuple-element.94.post_ref, ...), custom_call_target="tpu_custom_call" | custom-call | bytes 78000000 | tf_op jit(solution)/shard_map/mix_back/pallas_call | solution.py:1923
  507.3 1.0 collective-permute-start.3
  508.3 1.0 collective-permute-start.4
  509.4 1.5 collective-permute-start.5
  510.9 0.6 reduce_sum.29
  512.2 60.2 %attend_back.1 = (bf16[3072,256]{1,0:T(8,128)(2,1)}, bf16[3072,256]{1,0:T(8,128)(2,1)}, bf16[3072,256]{1,0:T(8,128)(2,1)}, bf16[3072,256]{1,0:T(8,128)(2,1)}) custom-call(s32[3,16]{1,0:T(4,128)} %order_ref.3, s32[3]{0:T(128)} %lens_ref.3, bf16[3072,256]{1,0:T(8,128)(2,1)} %get-tuple-element.74.q_ref, bf16[3072,256]{1,0:T(8,128)(2,1)} %get-tuple-element.99.do_ref, ...), custom_call_target="tpu_custom_call" | custom-call | bytes 225000000 | tf_op jit(solution)/shard_map/attend_back/pallas_call | solution.py:2701
  572.4 3.3 add_convert_fusion
  575.7 7.2 reduce-scatter.5.cloned.1.call-done
  582.9 113.2 %scatter_normed.1 = (bf16[384,2048]{1,0:T(8,128)(2,1)}, f32[2,2,256,256]{3,2,1,0:T(8,128)}, f32[40,128]{1,0:T(8,128)}, bf16[4,256,768]{2,1,0:T(8,128)(2,1)}, f32[512,256]{1,0:T(8,128)}) custom-call(bf16[3072,256]{1,0:T(8,128)(2,1)} %get-tuple-element.101.dq_ref, bf16[3072,256]{1,0:T(8,128)(2,1)} %get-tuple-element.102.dkv_ref, ...), custom_call_target="tpu_custom_call" | custom-call | bytes 330000000 | tf_op jit(solution)/shard_map/scatter_normed/pallas_call | solution.py:2353
  696.2 1.3 slice_bitcast_fusion
  697.5 1.9 slice_bitcast_fusion.2
  700.1 7.6 %finish.1 = (bf16[384,2048]{1,0:T(8,128)(2,1)}, f32[256,1536]{1,0:T(8,128)}, f32[256,1536]{1,0:T(8,128)}, f32[4,384,256]{2,1,0:T(8,128)}, f32[256,512]{1,0:T(8,1...) custom-call(bf16[384,2048]{1,0:T(8,128)(2,1)} %get-tuple-element.120.d_ref, ...), custom_call_target="tpu_custom_call" | custom-call | bytes 24000000 | tf_op jit(solution)/shard_map/finish/pallas_call | solution.py:2468
  707.7 1.1 copy.48
  (46 shorter events, 0.4 us)
Async XLA Ops:
  7.2 1.7 copy-start
  7.2 206.5 %all-gather.5.cloned.1.call-start = ((), (), s32[]{:S(2)}) async-start(), calls=%async_computation.4 | async-start | bytes 4915200 | tf_op jit(solution)/shard_map/all_gather | solution.py:2795
  8.9 2.8 copy-start.3
  8.9 3.2 copy-start.7
  9.7 2.6 copy-start.8
  9.7 2.8 copy-start.9
  9.7 3.1 copy-start.10
  129.2 9.2 %copy-start.1 = (s32[3]{0:T(128)S(1)}, s32[3]{0:T(128)}, u32[]{:S(2)}) copy-start(s32[3]{0:T(128)} %lens_ref.3) | copy-start | bytes 40
  129.3 147.6 %all-gather.7.cloned.1.call-start = ((), (), s32[]{:S(2)}) async-start(), calls=%async_computation.5 | async-start | bytes 3932160 | tf_op jit(solution)/shard_map/all_gather | solution.py:2797
  130.0 342.7 %reduce-scatter.3.cloned.1.call-start = ((), (), s32[]{:S(2)}) async-start(), calls=%async_computation.2 | async-start | bytes 3932160 | tf_op jit(solution)/shard_map/reduce_scatter | solution.py:2805
  130.1 45.6 %collective-permute-start = (bf16[2048,256]{1,0:T(8,128)(2,1)}, bf16[2048,256]{1,0:T(8,128)(2,1)S(1)}, u32[]{:S(2)}, u32[]{:S(2)}) collective-permute-start(bf16[2048,256]{1,0:T(8,128)(2,1)} %bitcast.44), channel_id=1, source_target_pairs={{0,8},{4,12},{8,0},{12,4},{16,24},{20,28},{24,16},{28,20},{1,9},{5... | collective-permute-start | bytes 3145736 | tf_op jit(solution)/shard_map/ppermute | solution.py:2794
  131.9 52.1 %collective-permute-start.1 = (bf16[2048,256]{1,0:T(8,128)(2,1)}, bf16[2048,256]{1,0:T(8,128)(2,1)}, u32[]{:S(2)}, u32[]{:S(2)}) collective-permute-start(bf16[2048,256]{1,0:T(8,128)(2,1)} %bitcast.45), channel_id=1, source_target_pairs={{0,16},{4,20},{8,24},{12,28},{16,0},{20,4},{24,8},{28,12},{1,17},{... | collective-permute-start | bytes 3145736 | tf_op jit(solution)/shard_map/ppermute | solution.py:2794
  138.5 45.6 %collective-permute-start.2 = (bf16[2048,256]{1,0:T(8,128)(2,1)}, bf16[2048,256]{1,0:T(8,128)(2,1)}, u32[]{:S(2)}, u32[]{:S(2)}) collective-permute-start(bf16[2048,256]{1,0:T(8,128)(2,1)} %bitcast.46), channel_id=1, source_target_pairs={{0,24},{4,28},{8,16},{12,20},{16,8},{20,12},{24,0},{28,4},{1,25},{... | collective-permute-start | bytes 3145736 | tf_op jit(solution)/shard_map/ppermute | solution.py:2794
  175.7 8.3 %copy-start.6 = (bf16[2048,256]{1,0:T(8,128)(2,1)}, bf16[2048,256]{1,0:T(8,128)(2,1)S(1)}, u32[]{:S(2)}) copy-start(bf16[2048,256]{1,0:T(8,128)(2,1)S(1)} %collective-permute-done.w1_ref) | copy-start | bytes 3145732
  406.2 176.7 %reduce-scatter.5.cloned.1.call-start = ((), (), s32[]{:S(2)}) async-start(), calls=%async_computation.3 | async-start | bytes 7864320 | tf_op jit(solution)/shard_map/reduce_scatter | solution.py:2805
  472.7 38.2 %copy-start.2 = (s32[3]{0:T(128)S(1)}, s32[3]{0:T(128)}, u32[]{:S(2)}) copy-start(s32[3]{0:T(128)} %lens_ref.3) | copy-start | bytes 40
  507.3 65.1 %collective-permute-start.3 = (bf16[2048,256]{1,0:T(8,128)(2,1)}, bf16[2048,256]{1,0:T(8,128)(2,1)}, u32[]{:S(2)}, u32[]{:S(2)}) collective-permute-start(bf16[2048,256]{1,0:T(8,128)(2,1)} %get-tuple-element.111), channel_id=1, source_target_pairs={{0,8},{4,12},{8,0},{12,4},{16,24},{20,28},{24,16},{28,20},{1,9},{5... | collective-permute-start | bytes 3145736 | tf_op jit(solution)/shard_map/ppermute | solution.py:2813
  508.3 64.0 %collective-permute-start.4 = (bf16[2048,256]{1,0:T(8,128)(2,1)}, bf16[2048,256]{1,0:T(8,128)(2,1)}, u32[]{:S(2)}, u32[]{:S(2)}) collective-permute-start(bf16[2048,256]{1,0:T(8,128)(2,1)} %get-tuple-element.113), channel_id=1, source_target_pairs={{0,16},{4,20},{8,24},{12,28},{16,0},{20,4},{24,8},{28,12},{1,17},{... | collective-permute-start | bytes 3145736 | tf_op jit(solution)/shard_map/ppermute | solution.py:2813
  509.4 63.0 %collective-permute-start.5 = (bf16[2048,256]{1,0:T(8,128)(2,1)}, bf16[2048,256]{1,0:T(8,128)(2,1)}, u32[]{:S(2)}, u32[]{:S(2)}) collective-permute-start(bf16[2048,256]{1,0:T(8,128)(2,1)} %get-tuple-element.115), channel_id=1, source_target_pairs={{0,24},{4,28},{8,16},{12,20},{16,8},{20,12},{24,0},{28,4},{1,25},{... | collective-permute-start | bytes 3145736 | tf_op jit(solution)/shard_map/ppermute | solution.py:2813
  512.1 60.2 %copy-start.5 = (bf16[2048,256]{1,0:T(8,128)(2,1)S(1)}, bf16[2048,256]{1,0:T(8,128)(2,1)}, u32[]{:S(2)}) copy-start(bf16[2048,256]{1,0:T(8,128)(2,1)} %get-tuple-element.110) | copy-start | bytes 3145732
  700.1 7.6 %copy-start.4 = (bf16[384,2048]{1,0:T(8,128)(2,1)S(1)}, bf16[384,2048]{1,0:T(8,128)(2,1)}, u32[]{:S(2)}) copy-start(bf16[384,2048]{1,0:T(8,128)(2,1)} %get-tuple-element.161) | copy-start | bytes 4718596
Sparse Core Ops, SparseCore 0:
  129.4 83.7 all-gather.4
  214.7 62.0 all-gather.6
  406.3 59.5 reduce-scatter.2
  472.8 110.0 reduce-scatter.4
